TPU v7x, 32 devices: a whole 2x2x4 slice. The times are simulated.
32 devices in a mesh: star: 4 (over y, x), tm: 8 (over z, core).
Axes of the slice: x: 2, y: 2, z: 4, core: 2. Of those that a mesh axis runs over, the one named last changes fastest.
Arguments:
- astro_coef: float32 [4, 5, 8192], P('star', None, 'tm'), may hold values from -1.5 to 1.5
- star_index: int32 [4, 8192], P('star', 'tm'), may hold values from 0 to 2047
- att_coef: float32 [4, 64, 64, 128], P('star', 'tm'), may hold values from -0.26516503 to 0.26516503
- att_start: int32 [4, 64], P('star', 'tm'), may hold values from 0 to 255, as said below
- inst_coef: float32 [4, 6, 8192], P('star', None, 'tm'), may hold values from -0.61237246 to 0.61237246
- inst_index: int32 [4, 6, 8192], P('star', None, 'tm'), may hold values from 0 to 1023
- observed: float32 [4, 8192], P('star', 'tm'), may hold values from -6 to 6
Outputs:
- solution_astro: float32 [5, 8192], P(None, ('star', 'tm'))
- solution_att: float32 [2048], P('tm')
- solution_inst: float32 [1024], replicated
Inputs may be any that keep to these rules, and one draw needn't show every extreme that they name: `att_start`: within each time range, block b starts between 32 * b and 32 * b + 31, so starts increase with the block; the last block of every range starts at 255, so its unknowns run into the next time range.
All inputs are finite; a program needn't handle non-finite values.
Results may differ from a plain program's by a relative error of at most 0.00021.
Values sent between devices are 32-bit elements; how exact they have to be, the bound alone decides.
No kernel may reach another device: no remote copies, remote signals or barrier semaphores. Data moves between devices by JAX's collectives and lax.ppermute only.
A program may use at most 64 MiB of HBM per device.

v0:
```python
import functools

import jax
import jax.numpy as jnp
from jax import lax
from jax.experimental import pallas as pl
from jax.experimental.pallas import tpu as pltpu
from jax.sharding import PartitionSpec as P

STARS_DEV = 2048
NINST = 1024
ITERS = 3
ATT_DEV = 256
LANES = 128

epsilon = 1e-06
STAR_COPIES = False
TM_COPIES = [False, False, False]
f32 = jnp.float32
bf16 = jnp.bfloat16
VMEM_LIMIT = 16 * 1024 * 1024


def halves(value):
    top = value.astype(bf16).astype(f32)
    return top, (value - top).astype(bf16).astype(f32)


def dot_lanes(left, right):
    return lax.dot_general(left, right, (((1,), (1,)), ((), ())), preferred_element_type=f32)


def dot_plain(left, right):
    return lax.dot_general(left, right, (((1,), (0,)), ((), ())), preferred_element_type=f32)


def lane_pick(row, lane_index):
    table = jnp.broadcast_to(row, lane_index.shape)
    return jnp.take_along_axis(table, lane_index, axis=1, mode="promise_in_bounds")


def table_pick(rows, index):
    high, low = index >> 7, index & (LANES - 1)
    total = jnp.zeros(index.shape, f32)
    for place, row in enumerate(rows):
        total = jnp.where(high == place, lane_pick(row, low), total)
    return total


def one_hot_low(index_row):
    shape = (LANES, LANES)
    low = jnp.broadcast_to(index_row & (LANES - 1), shape)
    hit = lax.broadcasted_iota(jnp.int32, shape, 0) == low
    return jnp.where(hit, 1.0, 0.0).astype(bf16)


def spread_high(index_row, value_row, count):
    shape = (count, LANES)
    high = jnp.broadcast_to(index_row >> 7, shape)
    hit = lax.broadcasted_iota(jnp.int32, shape, 0) == high
    return jnp.where(hit, jnp.broadcast_to(value_row, shape), 0.0)


def block_masks(blocks, width):
    shape = (blocks, LANES)
    row = lax.broadcasted_iota(jnp.int32, shape, 0)
    lane = lax.broadcasted_iota(jnp.int32, shape, 1)
    per_tile = LANES // width
    tiles = blocks // per_tile
    return [row == tile * per_tile + lane // width for tile in range(tiles)], row, lane


def inst_back(rows, coef_ref, index_ref, table_ref, spread_ref):
    slots, blocks = len(coef_ref), rows.shape[0]
    count = NINST // LANES
    for slot in range(slots):
        top, rest = halves(coef_ref[slot][...] * rows)
        index = index_ref[slot][...]
        for block in range(blocks):
            here = slice(block, block + 1)
            pieces = [spread_high(index[here], part[here], count) for part in (top, rest)]
            at = (slot * blocks + block) * LANES
            spread_ref[:, at : at + LANES] = jnp.concatenate(pieces, axis=0).astype(bf16)
    both = dot_lanes(spread_ref[...], table_ref[...])
    return both[:count] + both[count:]


def att_back(rows, att2, starts, width):
    blocks = rows.shape[0]
    size = att2.shape[0] // 2
    top, rest = halves(rows)
    both = dot_lanes(jnp.concatenate([top, rest], axis=0).astype(bf16), att2)
    both = both[:blocks] + both[blocks:]
    both = both[:, :size] + both[:, size:]
    masks, row, lane = block_masks(blocks, width)
    own = jnp.zeros((blocks, LANES), f32)
    for tile, mask in enumerate(masks):
        own = own + jnp.where(mask, both[:, tile * LANES : (tile + 1) * LANES], 0.0)
    shift = (row % (LANES // width)) * width
    out = []
    for tile in range((ATT_DEV + width + LANES - 1) // LANES):
        offset = lane + tile * LANES - starts
        inside = (offset >= 0) & (offset < width)
        picked = jnp.take_along_axis(
            own, jnp.where(inside, offset + shift, 0), axis=1, mode="promise_in_bounds"
        )
        out.append(jnp.sum(jnp.where(inside, picked, 0.0), axis=0, keepdims=True))
    return jnp.concatenate(out, axis=0)


def att_forward(att_rows, att2, starts, width):
    blocks = starts.shape[0]
    masks, row, lane = block_masks(blocks, width)
    tiles = [att_rows[tile : tile + 1] for tile in range(att_rows.shape[0])]
    window = table_pick(tiles, starts + lane % width)
    wide = jnp.concatenate([jnp.where(mask, window, 0.0) for mask in masks], axis=1)
    top, rest = halves(wide)
    left = jnp.concatenate([top, rest], axis=0).astype(bf16)
    both = dot_plain(jnp.concatenate([left, left], axis=1), att2)
    return both[:blocks] + both[blocks:]


def pack_places(slots, blocks, width):
    at = slots * 8
    return slice(0, at), slice(at, 2 * at), slice(2 * at, 2 * at + 8), slice(
        2 * at + 8, 2 * at + 8 + blocks * width
    )


def prepare_index(index_rows, starts, table_ref, ints_ref):
    count = index_rows.shape[0] // 8
    ints_ref[0 : count * 8] = index_rows
    ints_ref[count * 8 :] = starts
    for place in range(count * 8):
        table_ref[:, place * LANES : (place + 1) * LANES] = one_hot_low(
            index_rows[place : place + 1]
        )


def prepare_att(att, att2_ref):
    top = att.astype(bf16)
    att2_ref[...] = jnp.concatenate([top, (att - top.astype(f32)).astype(bf16)], axis=0)


def first_kernel(width, b_hbm, astro_hbm, star_hbm, att_hbm, starts_hbm, coef_hbm, index_hbm,
                 send_ref, pack_ref, table_ref, att2_ref, ints_ref,
                 b_ref, astro_ref, star_ref, starts_ref, coef_ref, index_ref,
                 spread_ref, sems):
    slots, blocks, _ = index_ref.shape
    comps = astro_ref.shape[0]
    places = pack_places(slots, blocks, width)
    pairs = [(index_hbm, index_ref), (starts_hbm, starts_ref), (att_hbm, pack_ref.at[places[3]]),
             (coef_hbm, coef_ref), (b_hbm, b_ref), (astro_hbm, astro_ref), (star_hbm, star_ref)]
    copies = [
        pltpu.make_async_copy(source, target, sems.at[place])
        for place, (source, target) in enumerate(pairs)
    ]
    for copy in copies:
        copy.start()
    for copy in copies[:2]:
        copy.wait()
    index = jnp.concatenate([index_ref[slot] for slot in range(slots)], axis=0)
    starts_row = jnp.broadcast_to(starts_ref[...].astype(f32), (blocks, blocks))
    diagonal = lax.broadcasted_iota(jnp.int32, (blocks, blocks), 0) == lax.broadcasted_iota(
        jnp.int32, (blocks, blocks), 1
    )
    starts = jnp.sum(jnp.where(diagonal, starts_row, 0.0), axis=1, keepdims=True)
    starts = jnp.broadcast_to(starts, (blocks, LANES))
    pack_ref[places[1]] = index.astype(f32)
    pack_ref[places[2]] = starts
    starts = starts.astype(jnp.int32)
    prepare_index(index, starts, table_ref, ints_ref)
    for copy in copies[2:]:
        copy.wait()
    prepare_att(pack_ref[places[3]], att2_ref)
    rows = b_ref[...]
    coefs = [coef_ref.at[slot] for slot in range(slots)]
    indices = [index_ref.at[slot] for slot in range(slots)]
    for slot in range(slots):
        pack_ref[slot * 8 : slot * 8 + 8] = coef_ref[slot]
    send_ref[0:8] = rows
    send_ref[8:16] = inst_back(rows, coefs, indices, table_ref, spread_ref)
    send_ref[16:19] = att_back(rows, att2_ref[...], starts, width)
    send_ref[19:20] = jnp.sum(rows * rows, axis=0, keepdims=True)
    send_ref[20:24] = jnp.zeros((4, LANES), f32)
    for comp in range(comps):
        send_ref[24 + comp * 8 : 32 + comp * 8] = astro_ref[comp]
    send_ref[24 + comps * 8 : 32 + comps * 8] = star_ref[...].astype(f32)


def prepare_kernel(slots, blocks, width, pack_ref, table_ref, att2_ref, ints_ref):
    places = pack_places(slots, blocks, width)
    index = pack_ref[places[1]].astype(jnp.int32)
    starts = pack_ref[places[2]].astype(jnp.int32)
    prepare_index(index, starts, table_ref, ints_ref)
    prepare_att(pack_ref[places[3]], att2_ref)


def put(ref, start, value):
    rows = slice(start, start + value.shape[0])
    if len(ref.shape) == 2:
        ref[rows] = value
    else:
        for copy in range(ref.shape[0]):
            ref[copy, rows] = value


def arrived(refs, count, here):
    if len(refs) == 1:
        return [refs[0].at[place] for place in range(count)], list(range(count))
    return list(refs), [here ^ gap for gap in range(count)]


def tree_sum(values):
    while len(values) > 1:
        values = [values[i] + values[i + 1] for i in range(0, len(values), 2)]
    return values[0]


def first_chip_kernel(count, *refs):
    ins, out_ref = refs[:count], refs[count]
    chip = lax.axis_index("tm") // 2
    extra = ins[0].shape[0] - 24
    base = 8 * count + 16
    for gap in range(count):
        where = chip ^ gap
        out_ref[pl.ds(pl.multiple_of(where * 8, 8), 8)] = ins[gap][0:8]
        out_ref[pl.ds(pl.multiple_of(base + where * 8, 8), 8)] = ins[gap][16:24]
        at = pl.multiple_of(base + 8 * count + where * extra, 8)
        out_ref[pl.ds(at, extra)] = ins[gap][24:]
    out_ref[8 * count : 8 * count + 8] = tree_sum([ref[8:16] for ref in ins])
    out_ref[8 * count + 8 : base] = tree_sum([ref[16:24] for ref in ins])


def group_rows(chip, count, mine, prev_row, after_row):
    half = lax.broadcasted_iota(jnp.int32, (1, LANES), 1) < 64
    first = mine[0:1] + jnp.where(half & (chip > 0), prev_row, 0.0)
    last = jnp.where(half & (chip < count - 1), mine[4:5] + after_row, 0.0)
    return [first, mine[1:4], last]


def chip_parts(core, own, other):
    low = jnp.where(core == 0, own, other)
    top = jnp.where(core == 0, other, own)
    return jnp.concatenate([low[0:2], low[2:3] + top[0:1], top[1:3]], axis=0)


def first_group_kernel(count, own_ref, other_ref, out_ref):
    me = lax.axis_index("tm")
    chip, core = me // 2, me % 2
    low = 8 * count
    base = low + 16

    def part(ref, where):
        where = jnp.clip(where, 0, count - 1)
        return ref[pl.ds(pl.multiple_of(base + where * 8, 8), 8)]

    def of_core(which, where):
        return jnp.where(core == which, part(own_ref, where), part(other_ref, where))

    mine = chip_parts(core, part(own_ref, chip)[0:3], part(other_ref, chip)[0:3])
    prev, after = of_core(1, chip - 1), of_core(0, chip + 1)
    scalars = own_ref[low + 8 : low + 16] + other_ref[low + 8 : low + 16]
    put(out_ref, 0, own_ref[low : low + 8] + other_ref[low : low + 8])
    att = group_rows(chip, count, mine, prev[2:3], after[0:1])
    put(out_ref, 8, jnp.concatenate(att + [scalars[3:6]], axis=0))


def group_kernel(count, *refs):
    *refs, rows_ref, out_ref = refs
    chip = lax.axis_index("tm") // 2
    ins, places = arrived(refs, count, chip)
    zero = jnp.zeros((8, LANES), f32)
    mine, prev, after = zero, zero, zero
    for ref, where in zip(ins, places):
        for half in range(2):
            at = (half * count + where) * 8
            at = at if isinstance(at, int) else pl.multiple_of(at, 8)
            rows_ref[pl.ds(at, 8)] = ref[half * 8 : half * 8 + 8]
        low = ref[24:32]
        mine = jnp.where(where == chip, low, mine)
        prev = jnp.where(where == chip - 1, low, prev)
        after = jnp.where(where == chip + 1, low, after)
    scalars = tree_sum([ref[24:32] for ref in ins])
    put(out_ref, 0, tree_sum([ref[16:24] for ref in ins]))
    att = group_rows(chip, count, mine, prev[4:5], after[0:1])
    put(out_ref, 8, jnp.concatenate(att + [scalars[5:8]], axis=0))


def astro_kernel(first, count, *refs):
    high = STARS_DEV // LANES
    if first:
        keep, (out_ref, table_ref, spread_ref) = refs[:2], refs[2:]
    else:
        keep, (table_ref, rows_ref, out_ref, spread_ref) = refs[:2], refs[2:]
    base = 16 * count + 16
    extra = (keep[0].shape[0] - base) // count
    comps = extra // 8 - 1
    long = 8 * LANES

    def one(place, totals):
        new = []
        for half in range(2):
            if first:
                rows = keep[half][pl.ds(pl.multiple_of(place * 8, 8), 8)]
            else:
                rows = rows_ref[pl.ds(pl.multiple_of((half * count + place) * 8, 8), 8)]
            packed = keep[half][pl.ds(pl.multiple_of(base + place * extra, 8), extra)]
            index = packed[comps * 8 :].astype(jnp.int32)
            at0 = pl.multiple_of((half * count + place) * long, long)
            split = [halves(packed[comp * 8 : comp * 8 + 8] * rows) for comp in range(comps)]
            for block in range(8):
                here = slice(block, block + 1)
                if first:
                    table_ref[:, pl.ds(at0 + block * LANES, LANES)] = one_hot_low(index[here])
                pieces = []
                for part in range(2):
                    for comp in range(comps):
                        pieces.append(spread_high(index[here], split[comp][part][here], high))
                spread_ref[half, :, block * LANES : (block + 1) * LANES] = jnp.concatenate(
                    pieces, axis=0
                ).astype(bf16)
            new.append(
                totals[half] + dot_lanes(spread_ref[half], table_ref[:, pl.ds(at0, long)])
            )
        return tuple(new)

    zero = jnp.zeros((2 * comps * high, LANES), f32)
    own, other = lax.fori_loop(0, count, one, (zero, zero))
    total = own + other
    out_ref[...] = total[: comps * high] + total[comps * high :]


def sum_kernel(count, *refs):
    ins, _ = arrived(refs[:-1], count, 0)
    put(refs[-1], 0, tree_sum([ref[...] for ref in ins]))


def lane_sum(row):
    return jnp.broadcast_to(jnp.sum(row, axis=1, keepdims=True), row.shape)


def next_bidiagonal(total, state):
    squares, mixed, size = (lane_sum(total[row : row + 1]) for row in (13, 14, 15))
    alpha2 = size + epsilon
    alpha = jnp.sqrt(alpha2)
    rest = jnp.maximum(squares / alpha2 - 2.0 * mixed + alpha2 * state[0:1], 0.0)
    beta2 = rest + epsilon
    return alpha, jnp.sqrt(beta2), rest / beta2


def step_kernel(step, width, slots, chips, star_count, *refs):
    keep, packs, tables, att2s, ints, sum_ref = refs[:2], refs[2:4], refs[4:6], refs[6:8], refs[8:10], refs[10]
    refs = refs[11:]
    if step > 0:
        state_ref, old_z_ref, old_g_ref, old_u_ref, old_s_ref = refs[:5]
        refs = refs[5:]
    gathered, refs = refs[:-7], refs[-7:]
    gathered, _ = arrived(gathered, star_count, 0)
    send_ref, state_out, z_ref, g_ref, u_ref, s_ref, spread_ref = refs
    me = lax.axis_index("tm")
    chip, core = me // 2, me % 2
    high = STARS_DEV // LANES
    comps = sum_ref.shape[0] // high
    blocks = 8
    total = tree_sum([ref[...] for ref in gathered])
    back = jnp.concatenate([sum_ref[...], total], axis=0)
    if step == 0:
        squares = lane_sum(total[13:14])
        beta2 = squares + epsilon
        beta = jnp.sqrt(beta2)
        at = pl.ds(pl.multiple_of(chip * 8, 8), 8)
        u = jnp.concatenate([ref[at] for ref in keep], axis=0) / beta
        g = back / beta
        z = g
        state_out[...] = jnp.concatenate(
            [squares / beta2, beta, jnp.zeros((14, LANES), f32)], axis=0
        )
    else:
        state = state_ref[...]
        alpha, beta, left2 = next_bidiagonal(total, state)
        u = (old_s_ref[...] / alpha - alpha * old_u_ref[...]) / beta
        g = (back / alpha - alpha * old_g_ref[...]) / beta
        z = g - (beta / alpha) * old_z_ref[...]
        pieces = [left2, state[1 : 1 + step], beta, jnp.zeros((7 - step, LANES), f32)]
        pieces += [state[9 : 8 + step]] if step > 1 else []
        pieces += [alpha, jnp.zeros((7 - step, LANES), f32)]
        state_out[...] = jnp.concatenate(pieces, axis=0)
    z_ref[...] = z
    g_ref[...] = g
    u_ref[...] = u
    base = comps * high
    inst_rows = z[base : base + 8]
    att_rows = z[base + 8 : base + 13]
    extra = 8 * comps + 8
    here = 16 * chips + 16 + chip * extra
    pieces = [inst_rows[place : place + 1] for place in range(8)]
    rows, insts, atts = [], [], []
    for half in range(2):
        starts = ints[half][slots * 8 :]
        own = jnp.where(core == half, att_rows[0:3], att_rows[2:5])
        part = att_forward(own, att2s[half][...], starts, width)
        packed = keep[half][pl.ds(pl.multiple_of(here, 8), extra)]
        star = packed[comps * 8 :].astype(jnp.int32)
        star_high, star_low = star >> 7, star & (LANES - 1)
        for comp in range(comps):
            picked = jnp.zeros((blocks, LANES), f32)
            for place in range(high):
                at = comp * high + place
                picked = jnp.where(star_high == place, lane_pick(z[at : at + 1], star_low), picked)
            part = part + packed[comp * 8 : comp * 8 + 8] * picked
        coefs = [packs[half].at[slot * 8 : slot * 8 + 8] for slot in range(slots)]
        indices = [ints[half].at[slot * 8 : slot * 8 + 8] for slot in range(slots)]
        for slot in range(slots):
            part = part + coefs[slot][...] * table_pick(pieces, indices[slot][...])
        rows.append(part)
        if step < ITERS - 1:
            insts.append(inst_back(part, coefs, indices, tables[half], spread_ref.at[half]))
            atts.append(att_back(part, att2s[half][...], starts, width))
    both = jnp.concatenate(rows, axis=0)
    s_ref[...] = both

    def squared(value):
        return jnp.sum(value * value, axis=0, keepdims=True)

    size = squared(z[:base]) * (1.0 / chips) + squared(att_rows[:4]) * (1.0 / star_count)
    size = size + squared(inst_rows) * (1.0 / (star_count * chips))
    mixed = [jnp.sum(rows[half] * u[half * 8 : half * 8 + 8], axis=0, keepdims=True) for half in range(2)]
    scalars = [squared(rows[0]) + squared(rows[1]), mixed[0] + mixed[1], size]
    if step == ITERS - 1:
        put(send_ref, 0, jnp.concatenate([jnp.zeros((5, LANES), f32)] + scalars, axis=0))
        return
    put(send_ref, 0, both)
    put(send_ref, 16, insts[0] + insts[1])
    put(send_ref, 24, jnp.concatenate([chip_parts(core, *atts)] + scalars, axis=0))


def last_kernel(comps, share, star_count, state_ref, *refs):
    gathered, refs = refs[: -ITERS - 3], refs[-ITERS - 3 :]
    gathered, _ = arrived(gathered, star_count, 0)
    z_refs = refs[:ITERS]
    astro_ref, att_ref, inst_ref = refs[ITERS:]
    high = STARS_DEV // LANES
    me = lax.axis_index("tm")
    total = tree_sum([ref[...] for ref in gathered])
    total = jnp.concatenate([jnp.zeros((8, LANES), f32), total], axis=0)
    state = state_ref[...]
    alpha, beta, _ = next_bidiagonal(total, state)
    betas = [state[1 + k : 2 + k] for k in range(ITERS)] + [beta]
    alphas = [state[9 + k : 10 + k] for k in range(ITERS - 1)] + [alpha]
    rho_bar, phi_bar = alphas[0], betas[0]
    weights = [jnp.zeros((1, LANES), f32)] * ITERS
    search = [jnp.zeros((1, LANES), f32)] * ITERS
    search[0] = 1.0 / alphas[0]
    for k in range(ITERS):
        rho = jnp.sqrt(rho_bar * rho_bar + betas[k + 1] * betas[k + 1])
        cosine, sine = rho_bar / rho, betas[k + 1] / rho
        phi = cosine * phi_bar
        phi_bar = sine * phi_bar
        weights = [x + phi / rho * w for x, w in zip(weights, search)]
        if k + 1 < ITERS:
            theta = sine * alphas[k + 1]
            rho_bar = -cosine * alphas[k + 1]
            search = [-(theta / rho) * w for w in search]
            search[k + 1] = 1.0 / alphas[k + 1]
    base = comps * high
    tiles = share // LANES

    def mix(read):
        total = weights[0] * read(z_refs[0])
        for k in range(1, ITERS):
            total = total + weights[k] * read(z_refs[k])
        return total

    for comp in range(comps):
        for tile in range(tiles):
            at = comp * high + me * tiles + tile
            astro_ref[comp : comp + 1, tile * LANES : (tile + 1) * LANES] = mix(
                lambda ref: ref[pl.ds(at, 1)]
            )
    inst_ref[...] = mix(lambda ref: ref[base : base + 8])
    rows = ATT_DEV // LANES
    att_ref[...] = mix(lambda ref: ref[pl.ds(base + 8 + (me % 2) * rows, rows)])


def call(kernel, name, out, args, scratch=(), space=pltpu.VMEM):
    vmem = pl.BlockSpec(memory_space=pltpu.VMEM)
    return pl.pallas_call(
        kernel,
        name=name,
        out_shape=[jax.ShapeDtypeStruct(shape, dtype) for shape, dtype in out],
        in_specs=[pl.BlockSpec(memory_space=space)] * len(args),
        out_specs=[vmem] * len(out),
        scratch_shapes=list(scratch),
        compiler_params=pltpu.CompilerParams(vmem_limit_bytes=VMEM_LIMIT),
    )(*args)


def exchange(value, axis, gaps):
    count = lax.axis_size(axis)
    if value.ndim == 3:
        members = [0] + list(gaps)
        groups = [[i ^ gap for gap in members] for i in range(count) if i == min(i ^ gap for gap in members)]
        return [lax.all_to_all(value, axis, 0, 0, axis_index_groups=groups if len(groups) > 1 else None)]
    return [value] + [
        lax.ppermute(value, axis, [(i, i ^ gap) for i in range(count)]) for gap in gaps
    ]


def rows_type(rows, copies=0):
    return ((copies, rows, LANES) if copies else (rows, LANES), f32)


def per_device(astro_coef, star_index, att_coef, att_start, inst_coef, inst_index, observed):
    tm_count, star_count = lax.axis_size("tm"), lax.axis_size("star")
    comps = astro_coef.shape[1]
    slots = inst_coef.shape[1]
    blocks, width, height = att_coef.shape[1:]
    share = STARS_DEV // tm_count
    high = STARS_DEV // LANES
    chips = tm_count // 2
    far = [2 * gap for gap in range(1, chips)]
    args = [
        observed.reshape(blocks, height),
        astro_coef.reshape(comps, blocks, height),
        star_index.reshape(blocks, height),
        att_coef.reshape(blocks * width, height),
        att_start,
        inst_coef.reshape(slots, blocks, height),
        inst_index.reshape(slots, blocks, height),
    ]
    long = slots * blocks * height
    extra = 8 * comps + 8
    spread = pltpu.VMEM((16, long), bf16)
    prepared = [((LANES, long), bf16), ((2 * blocks * width, height), bf16),
                ((8 * slots + 8, LANES), jnp.int32)]
    here = [pltpu.with_memory_space_constraint(arg, pltpu.HBM) for arg in args]
    send, pack, *mine = call(
        functools.partial(first_kernel, width),
        "first",
        [((24 + extra, LANES), f32), ((16 * slots + 8 + blocks * width, LANES), f32)] + prepared,
        here,
        [pltpu.VMEM(arg.shape, arg.dtype) for arg in args if arg is not args[3]]
        + [spread, pltpu.SemaphoreType.DMA((len(args),))],
        pl.ANY,
    )
    keep = star_table = state = z = g = u = rows = None
    kept = []
    group_type = rows_type(16)
    star_type = rows_type(16, STAR_COPIES and star_count)
    tm_copies = [TM_COPIES[step] and chips for step in range(ITERS)]
    for step in range(ITERS):
        wide = [pltpu.VMEM((2, 2 * comps * high, blocks * height), bf16)]
        sums_type = ((comps * high, LANES), f32)
        got = exchange(send, "tm", far)
        if step == 0:
            (gathered,) = call(
                functools.partial(first_chip_kernel, chips),
                "chip",
                [((16 * chips + 16 + chips * extra, LANES), f32)],
                got,
            )
            keep = exchange(gathered, "tm", [1])
            (group,) = call(
                functools.partial(first_group_kernel, chips), "group", [star_type], keep
            )
            group, late_pack = lax.optimization_barrier((group, pack))
            _, other_pack = exchange(late_pack, "tm", [1])
            theirs = call(
                functools.partial(prepare_kernel, slots, blocks, width),
                "prepare",
                prepared,
                [other_pack],
            )
            basics = [pack, other_pack] + [value for both in zip(mine, theirs) for value in both]
        else:
            all_rows, group = call(
                functools.partial(group_kernel, chips),
                "group",
                [rows_type(16 * chips), star_type],
                got,
            )
        across = exchange(group, "star", range(1, star_count))
        if step == 0:
            sums, star_table = call(
                functools.partial(astro_kernel, True, chips),
                "astro",
                [sums_type, ((LANES, tm_count * blocks * height), bf16)],
                keep,
                wide,
            )
        else:
            (sums,) = call(
                functools.partial(astro_kernel, False, chips),
                "astro",
                [sums_type],
                keep + [star_table, all_rows],
                wide,
            )
        tall = ((comps * high + 16, LANES), f32)
        pair = ((2 * blocks, height), f32)
        older = [] if step == 0 else [state, z, g, u, rows]
        send, state, z, g, u, rows = call(
            functools.partial(step_kernel, step, width, slots, chips, star_count),
            "step",
            [rows_type(32 if step < ITERS - 1 else 8, tm_copies[step]), group_type, tall, tall,
             pair, pair],
            keep + basics + [sums] + older + across,
            [pltpu.VMEM((2, 16, long), bf16)],
        )
        kept.append(z)
    (send,) = call(
        functools.partial(sum_kernel, chips),
        "sum",
        [rows_type(8, STAR_COPIES and star_count)],
        exchange(send, "tm", far),
    )
    across = exchange(send, "star", range(1, star_count))
    out_astro, out_att, out_inst = call(
        functools.partial(last_kernel, comps, share, star_count),
        "last",
        [((comps, share), f32), ((ATT_DEV // LANES, LANES), f32), ((NINST // LANES, LANES), f32)],
        [state] + across + kept,
    )
    return out_astro, out_att.reshape(-1), out_inst.reshape(-1)


def solution(mesh):
    return jax.shard_map(
        per_device,
        mesh=mesh,
        in_specs=(
            P("star", None, "tm"),
            P("star", "tm"),
            P("star", "tm", None, None),
            P("star", "tm"),
            P("star", None, "tm"),
            P("star", None, "tm"),
            P("star", "tm"),
        ),
        out_specs=(P(None, ("star", "tm")), P("tm"), P()),
        check_vma=False,
    )
```

profile of v0, /device:TPU:0, one launch (start us, length us, event | category | flops | bytes accessed | tf_op | source)
XLA Modules:
  0.0 64.3 jit_solution(18245626618845093412)
XLA Ops:
  0.6 1.9 %first.1 = (f32[72,128]{1,0:T(8,128)S(1)}, f32[616,128]{1,0:T(8,128)S(1)}, bf16[128,6144]{1,0:T(8,128)(2,1)S(1)}, bf16[1024,128]{1,0:T(8,128)(2,1)S(1)}, s32[56,128]{1,0:T(8,128)S(1)}) custom-call(f32[8,128]{1,0:T(8,128)} %bitcast.12, f32[5,8,128]{2,1,0:T(8,128)} %bitcast.11, s32[8,128]{1,0:T(8,128)} %bitcast.13, f32[512,128]{1,0:T(8,128)} %bitcast.8, ...), custom_call_target="tpu_custom_call" | custom-call | tf_op jit(solution)/shard_map/first/pallas_call | solution.py:488
  2.6 5.1 %collective-permute-start.2 = (f32[72,128]{1,0:T(8,128)S(1)}, f32[72,128]{1,0:T(8,128)S(1)}, u32[]{:S(2)}, u32[]{:S(2)}) collective-permute-start(f32[72,128]{1,0:T(8,128)S(1)} %get-tuple-element.37.refs_0_), channel_id=1, source_target_pairs={{0,6},{1,7},{2,4},{3,5},{4,2},{5,3},{6,0},{7,1},{8,14},{9,15},{10,... | collective-permute-start | bytes 110600 | tf_op jit(solution)/shard_map/ppermute | solution.py:506
  7.7 0.6 collective-permute-start
  8.3 1.3 %collective-permute-done.2.refs_3_ = f32[72,128]{1,0:T(8,128)S(1)} collective-permute-done((f32[72,128]{1,0:T(8,128)S(1)}, f32[72,128]{1,0:T(8,128)S(1)}, u32[]{:S(2)}, u32[]{:S(2)}) %collective-permute-start.2) | collective-permute-done | bytes 36896 | tf_op jit(solution)/shard_map/ppermute | solution.py:506
  9.6 2.9 %collective-permute-done.1.refs_2_ = f32[72,128]{1,0:T(8,128)S(1)} collective-permute-done((f32[72,128]{1,0:T(8,128)S(1)}, f32[72,128]{1,0:T(8,128)S(1)}, u32[]{:S(2)}, u32[]{:S(2)}) %collective-permute-start.1) | collective-permute-done | bytes 36896 | tf_op jit(solution)/shard_map/ppermute | solution.py:506
  12.7 1.3 %collective-permute-done.3.other_ref.refs_1_ = f32[272,128]{1,0:T(8,128)S(1)} collective-permute-done((f32[272,128]{1,0:T(8,128)S(1)}, f32[272,128]{1,0:T(8,128)S(1)}, u32[]{:S(2)}, u32[]{:S(2)}) %collective-permute-start.3) | collective-permute-done | bytes 139296 | tf_op jit(solution)/shard_map/ppermute | solution.py:506
  14.2 2.5 %collective-permute-start.7 = (f32[16,128]{1,0:T(8,128)S(1)}, f32[16,128]{1,0:T(8,128)S(1)}, u32[]{:S(2)}, u32[]{:S(2)}) collective-permute-start(f32[16,128]{1,0:T(8,128)S(1)} %group.3.refs_11_), channel_id=1, source_target_pairs={{0,24},{8,16},{16,8},{24,0},{1,25},{9,17},{17,9},{25,1},{2,26},{10... | collective-permute-start | bytes 24584 | tf_op jit(solution)/shard_map/ppermute | solution.py:506
  16.7 0.5 collective-permute-start.6
  17.2 0.5 collective-permute-start.5
  17.7 2.2 %astro.3 = (f32[80,128]{1,0:T(8,128)S(1)}, bf16[128,8192]{1,0:T(8,128)(2,1)S(1)}) custom-call(f32[272,128]{1,0:T(8,128)S(1)} %chip.1.own_ref.refs_0_, f32[272,128]{1,0:T(8,128)S(1)} %collective-permute-done.3.other_ref.refs_1_), custom_call_target="tpu_custom_call" | custom-call | tf_op jit(solution)/shard_map/astro/pallas_call | solution.py:488
  20.0 0.5 prepare.1
  20.9 1.6 %step.3 = (f32[32,128]{1,0:T(8,128)S(1)}, f32[16,128]{1,0:T(8,128)S(1)}, f32[96,128]{1,0:T(8,128)S(1)}, f32[96,128]{1,0:T(8,128)S(1)}, f32[16,128]{1,0:T(8,128)S(1)}, /*index=5*/f32[16,128]{1,0:T(8,128)S(1)}) custom-call(f32[272,128]{1,0:T(8,128)S(1)} %chip.1.own_ref.refs_0_, f32[272,128]{1,0:T(8,128)S(1)} %collective-permute-done.3.other_ref.refs_1_, ...), custom_call_target="tpu_custom_call" | custom-call | tf_op jit(solution)/shard_map/step/pallas_call | solution.py:488
  22.5 1.5 %collective-permute-start.10 = (f32[32,128]{1,0:T(8,128)S(1)}, f32[32,128]{1,0:T(8,128)S(1)}, u32[]{:S(2)}, u32[]{:S(2)}) collective-permute-start(f32[32,128]{1,0:T(8,128)S(1)} %get-tuple-element.49.refs_0_), channel_id=1, source_target_pairs={{0,6},{1,7},{2,4},{3,5},{4,2},{5,3},{6,0},{7,1},{8,14},{9,15},{10,... | collective-permute-start | bytes 49160 | tf_op jit(solution)/shard_map/ppermute | solution.py:506
  24.0 0.6 collective-permute-start.9
  24.6 2.3 %collective-permute-start.8 = (f32[32,128]{1,0:T(8,128)S(1)}, f32[32,128]{1,0:T(8,128)S(1)}, u32[]{:S(2)}, u32[]{:S(2)}) collective-permute-start(f32[32,128]{1,0:T(8,128)S(1)} %get-tuple-element.49.refs_0_), channel_id=1, source_target_pairs={{0,2},{1,3},{2,0},{3,1},{4,6},{5,7},{6,4},{7,5},{8,10},{9,11},{10,... | collective-permute-start | bytes 49160 | tf_op jit(solution)/shard_map/ppermute | solution.py:506
  26.9 1.1 %collective-permute-done.10.refs_3_ = f32[32,128]{1,0:T(8,128)S(1)} collective-permute-done((f32[32,128]{1,0:T(8,128)S(1)}, f32[32,128]{1,0:T(8,128)S(1)}, u32[]{:S(2)}, u32[]{:S(2)}) %collective-permute-start.10) | collective-permute-done | bytes 16416 | tf_op jit(solution)/shard_map/ppermute | solution.py:506
  28.1 0.6 collective-permute-done.9.refs_2_
  28.8 2.2 %collective-permute-start.13 = (f32[16,128]{1,0:T(8,128)S(1)}, f32[16,128]{1,0:T(8,128)S(1)}, u32[]{:S(2)}, u32[]{:S(2)}) collective-permute-start(f32[16,128]{1,0:T(8,128)S(1)} %get-tuple-element.56.refs_16_), channel_id=1, source_target_pairs={{0,24},{8,16},{16,8},{24,0},{1,25},{9,17},{17,9},{25,1},{2,26},{10... | collective-permute-start | bytes 24584 | tf_op jit(solution)/shard_map/ppermute | solution.py:506
  31.0 0.5 collective-permute-start.12
  31.5 0.9 %collective-permute-start.11 = (f32[16,128]{1,0:T(8,128)S(1)}, f32[16,128]{1,0:T(8,128)S(1)}, u32[]{:S(2)}, u32[]{:S(2)}) collective-permute-start(f32[16,128]{1,0:T(8,128)S(1)} %get-tuple-element.56.refs_16_), channel_id=1, source_target_pairs={{0,8},{8,0},{16,24},{24,16},{1,9},{9,1},{17,25},{25,17},{2,10},{10... | collective-permute-start | bytes 24584 | tf_op jit(solution)/shard_map/ppermute | solution.py:506
  32.4 1.5 %astro.4.refs_10_ = f32[80,128]{1,0:T(8,128)S(1)} custom-call(f32[272,128]{1,0:T(8,128)S(1)} %chip.1.own_ref.refs_0_, f32[272,128]{1,0:T(8,128)S(1)} %collective-permute-done.3.other_ref.refs_1_, bf16[128,8192]{1,0:T(8,128)(2,1)S(1)} %get-tuple-element.46.refs_2_, f32[64,128]{1,0:T(8,128)S(1)} %get-tuple-element.50.refs_3_), custom_call_target="tpu_custom_call" | custom-call | tf_op jit(solution)/shard_map/astro/pallas_call | solution.py:488
  33.9 0.7 %collective-permute-done.12.refs_18_ = f32[16,128]{1,0:T(8,128)S(1)} collective-permute-done((f32[16,128]{1,0:T(8,128)S(1)}, f32[16,128]{1,0:T(8,128)S(1)}, u32[]{:S(2)}, u32[]{:S(2)}) %collective-permute-start.12) | collective-permute-done | bytes 8224 | tf_op jit(solution)/shard_map/ppermute | solution.py:506
  34.7 0.5 collective-permute-done.11.refs_17_
  35.2 1.6 %step.4 = (f32[32,128]{1,0:T(8,128)S(1)}, f32[16,128]{1,0:T(8,128)S(1)}, f32[96,128]{1,0:T(8,128)S(1)}, f32[96,128]{1,0:T(8,128)S(1)}, f32[16,128]{1,0:T(8,128)S(1)}, /*index=5*/f32[16,128]{1,0:T(8,128)S(1)}) custom-call(f32[272,128]{1,0:T(8,128)S(1)} %chip.1.own_ref.refs_0_, f32[272,128]{1,0:T(8,128)S(1)} %collective-permute-done.3.other_ref.refs_1_, ...), custom_call_target="tpu_custom_call" | custom-call | tf_op jit(solution)/shard_map/step/pallas_call | solution.py:488
  36.8 2.5 %collective-permute-start.16 = (f32[32,128]{1,0:T(8,128)S(1)}, f32[32,128]{1,0:T(8,128)S(1)}, u32[]{:S(2)}, u32[]{:S(2)}) collective-permute-start(f32[32,128]{1,0:T(8,128)S(1)} %get-tuple-element.57.refs_0_), channel_id=1, source_target_pairs={{0,6},{1,7},{2,4},{3,5},{4,2},{5,3},{6,0},{7,1},{8,14},{9,15},{10,... | collective-permute-start | bytes 49160 | tf_op jit(solution)/shard_map/ppermute | solution.py:506
  39.3 0.9 %collective-permute-start.15 = (f32[32,128]{1,0:T(8,128)S(1)}, f32[32,128]{1,0:T(8,128)S(1)}, u32[]{:S(2)}, u32[]{:S(2)}) collective-permute-start(f32[32,128]{1,0:T(8,128)S(1)} %get-tuple-element.57.refs_0_), channel_id=1, source_target_pairs={{0,4},{1,5},{2,6},{3,7},{4,0},{5,1},{6,2},{7,3},{8,12},{9,13},{10,... | collective-permute-start | bytes 49160 | tf_op jit(solution)/shard_map/ppermute | solution.py:506
  40.2 1.1 %collective-permute-start.14 = (f32[32,128]{1,0:T(8,128)S(1)}, f32[32,128]{1,0:T(8,128)S(1)}, u32[]{:S(2)}, u32[]{:S(2)}) collective-permute-start(f32[32,128]{1,0:T(8,128)S(1)} %get-tuple-element.57.refs_0_), channel_id=1, source_target_pairs={{0,2},{1,3},{2,0},{3,1},{4,6},{5,7},{6,4},{7,5},{8,10},{9,11},{10,... | collective-permute-start | bytes 49160 | tf_op jit(solution)/shard_map/ppermute | solution.py:506
  41.3 1.1 %collective-permute-done.16.refs_3_ = f32[32,128]{1,0:T(8,128)S(1)} collective-permute-done((f32[32,128]{1,0:T(8,128)S(1)}, f32[32,128]{1,0:T(8,128)S(1)}, u32[]{:S(2)}, u32[]{:S(2)}) %collective-permute-start.16) | collective-permute-done | bytes 16416 | tf_op jit(solution)/shard_map/ppermute | solution.py:506
  42.4 1.5 %collective-permute-done.15.refs_2_ = f32[32,128]{1,0:T(8,128)S(1)} collective-permute-done((f32[32,128]{1,0:T(8,128)S(1)}, f32[32,128]{1,0:T(8,128)S(1)}, u32[]{:S(2)}, u32[]{:S(2)}) %collective-permute-start.15) | collective-permute-done | bytes 16416 | tf_op jit(solution)/shard_map/ppermute | solution.py:506
  44.1 1.9 %collective-permute-start.19 = (f32[16,128]{1,0:T(8,128)S(1)}, f32[16,128]{1,0:T(8,128)S(1)}, u32[]{:S(2)}, u32[]{:S(2)}) collective-permute-start(f32[16,128]{1,0:T(8,128)S(1)} %get-tuple-element.64.refs_16_), channel_id=1, source_target_pairs={{0,24},{8,16},{16,8},{24,0},{1,25},{9,17},{17,9},{25,1},{2,26},{10... | collective-permute-start | bytes 24584 | tf_op jit(solution)/shard_map/ppermute | solution.py:506
  46.0 0.5 collective-permute-start.18
  46.5 1.2 %collective-permute-start.17 = (f32[16,128]{1,0:T(8,128)S(1)}, f32[16,128]{1,0:T(8,128)S(1)}, u32[]{:S(2)}, u32[]{:S(2)}) collective-permute-start(f32[16,128]{1,0:T(8,128)S(1)} %get-tuple-element.64.refs_16_), channel_id=1, source_target_pairs={{0,8},{8,0},{16,24},{24,16},{1,9},{9,1},{17,25},{25,17},{2,10},{10... | collective-permute-start | bytes 24584 | tf_op jit(solution)/shard_map/ppermute | solution.py:506
  47.7 1.5 %astro.5.refs_10_ = f32[80,128]{1,0:T(8,128)S(1)} custom-call(f32[272,128]{1,0:T(8,128)S(1)} %chip.1.own_ref.refs_0_, f32[272,128]{1,0:T(8,128)S(1)} %collective-permute-done.3.other_ref.refs_1_, bf16[128,8192]{1,0:T(8,128)(2,1)S(1)} %get-tuple-element.46.refs_2_, f32[64,128]{1,0:T(8,128)S(1)} %get-tuple-element.58.refs_3_), custom_call_target="tpu_custom_call" | custom-call | tf_op jit(solution)/shard_map/astro/pallas_call | solution.py:488
  49.2 0.5 collective-permute-done.18.refs_18_
  49.7 0.5 collective-permute-done.17.refs_17_
  50.2 1.1 %step.5 = (f32[8,128]{1,0:T(8,128)S(1)}, f32[16,128]{1,0:T(8,128)S(1)}, f32[96,128]{1,0:T(8,128)S(1)}, f32[96,128]{1,0:T(8,128)}, f32[16,128]{1,0:T(8,128)}, /*index=5*/f32[16,128]{1,0:T(8,128)}) custom-call(f32[272,128]{1,0:T(8,128)S(1)} %chip.1.own_ref.refs_0_, f32[272,128]{1,0:T(8,128)S(1)} %collective-permute-done.3.other_ref.refs_1_, ...), custom_call_target="tpu_custom_call" | custom-call | tf_op jit(solution)/shard_map/step/pallas_call | solution.py:488
  51.3 1.4 %collective-permute-start.22 = (f32[8,128]{1,0:T(8,128)S(1)}, f32[8,128]{1,0:T(8,128)S(1)}, u32[]{:S(2)}, u32[]{:S(2)}) collective-permute-start(f32[8,128]{1,0:T(8,128)S(1)} %get-tuple-element.66.refs_0_), channel_id=1, source_target_pairs={{0,6},{1,7},{2,4},{3,5},{4,2},{5,3},{6,0},{7,1},{8,14},{9,15},{10,... | collective-permute-start | bytes 12296 | tf_op jit(solution)/shard_map/ppermute | solution.py:506
  52.7 1.0 %collective-permute-start.21 = (f32[8,128]{1,0:T(8,128)S(1)}, f32[8,128]{1,0:T(8,128)S(1)}, u32[]{:S(2)}, u32[]{:S(2)}) collective-permute-start(f32[8,128]{1,0:T(8,128)S(1)} %get-tuple-element.66.refs_0_), channel_id=1, source_target_pairs={{0,4},{1,5},{2,6},{3,7},{4,0},{5,1},{6,2},{7,3},{8,12},{9,13},{10,... | collective-permute-start | bytes 12296 | tf_op jit(solution)/shard_map/ppermute | solution.py:506
  53.7 2.0 %collective-permute-start.20 = (f32[8,128]{1,0:T(8,128)S(1)}, f32[8,128]{1,0:T(8,128)S(1)}, u32[]{:S(2)}, u32[]{:S(2)}) collective-permute-start(f32[8,128]{1,0:T(8,128)S(1)} %get-tuple-element.66.refs_0_), channel_id=1, source_target_pairs={{0,2},{1,3},{2,0},{3,1},{4,6},{5,7},{6,4},{7,5},{8,10},{9,11},{10,... | collective-permute-start | bytes 12296 | tf_op jit(solution)/shard_map/ppermute | solution.py:506
  55.7 1.0 %collective-permute-done.22.refs_3_ = f32[8,128]{1,0:T(8,128)S(1)} collective-permute-done((f32[8,128]{1,0:T(8,128)S(1)}, f32[8,128]{1,0:T(8,128)S(1)}, u32[]{:S(2)}, u32[]{:S(2)}) %collective-permute-start.22) | collective-permute-done | bytes 4128 | tf_op jit(solution)/shard_map/ppermute | solution.py:506
  56.7 0.5 collective-permute-done.21.refs_2_
  57.3 2.1 %collective-permute-start.25 = (f32[8,128]{1,0:T(8,128)S(1)}, f32[8,128]{1,0:T(8,128)S(1)}, u32[]{:S(2)}, u32[]{:S(2)}) collective-permute-start(f32[8,128]{1,0:T(8,128)S(1)} %sum.1.refs_0_), channel_id=1, source_target_pairs={{0,24},{8,16},{16,8},{24,0},{1,25},{9,17},{17,9},{25,1},{2,26},{10... | collective-permute-start | bytes 12296 | tf_op jit(solution)/shard_map/ppermute | solution.py:506
  59.4 0.5 collective-permute-start.24
  59.9 0.9 %collective-permute-start.23 = (f32[8,128]{1,0:T(8,128)S(1)}, f32[8,128]{1,0:T(8,128)S(1)}, u32[]{:S(2)}, u32[]{:S(2)}) collective-permute-start(f32[8,128]{1,0:T(8,128)S(1)} %sum.1.refs_0_), channel_id=1, source_target_pairs={{0,8},{8,0},{16,24},{24,16},{1,9},{9,1},{17,25},{25,17},{2,10},{10... | collective-permute-start | bytes 12296 | tf_op jit(solution)/shard_map/ppermute | solution.py:506
  60.8 1.0 %collective-permute-done.25.refs_3_ = f32[8,128]{1,0:T(8,128)S(1)} collective-permute-done((f32[8,128]{1,0:T(8,128)S(1)}, f32[8,128]{1,0:T(8,128)S(1)}, u32[]{:S(2)}, u32[]{:S(2)}) %collective-permute-start.25) | collective-permute-done | bytes 4128 | tf_op jit(solution)/shard_map/ppermute | solution.py:506
  61.8 1.2 %collective-permute-done.24.refs_2_ = f32[8,128]{1,0:T(8,128)S(1)} collective-permute-done((f32[8,128]{1,0:T(8,128)S(1)}, f32[8,128]{1,0:T(8,128)S(1)}, u32[]{:S(2)}, u32[]{:S(2)}) %collective-permute-start.24) | collective-permute-done | bytes 4128 | tf_op jit(solution)/shard_map/ppermute | solution.py:506
  63.0 0.5 collective-permute-done.23.refs_1_
  63.5 0.7 %last.1 = (f32[5,256]{1,0:T(8,128)}, f32[2,128]{1,0:T(2,128)}, f32[8,128]{1,0:T(8,128)}) custom-call(f32[16,128]{1,0:T(8,128)S(1)} %get-tuple-element.65.state_ref, f32[8,128]{1,0:T(8,128)S(1)} %sum.1.refs_0_, f32[8,128]{1,0:T(8,128)S(1)} %collective-permute-done.23.refs_1_, f32[8,128]{1,0:T(8,128)S(1)} %collective-permute-done.24.refs_2_, ...), custom_call_target="tpu_custom_call" | custom-call | tf_op jit(solution)/shard_map/last/pallas_call | solution.py:488
  (18 shorter events, 1.1 us)
Async XLA Ops:
  2.6 7.1 %collective-permute-start.2 = (f32[72,128]{1,0:T(8,128)S(1)}, f32[72,128]{1,0:T(8,128)S(1)}, u32[]{:S(2)}, u32[]{:S(2)}) collective-permute-start(f32[72,128]{1,0:T(8,128)S(1)} %get-tuple-element.37.refs_0_), channel_id=1, source_target_pairs={{0,6},{1,7},{2,4},{3,5},{4,2},{5,3},{6,0},{7,1},{8,14},{9,15},{10,... | collective-permute-start | bytes 110600 | tf_op jit(solution)/shard_map/ppermute | solution.py:506
  7.7 4.9 %collective-permute-start.1 = (f32[72,128]{1,0:T(8,128)S(1)}, f32[72,128]{1,0:T(8,128)S(1)}, u32[]{:S(2)}, u32[]{:S(2)}) collective-permute-start(f32[72,128]{1,0:T(8,128)S(1)} %get-tuple-element.37.refs_0_), channel_id=1, source_target_pairs={{0,4},{1,5},{2,6},{3,7},{4,0},{5,1},{6,2},{7,3},{8,12},{9,13},{10,... | collective-permute-start | bytes 110600 | tf_op jit(solution)/shard_map/ppermute | solution.py:506
  7.7 4.9 %collective-permute-start = (f32[72,128]{1,0:T(8,128)S(1)}, f32[72,128]{1,0:T(8,128)S(1)}, u32[]{:S(2)}, u32[]{:S(2)}) collective-permute-start(f32[72,128]{1,0:T(8,128)S(1)} %get-tuple-element.37.refs_0_), channel_id=1, source_target_pairs={{0,2},{1,3},{2,0},{3,1},{4,6},{5,7},{6,4},{7,5},{8,10},{9,11},{10,... | collective-permute-start | bytes 110600 | tf_op jit(solution)/shard_map/ppermute | solution.py:506
  12.6 1.4 %collective-permute-start.3 = (f32[272,128]{1,0:T(8,128)S(1)}, f32[272,128]{1,0:T(8,128)S(1)}, u32[]{:S(2)}, u32[]{:S(2)}) collective-permute-start(f32[272,128]{1,0:T(8,128)S(1)} %chip.1.own_ref.refs_0_), channel_id=1, source_target_pairs={{0,1},{1,0},{2,3},{3,2},{4,5},{5,4},{6,7},{7,6},{8,9},{9,8},{10,11... | collective-permute-start | bytes 417800 | tf_op jit(solution)/shard_map/ppermute | solution.py:506
  14.0 5.9 %collective-permute-start.4 = (f32[616,128]{1,0:T(8,128)S(1)}, f32[616,128]{1,0:T(8,128)S(1)}, u32[]{:S(2)}, u32[]{:S(2)}) collective-permute-start(f32[616,128]{1,0:T(8,128)S(1)} %get-tuple-element.39.refs_2_), channel_id=1, source_target_pairs={{0,1},{1,0},{2,3},{3,2},{4,5},{5,4},{6,7},{7,6},{8,9},{9,8},{10,11... | collective-permute-start | bytes 946184 | tf_op jit(solution)/shard_map/ppermute | solution.py:506
  14.2 6.2 %collective-permute-start.7 = (f32[16,128]{1,0:T(8,128)S(1)}, f32[16,128]{1,0:T(8,128)S(1)}, u32[]{:S(2)}, u32[]{:S(2)}) collective-permute-start(f32[16,128]{1,0:T(8,128)S(1)} %group.3.refs_11_), channel_id=1, source_target_pairs={{0,24},{8,16},{16,8},{24,0},{1,25},{9,17},{17,9},{25,1},{2,26},{10... | collective-permute-start | bytes 24584 | tf_op jit(solution)/shard_map/ppermute | solution.py:506
  16.7 3.8 %collective-permute-start.6 = (f32[16,128]{1,0:T(8,128)S(1)}, f32[16,128]{1,0:T(8,128)S(1)}, u32[]{:S(2)}, u32[]{:S(2)}) collective-permute-start(f32[16,128]{1,0:T(8,128)S(1)} %group.3.refs_11_), channel_id=1, source_target_pairs={{0,16},{8,24},{16,0},{24,8},{1,17},{9,25},{17,1},{25,9},{2,18},{10... | collective-permute-start | bytes 24584 | tf_op jit(solution)/shard_map/ppermute | solution.py:506
  17.2 3.7 %collective-permute-start.5 = (f32[16,128]{1,0:T(8,128)S(1)}, f32[16,128]{1,0:T(8,128)S(1)}, u32[]{:S(2)}, u32[]{:S(2)}) collective-permute-start(f32[16,128]{1,0:T(8,128)S(1)} %group.3.refs_11_), channel_id=1, source_target_pairs={{0,8},{8,0},{16,24},{24,16},{1,9},{9,1},{17,25},{25,17},{2,10},{10... | collective-permute-start | bytes 24584 | tf_op jit(solution)/shard_map/ppermute | solution.py:506
  22.5 5.6 %collective-permute-start.10 = (f32[32,128]{1,0:T(8,128)S(1)}, f32[32,128]{1,0:T(8,128)S(1)}, u32[]{:S(2)}, u32[]{:S(2)}) collective-permute-start(f32[32,128]{1,0:T(8,128)S(1)} %get-tuple-element.49.refs_0_), channel_id=1, source_target_pairs={{0,6},{1,7},{2,4},{3,5},{4,2},{5,3},{6,0},{7,1},{8,14},{9,15},{10,... | collective-permute-start | bytes 49160 | tf_op jit(solution)/shard_map/ppermute | solution.py:506
  24.0 4.7 %collective-permute-start.9 = (f32[32,128]{1,0:T(8,128)S(1)}, f32[32,128]{1,0:T(8,128)S(1)}, u32[]{:S(2)}, u32[]{:S(2)}) collective-permute-start(f32[32,128]{1,0:T(8,128)S(1)} %get-tuple-element.49.refs_0_), channel_id=1, source_target_pairs={{0,4},{1,5},{2,6},{3,7},{4,0},{5,1},{6,2},{7,3},{8,12},{9,13},{10,... | collective-permute-start | bytes 49160 | tf_op jit(solution)/shard_map/ppermute | solution.py:506
  24.6 4.2 %collective-permute-start.8 = (f32[32,128]{1,0:T(8,128)S(1)}, f32[32,128]{1,0:T(8,128)S(1)}, u32[]{:S(2)}, u32[]{:S(2)}) collective-permute-start(f32[32,128]{1,0:T(8,128)S(1)} %get-tuple-element.49.refs_0_), channel_id=1, source_target_pairs={{0,2},{1,3},{2,0},{3,1},{4,6},{5,7},{6,4},{7,5},{8,10},{9,11},{10,... | collective-permute-start | bytes 49160 | tf_op jit(solution)/shard_map/ppermute | solution.py:506
  28.8 5.1 %collective-permute-start.13 = (f32[16,128]{1,0:T(8,128)S(1)}, f32[16,128]{1,0:T(8,128)S(1)}, u32[]{:S(2)}, u32[]{:S(2)}) collective-permute-start(f32[16,128]{1,0:T(8,128)S(1)} %get-tuple-element.56.refs_16_), channel_id=1, source_target_pairs={{0,24},{8,16},{16,8},{24,0},{1,25},{9,17},{17,9},{25,1},{2,26},{10... | collective-permute-start | bytes 24584 | tf_op jit(solution)/shard_map/ppermute | solution.py:506
  31.0 3.7 %collective-permute-start.12 = (f32[16,128]{1,0:T(8,128)S(1)}, f32[16,128]{1,0:T(8,128)S(1)}, u32[]{:S(2)}, u32[]{:S(2)}) collective-permute-start(f32[16,128]{1,0:T(8,128)S(1)} %get-tuple-element.56.refs_16_), channel_id=1, source_target_pairs={{0,16},{8,24},{16,0},{24,8},{1,17},{9,25},{17,1},{25,9},{2,18},{10... | collective-permute-start | bytes 24584 | tf_op jit(solution)/shard_map/ppermute | solution.py:506
  31.5 3.7 %collective-permute-start.11 = (f32[16,128]{1,0:T(8,128)S(1)}, f32[16,128]{1,0:T(8,128)S(1)}, u32[]{:S(2)}, u32[]{:S(2)}) collective-permute-start(f32[16,128]{1,0:T(8,128)S(1)} %get-tuple-element.56.refs_16_), channel_id=1, source_target_pairs={{0,8},{8,0},{16,24},{24,16},{1,9},{9,1},{17,25},{25,17},{2,10},{10... | collective-permute-start | bytes 24584 | tf_op jit(solution)/shard_map/ppermute | solution.py:506
  36.8 5.6 %collective-permute-start.16 = (f32[32,128]{1,0:T(8,128)S(1)}, f32[32,128]{1,0:T(8,128)S(1)}, u32[]{:S(2)}, u32[]{:S(2)}) collective-permute-start(f32[32,128]{1,0:T(8,128)S(1)} %get-tuple-element.57.refs_0_), channel_id=1, source_target_pairs={{0,6},{1,7},{2,4},{3,5},{4,2},{5,3},{6,0},{7,1},{8,14},{9,15},{10,... | collective-permute-start | bytes 49160 | tf_op jit(solution)/shard_map/ppermute | solution.py:506
  39.3 4.7 %collective-permute-start.15 = (f32[32,128]{1,0:T(8,128)S(1)}, f32[32,128]{1,0:T(8,128)S(1)}, u32[]{:S(2)}, u32[]{:S(2)}) collective-permute-start(f32[32,128]{1,0:T(8,128)S(1)} %get-tuple-element.57.refs_0_), channel_id=1, source_target_pairs={{0,4},{1,5},{2,6},{3,7},{4,0},{5,1},{6,2},{7,3},{8,12},{9,13},{10,... | collective-permute-start | bytes 49160 | tf_op jit(solution)/shard_map/ppermute | solution.py:506
  40.2 3.9 %collective-permute-start.14 = (f32[32,128]{1,0:T(8,128)S(1)}, f32[32,128]{1,0:T(8,128)S(1)}, u32[]{:S(2)}, u32[]{:S(2)}) collective-permute-start(f32[32,128]{1,0:T(8,128)S(1)} %get-tuple-element.57.refs_0_), channel_id=1, source_target_pairs={{0,2},{1,3},{2,0},{3,1},{4,6},{5,7},{6,4},{7,5},{8,10},{9,11},{10,... | collective-permute-start | bytes 49160 | tf_op jit(solution)/shard_map/ppermute | solution.py:506
  44.1 5.1 %collective-permute-start.19 = (f32[16,128]{1,0:T(8,128)S(1)}, f32[16,128]{1,0:T(8,128)S(1)}, u32[]{:S(2)}, u32[]{:S(2)}) collective-permute-start(f32[16,128]{1,0:T(8,128)S(1)} %get-tuple-element.64.refs_16_), channel_id=1, source_target_pairs={{0,24},{8,16},{16,8},{24,0},{1,25},{9,17},{17,9},{25,1},{2,26},{10... | collective-permute-start | bytes 24584 | tf_op jit(solution)/shard_map/ppermute | solution.py:506
  46.0 3.7 %collective-permute-start.18 = (f32[16,128]{1,0:T(8,128)S(1)}, f32[16,128]{1,0:T(8,128)S(1)}, u32[]{:S(2)}, u32[]{:S(2)}) collective-permute-start(f32[16,128]{1,0:T(8,128)S(1)} %get-tuple-element.64.refs_16_), channel_id=1, source_target_pairs={{0,16},{8,24},{16,0},{24,8},{1,17},{9,25},{17,1},{25,9},{2,18},{10... | collective-permute-start | bytes 24584 | tf_op jit(solution)/shard_map/ppermute | solution.py:506
  46.5 3.7 %collective-permute-start.17 = (f32[16,128]{1,0:T(8,128)S(1)}, f32[16,128]{1,0:T(8,128)S(1)}, u32[]{:S(2)}, u32[]{:S(2)}) collective-permute-start(f32[16,128]{1,0:T(8,128)S(1)} %get-tuple-element.64.refs_16_), channel_id=1, source_target_pairs={{0,8},{8,0},{16,24},{24,16},{1,9},{9,1},{17,25},{25,17},{2,10},{10... | collective-permute-start | bytes 24584 | tf_op jit(solution)/shard_map/ppermute | solution.py:506
  51.3 5.4 %collective-permute-start.22 = (f32[8,128]{1,0:T(8,128)S(1)}, f32[8,128]{1,0:T(8,128)S(1)}, u32[]{:S(2)}, u32[]{:S(2)}) collective-permute-start(f32[8,128]{1,0:T(8,128)S(1)} %get-tuple-element.66.refs_0_), channel_id=1, source_target_pairs={{0,6},{1,7},{2,4},{3,5},{4,2},{5,3},{6,0},{7,1},{8,14},{9,15},{10,... | collective-permute-start | bytes 12296 | tf_op jit(solution)/shard_map/ppermute | solution.py:506
  52.7 4.5 %collective-permute-start.21 = (f32[8,128]{1,0:T(8,128)S(1)}, f32[8,128]{1,0:T(8,128)S(1)}, u32[]{:S(2)}, u32[]{:S(2)}) collective-permute-start(f32[8,128]{1,0:T(8,128)S(1)} %get-tuple-element.66.refs_0_), channel_id=1, source_target_pairs={{0,4},{1,5},{2,6},{3,7},{4,0},{5,1},{6,2},{7,3},{8,12},{9,13},{10,... | collective-permute-start | bytes 12296 | tf_op jit(solution)/shard_map/ppermute | solution.py:506
  53.7 3.6 %collective-permute-start.20 = (f32[8,128]{1,0:T(8,128)S(1)}, f32[8,128]{1,0:T(8,128)S(1)}, u32[]{:S(2)}, u32[]{:S(2)}) collective-permute-start(f32[8,128]{1,0:T(8,128)S(1)} %get-tuple-element.66.refs_0_), channel_id=1, source_target_pairs={{0,2},{1,3},{2,0},{3,1},{4,6},{5,7},{6,4},{7,5},{8,10},{9,11},{10,... | collective-permute-start | bytes 12296 | tf_op jit(solution)/shard_map/ppermute | solution.py:506
  57.3 4.5 %collective-permute-start.25 = (f32[8,128]{1,0:T(8,128)S(1)}, f32[8,128]{1,0:T(8,128)S(1)}, u32[]{:S(2)}, u32[]{:S(2)}) collective-permute-start(f32[8,128]{1,0:T(8,128)S(1)} %sum.1.refs_0_), channel_id=1, source_target_pairs={{0,24},{8,16},{16,8},{24,0},{1,25},{9,17},{17,9},{25,1},{2,26},{10... | collective-permute-start | bytes 12296 | tf_op jit(solution)/shard_map/ppermute | solution.py:506
  59.4 3.6 %collective-permute-start.24 = (f32[8,128]{1,0:T(8,128)S(1)}, f32[8,128]{1,0:T(8,128)S(1)}, u32[]{:S(2)}, u32[]{:S(2)}) collective-permute-start(f32[8,128]{1,0:T(8,128)S(1)} %sum.1.refs_0_), channel_id=1, source_target_pairs={{0,16},{8,24},{16,0},{24,8},{1,17},{9,25},{17,1},{25,9},{2,18},{10... | collective-permute-start | bytes 12296 | tf_op jit(solution)/shard_map/ppermute | solution.py:506
  59.9 3.6 %collective-permute-start.23 = (f32[8,128]{1,0:T(8,128)S(1)}, f32[8,128]{1,0:T(8,128)S(1)}, u32[]{:S(2)}, u32[]{:S(2)}) collective-permute-start(f32[8,128]{1,0:T(8,128)S(1)} %sum.1.refs_0_), channel_id=1, source_target_pairs={{0,8},{8,0},{16,24},{24,16},{1,9},{9,1},{17,25},{25,17},{2,10},{10... | collective-permute-start | bytes 12296 | tf_op jit(solution)/shard_map/ppermute | solution.py:506
where the time goes:
time: 64.4 us; the launch traced here: 64.3 us
  starting transfers between devices  33.4 us (52%)
  waiting for transfers between devices  17.2 us (27%)
  Pallas kernels  12.8 us (20%)
  between operations  0.76 us (1%)
    ppermute x26, starting transfers between devices, exchange(): lax.ppermute(value, axis, [(i, i ^ gap) for i in range(count)])  33.4 us
    ppermute x26, waiting for transfers between devices, exchange(): lax.ppermute(value, axis, [(i, i ^ gap) for i in range(count)])  17.2 us
    pallas_call x14, Pallas kernels, call(): pl.pallas_call(kernel, name=name, out_shape=[jax.ShapeDtypeStruct(shape,...  12.8 us
  transfers between devices with their start and end apart: 26, of which 20 were waited for; matrix products, arithmetic and copies ran while one was open for 0% of the time, Pallas kernels for 9%

commit v1 on v0

--- a/solution.py
+++ b/solution.py
@@ -14,8 +14,6 @@
 LANES = 128
 
 epsilon = 1e-06
-STAR_COPIES = False
-TM_COPIES = [False, False, False]
 f32 = jnp.float32
 bf16 = jnp.bfloat16
 VMEM_LIMIT = 16 * 1024 * 1024
@@ -196,19 +194,11 @@
     prepare_att(pack_ref[places[3]], att2_ref)
 
 
-def put(ref, start, value):
-    rows = slice(start, start + value.shape[0])
-    if len(ref.shape) == 2:
-        ref[rows] = value
-    else:
-        for copy in range(ref.shape[0]):
-            ref[copy, rows] = value
-
-
-def arrived(refs, count, here):
-    if len(refs) == 1:
-        return [refs[0].at[place] for place in range(count)], list(range(count))
-    return list(refs), [here ^ gap for gap in range(count)]
+def places_of(here, core, count):
+    out = [here, here ^ 1]
+    for pair in range(2, count, 2):
+        out += [here ^ (pair + 1 - core), here ^ (pair + core)]
+    return out
 
 
 def tree_sum(values):
@@ -261,30 +251,30 @@
     mine = chip_parts(core, part(own_ref, chip)[0:3], part(other_ref, chip)[0:3])
     prev, after = of_core(1, chip - 1), of_core(0, chip + 1)
     scalars = own_ref[low + 8 : low + 16] + other_ref[low + 8 : low + 16]
-    put(out_ref, 0, own_ref[low : low + 8] + other_ref[low : low + 8])
+    out_ref[0:8] = own_ref[low : low + 8] + other_ref[low : low + 8]
     att = group_rows(chip, count, mine, prev[2:3], after[0:1])
-    put(out_ref, 8, jnp.concatenate(att + [scalars[3:6]], axis=0))
+    out_ref[8:16] = jnp.concatenate(att + [scalars[3:6]], axis=0)
 
 
 def group_kernel(count, *refs):
-    *refs, rows_ref, out_ref = refs
-    chip = lax.axis_index("tm") // 2
-    ins, places = arrived(refs, count, chip)
+    *ins, rows_ref, out_ref = refs
+    me = lax.axis_index("tm")
+    chip = me // 2
+    places = places_of(chip, me % 2, count)
     zero = jnp.zeros((8, LANES), f32)
     mine, prev, after = zero, zero, zero
     for ref, where in zip(ins, places):
         for half in range(2):
-            at = (half * count + where) * 8
-            at = at if isinstance(at, int) else pl.multiple_of(at, 8)
+            at = pl.multiple_of((half * count + where) * 8, 8)
             rows_ref[pl.ds(at, 8)] = ref[half * 8 : half * 8 + 8]
         low = ref[24:32]
         mine = jnp.where(where == chip, low, mine)
         prev = jnp.where(where == chip - 1, low, prev)
         after = jnp.where(where == chip + 1, low, after)
     scalars = tree_sum([ref[24:32] for ref in ins])
-    put(out_ref, 0, tree_sum([ref[16:24] for ref in ins]))
+    out_ref[0:8] = tree_sum([ref[16:24] for ref in ins])
     att = group_rows(chip, count, mine, prev[4:5], after[0:1])
-    put(out_ref, 8, jnp.concatenate(att + [scalars[5:8]], axis=0))
+    out_ref[8:16] = jnp.concatenate(att + [scalars[5:8]], axis=0)
 
 
 def astro_kernel(first, count, *refs):
@@ -297,6 +287,7 @@
     extra = (keep[0].shape[0] - base) // count
     comps = extra // 8 - 1
     long = 8 * LANES
+    core = lax.axis_index("tm") % 2
 
     def one(place, totals):
         new = []
@@ -304,7 +295,8 @@
             if first:
                 rows = keep[half][pl.ds(pl.multiple_of(place * 8, 8), 8)]
             else:
-                rows = rows_ref[pl.ds(pl.multiple_of((half * count + place) * 8, 8), 8)]
+                at = ((half ^ core) * count + place) * 8
+                rows = rows_ref[pl.ds(pl.multiple_of(at, 8), 8)]
             packed = keep[half][pl.ds(pl.multiple_of(base + place * extra, 8), extra)]
             index = packed[comps * 8 :].astype(jnp.int32)
             at0 = pl.multiple_of((half * count + place) * long, long)
@@ -331,9 +323,8 @@
     out_ref[...] = total[: comps * high] + total[comps * high :]
 
 
-def sum_kernel(count, *refs):
-    ins, _ = arrived(refs[:-1], count, 0)
-    put(refs[-1], 0, tree_sum([ref[...] for ref in ins]))
+def sum_kernel(*refs):
+    refs[-1][...] = tree_sum([ref[...] for ref in refs[:-1]])
 
 
 def lane_sum(row):
@@ -356,7 +347,6 @@
         state_ref, old_z_ref, old_g_ref, old_u_ref, old_s_ref = refs[:5]
         refs = refs[5:]
     gathered, refs = refs[:-7], refs[-7:]
-    gathered, _ = arrived(gathered, star_count, 0)
     send_ref, state_out, z_ref, g_ref, u_ref, s_ref, spread_ref = refs
     me = lax.axis_index("tm")
     chip, core = me // 2, me % 2
@@ -428,16 +418,15 @@
     mixed = [jnp.sum(rows[half] * u[half * 8 : half * 8 + 8], axis=0, keepdims=True) for half in range(2)]
     scalars = [squared(rows[0]) + squared(rows[1]), mixed[0] + mixed[1], size]
     if step == ITERS - 1:
-        put(send_ref, 0, jnp.concatenate([jnp.zeros((5, LANES), f32)] + scalars, axis=0))
+        send_ref[...] = (jnp.concatenate([jnp.zeros((5, LANES), f32)] + scalars, axis=0))
         return
-    put(send_ref, 0, both)
-    put(send_ref, 16, insts[0] + insts[1])
-    put(send_ref, 24, jnp.concatenate([chip_parts(core, *atts)] + scalars, axis=0))
+    send_ref[0:16] = jnp.where(core == 0, both, jnp.concatenate(rows[::-1], axis=0))
+    send_ref[16:24] = insts[0] + insts[1]
+    send_ref[24:32] = jnp.concatenate([chip_parts(core, *atts)] + scalars, axis=0)
 
 
 def last_kernel(comps, share, star_count, state_ref, *refs):
     gathered, refs = refs[: -ITERS - 3], refs[-ITERS - 3 :]
-    gathered, _ = arrived(gathered, star_count, 0)
     z_refs = refs[:ITERS]
     astro_ref, att_ref, inst_ref = refs[ITERS:]
     high = STARS_DEV // LANES
@@ -496,19 +485,34 @@
     )(*args)
 
 
-def exchange(value, axis, gaps):
+def direct(value, axis, gaps):
     count = lax.axis_size(axis)
-    if value.ndim == 3:
-        members = [0] + list(gaps)
-        groups = [[i ^ gap for gap in members] for i in range(count) if i == min(i ^ gap for gap in members)]
-        return [lax.all_to_all(value, axis, 0, 0, axis_index_groups=groups if len(groups) > 1 else None)]
     return [value] + [
         lax.ppermute(value, axis, [(i, i ^ gap) for i in range(count)]) for gap in gaps
     ]
 
 
-def rows_type(rows, copies=0):
-    return ((copies, rows, LANES) if copies else (rows, LANES), f32)
+def exchange(value, axis):
+    tm_count, star_count = lax.axis_size("tm"), lax.axis_size("star")
+    count = star_count if axis == "star" else tm_count // 2
+    both = ("star", "tm")
+    got = []
+    for pair in range(2, count, 2):
+        steps = []
+        for star in range(star_count):
+            for tm in range(tm_count):
+                gap = pair + 1 - tm % 2
+                far = (star ^ gap, tm) if axis == "star" else (star, tm ^ (2 * gap))
+                steps.append((star * tm_count + tm, far[0] * tm_count + far[1]))
+        got.append(lax.ppermute(value, both, steps))
+    near = direct(value, axis, [1 if axis == "star" else 2])
+    for value in got:
+        near += direct(value, "tm", [1])
+    return near
+
+
+def rows_type(rows):
+    return ((rows, LANES), f32)
 
 
 def per_device(astro_coef, star_index, att_coef, att_start, inst_coef, inst_index, observed):
@@ -547,12 +551,10 @@
     keep = star_table = state = z = g = u = rows = None
     kept = []
     group_type = rows_type(16)
-    star_type = rows_type(16, STAR_COPIES and star_count)
-    tm_copies = [TM_COPIES[step] and chips for step in range(ITERS)]
     for step in range(ITERS):
         wide = [pltpu.VMEM((2, 2 * comps * high, blocks * height), bf16)]
         sums_type = ((comps * high, LANES), f32)
-        got = exchange(send, "tm", far)
+        got = exchange(send, "tm") if step else direct(send, "tm", far)
         if step == 0:
             (gathered,) = call(
                 functools.partial(first_chip_kernel, chips),
@@ -560,12 +562,12 @@
                 [((16 * chips + 16 + chips * extra, LANES), f32)],
                 got,
             )
-            keep = exchange(gathered, "tm", [1])
+            keep = direct(gathered, "tm", [1])
             (group,) = call(
-                functools.partial(first_group_kernel, chips), "group", [star_type], keep
+                functools.partial(first_group_kernel, chips), "group", [group_type], keep
             )
             group, late_pack = lax.optimization_barrier((group, pack))
-            _, other_pack = exchange(late_pack, "tm", [1])
+            _, other_pack = direct(late_pack, "tm", [1])
             theirs = call(
                 functools.partial(prepare_kernel, slots, blocks, width),
                 "prepare",
@@ -577,10 +579,10 @@
             all_rows, group = call(
                 functools.partial(group_kernel, chips),
                 "group",
-                [rows_type(16 * chips), star_type],
+                [rows_type(16 * chips), group_type],
                 got,
             )
-        across = exchange(group, "star", range(1, star_count))
+        across = exchange(group, "star")
         if step == 0:
             sums, star_table = call(
                 functools.partial(astro_kernel, True, chips),
@@ -603,19 +605,13 @@
         send, state, z, g, u, rows = call(
             functools.partial(step_kernel, step, width, slots, chips, star_count),
             "step",
-            [rows_type(32 if step < ITERS - 1 else 8, tm_copies[step]), group_type, tall, tall,
-             pair, pair],
+            [rows_type(32 if step < ITERS - 1 else 8), group_type, tall, tall, pair, pair],
             keep + basics + [sums] + older + across,
             [pltpu.VMEM((2, 16, long), bf16)],
         )
         kept.append(z)
-    (send,) = call(
-        functools.partial(sum_kernel, chips),
-        "sum",
-        [rows_type(8, STAR_COPIES and star_count)],
-        exchange(send, "tm", far),
-    )
-    across = exchange(send, "star", range(1, star_count))
+    (send,) = call(sum_kernel, "sum", [rows_type(8)], exchange(send, "tm"))
+    across = exchange(send, "star")
     out_astro, out_att, out_inst = call(
         functools.partial(last_kernel, comps, share, star_count),
         "last",

time: 64.4 us -> 65.4 us (1.016)
  waiting for transfers between devices: 17.2 us -> 27.8 us
  starting transfers between devices: 33.4 us -> 23.9 us
    ppermute x26, waiting for transfers between devices: 17.2 us -> 27.8 us  [the longest x7 17.1 us: exchange(): got.append(lax.ppermute(value, both, steps))]
    ppermute x26, starting transfers between devices: 33.4 us -> 23.9 us  [the longest x7 14.5 us: exchange(): got.append(lax.ppermute(value, both, steps))]
  transfers between devices with their start and end apart: 26 -> 26, of which waited for: 20 -> 15; matrix products, arithmetic and copies ran while one was open for 0% -> 0% of each run, Pallas kernels for 9% -> 9%
where the time goes in v1:
time: 65.4 us; the launch traced here: 65.2 us
  waiting for transfers between devices  27.8 us (43%)
  starting transfers between devices  23.9 us (37%)
  Pallas kernels  12.8 us (20%)
  between operations  0.75 us (1%)
    ppermute x7, waiting for transfers between devices, exchange(): got.append(lax.ppermute(value, both, steps))  17.1 us
    ppermute x7, starting transfers between devices, exchange(): got.append(lax.ppermute(value, both, steps))  14.5 us
    pallas_call x14, Pallas kernels, call(): pl.pallas_call(kernel, name=name, out_shape=[jax.ShapeDtypeStruct(shape,...  12.8 us
    ppermute x19, waiting for transfers between devices, direct(): lax.ppermute(value, axis, [(i, i ^ gap) for i in range(count)])  10.7 us
    ppermute x19, starting transfers between devices, direct(): lax.ppermute(value, axis, [(i, i ^ gap) for i in range(count)])  9.35 us
  transfers between devices with their start and end apart: 26, of which 15 were waited for; matrix products, arithmetic and copies ran while one was open for 0% of the time, Pallas kernels for 9%

profile of v1, /device:TPU:0, one launch (start us, length us, event | category | flops | bytes accessed | tf_op | source)
XLA Modules:
  0.0 65.2 jit_solution(800680608506553327)
XLA Ops:
  0.6 1.9 %first.1 = (f32[72,128]{1,0:T(8,128)S(1)}, f32[616,128]{1,0:T(8,128)S(1)}, bf16[128,6144]{1,0:T(8,128)(2,1)S(1)}, bf16[1024,128]{1,0:T(8,128)(2,1)S(1)}, s32[56,128]{1,0:T(8,128)S(1)}) custom-call(f32[8,128]{1,0:T(8,128)} %bitcast.12, f32[5,8,128]{2,1,0:T(8,128)} %bitcast.11, s32[8,128]{1,0:T(8,128)} %bitcast.13, f32[512,128]{1,0:T(8,128)} %bitcast.8, ...), custom_call_target="tpu_custom_call" | custom-call | tf_op jit(solution)/shard_map/first/pallas_call | solution.py:477
  2.6 5.1 %collective-permute-start.2 = (f32[72,128]{1,0:T(8,128)S(1)}, f32[72,128]{1,0:T(8,128)S(1)}, u32[]{:S(2)}, u32[]{:S(2)}) collective-permute-start(f32[72,128]{1,0:T(8,128)S(1)} %get-tuple-element.37.refs_0_), channel_id=1, source_target_pairs={{0,6},{1,7},{2,4},{3,5},{4,2},{5,3},{6,0},{7,1},{8,14},{9,15},{10,... | collective-permute-start | bytes 110600 | tf_op jit(solution)/shard_map/ppermute | solution.py:491
  7.7 0.6 collective-permute-start
  8.3 1.3 %collective-permute-done.2.refs_3_ = f32[72,128]{1,0:T(8,128)S(1)} collective-permute-done((f32[72,128]{1,0:T(8,128)S(1)}, f32[72,128]{1,0:T(8,128)S(1)}, u32[]{:S(2)}, u32[]{:S(2)}) %collective-permute-start.2) | collective-permute-done | bytes 36896 | tf_op jit(solution)/shard_map/ppermute | solution.py:491
  9.6 2.9 %collective-permute-done.1.refs_2_ = f32[72,128]{1,0:T(8,128)S(1)} collective-permute-done((f32[72,128]{1,0:T(8,128)S(1)}, f32[72,128]{1,0:T(8,128)S(1)}, u32[]{:S(2)}, u32[]{:S(2)}) %collective-permute-start.1) | collective-permute-done | bytes 36896 | tf_op jit(solution)/shard_map/ppermute | solution.py:491
  12.5 0.0 collective-permute-done.refs_1_
  12.6 0.1 collective-permute-start.3
  12.7 1.3 %collective-permute-done.3.other_ref.refs_1_ = f32[272,128]{1,0:T(8,128)S(1)} collective-permute-done((f32[272,128]{1,0:T(8,128)S(1)}, f32[272,128]{1,0:T(8,128)S(1)}, u32[]{:S(2)}, u32[]{:S(2)}) %collective-permute-start.3) | collective-permute-done | bytes 139296 | tf_op jit(solution)/shard_map/ppermute | solution.py:491
  14.0 0.2 collective-permute-start.4
  14.2 2.4 %collective-permute-start.6 = (f32[16,128]{1,0:T(8,128)S(1)}, f32[16,128]{1,0:T(8,128)S(1)}, u32[]{:S(2)}, u32[]{:S(2)}) collective-permute-start(f32[16,128]{1,0:T(8,128)S(1)} %group.3.refs_11_), channel_id=1, source_target_pairs={{0,24},{1,17},{2,26},{3,19},{4,28},{5,21},{6,30},{7,23},{8,16},{9,... | collective-permute-start | bytes 24584 | tf_op jit(solution)/shard_map/ppermute | solution.py:507
  16.7 0.5 collective-permute-start.5
  17.2 1.6 %collective-permute-done.6.refs_13_ = f32[16,128]{1,0:T(8,128)S(1)} collective-permute-done((f32[16,128]{1,0:T(8,128)S(1)}, f32[16,128]{1,0:T(8,128)S(1)}, u32[]{:S(2)}, u32[]{:S(2)}) %collective-permute-start.6) | collective-permute-done | bytes 8224 | tf_op jit(solution)/shard_map/ppermute | solution.py:507
  18.8 0.0 collective-permute-start.7
  18.8 2.2 %astro.3 = (f32[80,128]{1,0:T(8,128)S(1)}, bf16[128,8192]{1,0:T(8,128)(2,1)S(1)}) custom-call(f32[272,128]{1,0:T(8,128)S(1)} %chip.1.own_ref.refs_0_, f32[272,128]{1,0:T(8,128)S(1)} %collective-permute-done.3.other_ref.refs_1_), custom_call_target="tpu_custom_call" | custom-call | tf_op jit(solution)/shard_map/astro/pallas_call | solution.py:477
  21.0 0.0 collective-permute-done.4.pack_ref.refs_3_
  21.0 0.5 prepare.1
  21.5 0.0 collective-permute-done.7.refs_14_
  21.5 1.6 %step.3 = (f32[32,128]{1,0:T(8,128)S(1)}, f32[16,128]{1,0:T(8,128)S(1)}, f32[96,128]{1,0:T(8,128)S(1)}, f32[96,128]{1,0:T(8,128)S(1)}, f32[16,128]{1,0:T(8,128)S(1)}, /*index=5*/f32[16,128]{1,0:T(8,128)S(1)}) custom-call(f32[272,128]{1,0:T(8,128)S(1)} %chip.1.own_ref.refs_0_, f32[272,128]{1,0:T(8,128)S(1)} %collective-permute-done.3.other_ref.refs_1_, ...), custom_call_target="tpu_custom_call" | custom-call | tf_op jit(solution)/shard_map/step/pallas_call | solution.py:477
  23.2 1.5 %collective-permute-start.9 = (f32[32,128]{1,0:T(8,128)S(1)}, f32[32,128]{1,0:T(8,128)S(1)}, u32[]{:S(2)}, u32[]{:S(2)}) collective-permute-start(f32[32,128]{1,0:T(8,128)S(1)} %get-tuple-element.49.refs_0_), channel_id=1, source_target_pairs={{0,6},{1,5},{2,4},{3,7},{4,2},{5,1},{6,0},{7,3},{8,14},{9,13},{10,... | collective-permute-start | bytes 49160 | tf_op jit(solution)/shard_map/ppermute | solution.py:507
  24.7 1.1 %collective-permute-start.8 = (f32[32,128]{1,0:T(8,128)S(1)}, f32[32,128]{1,0:T(8,128)S(1)}, u32[]{:S(2)}, u32[]{:S(2)}) collective-permute-start(f32[32,128]{1,0:T(8,128)S(1)} %get-tuple-element.49.refs_0_), channel_id=1, source_target_pairs={{0,2},{1,3},{2,0},{3,1},{4,6},{5,7},{6,4},{7,5},{8,10},{9,11},{10,... | collective-permute-start | bytes 49160 | tf_op jit(solution)/shard_map/ppermute | solution.py:491
  25.8 2.9 %collective-permute-done.9.refs_2_ = f32[32,128]{1,0:T(8,128)S(1)} collective-permute-done((f32[32,128]{1,0:T(8,128)S(1)}, f32[32,128]{1,0:T(8,128)S(1)}, u32[]{:S(2)}, u32[]{:S(2)}) %collective-permute-start.9) | collective-permute-done | bytes 16416 | tf_op jit(solution)/shard_map/ppermute | solution.py:507
  28.8 0.0 collective-permute-start.10
  28.8 0.0 collective-permute-done.8.refs_1_
  28.8 1.2 %collective-permute-done.10.refs_3_ = f32[32,128]{1,0:T(8,128)S(1)} collective-permute-done((f32[32,128]{1,0:T(8,128)S(1)}, f32[32,128]{1,0:T(8,128)S(1)}, u32[]{:S(2)}, u32[]{:S(2)}) %collective-permute-start.10) | collective-permute-done | bytes 16416 | tf_op jit(solution)/shard_map/ppermute | solution.py:491
  30.0 2.5 %collective-permute-start.12 = (f32[16,128]{1,0:T(8,128)S(1)}, f32[16,128]{1,0:T(8,128)S(1)}, u32[]{:S(2)}, u32[]{:S(2)}) collective-permute-start(f32[16,128]{1,0:T(8,128)S(1)} %get-tuple-element.56.refs_16_), channel_id=1, source_target_pairs={{0,24},{1,17},{2,26},{3,19},{4,28},{5,21},{6,30},{7,23},{8,16},{9,... | collective-permute-start | bytes 24584 | tf_op jit(solution)/shard_map/ppermute | solution.py:507
  32.5 0.5 collective-permute-start.11
  33.0 1.6 %collective-permute-done.12.refs_18_ = f32[16,128]{1,0:T(8,128)S(1)} collective-permute-done((f32[16,128]{1,0:T(8,128)S(1)}, f32[16,128]{1,0:T(8,128)S(1)}, u32[]{:S(2)}, u32[]{:S(2)}) %collective-permute-start.12) | collective-permute-done | bytes 8224 | tf_op jit(solution)/shard_map/ppermute | solution.py:507
  34.6 1.5 %astro.4.refs_10_ = f32[80,128]{1,0:T(8,128)S(1)} custom-call(f32[272,128]{1,0:T(8,128)S(1)} %chip.1.own_ref.refs_0_, f32[272,128]{1,0:T(8,128)S(1)} %collective-permute-done.3.other_ref.refs_1_, bf16[128,8192]{1,0:T(8,128)(2,1)S(1)} %get-tuple-element.46.refs_2_, f32[64,128]{1,0:T(8,128)S(1)} %get-tuple-element.50.refs_3_), custom_call_target="tpu_custom_call" | custom-call | tf_op jit(solution)/shard_map/astro/pallas_call | solution.py:477
  36.1 0.1 collective-permute-done.11.refs_17_
  36.2 0.0 collective-permute-done.13.refs_19_
  36.2 1.6 %step.4 = (f32[32,128]{1,0:T(8,128)S(1)}, f32[16,128]{1,0:T(8,128)S(1)}, f32[96,128]{1,0:T(8,128)S(1)}, f32[96,128]{1,0:T(8,128)S(1)}, f32[16,128]{1,0:T(8,128)S(1)}, /*index=5*/f32[16,128]{1,0:T(8,128)S(1)}) custom-call(f32[272,128]{1,0:T(8,128)S(1)} %chip.1.own_ref.refs_0_, f32[272,128]{1,0:T(8,128)S(1)} %collective-permute-done.3.other_ref.refs_1_, ...), custom_call_target="tpu_custom_call" | custom-call | tf_op jit(solution)/shard_map/step/pallas_call | solution.py:477
  37.8 1.6 %collective-permute-start.15 = (f32[32,128]{1,0:T(8,128)S(1)}, f32[32,128]{1,0:T(8,128)S(1)}, u32[]{:S(2)}, u32[]{:S(2)}) collective-permute-start(f32[32,128]{1,0:T(8,128)S(1)} %get-tuple-element.57.refs_0_), channel_id=1, source_target_pairs={{0,6},{1,5},{2,4},{3,7},{4,2},{5,1},{6,0},{7,3},{8,14},{9,13},{10,... | collective-permute-start | bytes 49160 | tf_op jit(solution)/shard_map/ppermute | solution.py:507
  39.4 4.0 %collective-permute-done.15.refs_2_ = f32[32,128]{1,0:T(8,128)S(1)} collective-permute-done((f32[32,128]{1,0:T(8,128)S(1)}, f32[32,128]{1,0:T(8,128)S(1)}, u32[]{:S(2)}, u32[]{:S(2)}) %collective-permute-start.15) | collective-permute-done | bytes 16416 | tf_op jit(solution)/shard_map/ppermute | solution.py:507
  43.4 1.2 %collective-permute-done.16.refs_3_ = f32[32,128]{1,0:T(8,128)S(1)} collective-permute-done((f32[32,128]{1,0:T(8,128)S(1)}, f32[32,128]{1,0:T(8,128)S(1)}, u32[]{:S(2)}, u32[]{:S(2)}) %collective-permute-start.16) | collective-permute-done | bytes 16416 | tf_op jit(solution)/shard_map/ppermute | solution.py:491
  44.6 2.5 %collective-permute-start.18 = (f32[16,128]{1,0:T(8,128)S(1)}, f32[16,128]{1,0:T(8,128)S(1)}, u32[]{:S(2)}, u32[]{:S(2)}) collective-permute-start(f32[16,128]{1,0:T(8,128)S(1)} %get-tuple-element.64.refs_16_), channel_id=1, source_target_pairs={{0,24},{1,17},{2,26},{3,19},{4,28},{5,21},{6,30},{7,23},{8,16},{9,... | collective-permute-start | bytes 24584 | tf_op jit(solution)/shard_map/ppermute | solution.py:507
  47.1 0.5 collective-permute-start.17
  47.6 1.6 %collective-permute-done.18.refs_18_ = f32[16,128]{1,0:T(8,128)S(1)} collective-permute-done((f32[16,128]{1,0:T(8,128)S(1)}, f32[16,128]{1,0:T(8,128)S(1)}, u32[]{:S(2)}, u32[]{:S(2)}) %collective-permute-start.18) | collective-permute-done | bytes 8224 | tf_op jit(solution)/shard_map/ppermute | solution.py:507
  49.2 1.5 %astro.5.refs_10_ = f32[80,128]{1,0:T(8,128)S(1)} custom-call(f32[272,128]{1,0:T(8,128)S(1)} %chip.1.own_ref.refs_0_, f32[272,128]{1,0:T(8,128)S(1)} %collective-permute-done.3.other_ref.refs_1_, bf16[128,8192]{1,0:T(8,128)(2,1)S(1)} %get-tuple-element.46.refs_2_, f32[64,128]{1,0:T(8,128)S(1)} %get-tuple-element.58.refs_3_), custom_call_target="tpu_custom_call" | custom-call | tf_op jit(solution)/shard_map/astro/pallas_call | solution.py:477
  50.7 0.0 collective-permute-done.17.refs_17_
  50.7 1.1 %step.5 = (f32[8,128]{1,0:T(8,128)S(1)}, f32[16,128]{1,0:T(8,128)S(1)}, f32[96,128]{1,0:T(8,128)S(1)}, f32[96,128]{1,0:T(8,128)}, f32[16,128]{1,0:T(8,128)}, /*index=5*/f32[16,128]{1,0:T(8,128)}) custom-call(f32[272,128]{1,0:T(8,128)S(1)} %chip.1.own_ref.refs_0_, f32[272,128]{1,0:T(8,128)S(1)} %collective-permute-done.3.other_ref.refs_1_, ...), custom_call_target="tpu_custom_call" | custom-call | tf_op jit(solution)/shard_map/step/pallas_call | solution.py:477
  51.9 1.5 %collective-permute-start.21 = (f32[8,128]{1,0:T(8,128)S(1)}, f32[8,128]{1,0:T(8,128)S(1)}, u32[]{:S(2)}, u32[]{:S(2)}) collective-permute-start(f32[8,128]{1,0:T(8,128)S(1)} %get-tuple-element.66.refs_0_), channel_id=1, source_target_pairs={{0,6},{1,5},{2,4},{3,7},{4,2},{5,1},{6,0},{7,3},{8,14},{9,13},{10,... | collective-permute-start | bytes 12296 | tf_op jit(solution)/shard_map/ppermute | solution.py:507
  53.4 3.9 %collective-permute-done.21.refs_2_ = f32[8,128]{1,0:T(8,128)S(1)} collective-permute-done((f32[8,128]{1,0:T(8,128)S(1)}, f32[8,128]{1,0:T(8,128)S(1)}, u32[]{:S(2)}, u32[]{:S(2)}) %collective-permute-start.21) | collective-permute-done | bytes 4128 | tf_op jit(solution)/shard_map/ppermute | solution.py:507
  57.3 1.2 %collective-permute-done.22.refs_3_ = f32[8,128]{1,0:T(8,128)S(1)} collective-permute-done((f32[8,128]{1,0:T(8,128)S(1)}, f32[8,128]{1,0:T(8,128)S(1)}, u32[]{:S(2)}, u32[]{:S(2)}) %collective-permute-start.22) | collective-permute-done | bytes 4128 | tf_op jit(solution)/shard_map/ppermute | solution.py:491
  58.5 2.4 %collective-permute-start.24 = (f32[8,128]{1,0:T(8,128)S(1)}, f32[8,128]{1,0:T(8,128)S(1)}, u32[]{:S(2)}, u32[]{:S(2)}) collective-permute-start(f32[8,128]{1,0:T(8,128)S(1)} %sum.1.refs_0_), channel_id=1, source_target_pairs={{0,24},{1,17},{2,26},{3,19},{4,28},{5,21},{6,30},{7,23},{8,16},{9,... | collective-permute-start | bytes 12296 | tf_op jit(solution)/shard_map/ppermute | solution.py:507
  60.9 0.5 collective-permute-start.23
  61.4 1.6 %collective-permute-done.24.refs_2_ = f32[8,128]{1,0:T(8,128)S(1)} collective-permute-done((f32[8,128]{1,0:T(8,128)S(1)}, f32[8,128]{1,0:T(8,128)S(1)}, u32[]{:S(2)}, u32[]{:S(2)}) %collective-permute-start.24) | collective-permute-done | bytes 4128 | tf_op jit(solution)/shard_map/ppermute | solution.py:507
  63.0 1.5 %collective-permute-done.23.refs_1_ = f32[8,128]{1,0:T(8,128)S(1)} collective-permute-done((f32[8,128]{1,0:T(8,128)S(1)}, f32[8,128]{1,0:T(8,128)S(1)}, u32[]{:S(2)}, u32[]{:S(2)}) %collective-permute-start.23) | collective-permute-done | bytes 4128 | tf_op jit(solution)/shard_map/ppermute | solution.py:491
  64.5 0.7 %last.1 = (f32[5,256]{1,0:T(8,128)}, f32[2,128]{1,0:T(2,128)}, f32[8,128]{1,0:T(8,128)}) custom-call(f32[16,128]{1,0:T(8,128)S(1)} %get-tuple-element.65.state_ref, f32[8,128]{1,0:T(8,128)S(1)} %sum.1.refs_0_, f32[8,128]{1,0:T(8,128)S(1)} %collective-permute-done.23.refs_1_, f32[8,128]{1,0:T(8,128)S(1)} %collective-permute-done.24.refs_2_, ...), custom_call_target="tpu_custom_call" | custom-call | tf_op jit(solution)/shard_map/last/pallas_call | solution.py:477
  (18 shorter events, 0.1 us)
Async XLA Ops:
  2.6 7.1 %collective-permute-start.2 = (f32[72,128]{1,0:T(8,128)S(1)}, f32[72,128]{1,0:T(8,128)S(1)}, u32[]{:S(2)}, u32[]{:S(2)}) collective-permute-start(f32[72,128]{1,0:T(8,128)S(1)} %get-tuple-element.37.refs_0_), channel_id=1, source_target_pairs={{0,6},{1,7},{2,4},{3,5},{4,2},{5,3},{6,0},{7,1},{8,14},{9,15},{10,... | collective-permute-start | bytes 110600 | tf_op jit(solution)/shard_map/ppermute | solution.py:491
  7.7 4.9 %collective-permute-start.1 = (f32[72,128]{1,0:T(8,128)S(1)}, f32[72,128]{1,0:T(8,128)S(1)}, u32[]{:S(2)}, u32[]{:S(2)}) collective-permute-start(f32[72,128]{1,0:T(8,128)S(1)} %get-tuple-element.37.refs_0_), channel_id=1, source_target_pairs={{0,4},{1,5},{2,6},{3,7},{4,0},{5,1},{6,2},{7,3},{8,12},{9,13},{10,... | collective-permute-start | bytes 110600 | tf_op jit(solution)/shard_map/ppermute | solution.py:491
  7.7 4.9 %collective-permute-start = (f32[72,128]{1,0:T(8,128)S(1)}, f32[72,128]{1,0:T(8,128)S(1)}, u32[]{:S(2)}, u32[]{:S(2)}) collective-permute-start(f32[72,128]{1,0:T(8,128)S(1)} %get-tuple-element.37.refs_0_), channel_id=1, source_target_pairs={{0,2},{1,3},{2,0},{3,1},{4,6},{5,7},{6,4},{7,5},{8,10},{9,11},{10,... | collective-permute-start | bytes 110600 | tf_op jit(solution)/shard_map/ppermute | solution.py:491
  12.6 1.4 %collective-permute-start.3 = (f32[272,128]{1,0:T(8,128)S(1)}, f32[272,128]{1,0:T(8,128)S(1)}, u32[]{:S(2)}, u32[]{:S(2)}) collective-permute-start(f32[272,128]{1,0:T(8,128)S(1)} %chip.1.own_ref.refs_0_), channel_id=1, source_target_pairs={{0,1},{1,0},{2,3},{3,2},{4,5},{5,4},{6,7},{7,6},{8,9},{9,8},{10,11... | collective-permute-start | bytes 417800 | tf_op jit(solution)/shard_map/ppermute | solution.py:491
  14.0 7.0 %collective-permute-start.4 = (f32[616,128]{1,0:T(8,128)S(1)}, f32[616,128]{1,0:T(8,128)S(1)}, u32[]{:S(2)}, u32[]{:S(2)}) collective-permute-start(f32[616,128]{1,0:T(8,128)S(1)} %get-tuple-element.39.refs_2_), channel_id=1, source_target_pairs={{0,1},{1,0},{2,3},{3,2},{4,5},{5,4},{6,7},{7,6},{8,9},{9,8},{10,11... | collective-permute-start | bytes 946184 | tf_op jit(solution)/shard_map/ppermute | solution.py:491
  14.2 4.5 %collective-permute-start.6 = (f32[16,128]{1,0:T(8,128)S(1)}, f32[16,128]{1,0:T(8,128)S(1)}, u32[]{:S(2)}, u32[]{:S(2)}) collective-permute-start(f32[16,128]{1,0:T(8,128)S(1)} %group.3.refs_11_), channel_id=1, source_target_pairs={{0,24},{1,17},{2,26},{3,19},{4,28},{5,21},{6,30},{7,23},{8,16},{9,... | collective-permute-start | bytes 24584 | tf_op jit(solution)/shard_map/ppermute | solution.py:507
  16.7 4.8 %collective-permute-start.5 = (f32[16,128]{1,0:T(8,128)S(1)}, f32[16,128]{1,0:T(8,128)S(1)}, u32[]{:S(2)}, u32[]{:S(2)}) collective-permute-start(f32[16,128]{1,0:T(8,128)S(1)} %group.3.refs_11_), channel_id=1, source_target_pairs={{0,8},{8,0},{16,24},{24,16},{1,9},{9,1},{17,25},{25,17},{2,10},{10... | collective-permute-start | bytes 24584 | tf_op jit(solution)/shard_map/ppermute | solution.py:491
  18.8 2.8 %collective-permute-start.7 = (f32[16,128]{1,0:T(8,128)S(1)}, f32[16,128]{1,0:T(8,128)S(1)}, u32[]{:S(2)}, u32[]{:S(2)}) collective-permute-start(f32[16,128]{1,0:T(8,128)S(1)} %collective-permute-done.6.refs_13_), channel_id=1, source_target_pairs={{0,1},{1,0},{2,3},{3,2},{4,5},{5,4},{6,7},{7,6},{8,9},{9,8},{10,11... | collective-permute-start | bytes 24584 | tf_op jit(solution)/shard_map/ppermute | solution.py:491
  23.2 5.6 %collective-permute-start.9 = (f32[32,128]{1,0:T(8,128)S(1)}, f32[32,128]{1,0:T(8,128)S(1)}, u32[]{:S(2)}, u32[]{:S(2)}) collective-permute-start(f32[32,128]{1,0:T(8,128)S(1)} %get-tuple-element.49.refs_0_), channel_id=1, source_target_pairs={{0,6},{1,5},{2,4},{3,7},{4,2},{5,1},{6,0},{7,3},{8,14},{9,13},{10,... | collective-permute-start | bytes 49160 | tf_op jit(solution)/shard_map/ppermute | solution.py:507
  24.7 4.1 %collective-permute-start.8 = (f32[32,128]{1,0:T(8,128)S(1)}, f32[32,128]{1,0:T(8,128)S(1)}, u32[]{:S(2)}, u32[]{:S(2)}) collective-permute-start(f32[32,128]{1,0:T(8,128)S(1)} %get-tuple-element.49.refs_0_), channel_id=1, source_target_pairs={{0,2},{1,3},{2,0},{3,1},{4,6},{5,7},{6,4},{7,5},{8,10},{9,11},{10,... | collective-permute-start | bytes 49160 | tf_op jit(solution)/shard_map/ppermute | solution.py:491
  28.8 1.2 %collective-permute-start.10 = (f32[32,128]{1,0:T(8,128)S(1)}, f32[32,128]{1,0:T(8,128)S(1)}, u32[]{:S(2)}, u32[]{:S(2)}) collective-permute-start(f32[32,128]{1,0:T(8,128)S(1)} %collective-permute-done.9.refs_2_), channel_id=1, source_target_pairs={{0,1},{1,0},{2,3},{3,2},{4,5},{5,4},{6,7},{7,6},{8,9},{9,8},{10,11... | collective-permute-start | bytes 49160 | tf_op jit(solution)/shard_map/ppermute | solution.py:491
  30.0 4.6 %collective-permute-start.12 = (f32[16,128]{1,0:T(8,128)S(1)}, f32[16,128]{1,0:T(8,128)S(1)}, u32[]{:S(2)}, u32[]{:S(2)}) collective-permute-start(f32[16,128]{1,0:T(8,128)S(1)} %get-tuple-element.56.refs_16_), channel_id=1, source_target_pairs={{0,24},{1,17},{2,26},{3,19},{4,28},{5,21},{6,30},{7,23},{8,16},{9,... | collective-permute-start | bytes 24584 | tf_op jit(solution)/shard_map/ppermute | solution.py:507
  32.5 3.7 %collective-permute-start.11 = (f32[16,128]{1,0:T(8,128)S(1)}, f32[16,128]{1,0:T(8,128)S(1)}, u32[]{:S(2)}, u32[]{:S(2)}) collective-permute-start(f32[16,128]{1,0:T(8,128)S(1)} %get-tuple-element.56.refs_16_), channel_id=1, source_target_pairs={{0,8},{8,0},{16,24},{24,16},{1,9},{9,1},{17,25},{25,17},{2,10},{10... | collective-permute-start | bytes 24584 | tf_op jit(solution)/shard_map/ppermute | solution.py:491
  34.6 1.6 %collective-permute-start.13 = (f32[16,128]{1,0:T(8,128)S(1)}, f32[16,128]{1,0:T(8,128)S(1)}, u32[]{:S(2)}, u32[]{:S(2)}) collective-permute-start(f32[16,128]{1,0:T(8,128)S(1)} %collective-permute-done.12.refs_18_), channel_id=1, source_target_pairs={{0,1},{1,0},{2,3},{3,2},{4,5},{5,4},{6,7},{7,6},{8,9},{9,8},{10,11... | collective-permute-start | bytes 24584 | tf_op jit(solution)/shard_map/ppermute | solution.py:491
  37.8 5.6 %collective-permute-start.15 = (f32[32,128]{1,0:T(8,128)S(1)}, f32[32,128]{1,0:T(8,128)S(1)}, u32[]{:S(2)}, u32[]{:S(2)}) collective-permute-start(f32[32,128]{1,0:T(8,128)S(1)} %get-tuple-element.57.refs_0_), channel_id=1, source_target_pairs={{0,6},{1,5},{2,4},{3,7},{4,2},{5,1},{6,0},{7,3},{8,14},{9,13},{10,... | collective-permute-start | bytes 49160 | tf_op jit(solution)/shard_map/ppermute | solution.py:507
  39.4 4.0 %collective-permute-start.14 = (f32[32,128]{1,0:T(8,128)S(1)}, f32[32,128]{1,0:T(8,128)S(1)}, u32[]{:S(2)}, u32[]{:S(2)}) collective-permute-start(f32[32,128]{1,0:T(8,128)S(1)} %get-tuple-element.57.refs_0_), channel_id=1, source_target_pairs={{0,2},{1,3},{2,0},{3,1},{4,6},{5,7},{6,4},{7,5},{8,10},{9,11},{10,... | collective-permute-start | bytes 49160 | tf_op jit(solution)/shard_map/ppermute | solution.py:491
  43.4 1.2 %collective-permute-start.16 = (f32[32,128]{1,0:T(8,128)S(1)}, f32[32,128]{1,0:T(8,128)S(1)}, u32[]{:S(2)}, u32[]{:S(2)}) collective-permute-start(f32[32,128]{1,0:T(8,128)S(1)} %collective-permute-done.15.refs_2_), channel_id=1, source_target_pairs={{0,1},{1,0},{2,3},{3,2},{4,5},{5,4},{6,7},{7,6},{8,9},{9,8},{10,11... | collective-permute-start | bytes 49160 | tf_op jit(solution)/shard_map/ppermute | solution.py:491
  44.6 4.6 %collective-permute-start.18 = (f32[16,128]{1,0:T(8,128)S(1)}, f32[16,128]{1,0:T(8,128)S(1)}, u32[]{:S(2)}, u32[]{:S(2)}) collective-permute-start(f32[16,128]{1,0:T(8,128)S(1)} %get-tuple-element.64.refs_16_), channel_id=1, source_target_pairs={{0,24},{1,17},{2,26},{3,19},{4,28},{5,21},{6,30},{7,23},{8,16},{9,... | collective-permute-start | bytes 24584 | tf_op jit(solution)/shard_map/ppermute | solution.py:507
  47.1 3.7 %collective-permute-start.17 = (f32[16,128]{1,0:T(8,128)S(1)}, f32[16,128]{1,0:T(8,128)S(1)}, u32[]{:S(2)}, u32[]{:S(2)}) collective-permute-start(f32[16,128]{1,0:T(8,128)S(1)} %get-tuple-element.64.refs_16_), channel_id=1, source_target_pairs={{0,8},{8,0},{16,24},{24,16},{1,9},{9,1},{17,25},{25,17},{2,10},{10... | collective-permute-start | bytes 24584 | tf_op jit(solution)/shard_map/ppermute | solution.py:491
  49.2 1.5 %collective-permute-start.19 = (f32[16,128]{1,0:T(8,128)S(1)}, f32[16,128]{1,0:T(8,128)S(1)}, u32[]{:S(2)}, u32[]{:S(2)}) collective-permute-start(f32[16,128]{1,0:T(8,128)S(1)} %collective-permute-done.18.refs_18_), channel_id=1, source_target_pairs={{0,1},{1,0},{2,3},{3,2},{4,5},{5,4},{6,7},{7,6},{8,9},{9,8},{10,11... | collective-permute-start | bytes 24584 | tf_op jit(solution)/shard_map/ppermute | solution.py:491
  51.9 5.4 %collective-permute-start.21 = (f32[8,128]{1,0:T(8,128)S(1)}, f32[8,128]{1,0:T(8,128)S(1)}, u32[]{:S(2)}, u32[]{:S(2)}) collective-permute-start(f32[8,128]{1,0:T(8,128)S(1)} %get-tuple-element.66.refs_0_), channel_id=1, source_target_pairs={{0,6},{1,5},{2,4},{3,7},{4,2},{5,1},{6,0},{7,3},{8,14},{9,13},{10,... | collective-permute-start | bytes 12296 | tf_op jit(solution)/shard_map/ppermute | solution.py:507
  53.4 3.9 %collective-permute-start.20 = (f32[8,128]{1,0:T(8,128)S(1)}, f32[8,128]{1,0:T(8,128)S(1)}, u32[]{:S(2)}, u32[]{:S(2)}) collective-permute-start(f32[8,128]{1,0:T(8,128)S(1)} %get-tuple-element.66.refs_0_), channel_id=1, source_target_pairs={{0,2},{1,3},{2,0},{3,1},{4,6},{5,7},{6,4},{7,5},{8,10},{9,11},{10,... | collective-permute-start | bytes 12296 | tf_op jit(solution)/shard_map/ppermute | solution.py:491
  57.3 1.2 %collective-permute-start.22 = (f32[8,128]{1,0:T(8,128)S(1)}, f32[8,128]{1,0:T(8,128)S(1)}, u32[]{:S(2)}, u32[]{:S(2)}) collective-permute-start(f32[8,128]{1,0:T(8,128)S(1)} %collective-permute-done.21.refs_2_), channel_id=1, source_target_pairs={{0,1},{1,0},{2,3},{3,2},{4,5},{5,4},{6,7},{7,6},{8,9},{9,8},{10,11... | collective-permute-start | bytes 12296 | tf_op jit(solution)/shard_map/ppermute | solution.py:491
  58.5 4.5 %collective-permute-start.24 = (f32[8,128]{1,0:T(8,128)S(1)}, f32[8,128]{1,0:T(8,128)S(1)}, u32[]{:S(2)}, u32[]{:S(2)}) collective-permute-start(f32[8,128]{1,0:T(8,128)S(1)} %sum.1.refs_0_), channel_id=1, source_target_pairs={{0,24},{1,17},{2,26},{3,19},{4,28},{5,21},{6,30},{7,23},{8,16},{9,... | collective-permute-start | bytes 12296 | tf_op jit(solution)/shard_map/ppermute | solution.py:507
  60.9 3.6 %collective-permute-start.23 = (f32[8,128]{1,0:T(8,128)S(1)}, f32[8,128]{1,0:T(8,128)S(1)}, u32[]{:S(2)}, u32[]{:S(2)}) collective-permute-start(f32[8,128]{1,0:T(8,128)S(1)} %sum.1.refs_0_), channel_id=1, source_target_pairs={{0,8},{8,0},{16,24},{24,16},{1,9},{9,1},{17,25},{25,17},{2,10},{10... | collective-permute-start | bytes 12296 | tf_op jit(solution)/shard_map/ppermute | solution.py:491
  63.0 1.5 %collective-permute-start.25 = (f32[8,128]{1,0:T(8,128)S(1)}, f32[8,128]{1,0:T(8,128)S(1)}, u32[]{:S(2)}, u32[]{:S(2)}) collective-permute-start(f32[8,128]{1,0:T(8,128)S(1)} %collective-permute-done.24.refs_2_), channel_id=1, source_target_pairs={{0,1},{1,0},{2,3},{3,2},{4,5},{5,4},{6,7},{7,6},{8,9},{9,8},{10,11... | collective-permute-start | bytes 12296 | tf_op jit(solution)/shard_map/ppermute | solution.py:491

commit v2 on v1

--- a/solution.py
+++ b/solution.py
@@ -194,32 +194,24 @@
     prepare_att(pack_ref[places[3]], att2_ref)
 
 
-def places_of(here, core, count):
-    out = [here, here ^ 1]
-    for pair in range(2, count, 2):
-        out += [here ^ (pair + 1 - core), here ^ (pair + core)]
-    return out
-
-
 def tree_sum(values):
     while len(values) > 1:
         values = [values[i] + values[i + 1] for i in range(0, len(values), 2)]
     return values[0]
 
 
-def first_chip_kernel(count, *refs):
-    ins, out_ref = refs[:count], refs[count]
-    chip = lax.axis_index("tm") // 2
-    extra = ins[0].shape[0] - 24
-    base = 8 * count + 16
-    for gap in range(count):
-        where = chip ^ gap
-        out_ref[pl.ds(pl.multiple_of(where * 8, 8), 8)] = ins[gap][0:8]
-        out_ref[pl.ds(pl.multiple_of(base + where * 8, 8), 8)] = ins[gap][16:24]
-        at = pl.multiple_of(base + 8 * count + where * extra, 8)
-        out_ref[pl.ds(at, extra)] = ins[gap][24:]
-    out_ref[8 * count : 8 * count + 8] = tree_sum([ref[8:16] for ref in ins])
-    out_ref[8 * count + 8 : base] = tree_sum([ref[16:24] for ref in ins])
+def merge_kernel(own_ref, other_ref, out_ref):
+    core = lax.axis_index("tm") % 2
+    extra = own_ref.shape[0] - 24
+    low, top = own_ref[...], other_ref[...]
+    low, top = jnp.where(core == 0, low, top), jnp.where(core == 0, top, low)
+    out_ref[0:8] = low[0:8]
+    out_ref[8:16] = top[0:8]
+    out_ref[16:24] = low[8:16] + top[8:16]
+    att = chip_parts(low[16:19], top[16:19])
+    out_ref[24:32] = jnp.concatenate([att, low[19:22] + top[19:22]], axis=0)
+    out_ref[32 : 32 + extra] = low[24:]
+    out_ref[32 + extra :] = top[24:]
 
 
 def group_rows(chip, count, mine, prev_row, after_row):
@@ -229,75 +221,50 @@
     return [first, mine[1:4], last]
 
 
-def chip_parts(core, own, other):
-    low = jnp.where(core == 0, own, other)
-    top = jnp.where(core == 0, other, own)
+def chip_parts(low, top):
     return jnp.concatenate([low[0:2], low[2:3] + top[0:1], top[1:3]], axis=0)
 
 
-def first_group_kernel(count, own_ref, other_ref, out_ref):
-    me = lax.axis_index("tm")
-    chip, core = me // 2, me % 2
-    low = 8 * count
-    base = low + 16
-
-    def part(ref, where):
-        where = jnp.clip(where, 0, count - 1)
-        return ref[pl.ds(pl.multiple_of(base + where * 8, 8), 8)]
-
-    def of_core(which, where):
-        return jnp.where(core == which, part(own_ref, where), part(other_ref, where))
-
-    mine = chip_parts(core, part(own_ref, chip)[0:3], part(other_ref, chip)[0:3])
-    prev, after = of_core(1, chip - 1), of_core(0, chip + 1)
-    scalars = own_ref[low + 8 : low + 16] + other_ref[low + 8 : low + 16]
-    out_ref[0:8] = own_ref[low : low + 8] + other_ref[low : low + 8]
-    att = group_rows(chip, count, mine, prev[2:3], after[0:1])
-    out_ref[8:16] = jnp.concatenate(att + [scalars[3:6]], axis=0)
-
-
 def group_kernel(count, *refs):
-    *ins, rows_ref, out_ref = refs
-    me = lax.axis_index("tm")
-    chip = me // 2
-    places = places_of(chip, me % 2, count)
+    ins, (rows_ref, out_ref, *keep) = refs[:count], refs[count:]
+    chip = lax.axis_index("tm") // 2
+    extra = (ins[0].shape[0] - 32) // 2
     zero = jnp.zeros((8, LANES), f32)
-    mine, prev, after = zero, zero, zero
-    for ref, where in zip(ins, places):
+    prev, after = zero, zero
+    for gap, ref in enumerate(ins):
+        where = chip ^ gap
         for half in range(2):
             at = pl.multiple_of((half * count + where) * 8, 8)
             rows_ref[pl.ds(at, 8)] = ref[half * 8 : half * 8 + 8]
+            if keep:
+                at = pl.multiple_of((half * count + where) * extra, 8)
+                keep[0][pl.ds(at, extra)] = ref[32 + half * extra : 32 + (half + 1) * extra]
         low = ref[24:32]
-        mine = jnp.where(where == chip, low, mine)
         prev = jnp.where(where == chip - 1, low, prev)
         after = jnp.where(where == chip + 1, low, after)
+    mine = ins[0][24:32]
     scalars = tree_sum([ref[24:32] for ref in ins])
     out_ref[0:8] = tree_sum([ref[16:24] for ref in ins])
     att = group_rows(chip, count, mine, prev[4:5], after[0:1])
     out_ref[8:16] = jnp.concatenate(att + [scalars[5:8]], axis=0)
 
 
-def astro_kernel(first, count, *refs):
+def astro_kernel(first, count, keep_ref, rows_ref, *refs):
     high = STARS_DEV // LANES
     if first:
-        keep, (out_ref, table_ref, spread_ref) = refs[:2], refs[2:]
+        out_ref, table_ref, spread_ref = refs
     else:
-        keep, (table_ref, rows_ref, out_ref, spread_ref) = refs[:2], refs[2:]
-    base = 16 * count + 16
-    extra = (keep[0].shape[0] - base) // count
+        table_ref, out_ref, spread_ref = refs
+    extra = keep_ref.shape[0] // (2 * count)
     comps = extra // 8 - 1
     long = 8 * LANES
-    core = lax.axis_index("tm") % 2
 
     def one(place, totals):
         new = []
         for half in range(2):
-            if first:
-                rows = keep[half][pl.ds(pl.multiple_of(place * 8, 8), 8)]
-            else:
-                at = ((half ^ core) * count + place) * 8
-                rows = rows_ref[pl.ds(pl.multiple_of(at, 8), 8)]
-            packed = keep[half][pl.ds(pl.multiple_of(base + place * extra, 8), extra)]
+            slot = half * count + place
+            rows = rows_ref[pl.ds(pl.multiple_of(slot * 8, 8), 8)]
+            packed = keep_ref[pl.ds(pl.multiple_of(slot * extra, 8), extra)]
             index = packed[comps * 8 :].astype(jnp.int32)
             at0 = pl.multiple_of((half * count + place) * long, long)
             split = [halves(packed[comp * 8 : comp * 8 + 8] * rows) for comp in range(comps)]
@@ -318,8 +285,8 @@
         return tuple(new)
 
     zero = jnp.zeros((2 * comps * high, LANES), f32)
-    own, other = lax.fori_loop(0, count, one, (zero, zero))
-    total = own + other
+    low, top = lax.fori_loop(0, count, one, (zero, zero))
+    total = low + top
     out_ref[...] = total[: comps * high] + total[comps * high :]
 
 
@@ -341,11 +308,13 @@
 
 
 def step_kernel(step, width, slots, chips, star_count, *refs):
-    keep, packs, tables, att2s, ints, sum_ref = refs[:2], refs[2:4], refs[4:6], refs[6:8], refs[8:10], refs[10]
-    refs = refs[11:]
+    keep_ref, packs, tables, att2s, ints = refs[0], refs[1:3], refs[3:5], refs[5:7], refs[7:9]
+    sum_ref, refs = refs[9], refs[10:]
     if step > 0:
         state_ref, old_z_ref, old_g_ref, old_u_ref, old_s_ref = refs[:5]
         refs = refs[5:]
+    else:
+        first_rows_ref, refs = refs[0], refs[1:]
     gathered, refs = refs[:-7], refs[-7:]
     send_ref, state_out, z_ref, g_ref, u_ref, s_ref, spread_ref = refs
     me = lax.axis_index("tm")
@@ -359,8 +328,8 @@
         squares = lane_sum(total[13:14])
         beta2 = squares + epsilon
         beta = jnp.sqrt(beta2)
-        at = pl.ds(pl.multiple_of(chip * 8, 8), 8)
-        u = jnp.concatenate([ref[at] for ref in keep], axis=0) / beta
+        places = [pl.multiple_of(((half ^ core) * chips + chip) * 8, 8) for half in range(2)]
+        u = jnp.concatenate([first_rows_ref[pl.ds(at, 8)] for at in places], axis=0) / beta
         g = back / beta
         z = g
         state_out[...] = jnp.concatenate(
@@ -383,14 +352,14 @@
     inst_rows = z[base : base + 8]
     att_rows = z[base + 8 : base + 13]
     extra = 8 * comps + 8
-    here = 16 * chips + 16 + chip * extra
     pieces = [inst_rows[place : place + 1] for place in range(8)]
     rows, insts, atts = [], [], []
     for half in range(2):
         starts = ints[half][slots * 8 :]
         own = jnp.where(core == half, att_rows[0:3], att_rows[2:5])
         part = att_forward(own, att2s[half][...], starts, width)
-        packed = keep[half][pl.ds(pl.multiple_of(here, 8), extra)]
+        at = pl.multiple_of(((half ^ core) * chips + chip) * extra, 8)
+        packed = keep_ref[pl.ds(at, extra)]
         star = packed[comps * 8 :].astype(jnp.int32)
         star_high, star_low = star >> 7, star & (LANES - 1)
         for comp in range(comps):
@@ -422,13 +391,12 @@
         return
     send_ref[0:16] = jnp.where(core == 0, both, jnp.concatenate(rows[::-1], axis=0))
     send_ref[16:24] = insts[0] + insts[1]
-    send_ref[24:32] = jnp.concatenate([chip_parts(core, *atts)] + scalars, axis=0)
-
-
-def last_kernel(comps, share, star_count, state_ref, *refs):
-    gathered, refs = refs[: -ITERS - 3], refs[-ITERS - 3 :]
-    z_refs = refs[:ITERS]
-    astro_ref, att_ref, inst_ref = refs[ITERS:]
+    low, top = (jnp.where(core == half, atts[0], atts[1]) for half in range(2))
+    send_ref[24:32] = jnp.concatenate([chip_parts(low, top)] + scalars, axis=0)
+
+
+def last_kernel(comps, share, state_ref, *refs):
+    gathered, z_refs, out_ref = refs[: -ITERS - 1], refs[-ITERS - 1 : -1], refs[-1]
     high = STARS_DEV // LANES
     me = lax.axis_index("tm")
     total = tree_sum([ref[...] for ref in gathered])
@@ -461,15 +429,32 @@
             total = total + weights[k] * read(z_refs[k])
         return total
 
+    rows = ATT_DEV // LANES
+    pieces = [mix(lambda ref: ref[base : base + 8])]
+    for core in range(2):
+        at = base + 8 + core * rows
+        pieces.append(mix(lambda ref: ref[at : at + rows]))
+        for comp in range(comps):
+            place = comp * high + (me // 2 * 2 + core) * tiles
+            pieces.append(mix(lambda ref: ref[pl.ds(place, tiles)]))
+    unused = out_ref.shape[0] - sum(piece.shape[0] for piece in pieces)
+    if unused:
+        pieces.append(jnp.zeros((unused, LANES), f32))
+    out_ref[...] = jnp.concatenate(pieces, axis=0)
+
+
+def place_kernel(comps, share, own_ref, other_ref, astro_ref, att_ref, inst_ref):
+    core = lax.axis_index("tm") % 2
+    tiles, rows = share // LANES, ATT_DEV // LANES
+    value = jnp.where(core == 1, own_ref[...], other_ref[...])
+    at = 8 + rows + comps * tiles
+    mine = jnp.where(core == 0, value[8:at], value[at : 2 * at - 8])
+    inst_ref[...] = value[0:8]
+    att_ref[...] = mine[:rows]
     for comp in range(comps):
         for tile in range(tiles):
-            at = comp * high + me * tiles + tile
-            astro_ref[comp : comp + 1, tile * LANES : (tile + 1) * LANES] = mix(
-                lambda ref: ref[pl.ds(at, 1)]
-            )
-    inst_ref[...] = mix(lambda ref: ref[base : base + 8])
-    rows = ATT_DEV // LANES
-    att_ref[...] = mix(lambda ref: ref[pl.ds(base + 8 + (me % 2) * rows, rows)])
+            row = rows + comp * tiles + tile
+            astro_ref[comp : comp + 1, tile * LANES : (tile + 1) * LANES] = mine[row : row + 1]
 
 
 def call(kernel, name, out, args, scratch=(), space=pltpu.VMEM):
@@ -494,21 +479,15 @@
 
 def exchange(value, axis):
     tm_count, star_count = lax.axis_size("tm"), lax.axis_size("star")
-    count = star_count if axis == "star" else tm_count // 2
-    both = ("star", "tm")
-    got = []
-    for pair in range(2, count, 2):
+    got = [value]
+    for gap in range(1, star_count if axis == "star" else tm_count // 2):
         steps = []
         for star in range(star_count):
-            for tm in range(tm_count):
-                gap = pair + 1 - tm % 2
+            for tm in range(1, tm_count, 2):
                 far = (star ^ gap, tm) if axis == "star" else (star, tm ^ (2 * gap))
                 steps.append((star * tm_count + tm, far[0] * tm_count + far[1]))
-        got.append(lax.ppermute(value, both, steps))
-    near = direct(value, axis, [1 if axis == "star" else 2])
-    for value in got:
-        near += direct(value, "tm", [1])
-    return near
+        got.append(lax.ppermute(value, ("star", "tm"), steps))
+    return got
 
 
 def rows_type(rows):
@@ -523,7 +502,6 @@
     share = STARS_DEV // tm_count
     high = STARS_DEV // LANES
     chips = tm_count // 2
-    far = [2 * gap for gap in range(1, chips)]
     args = [
         observed.reshape(blocks, height),
         astro_coef.reshape(comps, blocks, height),
@@ -548,47 +526,38 @@
         + [spread, pltpu.SemaphoreType.DMA((len(args),))],
         pl.ANY,
     )
+    (send,) = call(
+        merge_kernel, "merge", [rows_type(32 + 2 * extra)], direct(send, "tm", [1])
+    )
+    send, late_pack = lax.optimization_barrier((send, pack))
+    _, other_pack = direct(late_pack, "tm", [1])
+    theirs = call(
+        functools.partial(prepare_kernel, slots, blocks, width), "prepare", prepared, [other_pack]
+    )
+    got = exchange(send, "tm")
+    theirs, got = lax.optimization_barrier((theirs, got))
+    basics = [pack, other_pack] + [value for both in zip(mine, theirs) for value in both]
     keep = star_table = state = z = g = u = rows = None
     kept = []
     group_type = rows_type(16)
     for step in range(ITERS):
         wide = [pltpu.VMEM((2, 2 * comps * high, blocks * height), bf16)]
-        sums_type = ((comps * high, LANES), f32)
-        got = exchange(send, "tm") if step else direct(send, "tm", far)
-        if step == 0:
-            (gathered,) = call(
-                functools.partial(first_chip_kernel, chips),
-                "chip",
-                [((16 * chips + 16 + chips * extra, LANES), f32)],
-                got,
-            )
-            keep = direct(gathered, "tm", [1])
-            (group,) = call(
-                functools.partial(first_group_kernel, chips), "group", [group_type], keep
-            )
-            group, late_pack = lax.optimization_barrier((group, pack))
-            _, other_pack = direct(late_pack, "tm", [1])
-            theirs = call(
-                functools.partial(prepare_kernel, slots, blocks, width),
-                "prepare",
-                prepared,
-                [other_pack],
-            )
-            basics = [pack, other_pack] + [value for both in zip(mine, theirs) for value in both]
-        else:
-            all_rows, group = call(
-                functools.partial(group_kernel, chips),
-                "group",
-                [rows_type(16 * chips), group_type],
-                got,
-            )
+        sums_type = rows_type(comps * high)
+        all_rows, group, *new = call(
+            functools.partial(group_kernel, chips),
+            "group",
+            [rows_type(16 * chips), group_type]
+            + ([rows_type(2 * chips * extra)] if step == 0 else []),
+            exchange(send, "tm") if step else got,
+        )
         across = exchange(group, "star")
         if step == 0:
+            (keep,) = new
             sums, star_table = call(
                 functools.partial(astro_kernel, True, chips),
                 "astro",
                 [sums_type, ((LANES, tm_count * blocks * height), bf16)],
-                keep,
+                [keep, all_rows],
                 wide,
             )
         else:
@@ -596,27 +565,35 @@
                 functools.partial(astro_kernel, False, chips),
                 "astro",
                 [sums_type],
-                keep + [star_table, all_rows],
+                [keep, all_rows, star_table],
                 wide,
             )
         tall = ((comps * high + 16, LANES), f32)
         pair = ((2 * blocks, height), f32)
-        older = [] if step == 0 else [state, z, g, u, rows]
+        older = [all_rows] if step == 0 else [state, z, g, u, rows]
         send, state, z, g, u, rows = call(
             functools.partial(step_kernel, step, width, slots, chips, star_count),
             "step",
             [rows_type(32 if step < ITERS - 1 else 8), group_type, tall, tall, pair, pair],
-            keep + basics + [sums] + older + across,
+            [keep] + basics + [sums] + older + across,
             [pltpu.VMEM((2, 16, long), bf16)],
         )
         kept.append(z)
     (send,) = call(sum_kernel, "sum", [rows_type(8)], exchange(send, "tm"))
     across = exchange(send, "star")
+    both_parts = 2 * (ATT_DEV // LANES + comps * share // LANES)
+    (parts,) = call(
+        functools.partial(last_kernel, comps, share),
+        "last",
+        [rows_type(8 + (both_parts + 7) // 8 * 8)],
+        [state] + across + kept,
+    )
+    received = lax.ppermute(parts, "tm", [(i, i - 1) for i in range(1, tm_count, 2)])
     out_astro, out_att, out_inst = call(
-        functools.partial(last_kernel, comps, share, star_count),
-        "last",
+        functools.partial(place_kernel, comps, share),
+        "place",
         [((comps, share), f32), ((ATT_DEV // LANES, LANES), f32), ((NINST // LANES, LANES), f32)],
-        [state] + across + kept,
+        [parts, received],
     )
     return out_astro, out_att.reshape(-1), out_inst.reshape(-1)
 

time: 65.4 us -> 99.4 us (1.52)
  waiting for transfers between devices: 27.8 us -> 66.6 us
  starting transfers between devices: 23.9 us -> 18.1 us
    ppermute x7 -> x25, waiting for transfers between devices: 17.1 us -> 65.7 us  [the longest x1 65.6 us: per_device(): lax.ppermute(parts, 'tm', [(i, i - 1) for i in range(1, tm_count, 2)])]
    ppermute x19 -> x2, waiting for transfers between devices: 10.7 us -> 0.87 us  [direct(): lax.ppermute(value, axis, [(i, i ^ gap) for i in range(count)])]
    ppermute x19 -> x2, starting transfers between devices: 9.35 us -> 0.93 us  [direct(): lax.ppermute(value, axis, [(i, i ^ gap) for i in range(count)])]
    ppermute x7 -> x25, starting transfers between devices: 14.5 us -> 17.2 us  [the longest x24 15.9 us: exchange(): got.append(lax.ppermute(value, ('star', 'tm'), steps))]
    pallas_call x14 -> x15, Pallas kernels: 12.8 us -> 12.9 us  [call(): pl.pallas_call(kernel, name=name, out_shape=[jax.ShapeDtypeStruct(shape,...]
  transfers between devices with their start and end apart: 26 -> 27, of which waited for: 15 -> 2; matrix products, arithmetic and copies ran while one was open for 0% -> 0% of each run, Pallas kernels for 9% -> 6%
where the time goes in v2:
time: 99.4 us; the launch traced here: 98.7 us
  waiting for transfers between devices  66.6 us (67%)
  starting transfers between devices  18.1 us (18%)
  Pallas kernels  12.9 us (13%)
  between operations  1.11 us (1%)
    ppermute x1, waiting for transfers between devices, per_device(): lax.ppermute(parts, 'tm', [(i, i - 1) for i in range(1, tm_count, 2)])  65.6 us
    ppermute x24, starting transfers between devices, exchange(): got.append(lax.ppermute(value, ('star', 'tm'), steps))  15.9 us
    pallas_call x15, Pallas kernels, call(): pl.pallas_call(kernel, name=name, out_shape=[jax.ShapeDtypeStruct(shape,...  12.9 us
  transfers between devices with their start and end apart: 27, of which 2 were waited for; matrix products, arithmetic and copies ran while one was open for 0% of the time, Pallas kernels for 6%

profile of v2, /device:TPU:0, one launch (start us, length us, event | category | flops | bytes accessed | tf_op | source)
XLA Modules:
  0.0 98.7 jit_solution(17034509246729938913)
XLA Ops:
  0.6 1.9 %first.1 = (f32[72,128]{1,0:T(8,128)S(1)}, f32[616,128]{1,0:T(8,128)S(1)}, bf16[128,6144]{1,0:T(8,128)(2,1)S(1)}, bf16[1024,128]{1,0:T(8,128)(2,1)S(1)}, s32[56,128]{1,0:T(8,128)S(1)}) custom-call(f32[8,128]{1,0:T(8,128)} %bitcast.12, f32[5,8,128]{2,1,0:T(8,128)} %bitcast.11, s32[8,128]{1,0:T(8,128)} %bitcast.13, f32[512,128]{1,0:T(8,128)} %bitcast.8, ...), custom_call_target="tpu_custom_call" | custom-call | tf_op jit(solution)/shard_map/first/pallas_call | solution.py:462
  2.6 0.5 collective-permute-start
  3.1 0.9 collective-permute-done.other_ref
  4.0 0.4 collective-permute-start.1
  4.4 0.7 collective-permute-start.4
  5.0 0.7 collective-permute-start.3
  5.7 0.7 collective-permute-start.2
  6.4 0.0 collective-permute-done.1.pack_ref.refs_2_
  6.4 0.5 prepare.1
  6.9 0.0 collective-permute-done.2.refs_1_
  7.0 0.7 collective-permute-start.7
  7.6 0.7 collective-permute-start.6
  8.3 0.7 collective-permute-start.5
  9.0 2.2 %astro.3 = (f32[80,128]{1,0:T(8,128)S(1)}, bf16[128,8192]{1,0:T(8,128)(2,1)S(1)}) custom-call(f32[384,128]{1,0:T(8,128)S(1)} %get-tuple-element.58.keep_ref.refs_0_, f32[64,128]{1,0:T(8,128)S(1)} %get-tuple-element.65.rows_ref.refs_10_), custom_call_target="tpu_custom_call" | custom-call | tf_op jit(solution)/shard_map/astro/pallas_call | solution.py:462
  11.2 0.0 collective-permute-done.7.refs_14_
  11.2 0.0 collective-permute-done.6.refs_13_
  11.3 1.6 %step.3 = (f32[32,128]{1,0:T(8,128)S(1)}, f32[16,128]{1,0:T(8,128)S(1)}, f32[96,128]{1,0:T(8,128)S(1)}, f32[96,128]{1,0:T(8,128)S(1)}, f32[16,128]{1,0:T(8,128)S(1)}, /*index=5*/f32[16,128]{1,0:T(8,128)S(1)}) custom-call(f32[384,128]{1,0:T(8,128)S(1)} %get-tuple-element.58.keep_ref.refs_0_, f32[616,128]{1,0:T(8,128)S(1)} %get-tuple-element.49.refs_1_, ...), custom_call_target="tpu_custom_call" | custom-call | tf_op jit(solution)/shard_map/step/pallas_call | solution.py:462
  12.9 0.7 collective-permute-start.10
  13.5 0.7 collective-permute-start.9
  14.2 0.7 collective-permute-start.8
  14.9 0.0 collective-permute-done.10.refs_3_
  15.0 0.7 collective-permute-start.13
  15.6 0.7 collective-permute-start.12
  16.3 0.7 collective-permute-start.11
  17.0 1.5 %astro.4.refs_9_ = f32[80,128]{1,0:T(8,128)S(1)} custom-call(f32[384,128]{1,0:T(8,128)S(1)} %get-tuple-element.58.keep_ref.refs_0_, f32[64,128]{1,0:T(8,128)S(1)} %get-tuple-element.69.rows_ref, bf16[128,8192]{1,0:T(8,128)(2,1)S(1)} %get-tuple-element.70.refs_0_), custom_call_target="tpu_custom_call" | custom-call | tf_op jit(solution)/shard_map/astro/pallas_call | solution.py:462
  18.5 0.0 collective-permute-done.13.refs_18_
  18.5 1.6 %step.4 = (f32[32,128]{1,0:T(8,128)S(1)}, f32[16,128]{1,0:T(8,128)S(1)}, f32[96,128]{1,0:T(8,128)S(1)}, f32[96,128]{1,0:T(8,128)S(1)}, f32[16,128]{1,0:T(8,128)S(1)}, /*index=5*/f32[16,128]{1,0:T(8,128)S(1)}) custom-call(f32[384,128]{1,0:T(8,128)S(1)} %get-tuple-element.58.keep_ref.refs_0_, f32[616,128]{1,0:T(8,128)S(1)} %get-tuple-element.49.refs_1_, ...), custom_call_target="tpu_custom_call" | custom-call | tf_op jit(solution)/shard_map/step/pallas_call | solution.py:462
  20.1 0.7 collective-permute-start.16
  20.8 0.7 collective-permute-start.15
  21.5 0.7 collective-permute-start.14
  22.2 0.0 collective-permute-done.16.refs_3_
  22.2 0.0 collective-permute-done.15.refs_2_
  22.2 0.7 collective-permute-start.19
  22.9 0.7 collective-permute-start.18
  23.6 0.7 collective-permute-start.17
  24.2 1.5 %astro.5.refs_9_ = f32[80,128]{1,0:T(8,128)S(1)} custom-call(f32[384,128]{1,0:T(8,128)S(1)} %get-tuple-element.58.keep_ref.refs_0_, f32[64,128]{1,0:T(8,128)S(1)} %get-tuple-element.78.rows_ref, bf16[128,8192]{1,0:T(8,128)(2,1)S(1)} %get-tuple-element.70.refs_0_), custom_call_target="tpu_custom_call" | custom-call | tf_op jit(solution)/shard_map/astro/pallas_call | solution.py:462
  25.7 0.0 collective-permute-done.18.refs_17_
  25.8 1.1 %step.5 = (f32[8,128]{1,0:T(8,128)S(1)}, f32[16,128]{1,0:T(8,128)S(1)}, f32[96,128]{1,0:T(8,128)S(1)}, f32[96,128]{1,0:T(8,128)}, f32[16,128]{1,0:T(8,128)}, /*index=5*/f32[16,128]{1,0:T(8,128)}) custom-call(f32[384,128]{1,0:T(8,128)S(1)} %get-tuple-element.58.keep_ref.refs_0_, f32[616,128]{1,0:T(8,128)S(1)} %get-tuple-element.49.refs_1_, ...), custom_call_target="tpu_custom_call" | custom-call | tf_op jit(solution)/shard_map/step/pallas_call | solution.py:462
  26.9 0.6 collective-permute-start.22
  27.5 0.7 collective-permute-start.21
  28.2 0.7 collective-permute-start.20
  28.9 0.7 collective-permute-start.25
  29.6 0.7 collective-permute-start.24
  30.3 0.7 collective-permute-start.23
  31.0 0.1 last.1.own_ref
  31.1 1.3 %collective-permute-start.26 = (f32[32,128]{1,0:T(8,128)S(1)}, f32[32,128]{1,0:T(8,128)S(1)}, u32[]{:S(2)}, u32[]{:S(2)}) collective-permute-start(f32[32,128]{1,0:T(8,128)S(1)} %last.1.own_ref), channel_id=1, source_target_pairs={{1,0},{3,2},{5,4},{7,6},{9,8},{11,10},{13,12},{15,14},{17,16},{19,... | collective-permute-start | bytes 49160 | tf_op jit(solution)/shard_map/ppermute | solution.py:591
  32.4 65.6 %collective-permute-done.26.other_ref = f32[32,128]{1,0:T(8,128)S(1)} collective-permute-done((f32[32,128]{1,0:T(8,128)S(1)}, f32[32,128]{1,0:T(8,128)S(1)}, u32[]{:S(2)}, u32[]{:S(2)}) %collective-permute-start.26) | collective-permute-done | bytes 16416 | tf_op jit(solution)/shard_map/ppermute | solution.py:591
  98.0 0.6 place.1
  (21 shorter events, 0.2 us)
Async XLA Ops:
  2.6 1.4 %collective-permute-start = (f32[72,128]{1,0:T(8,128)S(1)}, f32[72,128]{1,0:T(8,128)S(1)}, u32[]{:S(2)}, u32[]{:S(2)}) collective-permute-start(f32[72,128]{1,0:T(8,128)S(1)} %get-tuple-element.47.own_ref), channel_id=1, source_target_pairs={{0,1},{1,0},{2,3},{3,2},{4,5},{5,4},{6,7},{7,6},{8,9},{9,8},{10,11... | collective-permute-start | bytes 110600 | tf_op jit(solution)/shard_map/ppermute | solution.py:476
  4.0 2.4 %collective-permute-start.1 = (f32[616,128]{1,0:T(8,128)S(1)}, f32[616,128]{1,0:T(8,128)S(1)}, u32[]{:S(2)}, u32[]{:S(2)}) collective-permute-start(f32[616,128]{1,0:T(8,128)S(1)} %get-tuple-element.49.refs_1_), channel_id=1, source_target_pairs={{0,1},{1,0},{2,3},{3,2},{4,5},{5,4},{6,7},{7,6},{8,9},{9,8},{10,11... | collective-permute-start | bytes 946184 | tf_op jit(solution)/shard_map/ppermute | solution.py:476
  4.4 2.5 %collective-permute-start.4 = (f32[128,128]{1,0:T(8,128)S(1)}, f32[128,128]{1,0:T(8,128)S(1)}, u32[]{:S(2)}, u32[]{:S(2)}) collective-permute-start(f32[128,128]{1,0:T(8,128)S(1)} %merge.1.refs_0_), channel_id=1, source_target_pairs={{1,7},{3,5},{5,3},{7,1},{9,15},{11,13},{13,11},{15,9},{17,23},{19,... | collective-permute-start | bytes 196616 | tf_op jit(solution)/shard_map/ppermute | solution.py:489
  5.0 1.9 %collective-permute-start.3 = (f32[128,128]{1,0:T(8,128)S(1)}, f32[128,128]{1,0:T(8,128)S(1)}, u32[]{:S(2)}, u32[]{:S(2)}) collective-permute-start(f32[128,128]{1,0:T(8,128)S(1)} %merge.1.refs_0_), channel_id=1, source_target_pairs={{1,5},{3,7},{5,1},{7,3},{9,13},{11,15},{13,9},{15,11},{17,21},{19,... | collective-permute-start | bytes 196616 | tf_op jit(solution)/shard_map/ppermute | solution.py:489
  5.7 1.2 %collective-permute-start.2 = (f32[128,128]{1,0:T(8,128)S(1)}, f32[128,128]{1,0:T(8,128)S(1)}, u32[]{:S(2)}, u32[]{:S(2)}) collective-permute-start(f32[128,128]{1,0:T(8,128)S(1)} %merge.1.refs_0_), channel_id=1, source_target_pairs={{1,3},{3,1},{5,7},{7,5},{9,11},{11,9},{13,15},{15,13},{17,19},{19,... | collective-permute-start | bytes 196616 | tf_op jit(solution)/shard_map/ppermute | solution.py:489
  7.0 4.2 %collective-permute-start.7 = (f32[16,128]{1,0:T(8,128)S(1)}, f32[16,128]{1,0:T(8,128)S(1)}, u32[]{:S(2)}, u32[]{:S(2)}) collective-permute-start(f32[16,128]{1,0:T(8,128)S(1)} %get-tuple-element.67.refs_11_), channel_id=1, source_target_pairs={{1,25},{3,27},{5,29},{7,31},{9,17},{11,19},{13,21},{15,23},{17,9},... | collective-permute-start | bytes 24584 | tf_op jit(solution)/shard_map/ppermute | solution.py:489
  7.6 3.6 %collective-permute-start.6 = (f32[16,128]{1,0:T(8,128)S(1)}, f32[16,128]{1,0:T(8,128)S(1)}, u32[]{:S(2)}, u32[]{:S(2)}) collective-permute-start(f32[16,128]{1,0:T(8,128)S(1)} %get-tuple-element.67.refs_11_), channel_id=1, source_target_pairs={{1,17},{3,19},{5,21},{7,23},{9,25},{11,27},{13,29},{15,31},{17,1},... | collective-permute-start | bytes 24584 | tf_op jit(solution)/shard_map/ppermute | solution.py:489
  8.3 2.9 %collective-permute-start.5 = (f32[16,128]{1,0:T(8,128)S(1)}, f32[16,128]{1,0:T(8,128)S(1)}, u32[]{:S(2)}, u32[]{:S(2)}) collective-permute-start(f32[16,128]{1,0:T(8,128)S(1)} %get-tuple-element.67.refs_11_), channel_id=1, source_target_pairs={{1,9},{3,11},{5,13},{7,15},{9,1},{11,3},{13,5},{15,7},{17,25},{19,... | collective-permute-start | bytes 24584 | tf_op jit(solution)/shard_map/ppermute | solution.py:489
  12.9 2.0 %collective-permute-start.10 = (f32[32,128]{1,0:T(8,128)S(1)}, f32[32,128]{1,0:T(8,128)S(1)}, u32[]{:S(2)}, u32[]{:S(2)}) collective-permute-start(f32[32,128]{1,0:T(8,128)S(1)} %get-tuple-element.68.refs_0_), channel_id=1, source_target_pairs={{1,7},{3,5},{5,3},{7,1},{9,15},{11,13},{13,11},{15,9},{17,23},{19,... | collective-permute-start | bytes 49160 | tf_op jit(solution)/shard_map/ppermute | solution.py:489
  13.5 1.4 %collective-permute-start.9 = (f32[32,128]{1,0:T(8,128)S(1)}, f32[32,128]{1,0:T(8,128)S(1)}, u32[]{:S(2)}, u32[]{:S(2)}) collective-permute-start(f32[32,128]{1,0:T(8,128)S(1)} %get-tuple-element.68.refs_0_), channel_id=1, source_target_pairs={{1,5},{3,7},{5,1},{7,3},{9,13},{11,15},{13,9},{15,11},{17,21},{19,... | collective-permute-start | bytes 49160 | tf_op jit(solution)/shard_map/ppermute | solution.py:489
  14.2 0.7 collective-permute-start.8
  15.0 3.5 %collective-permute-start.13 = (f32[16,128]{1,0:T(8,128)S(1)}, f32[16,128]{1,0:T(8,128)S(1)}, u32[]{:S(2)}, u32[]{:S(2)}) collective-permute-start(f32[16,128]{1,0:T(8,128)S(1)} %get-tuple-element.76.refs_15_), channel_id=1, source_target_pairs={{1,25},{3,27},{5,29},{7,31},{9,17},{11,19},{13,21},{15,23},{17,9},... | collective-permute-start | bytes 24584 | tf_op jit(solution)/shard_map/ppermute | solution.py:489
  15.6 2.9 %collective-permute-start.12 = (f32[16,128]{1,0:T(8,128)S(1)}, f32[16,128]{1,0:T(8,128)S(1)}, u32[]{:S(2)}, u32[]{:S(2)}) collective-permute-start(f32[16,128]{1,0:T(8,128)S(1)} %get-tuple-element.76.refs_15_), channel_id=1, source_target_pairs={{1,17},{3,19},{5,21},{7,23},{9,25},{11,27},{13,29},{15,31},{17,1},... | collective-permute-start | bytes 24584 | tf_op jit(solution)/shard_map/ppermute | solution.py:489
  16.3 2.2 %collective-permute-start.11 = (f32[16,128]{1,0:T(8,128)S(1)}, f32[16,128]{1,0:T(8,128)S(1)}, u32[]{:S(2)}, u32[]{:S(2)}) collective-permute-start(f32[16,128]{1,0:T(8,128)S(1)} %get-tuple-element.76.refs_15_), channel_id=1, source_target_pairs={{1,9},{3,11},{5,13},{7,15},{9,1},{11,3},{13,5},{15,7},{17,25},{19,... | collective-permute-start | bytes 24584 | tf_op jit(solution)/shard_map/ppermute | solution.py:489
  20.1 2.0 %collective-permute-start.16 = (f32[32,128]{1,0:T(8,128)S(1)}, f32[32,128]{1,0:T(8,128)S(1)}, u32[]{:S(2)}, u32[]{:S(2)}) collective-permute-start(f32[32,128]{1,0:T(8,128)S(1)} %get-tuple-element.77.refs_0_), channel_id=1, source_target_pairs={{1,7},{3,5},{5,3},{7,1},{9,15},{11,13},{13,11},{15,9},{17,23},{19,... | collective-permute-start | bytes 49160 | tf_op jit(solution)/shard_map/ppermute | solution.py:489
  20.8 1.4 %collective-permute-start.15 = (f32[32,128]{1,0:T(8,128)S(1)}, f32[32,128]{1,0:T(8,128)S(1)}, u32[]{:S(2)}, u32[]{:S(2)}) collective-permute-start(f32[32,128]{1,0:T(8,128)S(1)} %get-tuple-element.77.refs_0_), channel_id=1, source_target_pairs={{1,5},{3,7},{5,1},{7,3},{9,13},{11,15},{13,9},{15,11},{17,21},{19,... | collective-permute-start | bytes 49160 | tf_op jit(solution)/shard_map/ppermute | solution.py:489
  21.5 0.7 collective-permute-start.14
  22.2 3.5 %collective-permute-start.19 = (f32[16,128]{1,0:T(8,128)S(1)}, f32[16,128]{1,0:T(8,128)S(1)}, u32[]{:S(2)}, u32[]{:S(2)}) collective-permute-start(f32[16,128]{1,0:T(8,128)S(1)} %get-tuple-element.84.refs_15_), channel_id=1, source_target_pairs={{1,25},{3,27},{5,29},{7,31},{9,17},{11,19},{13,21},{15,23},{17,9},... | collective-permute-start | bytes 24584 | tf_op jit(solution)/shard_map/ppermute | solution.py:489
  22.9 2.9 %collective-permute-start.18 = (f32[16,128]{1,0:T(8,128)S(1)}, f32[16,128]{1,0:T(8,128)S(1)}, u32[]{:S(2)}, u32[]{:S(2)}) collective-permute-start(f32[16,128]{1,0:T(8,128)S(1)} %get-tuple-element.84.refs_15_), channel_id=1, source_target_pairs={{1,17},{3,19},{5,21},{7,23},{9,25},{11,27},{13,29},{15,31},{17,1},... | collective-permute-start | bytes 24584 | tf_op jit(solution)/shard_map/ppermute | solution.py:489
  23.6 2.2 %collective-permute-start.17 = (f32[16,128]{1,0:T(8,128)S(1)}, f32[16,128]{1,0:T(8,128)S(1)}, u32[]{:S(2)}, u32[]{:S(2)}) collective-permute-start(f32[16,128]{1,0:T(8,128)S(1)} %get-tuple-element.84.refs_15_), channel_id=1, source_target_pairs={{1,9},{3,11},{5,13},{7,15},{9,1},{11,3},{13,5},{15,7},{17,25},{19,... | collective-permute-start | bytes 24584 | tf_op jit(solution)/shard_map/ppermute | solution.py:489
  26.9 2.0 %collective-permute-start.22 = (f32[8,128]{1,0:T(8,128)S(1)}, f32[8,128]{1,0:T(8,128)S(1)}, u32[]{:S(2)}, u32[]{:S(2)}) collective-permute-start(f32[8,128]{1,0:T(8,128)S(1)} %get-tuple-element.86.refs_0_), channel_id=1, source_target_pairs={{1,7},{3,5},{5,3},{7,1},{9,15},{11,13},{13,11},{15,9},{17,23},{19,... | collective-permute-start | bytes 12296 | tf_op jit(solution)/shard_map/ppermute | solution.py:489
  27.5 1.4 %collective-permute-start.21 = (f32[8,128]{1,0:T(8,128)S(1)}, f32[8,128]{1,0:T(8,128)S(1)}, u32[]{:S(2)}, u32[]{:S(2)}) collective-permute-start(f32[8,128]{1,0:T(8,128)S(1)} %get-tuple-element.86.refs_0_), channel_id=1, source_target_pairs={{1,5},{3,7},{5,1},{7,3},{9,13},{11,15},{13,9},{15,11},{17,21},{19,... | collective-permute-start | bytes 12296 | tf_op jit(solution)/shard_map/ppermute | solution.py:489
  28.2 0.7 collective-permute-start.20
  28.9 2.0 %collective-permute-start.25 = (f32[8,128]{1,0:T(8,128)S(1)}, f32[8,128]{1,0:T(8,128)S(1)}, u32[]{:S(2)}, u32[]{:S(2)}) collective-permute-start(f32[8,128]{1,0:T(8,128)S(1)} %sum.1.refs_0_), channel_id=1, source_target_pairs={{1,25},{3,27},{5,29},{7,31},{9,17},{11,19},{13,21},{15,23},{17,9},... | collective-permute-start | bytes 12296 | tf_op jit(solution)/shard_map/ppermute | solution.py:489
  29.6 1.4 %collective-permute-start.24 = (f32[8,128]{1,0:T(8,128)S(1)}, f32[8,128]{1,0:T(8,128)S(1)}, u32[]{:S(2)}, u32[]{:S(2)}) collective-permute-start(f32[8,128]{1,0:T(8,128)S(1)} %sum.1.refs_0_), channel_id=1, source_target_pairs={{1,17},{3,19},{5,21},{7,23},{9,25},{11,27},{13,29},{15,31},{17,1},... | collective-permute-start | bytes 12296 | tf_op jit(solution)/shard_map/ppermute | solution.py:489
  30.3 0.7 collective-permute-start.23
  31.1 66.9 %collective-permute-start.26 = (f32[32,128]{1,0:T(8,128)S(1)}, f32[32,128]{1,0:T(8,128)S(1)}, u32[]{:S(2)}, u32[]{:S(2)}) collective-permute-start(f32[32,128]{1,0:T(8,128)S(1)} %last.1.own_ref), channel_id=1, source_target_pairs={{1,0},{3,2},{5,4},{7,6},{9,8},{11,10},{13,12},{15,14},{17,16},{19,... | collective-permute-start | bytes 49160 | tf_op jit(solution)/shard_map/ppermute | solution.py:591

commit v3 on v2

--- a/solution.py
+++ b/solution.py
@@ -483,8 +483,9 @@
     for gap in range(1, star_count if axis == "star" else tm_count // 2):
         steps = []
         for star in range(star_count):
-            for tm in range(1, tm_count, 2):
+            for tm in range(tm_count):
                 far = (star ^ gap, tm) if axis == "star" else (star, tm ^ (2 * gap))
+                far = far if tm % 2 else (star, tm)
                 steps.append((star * tm_count + tm, far[0] * tm_count + far[1]))
         got.append(lax.ppermute(value, ("star", "tm"), steps))
     return got
@@ -588,7 +589,7 @@
         [rows_type(8 + (both_parts + 7) // 8 * 8)],
         [state] + across + kept,
     )
-    received = lax.ppermute(parts, "tm", [(i, i - 1) for i in range(1, tm_count, 2)])
+    _, received = direct(parts, "tm", [1])
     out_astro, out_att, out_inst = call(
         functools.partial(place_kernel, comps, share),
         "place",

time: 99.4 us -> 98.3 us (0.989)
  waiting for transfers between devices: 66.6 us -> 1.77 us
  starting transfers between devices: 18.1 us -> 81.8 us
    ppermute x1 -> x0, waiting for transfers between devices: 65.6 us -> none  [per_device(): lax.ppermute(parts, 'tm', [(i, i - 1) for i in range(1, tm_count, 2)])]
    ppermute x2 -> x3, starting transfers between devices: 0.93 us -> 66 us  [direct(): lax.ppermute(value, axis, [(i, i ^ gap) for i in range(count)])]
    ppermute x1 -> x0, starting transfers between devices: 1.29 us -> none  [per_device(): lax.ppermute(parts, 'tm', [(i, i - 1) for i in range(1, tm_count, 2)])]
where the time goes in v3:
time: 98.3 us; the launch traced here: 97.6 us
  starting transfers between devices  81.8 us (83%)
  Pallas kernels  12.9 us (13%)
  waiting for transfers between devices  1.77 us (2%)
  between operations  1.11 us (1%)
    ppermute x3, starting transfers between devices, direct(): lax.ppermute(value, axis, [(i, i ^ gap) for i in range(count)])  66 us
    ppermute x24, starting transfers between devices, exchange(): got.append(lax.ppermute(value, ('star', 'tm'), steps))  15.9 us
    pallas_call x15, Pallas kernels, call(): pl.pallas_call(kernel, name=name, out_shape=[jax.ShapeDtypeStruct(shape,...  12.9 us
  transfers between devices with their start and end apart: 27, of which 2 were waited for; matrix products, arithmetic and copies ran while one was open for 0% of the time, Pallas kernels for 6%

profile of v3, /device:TPU:0, one launch (start us, length us, event | category | flops | bytes accessed | tf_op | source)
XLA Modules:
  0.0 97.6 jit_solution(5019593958227081022)
XLA Ops:
  0.6 1.9 %first.1 = (f32[72,128]{1,0:T(8,128)S(1)}, f32[616,128]{1,0:T(8,128)S(1)}, bf16[128,6144]{1,0:T(8,128)(2,1)S(1)}, bf16[1024,128]{1,0:T(8,128)(2,1)S(1)}, s32[56,128]{1,0:T(8,128)S(1)}) custom-call(f32[8,128]{1,0:T(8,128)} %bitcast.12, f32[5,8,128]{2,1,0:T(8,128)} %bitcast.11, s32[8,128]{1,0:T(8,128)} %bitcast.13, f32[512,128]{1,0:T(8,128)} %bitcast.8, ...), custom_call_target="tpu_custom_call" | custom-call | tf_op jit(solution)/shard_map/first/pallas_call | solution.py:462
  2.6 0.5 collective-permute-start
  3.1 0.9 collective-permute-done.other_ref
  4.0 0.4 collective-permute-start.1
  4.4 0.7 collective-permute-start.4
  5.0 0.7 collective-permute-start.3
  5.7 0.7 collective-permute-start.2
  6.4 0.0 collective-permute-done.1.pack_ref.refs_2_
  6.4 0.5 prepare.1
  6.9 0.0 collective-permute-done.2.refs_1_
  7.0 0.7 collective-permute-start.7
  7.6 0.7 collective-permute-start.6
  8.3 0.7 collective-permute-start.5
  9.0 2.2 %astro.3 = (f32[80,128]{1,0:T(8,128)S(1)}, bf16[128,8192]{1,0:T(8,128)(2,1)S(1)}) custom-call(f32[384,128]{1,0:T(8,128)S(1)} %get-tuple-element.58.keep_ref.refs_0_, f32[64,128]{1,0:T(8,128)S(1)} %get-tuple-element.65.rows_ref.refs_10_), custom_call_target="tpu_custom_call" | custom-call | tf_op jit(solution)/shard_map/astro/pallas_call | solution.py:462
  11.2 0.0 collective-permute-done.7.refs_14_
  11.2 0.0 collective-permute-done.6.refs_13_
  11.3 1.6 %step.3 = (f32[32,128]{1,0:T(8,128)S(1)}, f32[16,128]{1,0:T(8,128)S(1)}, f32[96,128]{1,0:T(8,128)S(1)}, f32[96,128]{1,0:T(8,128)S(1)}, f32[16,128]{1,0:T(8,128)S(1)}, /*index=5*/f32[16,128]{1,0:T(8,128)S(1)}) custom-call(f32[384,128]{1,0:T(8,128)S(1)} %get-tuple-element.58.keep_ref.refs_0_, f32[616,128]{1,0:T(8,128)S(1)} %get-tuple-element.49.refs_1_, ...), custom_call_target="tpu_custom_call" | custom-call | tf_op jit(solution)/shard_map/step/pallas_call | solution.py:462
  12.9 0.7 collective-permute-start.10
  13.5 0.7 collective-permute-start.9
  14.2 0.7 collective-permute-start.8
  14.9 0.0 collective-permute-done.10.refs_3_
  15.0 0.7 collective-permute-start.13
  15.6 0.7 collective-permute-start.12
  16.3 0.7 collective-permute-start.11
  17.0 1.5 %astro.4.refs_9_ = f32[80,128]{1,0:T(8,128)S(1)} custom-call(f32[384,128]{1,0:T(8,128)S(1)} %get-tuple-element.58.keep_ref.refs_0_, f32[64,128]{1,0:T(8,128)S(1)} %get-tuple-element.69.rows_ref, bf16[128,8192]{1,0:T(8,128)(2,1)S(1)} %get-tuple-element.70.refs_0_), custom_call_target="tpu_custom_call" | custom-call | tf_op jit(solution)/shard_map/astro/pallas_call | solution.py:462
  18.5 0.0 collective-permute-done.13.refs_18_
  18.5 1.6 %step.4 = (f32[32,128]{1,0:T(8,128)S(1)}, f32[16,128]{1,0:T(8,128)S(1)}, f32[96,128]{1,0:T(8,128)S(1)}, f32[96,128]{1,0:T(8,128)S(1)}, f32[16,128]{1,0:T(8,128)S(1)}, /*index=5*/f32[16,128]{1,0:T(8,128)S(1)}) custom-call(f32[384,128]{1,0:T(8,128)S(1)} %get-tuple-element.58.keep_ref.refs_0_, f32[616,128]{1,0:T(8,128)S(1)} %get-tuple-element.49.refs_1_, ...), custom_call_target="tpu_custom_call" | custom-call | tf_op jit(solution)/shard_map/step/pallas_call | solution.py:462
  20.1 0.7 collective-permute-start.16
  20.8 0.7 collective-permute-start.15
  21.5 0.7 collective-permute-start.14
  22.2 0.0 collective-permute-done.16.refs_3_
  22.2 0.0 collective-permute-done.15.refs_2_
  22.2 0.7 collective-permute-start.19
  22.9 0.7 collective-permute-start.18
  23.6 0.7 collective-permute-start.17
  24.2 1.5 %astro.5.refs_9_ = f32[80,128]{1,0:T(8,128)S(1)} custom-call(f32[384,128]{1,0:T(8,128)S(1)} %get-tuple-element.58.keep_ref.refs_0_, f32[64,128]{1,0:T(8,128)S(1)} %get-tuple-element.78.rows_ref, bf16[128,8192]{1,0:T(8,128)(2,1)S(1)} %get-tuple-element.70.refs_0_), custom_call_target="tpu_custom_call" | custom-call | tf_op jit(solution)/shard_map/astro/pallas_call | solution.py:462
  25.7 0.0 collective-permute-done.18.refs_17_
  25.8 1.1 %step.5 = (f32[8,128]{1,0:T(8,128)S(1)}, f32[16,128]{1,0:T(8,128)S(1)}, f32[96,128]{1,0:T(8,128)S(1)}, f32[96,128]{1,0:T(8,128)}, f32[16,128]{1,0:T(8,128)}, /*index=5*/f32[16,128]{1,0:T(8,128)}) custom-call(f32[384,128]{1,0:T(8,128)S(1)} %get-tuple-element.58.keep_ref.refs_0_, f32[616,128]{1,0:T(8,128)S(1)} %get-tuple-element.49.refs_1_, ...), custom_call_target="tpu_custom_call" | custom-call | tf_op jit(solution)/shard_map/step/pallas_call | solution.py:462
  26.9 0.6 collective-permute-start.22
  27.5 0.7 collective-permute-start.21
  28.2 0.7 collective-permute-start.20
  28.9 0.7 collective-permute-start.25
  29.6 0.7 collective-permute-start.24
  30.3 0.7 collective-permute-start.23
  31.0 0.1 last.1.own_ref
  31.1 65.0 %collective-permute-start.26 = (f32[32,128]{1,0:T(8,128)S(1)}, f32[32,128]{1,0:T(8,128)S(1)}, u32[]{:S(2)}, u32[]{:S(2)}) collective-permute-start(f32[32,128]{1,0:T(8,128)S(1)} %last.1.own_ref), channel_id=1, source_target_pairs={{0,1},{1,0},{2,3},{3,2},{4,5},{5,4},{6,7},{7,6},{8,9},{9,8},{10,11... | collective-permute-start | bytes 49160 | tf_op jit(solution)/shard_map/ppermute | solution.py:476
  96.2 0.8 collective-permute-done.26.other_ref
  97.0 0.6 place.1
  (21 shorter events, 0.2 us)
Async XLA Ops:
  2.6 1.4 %collective-permute-start = (f32[72,128]{1,0:T(8,128)S(1)}, f32[72,128]{1,0:T(8,128)S(1)}, u32[]{:S(2)}, u32[]{:S(2)}) collective-permute-start(f32[72,128]{1,0:T(8,128)S(1)} %get-tuple-element.47.own_ref), channel_id=1, source_target_pairs={{0,1},{1,0},{2,3},{3,2},{4,5},{5,4},{6,7},{7,6},{8,9},{9,8},{10,11... | collective-permute-start | bytes 110600 | tf_op jit(solution)/shard_map/ppermute | solution.py:476
  4.0 2.4 %collective-permute-start.1 = (f32[616,128]{1,0:T(8,128)S(1)}, f32[616,128]{1,0:T(8,128)S(1)}, u32[]{:S(2)}, u32[]{:S(2)}) collective-permute-start(f32[616,128]{1,0:T(8,128)S(1)} %get-tuple-element.49.refs_1_), channel_id=1, source_target_pairs={{0,1},{1,0},{2,3},{3,2},{4,5},{5,4},{6,7},{7,6},{8,9},{9,8},{10,11... | collective-permute-start | bytes 946184 | tf_op jit(solution)/shard_map/ppermute | solution.py:476
  4.4 2.5 %collective-permute-start.4 = (f32[128,128]{1,0:T(8,128)S(1)}, f32[128,128]{1,0:T(8,128)S(1)}, u32[]{:S(2)}, u32[]{:S(2)}) collective-permute-start(f32[128,128]{1,0:T(8,128)S(1)} %merge.1.refs_0_), channel_id=1, source_target_pairs={{0,0},{1,7},{2,2},{3,5},{4,4},{5,3},{6,6},{7,1},{8,8},{9,15},{10,1... | collective-permute-start | bytes 196616 | tf_op jit(solution)/shard_map/ppermute | solution.py:490
  5.0 1.9 %collective-permute-start.3 = (f32[128,128]{1,0:T(8,128)S(1)}, f32[128,128]{1,0:T(8,128)S(1)}, u32[]{:S(2)}, u32[]{:S(2)}) collective-permute-start(f32[128,128]{1,0:T(8,128)S(1)} %merge.1.refs_0_), channel_id=1, source_target_pairs={{0,0},{1,5},{2,2},{3,7},{4,4},{5,1},{6,6},{7,3},{8,8},{9,13},{10,1... | collective-permute-start | bytes 196616 | tf_op jit(solution)/shard_map/ppermute | solution.py:490
  5.7 1.2 %collective-permute-start.2 = (f32[128,128]{1,0:T(8,128)S(1)}, f32[128,128]{1,0:T(8,128)S(1)}, u32[]{:S(2)}, u32[]{:S(2)}) collective-permute-start(f32[128,128]{1,0:T(8,128)S(1)} %merge.1.refs_0_), channel_id=1, source_target_pairs={{0,0},{1,3},{2,2},{3,1},{4,4},{5,7},{6,6},{7,5},{8,8},{9,11},{10,1... | collective-permute-start | bytes 196616 | tf_op jit(solution)/shard_map/ppermute | solution.py:490
  7.0 4.2 %collective-permute-start.7 = (f32[16,128]{1,0:T(8,128)S(1)}, f32[16,128]{1,0:T(8,128)S(1)}, u32[]{:S(2)}, u32[]{:S(2)}) collective-permute-start(f32[16,128]{1,0:T(8,128)S(1)} %get-tuple-element.67.refs_11_), channel_id=1, source_target_pairs={{0,0},{1,25},{2,2},{3,27},{4,4},{5,29},{6,6},{7,31},{8,8},{9,17},{... | collective-permute-start | bytes 24584 | tf_op jit(solution)/shard_map/ppermute | solution.py:490
  7.6 3.6 %collective-permute-start.6 = (f32[16,128]{1,0:T(8,128)S(1)}, f32[16,128]{1,0:T(8,128)S(1)}, u32[]{:S(2)}, u32[]{:S(2)}) collective-permute-start(f32[16,128]{1,0:T(8,128)S(1)} %get-tuple-element.67.refs_11_), channel_id=1, source_target_pairs={{0,0},{1,17},{2,2},{3,19},{4,4},{5,21},{6,6},{7,23},{8,8},{9,25},{... | collective-permute-start | bytes 24584 | tf_op jit(solution)/shard_map/ppermute | solution.py:490
  8.3 2.9 %collective-permute-start.5 = (f32[16,128]{1,0:T(8,128)S(1)}, f32[16,128]{1,0:T(8,128)S(1)}, u32[]{:S(2)}, u32[]{:S(2)}) collective-permute-start(f32[16,128]{1,0:T(8,128)S(1)} %get-tuple-element.67.refs_11_), channel_id=1, source_target_pairs={{0,0},{1,9},{2,2},{3,11},{4,4},{5,13},{6,6},{7,15},{8,8},{9,1},{10... | collective-permute-start | bytes 24584 | tf_op jit(solution)/shard_map/ppermute | solution.py:490
  12.9 2.0 %collective-permute-start.10 = (f32[32,128]{1,0:T(8,128)S(1)}, f32[32,128]{1,0:T(8,128)S(1)}, u32[]{:S(2)}, u32[]{:S(2)}) collective-permute-start(f32[32,128]{1,0:T(8,128)S(1)} %get-tuple-element.68.refs_0_), channel_id=1, source_target_pairs={{0,0},{1,7},{2,2},{3,5},{4,4},{5,3},{6,6},{7,1},{8,8},{9,15},{10,1... | collective-permute-start | bytes 49160 | tf_op jit(solution)/shard_map/ppermute | solution.py:490
  13.5 1.4 %collective-permute-start.9 = (f32[32,128]{1,0:T(8,128)S(1)}, f32[32,128]{1,0:T(8,128)S(1)}, u32[]{:S(2)}, u32[]{:S(2)}) collective-permute-start(f32[32,128]{1,0:T(8,128)S(1)} %get-tuple-element.68.refs_0_), channel_id=1, source_target_pairs={{0,0},{1,5},{2,2},{3,7},{4,4},{5,1},{6,6},{7,3},{8,8},{9,13},{10,1... | collective-permute-start | bytes 49160 | tf_op jit(solution)/shard_map/ppermute | solution.py:490
  14.2 0.7 collective-permute-start.8
  15.0 3.5 %collective-permute-start.13 = (f32[16,128]{1,0:T(8,128)S(1)}, f32[16,128]{1,0:T(8,128)S(1)}, u32[]{:S(2)}, u32[]{:S(2)}) collective-permute-start(f32[16,128]{1,0:T(8,128)S(1)} %get-tuple-element.76.refs_15_), channel_id=1, source_target_pairs={{0,0},{1,25},{2,2},{3,27},{4,4},{5,29},{6,6},{7,31},{8,8},{9,17},{... | collective-permute-start | bytes 24584 | tf_op jit(solution)/shard_map/ppermute | solution.py:490
  15.6 2.9 %collective-permute-start.12 = (f32[16,128]{1,0:T(8,128)S(1)}, f32[16,128]{1,0:T(8,128)S(1)}, u32[]{:S(2)}, u32[]{:S(2)}) collective-permute-start(f32[16,128]{1,0:T(8,128)S(1)} %get-tuple-element.76.refs_15_), channel_id=1, source_target_pairs={{0,0},{1,17},{2,2},{3,19},{4,4},{5,21},{6,6},{7,23},{8,8},{9,25},{... | collective-permute-start | bytes 24584 | tf_op jit(solution)/shard_map/ppermute | solution.py:490
  16.3 2.2 %collective-permute-start.11 = (f32[16,128]{1,0:T(8,128)S(1)}, f32[16,128]{1,0:T(8,128)S(1)}, u32[]{:S(2)}, u32[]{:S(2)}) collective-permute-start(f32[16,128]{1,0:T(8,128)S(1)} %get-tuple-element.76.refs_15_), channel_id=1, source_target_pairs={{0,0},{1,9},{2,2},{3,11},{4,4},{5,13},{6,6},{7,15},{8,8},{9,1},{10... | collective-permute-start | bytes 24584 | tf_op jit(solution)/shard_map/ppermute | solution.py:490
  20.1 2.0 %collective-permute-start.16 = (f32[32,128]{1,0:T(8,128)S(1)}, f32[32,128]{1,0:T(8,128)S(1)}, u32[]{:S(2)}, u32[]{:S(2)}) collective-permute-start(f32[32,128]{1,0:T(8,128)S(1)} %get-tuple-element.77.refs_0_), channel_id=1, source_target_pairs={{0,0},{1,7},{2,2},{3,5},{4,4},{5,3},{6,6},{7,1},{8,8},{9,15},{10,1... | collective-permute-start | bytes 49160 | tf_op jit(solution)/shard_map/ppermute | solution.py:490
  20.8 1.4 %collective-permute-start.15 = (f32[32,128]{1,0:T(8,128)S(1)}, f32[32,128]{1,0:T(8,128)S(1)}, u32[]{:S(2)}, u32[]{:S(2)}) collective-permute-start(f32[32,128]{1,0:T(8,128)S(1)} %get-tuple-element.77.refs_0_), channel_id=1, source_target_pairs={{0,0},{1,5},{2,2},{3,7},{4,4},{5,1},{6,6},{7,3},{8,8},{9,13},{10,1... | collective-permute-start | bytes 49160 | tf_op jit(solution)/shard_map/ppermute | solution.py:490
  21.5 0.7 collective-permute-start.14
  22.2 3.5 %collective-permute-start.19 = (f32[16,128]{1,0:T(8,128)S(1)}, f32[16,128]{1,0:T(8,128)S(1)}, u32[]{:S(2)}, u32[]{:S(2)}) collective-permute-start(f32[16,128]{1,0:T(8,128)S(1)} %get-tuple-element.84.refs_15_), channel_id=1, source_target_pairs={{0,0},{1,25},{2,2},{3,27},{4,4},{5,29},{6,6},{7,31},{8,8},{9,17},{... | collective-permute-start | bytes 24584 | tf_op jit(solution)/shard_map/ppermute | solution.py:490
  22.9 2.9 %collective-permute-start.18 = (f32[16,128]{1,0:T(8,128)S(1)}, f32[16,128]{1,0:T(8,128)S(1)}, u32[]{:S(2)}, u32[]{:S(2)}) collective-permute-start(f32[16,128]{1,0:T(8,128)S(1)} %get-tuple-element.84.refs_15_), channel_id=1, source_target_pairs={{0,0},{1,17},{2,2},{3,19},{4,4},{5,21},{6,6},{7,23},{8,8},{9,25},{... | collective-permute-start | bytes 24584 | tf_op jit(solution)/shard_map/ppermute | solution.py:490
  23.6 2.2 %collective-permute-start.17 = (f32[16,128]{1,0:T(8,128)S(1)}, f32[16,128]{1,0:T(8,128)S(1)}, u32[]{:S(2)}, u32[]{:S(2)}) collective-permute-start(f32[16,128]{1,0:T(8,128)S(1)} %get-tuple-element.84.refs_15_), channel_id=1, source_target_pairs={{0,0},{1,9},{2,2},{3,11},{4,4},{5,13},{6,6},{7,15},{8,8},{9,1},{10... | collective-permute-start | bytes 24584 | tf_op jit(solution)/shard_map/ppermute | solution.py:490
  26.9 2.0 %collective-permute-start.22 = (f32[8,128]{1,0:T(8,128)S(1)}, f32[8,128]{1,0:T(8,128)S(1)}, u32[]{:S(2)}, u32[]{:S(2)}) collective-permute-start(f32[8,128]{1,0:T(8,128)S(1)} %get-tuple-element.86.refs_0_), channel_id=1, source_target_pairs={{0,0},{1,7},{2,2},{3,5},{4,4},{5,3},{6,6},{7,1},{8,8},{9,15},{10,1... | collective-permute-start | bytes 12296 | tf_op jit(solution)/shard_map/ppermute | solution.py:490
  27.5 1.4 %collective-permute-start.21 = (f32[8,128]{1,0:T(8,128)S(1)}, f32[8,128]{1,0:T(8,128)S(1)}, u32[]{:S(2)}, u32[]{:S(2)}) collective-permute-start(f32[8,128]{1,0:T(8,128)S(1)} %get-tuple-element.86.refs_0_), channel_id=1, source_target_pairs={{0,0},{1,5},{2,2},{3,7},{4,4},{5,1},{6,6},{7,3},{8,8},{9,13},{10,1... | collective-permute-start | bytes 12296 | tf_op jit(solution)/shard_map/ppermute | solution.py:490
  28.2 0.7 collective-permute-start.20
  28.9 2.0 %collective-permute-start.25 = (f32[8,128]{1,0:T(8,128)S(1)}, f32[8,128]{1,0:T(8,128)S(1)}, u32[]{:S(2)}, u32[]{:S(2)}) collective-permute-start(f32[8,128]{1,0:T(8,128)S(1)} %sum.1.refs_0_), channel_id=1, source_target_pairs={{0,0},{1,25},{2,2},{3,27},{4,4},{5,29},{6,6},{7,31},{8,8},{9,17},{... | collective-permute-start | bytes 12296 | tf_op jit(solution)/shard_map/ppermute | solution.py:490
  29.6 1.4 %collective-permute-start.24 = (f32[8,128]{1,0:T(8,128)S(1)}, f32[8,128]{1,0:T(8,128)S(1)}, u32[]{:S(2)}, u32[]{:S(2)}) collective-permute-start(f32[8,128]{1,0:T(8,128)S(1)} %sum.1.refs_0_), channel_id=1, source_target_pairs={{0,0},{1,17},{2,2},{3,19},{4,4},{5,21},{6,6},{7,23},{8,8},{9,25},{... | collective-permute-start | bytes 12296 | tf_op jit(solution)/shard_map/ppermute | solution.py:490
  30.3 0.7 collective-permute-start.23
  31.1 65.9 %collective-permute-start.26 = (f32[32,128]{1,0:T(8,128)S(1)}, f32[32,128]{1,0:T(8,128)S(1)}, u32[]{:S(2)}, u32[]{:S(2)}) collective-permute-start(f32[32,128]{1,0:T(8,128)S(1)} %last.1.own_ref), channel_id=1, source_target_pairs={{0,1},{1,0},{2,3},{3,2},{4,5},{5,4},{6,7},{7,6},{8,9},{9,8},{10,11... | collective-permute-start | bytes 49160 | tf_op jit(solution)/shard_map/ppermute | solution.py:476

commit v4 on v1

--- a/solution.py
+++ b/solution.py
@@ -194,13 +194,6 @@
     prepare_att(pack_ref[places[3]], att2_ref)
 
 
-def places_of(here, core, count):
-    out = [here, here ^ 1]
-    for pair in range(2, count, 2):
-        out += [here ^ (pair + 1 - core), here ^ (pair + core)]
-    return out
-
-
 def tree_sum(values):
     while len(values) > 1:
         values = [values[i] + values[i + 1] for i in range(0, len(values), 2)]
@@ -260,7 +253,7 @@
     *ins, rows_ref, out_ref = refs
     me = lax.axis_index("tm")
     chip = me // 2
-    places = places_of(chip, me % 2, count)
+    places = [chip ^ gap for gap in range(count)]
     zero = jnp.zeros((8, LANES), f32)
     mine, prev, after = zero, zero, zero
     for ref, where in zip(ins, places):
@@ -494,21 +487,15 @@
 
 def exchange(value, axis):
     tm_count, star_count = lax.axis_size("tm"), lax.axis_size("star")
-    count = star_count if axis == "star" else tm_count // 2
-    both = ("star", "tm")
-    got = []
-    for pair in range(2, count, 2):
+    got = [value]
+    for gap in range(1, star_count if axis == "star" else tm_count // 2):
         steps = []
         for star in range(star_count):
             for tm in range(tm_count):
-                gap = pair + 1 - tm % 2
-                far = (star ^ gap, tm) if axis == "star" else (star, tm ^ (2 * gap))
+                far = (star ^ gap, tm ^ 1) if axis == "star" else (star, tm ^ (2 * gap + 1))
                 steps.append((star * tm_count + tm, far[0] * tm_count + far[1]))
-        got.append(lax.ppermute(value, both, steps))
-    near = direct(value, axis, [1 if axis == "star" else 2])
-    for value in got:
-        near += direct(value, "tm", [1])
-    return near
+        got.append(lax.ppermute(value, ("star", "tm"), steps))
+    return got
 
 
 def rows_type(rows):

time: 65.4 us -> 59.5 us (0.910)
  waiting for transfers between devices: 27.8 us -> 15.4 us
  starting transfers between devices: 23.9 us -> 30.3 us
    ppermute x7 -> x21, starting transfers between devices: 14.5 us -> 24.3 us  [exchange(): got.append(lax.ppermute(value, ('star', 'tm'), steps))]
    ppermute x7 -> x21, waiting for transfers between devices: 17.1 us -> 9.88 us  [exchange(): got.append(lax.ppermute(value, ('star', 'tm'), steps))]
    ppermute x19 -> x5, waiting for transfers between devices: 10.7 us -> 5.57 us  [direct(): lax.ppermute(value, axis, [(i, i ^ gap) for i in range(count)])]
    ppermute x19 -> x5, starting transfers between devices: 9.35 us -> 6.04 us  [direct(): lax.ppermute(value, axis, [(i, i ^ gap) for i in range(count)])]
  transfers between devices with their start and end apart: 26 -> 26, of which waited for: 15 -> 16; matrix products, arithmetic and copies ran while one was open for 0% -> 0% of each run, Pallas kernels for 9% -> 10%
where the time goes in v4:
time: 59.5 us; the launch traced here: 59.4 us
  starting transfers between devices  30.3 us (51%)
  waiting for transfers between devices  15.4 us (26%)
  Pallas kernels  12.8 us (22%)
  between operations  0.78 us (1%)
    ppermute x21, starting transfers between devices, exchange(): got.append(lax.ppermute(value, ('star', 'tm'), steps))  24.3 us
    pallas_call x14, Pallas kernels, call(): pl.pallas_call(kernel, name=name, out_shape=[jax.ShapeDtypeStruct(shape,...  12.8 us
    ppermute x21, waiting for transfers between devices, exchange(): got.append(lax.ppermute(value, ('star', 'tm'), steps))  9.88 us
    ppermute x5, starting transfers between devices, direct(): lax.ppermute(value, axis, [(i, i ^ gap) for i in range(count)])  6.04 us
    ppermute x5, waiting for transfers between devices, direct(): lax.ppermute(value, axis, [(i, i ^ gap) for i in range(count)])  5.57 us
  transfers between devices with their start and end apart: 26, of which 16 were waited for; matrix products, arithmetic and copies ran while one was open for 0% of the time, Pallas kernels for 10%

profile of v4, /device:TPU:0, one launch (start us, length us, event | category | flops | bytes accessed | tf_op | source)
XLA Modules:
  0.0 59.4 jit_solution(3382656240845671431)
XLA Ops:
  0.6 1.9 %first.1 = (f32[72,128]{1,0:T(8,128)S(1)}, f32[616,128]{1,0:T(8,128)S(1)}, bf16[128,6144]{1,0:T(8,128)(2,1)S(1)}, bf16[1024,128]{1,0:T(8,128)(2,1)S(1)}, s32[56,128]{1,0:T(8,128)S(1)}) custom-call(f32[8,128]{1,0:T(8,128)} %bitcast.12, f32[5,8,128]{2,1,0:T(8,128)} %bitcast.11, s32[8,128]{1,0:T(8,128)} %bitcast.13, f32[512,128]{1,0:T(8,128)} %bitcast.8, ...), custom_call_target="tpu_custom_call" | custom-call | tf_op jit(solution)/shard_map/first/pallas_call | solution.py:470
  2.6 5.1 %collective-permute-start.2 = (f32[72,128]{1,0:T(8,128)S(1)}, f32[72,128]{1,0:T(8,128)S(1)}, u32[]{:S(2)}, u32[]{:S(2)}) collective-permute-start(f32[72,128]{1,0:T(8,128)S(1)} %get-tuple-element.37.refs_0_), channel_id=1, source_target_pairs={{0,6},{1,7},{2,4},{3,5},{4,2},{5,3},{6,0},{7,1},{8,14},{9,15},{10,... | collective-permute-start | bytes 110600 | tf_op jit(solution)/shard_map/ppermute | solution.py:484
  7.7 0.6 %collective-permute-start = (f32[72,128]{1,0:T(8,128)S(1)}, f32[72,128]{1,0:T(8,128)S(1)}, u32[]{:S(2)}, u32[]{:S(2)}) collective-permute-start(f32[72,128]{1,0:T(8,128)S(1)} %get-tuple-element.37.refs_0_), channel_id=1, source_target_pairs={{0,2},{1,3},{2,0},{3,1},{4,6},{5,7},{6,4},{7,5},{8,10},{9,11},{10,... | collective-permute-start | bytes 110600 | tf_op jit(solution)/shard_map/ppermute | solution.py:484
  8.3 1.3 %collective-permute-done.2.refs_3_ = f32[72,128]{1,0:T(8,128)S(1)} collective-permute-done((f32[72,128]{1,0:T(8,128)S(1)}, f32[72,128]{1,0:T(8,128)S(1)}, u32[]{:S(2)}, u32[]{:S(2)}) %collective-permute-start.2) | collective-permute-done | bytes 36896 | tf_op jit(solution)/shard_map/ppermute | solution.py:484
  9.6 2.9 %collective-permute-done.1.refs_2_ = f32[72,128]{1,0:T(8,128)S(1)} collective-permute-done((f32[72,128]{1,0:T(8,128)S(1)}, f32[72,128]{1,0:T(8,128)S(1)}, u32[]{:S(2)}, u32[]{:S(2)}) %collective-permute-start.1) | collective-permute-done | bytes 36896 | tf_op jit(solution)/shard_map/ppermute | solution.py:484
  12.7 1.3 %collective-permute-done.3.other_ref.refs_1_ = f32[272,128]{1,0:T(8,128)S(1)} collective-permute-done((f32[272,128]{1,0:T(8,128)S(1)}, f32[272,128]{1,0:T(8,128)S(1)}, u32[]{:S(2)}, u32[]{:S(2)}) %collective-permute-start.3) | collective-permute-done | bytes 139296 | tf_op jit(solution)/shard_map/ppermute | solution.py:484
  14.0 0.2 collective-permute-start.4
  14.2 2.4 %collective-permute-start.7 = (f32[16,128]{1,0:T(8,128)S(1)}, f32[16,128]{1,0:T(8,128)S(1)}, u32[]{:S(2)}, u32[]{:S(2)}) collective-permute-start(f32[16,128]{1,0:T(8,128)S(1)} %group.3.refs_11_), channel_id=1, source_target_pairs={{0,25},{1,24},{2,27},{3,26},{4,29},{5,28},{6,31},{7,30},{8,17},{9,... | collective-permute-start | bytes 24584 | tf_op jit(solution)/shard_map/ppermute | solution.py:497
  16.6 0.3 collective-permute-start.6
  16.9 0.5 collective-permute-start.5
  17.4 2.2 %astro.3 = (f32[80,128]{1,0:T(8,128)S(1)}, bf16[128,8192]{1,0:T(8,128)(2,1)S(1)}) custom-call(f32[272,128]{1,0:T(8,128)S(1)} %chip.1.own_ref.refs_0_, f32[272,128]{1,0:T(8,128)S(1)} %collective-permute-done.3.other_ref.refs_1_), custom_call_target="tpu_custom_call" | custom-call | tf_op jit(solution)/shard_map/astro/pallas_call | solution.py:470
  19.7 0.5 prepare.1
  20.2 1.6 %step.3 = (f32[32,128]{1,0:T(8,128)S(1)}, f32[16,128]{1,0:T(8,128)S(1)}, f32[96,128]{1,0:T(8,128)S(1)}, f32[96,128]{1,0:T(8,128)S(1)}, f32[16,128]{1,0:T(8,128)S(1)}, /*index=5*/f32[16,128]{1,0:T(8,128)S(1)}) custom-call(f32[272,128]{1,0:T(8,128)S(1)} %chip.1.own_ref.refs_0_, f32[272,128]{1,0:T(8,128)S(1)} %collective-permute-done.3.other_ref.refs_1_, ...), custom_call_target="tpu_custom_call" | custom-call | tf_op jit(solution)/shard_map/step/pallas_call | solution.py:470
  21.8 1.3 %collective-permute-start.10 = (f32[32,128]{1,0:T(8,128)S(1)}, f32[32,128]{1,0:T(8,128)S(1)}, u32[]{:S(2)}, u32[]{:S(2)}) collective-permute-start(f32[32,128]{1,0:T(8,128)S(1)} %get-tuple-element.49.refs_0_), channel_id=1, source_target_pairs={{0,7},{1,6},{2,5},{3,4},{4,3},{5,2},{6,1},{7,0},{8,15},{9,14},{10,... | collective-permute-start | bytes 49160 | tf_op jit(solution)/shard_map/ppermute | solution.py:497
  23.1 0.6 %collective-permute-start.9 = (f32[32,128]{1,0:T(8,128)S(1)}, f32[32,128]{1,0:T(8,128)S(1)}, u32[]{:S(2)}, u32[]{:S(2)}) collective-permute-start(f32[32,128]{1,0:T(8,128)S(1)} %get-tuple-element.49.refs_0_), channel_id=1, source_target_pairs={{0,5},{1,4},{2,7},{3,6},{4,1},{5,0},{6,3},{7,2},{8,13},{9,12},{10,... | collective-permute-start | bytes 49160 | tf_op jit(solution)/shard_map/ppermute | solution.py:497
  23.7 2.0 %collective-permute-start.8 = (f32[32,128]{1,0:T(8,128)S(1)}, f32[32,128]{1,0:T(8,128)S(1)}, u32[]{:S(2)}, u32[]{:S(2)}) collective-permute-start(f32[32,128]{1,0:T(8,128)S(1)} %get-tuple-element.49.refs_0_), channel_id=1, source_target_pairs={{0,3},{1,2},{2,1},{3,0},{4,7},{5,6},{6,5},{7,4},{8,11},{9,10},{10,... | collective-permute-start | bytes 49160 | tf_op jit(solution)/shard_map/ppermute | solution.py:497
  25.8 1.1 %collective-permute-done.10.refs_3_ = f32[32,128]{1,0:T(8,128)S(1)} collective-permute-done((f32[32,128]{1,0:T(8,128)S(1)}, f32[32,128]{1,0:T(8,128)S(1)}, u32[]{:S(2)}, u32[]{:S(2)}) %collective-permute-start.10) | collective-permute-done | bytes 16416 | tf_op jit(solution)/shard_map/ppermute | solution.py:497
  26.8 0.5 collective-permute-done.9.refs_2_
  27.6 2.3 %collective-permute-start.13 = (f32[16,128]{1,0:T(8,128)S(1)}, f32[16,128]{1,0:T(8,128)S(1)}, u32[]{:S(2)}, u32[]{:S(2)}) collective-permute-start(f32[16,128]{1,0:T(8,128)S(1)} %get-tuple-element.56.refs_16_), channel_id=1, source_target_pairs={{0,25},{1,24},{2,27},{3,26},{4,29},{5,28},{6,31},{7,30},{8,17},{9,... | collective-permute-start | bytes 24584 | tf_op jit(solution)/shard_map/ppermute | solution.py:497
  29.9 0.4 collective-permute-start.12
  30.3 0.3 collective-permute-start.11
  30.6 1.5 %astro.4.refs_10_ = f32[80,128]{1,0:T(8,128)S(1)} custom-call(f32[272,128]{1,0:T(8,128)S(1)} %chip.1.own_ref.refs_0_, f32[272,128]{1,0:T(8,128)S(1)} %collective-permute-done.3.other_ref.refs_1_, bf16[128,8192]{1,0:T(8,128)(2,1)S(1)} %get-tuple-element.46.refs_2_, f32[64,128]{1,0:T(8,128)S(1)} %get-tuple-element.50.refs_3_), custom_call_target="tpu_custom_call" | custom-call | tf_op jit(solution)/shard_map/astro/pallas_call | solution.py:470
  32.1 0.8 %collective-permute-done.12.refs_18_ = f32[16,128]{1,0:T(8,128)S(1)} collective-permute-done((f32[16,128]{1,0:T(8,128)S(1)}, f32[16,128]{1,0:T(8,128)S(1)}, u32[]{:S(2)}, u32[]{:S(2)}) %collective-permute-start.12) | collective-permute-done | bytes 8224 | tf_op jit(solution)/shard_map/ppermute | solution.py:497
  32.9 0.4 collective-permute-done.11.refs_17_
  33.4 1.6 %step.4 = (f32[32,128]{1,0:T(8,128)S(1)}, f32[16,128]{1,0:T(8,128)S(1)}, f32[96,128]{1,0:T(8,128)S(1)}, f32[96,128]{1,0:T(8,128)S(1)}, f32[16,128]{1,0:T(8,128)S(1)}, /*index=5*/f32[16,128]{1,0:T(8,128)S(1)}) custom-call(f32[272,128]{1,0:T(8,128)S(1)} %chip.1.own_ref.refs_0_, f32[272,128]{1,0:T(8,128)S(1)} %collective-permute-done.3.other_ref.refs_1_, ...), custom_call_target="tpu_custom_call" | custom-call | tf_op jit(solution)/shard_map/step/pallas_call | solution.py:470
  35.0 2.2 %collective-permute-start.16 = (f32[32,128]{1,0:T(8,128)S(1)}, f32[32,128]{1,0:T(8,128)S(1)}, u32[]{:S(2)}, u32[]{:S(2)}) collective-permute-start(f32[32,128]{1,0:T(8,128)S(1)} %get-tuple-element.57.refs_0_), channel_id=1, source_target_pairs={{0,7},{1,6},{2,5},{3,4},{4,3},{5,2},{6,1},{7,0},{8,15},{9,14},{10,... | collective-permute-start | bytes 49160 | tf_op jit(solution)/shard_map/ppermute | solution.py:497
  37.2 0.7 %collective-permute-start.15 = (f32[32,128]{1,0:T(8,128)S(1)}, f32[32,128]{1,0:T(8,128)S(1)}, u32[]{:S(2)}, u32[]{:S(2)}) collective-permute-start(f32[32,128]{1,0:T(8,128)S(1)} %get-tuple-element.57.refs_0_), channel_id=1, source_target_pairs={{0,5},{1,4},{2,7},{3,6},{4,1},{5,0},{6,3},{7,2},{8,13},{9,12},{10,... | collective-permute-start | bytes 49160 | tf_op jit(solution)/shard_map/ppermute | solution.py:497
  37.9 1.1 %collective-permute-start.14 = (f32[32,128]{1,0:T(8,128)S(1)}, f32[32,128]{1,0:T(8,128)S(1)}, u32[]{:S(2)}, u32[]{:S(2)}) collective-permute-start(f32[32,128]{1,0:T(8,128)S(1)} %get-tuple-element.57.refs_0_), channel_id=1, source_target_pairs={{0,3},{1,2},{2,1},{3,0},{4,7},{5,6},{6,5},{7,4},{8,11},{9,10},{10,... | collective-permute-start | bytes 49160 | tf_op jit(solution)/shard_map/ppermute | solution.py:497
  39.0 1.1 %collective-permute-done.16.refs_3_ = f32[32,128]{1,0:T(8,128)S(1)} collective-permute-done((f32[32,128]{1,0:T(8,128)S(1)}, f32[32,128]{1,0:T(8,128)S(1)}, u32[]{:S(2)}, u32[]{:S(2)}) %collective-permute-start.16) | collective-permute-done | bytes 16416 | tf_op jit(solution)/shard_map/ppermute | solution.py:497
  40.0 1.2 %collective-permute-done.15.refs_2_ = f32[32,128]{1,0:T(8,128)S(1)} collective-permute-done((f32[32,128]{1,0:T(8,128)S(1)}, f32[32,128]{1,0:T(8,128)S(1)}, u32[]{:S(2)}, u32[]{:S(2)}) %collective-permute-start.15) | collective-permute-done | bytes 16416 | tf_op jit(solution)/shard_map/ppermute | solution.py:497
  41.3 1.3 %collective-permute-start.19 = (f32[16,128]{1,0:T(8,128)S(1)}, f32[16,128]{1,0:T(8,128)S(1)}, u32[]{:S(2)}, u32[]{:S(2)}) collective-permute-start(f32[16,128]{1,0:T(8,128)S(1)} %get-tuple-element.64.refs_16_), channel_id=1, source_target_pairs={{0,25},{1,24},{2,27},{3,26},{4,29},{5,28},{6,31},{7,30},{8,17},{9,... | collective-permute-start | bytes 24584 | tf_op jit(solution)/shard_map/ppermute | solution.py:497
  42.6 0.4 collective-permute-start.18
  43.1 1.3 %collective-permute-start.17 = (f32[16,128]{1,0:T(8,128)S(1)}, f32[16,128]{1,0:T(8,128)S(1)}, u32[]{:S(2)}, u32[]{:S(2)}) collective-permute-start(f32[16,128]{1,0:T(8,128)S(1)} %get-tuple-element.64.refs_16_), channel_id=1, source_target_pairs={{0,9},{1,8},{2,11},{3,10},{4,13},{5,12},{6,15},{7,14},{8,1},{9,0},... | collective-permute-start | bytes 24584 | tf_op jit(solution)/shard_map/ppermute | solution.py:497
  44.4 1.5 %astro.5.refs_10_ = f32[80,128]{1,0:T(8,128)S(1)} custom-call(f32[272,128]{1,0:T(8,128)S(1)} %chip.1.own_ref.refs_0_, f32[272,128]{1,0:T(8,128)S(1)} %collective-permute-done.3.other_ref.refs_1_, bf16[128,8192]{1,0:T(8,128)(2,1)S(1)} %get-tuple-element.46.refs_2_, f32[64,128]{1,0:T(8,128)S(1)} %get-tuple-element.58.refs_3_), custom_call_target="tpu_custom_call" | custom-call | tf_op jit(solution)/shard_map/astro/pallas_call | solution.py:470
  45.9 0.3 collective-permute-done.17.refs_17_
  46.2 1.1 %step.5 = (f32[8,128]{1,0:T(8,128)S(1)}, f32[16,128]{1,0:T(8,128)S(1)}, f32[96,128]{1,0:T(8,128)S(1)}, f32[96,128]{1,0:T(8,128)}, f32[16,128]{1,0:T(8,128)}, /*index=5*/f32[16,128]{1,0:T(8,128)}) custom-call(f32[272,128]{1,0:T(8,128)S(1)} %chip.1.own_ref.refs_0_, f32[272,128]{1,0:T(8,128)S(1)} %collective-permute-done.3.other_ref.refs_1_, ...), custom_call_target="tpu_custom_call" | custom-call | tf_op jit(solution)/shard_map/step/pallas_call | solution.py:470
  47.3 1.6 %collective-permute-start.22 = (f32[8,128]{1,0:T(8,128)S(1)}, f32[8,128]{1,0:T(8,128)S(1)}, u32[]{:S(2)}, u32[]{:S(2)}) collective-permute-start(f32[8,128]{1,0:T(8,128)S(1)} %get-tuple-element.66.refs_0_), channel_id=1, source_target_pairs={{0,7},{1,6},{2,5},{3,4},{4,3},{5,2},{6,1},{7,0},{8,15},{9,14},{10,... | collective-permute-start | bytes 12296 | tf_op jit(solution)/shard_map/ppermute | solution.py:497
  48.9 0.7 %collective-permute-start.21 = (f32[8,128]{1,0:T(8,128)S(1)}, f32[8,128]{1,0:T(8,128)S(1)}, u32[]{:S(2)}, u32[]{:S(2)}) collective-permute-start(f32[8,128]{1,0:T(8,128)S(1)} %get-tuple-element.66.refs_0_), channel_id=1, source_target_pairs={{0,5},{1,4},{2,7},{3,6},{4,1},{5,0},{6,3},{7,2},{8,13},{9,12},{10,... | collective-permute-start | bytes 12296 | tf_op jit(solution)/shard_map/ppermute | solution.py:497
  49.6 1.6 %collective-permute-start.20 = (f32[8,128]{1,0:T(8,128)S(1)}, f32[8,128]{1,0:T(8,128)S(1)}, u32[]{:S(2)}, u32[]{:S(2)}) collective-permute-start(f32[8,128]{1,0:T(8,128)S(1)} %get-tuple-element.66.refs_0_), channel_id=1, source_target_pairs={{0,3},{1,2},{2,1},{3,0},{4,7},{5,6},{6,5},{7,4},{8,11},{9,10},{10,... | collective-permute-start | bytes 12296 | tf_op jit(solution)/shard_map/ppermute | solution.py:497
  51.2 0.9 %collective-permute-done.22.refs_3_ = f32[8,128]{1,0:T(8,128)S(1)} collective-permute-done((f32[8,128]{1,0:T(8,128)S(1)}, f32[8,128]{1,0:T(8,128)S(1)}, u32[]{:S(2)}, u32[]{:S(2)}) %collective-permute-start.22) | collective-permute-done | bytes 4128 | tf_op jit(solution)/shard_map/ppermute | solution.py:497
  52.1 0.7 %collective-permute-done.21.refs_2_ = f32[8,128]{1,0:T(8,128)S(1)} collective-permute-done((f32[8,128]{1,0:T(8,128)S(1)}, f32[8,128]{1,0:T(8,128)S(1)}, u32[]{:S(2)}, u32[]{:S(2)}) %collective-permute-start.21) | collective-permute-done | bytes 4128 | tf_op jit(solution)/shard_map/ppermute | solution.py:497
  52.9 2.4 %collective-permute-start.25 = (f32[8,128]{1,0:T(8,128)S(1)}, f32[8,128]{1,0:T(8,128)S(1)}, u32[]{:S(2)}, u32[]{:S(2)}) collective-permute-start(f32[8,128]{1,0:T(8,128)S(1)} %sum.1.refs_0_), channel_id=1, source_target_pairs={{0,25},{1,24},{2,27},{3,26},{4,29},{5,28},{6,31},{7,30},{8,17},{9,... | collective-permute-start | bytes 12296 | tf_op jit(solution)/shard_map/ppermute | solution.py:497
  55.3 0.3 collective-permute-start.24
  55.6 0.5 collective-permute-start.23
  56.1 0.8 %collective-permute-done.25.refs_3_ = f32[8,128]{1,0:T(8,128)S(1)} collective-permute-done((f32[8,128]{1,0:T(8,128)S(1)}, f32[8,128]{1,0:T(8,128)S(1)}, u32[]{:S(2)}, u32[]{:S(2)}) %collective-permute-start.25) | collective-permute-done | bytes 4128 | tf_op jit(solution)/shard_map/ppermute | solution.py:497
  56.9 1.5 %collective-permute-done.24.refs_2_ = f32[8,128]{1,0:T(8,128)S(1)} collective-permute-done((f32[8,128]{1,0:T(8,128)S(1)}, f32[8,128]{1,0:T(8,128)S(1)}, u32[]{:S(2)}, u32[]{:S(2)}) %collective-permute-start.24) | collective-permute-done | bytes 4128 | tf_op jit(solution)/shard_map/ppermute | solution.py:497
  58.4 0.3 collective-permute-done.23.refs_1_
  58.6 0.7 %last.1 = (f32[5,256]{1,0:T(8,128)}, f32[2,128]{1,0:T(2,128)}, f32[8,128]{1,0:T(8,128)}) custom-call(f32[16,128]{1,0:T(8,128)S(1)} %get-tuple-element.65.state_ref, f32[8,128]{1,0:T(8,128)S(1)} %sum.1.refs_0_, f32[8,128]{1,0:T(8,128)S(1)} %collective-permute-done.23.refs_1_, f32[8,128]{1,0:T(8,128)S(1)} %collective-permute-done.24.refs_2_, ...), custom_call_target="tpu_custom_call" | custom-call | tf_op jit(solution)/shard_map/last/pallas_call | solution.py:470
  (18 shorter events, 0.4 us)
Async XLA Ops:
  2.6 7.1 %collective-permute-start.2 = (f32[72,128]{1,0:T(8,128)S(1)}, f32[72,128]{1,0:T(8,128)S(1)}, u32[]{:S(2)}, u32[]{:S(2)}) collective-permute-start(f32[72,128]{1,0:T(8,128)S(1)} %get-tuple-element.37.refs_0_), channel_id=1, source_target_pairs={{0,6},{1,7},{2,4},{3,5},{4,2},{5,3},{6,0},{7,1},{8,14},{9,15},{10,... | collective-permute-start | bytes 110600 | tf_op jit(solution)/shard_map/ppermute | solution.py:484
  7.7 4.9 %collective-permute-start.1 = (f32[72,128]{1,0:T(8,128)S(1)}, f32[72,128]{1,0:T(8,128)S(1)}, u32[]{:S(2)}, u32[]{:S(2)}) collective-permute-start(f32[72,128]{1,0:T(8,128)S(1)} %get-tuple-element.37.refs_0_), channel_id=1, source_target_pairs={{0,4},{1,5},{2,6},{3,7},{4,0},{5,1},{6,2},{7,3},{8,12},{9,13},{10,... | collective-permute-start | bytes 110600 | tf_op jit(solution)/shard_map/ppermute | solution.py:484
  7.7 4.9 %collective-permute-start = (f32[72,128]{1,0:T(8,128)S(1)}, f32[72,128]{1,0:T(8,128)S(1)}, u32[]{:S(2)}, u32[]{:S(2)}) collective-permute-start(f32[72,128]{1,0:T(8,128)S(1)} %get-tuple-element.37.refs_0_), channel_id=1, source_target_pairs={{0,2},{1,3},{2,0},{3,1},{4,6},{5,7},{6,4},{7,5},{8,10},{9,11},{10,... | collective-permute-start | bytes 110600 | tf_op jit(solution)/shard_map/ppermute | solution.py:484
  12.6 1.4 %collective-permute-start.3 = (f32[272,128]{1,0:T(8,128)S(1)}, f32[272,128]{1,0:T(8,128)S(1)}, u32[]{:S(2)}, u32[]{:S(2)}) collective-permute-start(f32[272,128]{1,0:T(8,128)S(1)} %chip.1.own_ref.refs_0_), channel_id=1, source_target_pairs={{0,1},{1,0},{2,3},{3,2},{4,5},{5,4},{6,7},{7,6},{8,9},{9,8},{10,11... | collective-permute-start | bytes 417800 | tf_op jit(solution)/shard_map/ppermute | solution.py:484
  14.0 5.6 %collective-permute-start.4 = (f32[616,128]{1,0:T(8,128)S(1)}, f32[616,128]{1,0:T(8,128)S(1)}, u32[]{:S(2)}, u32[]{:S(2)}) collective-permute-start(f32[616,128]{1,0:T(8,128)S(1)} %get-tuple-element.39.refs_2_), channel_id=1, source_target_pairs={{0,1},{1,0},{2,3},{3,2},{4,5},{5,4},{6,7},{7,6},{8,9},{9,8},{10,11... | collective-permute-start | bytes 946184 | tf_op jit(solution)/shard_map/ppermute | solution.py:484
  14.2 5.9 %collective-permute-start.7 = (f32[16,128]{1,0:T(8,128)S(1)}, f32[16,128]{1,0:T(8,128)S(1)}, u32[]{:S(2)}, u32[]{:S(2)}) collective-permute-start(f32[16,128]{1,0:T(8,128)S(1)} %group.3.refs_11_), channel_id=1, source_target_pairs={{0,25},{1,24},{2,27},{3,26},{4,29},{5,28},{6,31},{7,30},{8,17},{9,... | collective-permute-start | bytes 24584 | tf_op jit(solution)/shard_map/ppermute | solution.py:497
  16.6 3.5 %collective-permute-start.6 = (f32[16,128]{1,0:T(8,128)S(1)}, f32[16,128]{1,0:T(8,128)S(1)}, u32[]{:S(2)}, u32[]{:S(2)}) collective-permute-start(f32[16,128]{1,0:T(8,128)S(1)} %group.3.refs_11_), channel_id=1, source_target_pairs={{0,17},{1,16},{2,19},{3,18},{4,21},{5,20},{6,23},{7,22},{8,25},{9,... | collective-permute-start | bytes 24584 | tf_op jit(solution)/shard_map/ppermute | solution.py:497
  16.9 3.3 %collective-permute-start.5 = (f32[16,128]{1,0:T(8,128)S(1)}, f32[16,128]{1,0:T(8,128)S(1)}, u32[]{:S(2)}, u32[]{:S(2)}) collective-permute-start(f32[16,128]{1,0:T(8,128)S(1)} %group.3.refs_11_), channel_id=1, source_target_pairs={{0,9},{1,8},{2,11},{3,10},{4,13},{5,12},{6,15},{7,14},{8,1},{9,0},... | collective-permute-start | bytes 24584 | tf_op jit(solution)/shard_map/ppermute | solution.py:497
  21.8 5.0 %collective-permute-start.10 = (f32[32,128]{1,0:T(8,128)S(1)}, f32[32,128]{1,0:T(8,128)S(1)}, u32[]{:S(2)}, u32[]{:S(2)}) collective-permute-start(f32[32,128]{1,0:T(8,128)S(1)} %get-tuple-element.49.refs_0_), channel_id=1, source_target_pairs={{0,7},{1,6},{2,5},{3,4},{4,3},{5,2},{6,1},{7,0},{8,15},{9,14},{10,... | collective-permute-start | bytes 49160 | tf_op jit(solution)/shard_map/ppermute | solution.py:497
  23.1 4.3 %collective-permute-start.9 = (f32[32,128]{1,0:T(8,128)S(1)}, f32[32,128]{1,0:T(8,128)S(1)}, u32[]{:S(2)}, u32[]{:S(2)}) collective-permute-start(f32[32,128]{1,0:T(8,128)S(1)} %get-tuple-element.49.refs_0_), channel_id=1, source_target_pairs={{0,5},{1,4},{2,7},{3,6},{4,1},{5,0},{6,3},{7,2},{8,13},{9,12},{10,... | collective-permute-start | bytes 49160 | tf_op jit(solution)/shard_map/ppermute | solution.py:497
  23.7 3.8 %collective-permute-start.8 = (f32[32,128]{1,0:T(8,128)S(1)}, f32[32,128]{1,0:T(8,128)S(1)}, u32[]{:S(2)}, u32[]{:S(2)}) collective-permute-start(f32[32,128]{1,0:T(8,128)S(1)} %get-tuple-element.49.refs_0_), channel_id=1, source_target_pairs={{0,3},{1,2},{2,1},{3,0},{4,7},{5,6},{6,5},{7,4},{8,11},{9,10},{10,... | collective-permute-start | bytes 49160 | tf_op jit(solution)/shard_map/ppermute | solution.py:497
  27.6 4.5 %collective-permute-start.13 = (f32[16,128]{1,0:T(8,128)S(1)}, f32[16,128]{1,0:T(8,128)S(1)}, u32[]{:S(2)}, u32[]{:S(2)}) collective-permute-start(f32[16,128]{1,0:T(8,128)S(1)} %get-tuple-element.56.refs_16_), channel_id=1, source_target_pairs={{0,25},{1,24},{2,27},{3,26},{4,29},{5,28},{6,31},{7,30},{8,17},{9,... | collective-permute-start | bytes 24584 | tf_op jit(solution)/shard_map/ppermute | solution.py:497
  29.9 3.1 %collective-permute-start.12 = (f32[16,128]{1,0:T(8,128)S(1)}, f32[16,128]{1,0:T(8,128)S(1)}, u32[]{:S(2)}, u32[]{:S(2)}) collective-permute-start(f32[16,128]{1,0:T(8,128)S(1)} %get-tuple-element.56.refs_16_), channel_id=1, source_target_pairs={{0,17},{1,16},{2,19},{3,18},{4,21},{5,20},{6,23},{7,22},{8,25},{9,... | collective-permute-start | bytes 24584 | tf_op jit(solution)/shard_map/ppermute | solution.py:497
  30.3 3.1 %collective-permute-start.11 = (f32[16,128]{1,0:T(8,128)S(1)}, f32[16,128]{1,0:T(8,128)S(1)}, u32[]{:S(2)}, u32[]{:S(2)}) collective-permute-start(f32[16,128]{1,0:T(8,128)S(1)} %get-tuple-element.56.refs_16_), channel_id=1, source_target_pairs={{0,9},{1,8},{2,11},{3,10},{4,13},{5,12},{6,15},{7,14},{8,1},{9,0},... | collective-permute-start | bytes 24584 | tf_op jit(solution)/shard_map/ppermute | solution.py:497
  35.0 5.0 %collective-permute-start.16 = (f32[32,128]{1,0:T(8,128)S(1)}, f32[32,128]{1,0:T(8,128)S(1)}, u32[]{:S(2)}, u32[]{:S(2)}) collective-permute-start(f32[32,128]{1,0:T(8,128)S(1)} %get-tuple-element.57.refs_0_), channel_id=1, source_target_pairs={{0,7},{1,6},{2,5},{3,4},{4,3},{5,2},{6,1},{7,0},{8,15},{9,14},{10,... | collective-permute-start | bytes 49160 | tf_op jit(solution)/shard_map/ppermute | solution.py:497
  37.2 4.1 %collective-permute-start.15 = (f32[32,128]{1,0:T(8,128)S(1)}, f32[32,128]{1,0:T(8,128)S(1)}, u32[]{:S(2)}, u32[]{:S(2)}) collective-permute-start(f32[32,128]{1,0:T(8,128)S(1)} %get-tuple-element.57.refs_0_), channel_id=1, source_target_pairs={{0,5},{1,4},{2,7},{3,6},{4,1},{5,0},{6,3},{7,2},{8,13},{9,12},{10,... | collective-permute-start | bytes 49160 | tf_op jit(solution)/shard_map/ppermute | solution.py:497
  37.9 3.4 %collective-permute-start.14 = (f32[32,128]{1,0:T(8,128)S(1)}, f32[32,128]{1,0:T(8,128)S(1)}, u32[]{:S(2)}, u32[]{:S(2)}) collective-permute-start(f32[32,128]{1,0:T(8,128)S(1)} %get-tuple-element.57.refs_0_), channel_id=1, source_target_pairs={{0,3},{1,2},{2,1},{3,0},{4,7},{5,6},{6,5},{7,4},{8,11},{9,10},{10,... | collective-permute-start | bytes 49160 | tf_op jit(solution)/shard_map/ppermute | solution.py:497
  41.3 4.5 %collective-permute-start.19 = (f32[16,128]{1,0:T(8,128)S(1)}, f32[16,128]{1,0:T(8,128)S(1)}, u32[]{:S(2)}, u32[]{:S(2)}) collective-permute-start(f32[16,128]{1,0:T(8,128)S(1)} %get-tuple-element.64.refs_16_), channel_id=1, source_target_pairs={{0,25},{1,24},{2,27},{3,26},{4,29},{5,28},{6,31},{7,30},{8,17},{9,... | collective-permute-start | bytes 24584 | tf_op jit(solution)/shard_map/ppermute | solution.py:497
  42.6 3.2 %collective-permute-start.18 = (f32[16,128]{1,0:T(8,128)S(1)}, f32[16,128]{1,0:T(8,128)S(1)}, u32[]{:S(2)}, u32[]{:S(2)}) collective-permute-start(f32[16,128]{1,0:T(8,128)S(1)} %get-tuple-element.64.refs_16_), channel_id=1, source_target_pairs={{0,17},{1,16},{2,19},{3,18},{4,21},{5,20},{6,23},{7,22},{8,25},{9,... | collective-permute-start | bytes 24584 | tf_op jit(solution)/shard_map/ppermute | solution.py:497
  43.1 3.1 %collective-permute-start.17 = (f32[16,128]{1,0:T(8,128)S(1)}, f32[16,128]{1,0:T(8,128)S(1)}, u32[]{:S(2)}, u32[]{:S(2)}) collective-permute-start(f32[16,128]{1,0:T(8,128)S(1)} %get-tuple-element.64.refs_16_), channel_id=1, source_target_pairs={{0,9},{1,8},{2,11},{3,10},{4,13},{5,12},{6,15},{7,14},{8,1},{9,0},... | collective-permute-start | bytes 24584 | tf_op jit(solution)/shard_map/ppermute | solution.py:497
  47.3 4.8 %collective-permute-start.22 = (f32[8,128]{1,0:T(8,128)S(1)}, f32[8,128]{1,0:T(8,128)S(1)}, u32[]{:S(2)}, u32[]{:S(2)}) collective-permute-start(f32[8,128]{1,0:T(8,128)S(1)} %get-tuple-element.66.refs_0_), channel_id=1, source_target_pairs={{0,7},{1,6},{2,5},{3,4},{4,3},{5,2},{6,1},{7,0},{8,15},{9,14},{10,... | collective-permute-start | bytes 12296 | tf_op jit(solution)/shard_map/ppermute | solution.py:497
  48.9 3.9 %collective-permute-start.21 = (f32[8,128]{1,0:T(8,128)S(1)}, f32[8,128]{1,0:T(8,128)S(1)}, u32[]{:S(2)}, u32[]{:S(2)}) collective-permute-start(f32[8,128]{1,0:T(8,128)S(1)} %get-tuple-element.66.refs_0_), channel_id=1, source_target_pairs={{0,5},{1,4},{2,7},{3,6},{4,1},{5,0},{6,3},{7,2},{8,13},{9,12},{10,... | collective-permute-start | bytes 12296 | tf_op jit(solution)/shard_map/ppermute | solution.py:497
  49.6 3.3 %collective-permute-start.20 = (f32[8,128]{1,0:T(8,128)S(1)}, f32[8,128]{1,0:T(8,128)S(1)}, u32[]{:S(2)}, u32[]{:S(2)}) collective-permute-start(f32[8,128]{1,0:T(8,128)S(1)} %get-tuple-element.66.refs_0_), channel_id=1, source_target_pairs={{0,3},{1,2},{2,1},{3,0},{4,7},{5,6},{6,5},{7,4},{8,11},{9,10},{10,... | collective-permute-start | bytes 12296 | tf_op jit(solution)/shard_map/ppermute | solution.py:497
  52.9 4.0 %collective-permute-start.25 = (f32[8,128]{1,0:T(8,128)S(1)}, f32[8,128]{1,0:T(8,128)S(1)}, u32[]{:S(2)}, u32[]{:S(2)}) collective-permute-start(f32[8,128]{1,0:T(8,128)S(1)} %sum.1.refs_0_), channel_id=1, source_target_pairs={{0,25},{1,24},{2,27},{3,26},{4,29},{5,28},{6,31},{7,30},{8,17},{9,... | collective-permute-start | bytes 12296 | tf_op jit(solution)/shard_map/ppermute | solution.py:497
  55.3 3.0 %collective-permute-start.24 = (f32[8,128]{1,0:T(8,128)S(1)}, f32[8,128]{1,0:T(8,128)S(1)}, u32[]{:S(2)}, u32[]{:S(2)}) collective-permute-start(f32[8,128]{1,0:T(8,128)S(1)} %sum.1.refs_0_), channel_id=1, source_target_pairs={{0,17},{1,16},{2,19},{3,18},{4,21},{5,20},{6,23},{7,22},{8,25},{9,... | collective-permute-start | bytes 12296 | tf_op jit(solution)/shard_map/ppermute | solution.py:497
  55.6 3.0 %collective-permute-start.23 = (f32[8,128]{1,0:T(8,128)S(1)}, f32[8,128]{1,0:T(8,128)S(1)}, u32[]{:S(2)}, u32[]{:S(2)}) collective-permute-start(f32[8,128]{1,0:T(8,128)S(1)} %sum.1.refs_0_), channel_id=1, source_target_pairs={{0,9},{1,8},{2,11},{3,10},{4,13},{5,12},{6,15},{7,14},{8,1},{9,0},... | collective-permute-start | bytes 12296 | tf_op jit(solution)/shard_map/ppermute | solution.py:497

commit v5 on v4

--- a/solution.py
+++ b/solution.py
@@ -270,50 +270,95 @@
     out_ref[8:16] = jnp.concatenate(att + [scalars[5:8]], axis=0)
 
 
-def astro_kernel(first, count, *refs):
+def kept(count, keep_ref):
+    base = 16 * count + 16
+    extra = (keep_ref.shape[0] - base) // count
+    return base, extra, extra // 8 - 1
+
+
+def star_sums(count, place, keep_ref, rows, table_ref, spread_ref, build):
     high = STARS_DEV // LANES
-    if first:
-        keep, (out_ref, table_ref, spread_ref) = refs[:2], refs[2:]
-    else:
-        keep, (table_ref, rows_ref, out_ref, spread_ref) = refs[:2], refs[2:]
-    base = 16 * count + 16
-    extra = (keep[0].shape[0] - base) // count
-    comps = extra // 8 - 1
+    base, extra, comps = kept(count, keep_ref)
     long = 8 * LANES
+    packed = keep_ref[pl.ds(pl.multiple_of(base + place * extra, 8), extra)]
+    index = packed[comps * 8 :].astype(jnp.int32)
+    at0 = pl.multiple_of(place * long, long)
+    split = [halves(packed[comp * 8 : comp * 8 + 8] * rows) for comp in range(comps)]
+    for block in range(8):
+        here = slice(block, block + 1)
+        if build:
+            table_ref[:, pl.ds(at0 + block * LANES, LANES)] = one_hot_low(index[here])
+        pieces = []
+        for part in range(2):
+            for comp in range(comps):
+                pieces.append(spread_high(index[here], split[comp][part][here], high))
+        spread_ref[:, block * LANES : (block + 1) * LANES] = jnp.concatenate(
+            pieces, axis=0
+        ).astype(bf16)
+    return dot_lanes(spread_ref[...], table_ref[:, pl.ds(at0, long)])
+
+
+def star_rows(count, keep_ref, sums):
+    high = STARS_DEV // LANES
+    base, extra, comps = kept(count, keep_ref)
+    chip = lax.axis_index("tm") // 2
+    packed = keep_ref[pl.ds(pl.multiple_of(base + chip * extra, 8), extra)]
+    star = packed[comps * 8 :].astype(jnp.int32)
+    star_high, star_low = star >> 7, star & (LANES - 1)
+    total = jnp.zeros((8, LANES), f32)
+    for comp in range(comps):
+        picked = jnp.zeros((8, LANES), f32)
+        for place in range(high):
+            at = comp * high + place
+            picked = jnp.where(star_high == place, lane_pick(sums[at : at + 1], star_low), picked)
+        total = total + packed[comp * 8 : comp * 8 + 8] * picked
+    return total
+
+
+def first_sums(count, keep_ref, table_ref, spread_ref):
+    size = spread_ref.shape[0]
+
+    def one(place, total):
+        rows = keep_ref[pl.ds(pl.multiple_of(place * 8, 8), 8)]
+        return total + star_sums(count, place, keep_ref, rows, table_ref, spread_ref, True)
+
+    total = lax.fori_loop(0, count, one, jnp.zeros((size, LANES), f32))
+    return total[: size // 2] + total[size // 2 :]
+
+
+def astro_own_kernel(count, keep_ref, out_ref, table_ref, spread_ref):
+    out_ref[...] = first_sums(count, keep_ref, table_ref, spread_ref)
+
+
+def astro_other_kernel(count, own_ref, keep_ref, part_ref, out_ref, ya_ref, table_ref, spread_ref):
+    total = part_ref[...] + first_sums(count, keep_ref, table_ref, spread_ref)
+    out_ref[...] = total
+    ya_ref[0:8] = star_rows(count, own_ref, total)
+    ya_ref[8:16] = star_rows(count, keep_ref, total)
+
+
+def astro_kernel(count, own_ref, other_ref, own_table, other_table, rows_ref, out_ref, ya_ref,
+                 spread_ref):
     core = lax.axis_index("tm") % 2
+    size = spread_ref.shape[1]
+    sources = ((own_ref, own_table), (other_ref, other_table))
 
     def one(place, totals):
         new = []
-        for half in range(2):
-            if first:
-                rows = keep[half][pl.ds(pl.multiple_of(place * 8, 8), 8)]
-            else:
-                at = ((half ^ core) * count + place) * 8
-                rows = rows_ref[pl.ds(pl.multiple_of(at, 8), 8)]
-            packed = keep[half][pl.ds(pl.multiple_of(base + place * extra, 8), extra)]
-            index = packed[comps * 8 :].astype(jnp.int32)
-            at0 = pl.multiple_of((half * count + place) * long, long)
-            split = [halves(packed[comp * 8 : comp * 8 + 8] * rows) for comp in range(comps)]
-            for block in range(8):
-                here = slice(block, block + 1)
-                if first:
-                    table_ref[:, pl.ds(at0 + block * LANES, LANES)] = one_hot_low(index[here])
-                pieces = []
-                for part in range(2):
-                    for comp in range(comps):
-                        pieces.append(spread_high(index[here], split[comp][part][here], high))
-                spread_ref[half, :, block * LANES : (block + 1) * LANES] = jnp.concatenate(
-                    pieces, axis=0
-                ).astype(bf16)
-            new.append(
-                totals[half] + dot_lanes(spread_ref[half], table_ref[:, pl.ds(at0, long)])
-            )
+        for half, (keep_ref, table_ref) in enumerate(sources):
+            at = ((half ^ core) * count + place) * 8
+            rows = rows_ref[pl.ds(pl.multiple_of(at, 8), 8)]
+            part = star_sums(count, place, keep_ref, rows, table_ref, spread_ref.at[half], False)
+            new.append(totals[half] + part)
         return tuple(new)
 
-    zero = jnp.zeros((2 * comps * high, LANES), f32)
+    zero = jnp.zeros((size, LANES), f32)
     own, other = lax.fori_loop(0, count, one, (zero, zero))
     total = own + other
-    out_ref[...] = total[: comps * high] + total[comps * high :]
+    total = total[: size // 2] + total[size // 2 :]
+    out_ref[...] = total
+    ya_ref[0:8] = star_rows(count, own_ref, total)
+    ya_ref[8:16] = star_rows(count, other_ref, total)
 
 
 def sum_kernel(*refs):
@@ -334,13 +379,15 @@
 
 
 def step_kernel(step, width, slots, chips, star_count, *refs):
-    keep, packs, tables, att2s, ints, sum_ref = refs[:2], refs[2:4], refs[4:6], refs[6:8], refs[8:10], refs[10]
-    refs = refs[11:]
+    packs, tables, att2s, ints = refs[0:2], refs[2:4], refs[4:6], refs[6:8]
+    sum_ref, ya_ref, refs = refs[8], refs[9], refs[10:]
     if step > 0:
-        state_ref, old_z_ref, old_g_ref, old_u_ref, old_s_ref = refs[:5]
-        refs = refs[5:]
-    gathered, refs = refs[:-7], refs[-7:]
-    send_ref, state_out, z_ref, g_ref, u_ref, s_ref, spread_ref = refs
+        state_ref, old_z_ref, old_g_ref, old_u_ref, old_s_ref, old_gs_ref = refs[:6]
+        refs = refs[6:]
+    else:
+        keep, refs = refs[:2], refs[2:]
+    gathered, refs = refs[:-8], refs[-8:]
+    send_ref, state_out, z_ref, g_ref, u_ref, s_ref, gs_ref, spread_ref = refs
     me = lax.axis_index("tm")
     chip, core = me // 2, me % 2
     high = STARS_DEV // LANES
@@ -348,6 +395,21 @@
     blocks = 8
     total = tree_sum([ref[...] for ref in gathered])
     back = jnp.concatenate([sum_ref[...], total], axis=0)
+    base = comps * high
+    pieces = [total[place : place + 1] for place in range(8)]
+    att_back_rows = total[8:13]
+    forward, starts, coefs, indices = [], [], [], []
+    for half in range(2):
+        starts.append(ints[half][slots * 8 :])
+        own = jnp.where(core == half, att_back_rows[0:3], att_back_rows[2:5])
+        part = att_forward(own, att2s[half][...], starts[half], width)
+        part = part + ya_ref[half * 8 : half * 8 + 8]
+        coefs.append([packs[half].at[slot * 8 : slot * 8 + 8] for slot in range(slots)])
+        indices.append([ints[half].at[slot * 8 : slot * 8 + 8] for slot in range(slots)])
+        for slot in range(slots):
+            part = part + coefs[half][slot][...] * table_pick(pieces, indices[half][slot][...])
+        forward.append(part)
+    forward = jnp.concatenate(forward, axis=0)
     if step == 0:
         squares = lane_sum(total[13:14])
         beta2 = squares + epsilon
@@ -356,6 +418,8 @@
         u = jnp.concatenate([ref[at] for ref in keep], axis=0) / beta
         g = back / beta
         z = g
+        gs = forward / beta
+        both = gs
         state_out[...] = jnp.concatenate(
             [squares / beta2, beta, jnp.zeros((14, LANES), f32)], axis=0
         )
@@ -365,6 +429,8 @@
         u = (old_s_ref[...] / alpha - alpha * old_u_ref[...]) / beta
         g = (back / alpha - alpha * old_g_ref[...]) / beta
         z = g - (beta / alpha) * old_z_ref[...]
+        gs = (forward / alpha - alpha * old_gs_ref[...]) / beta
+        both = gs - (beta / alpha) * old_s_ref[...]
         pieces = [left2, state[1 : 1 + step], beta, jnp.zeros((7 - step, LANES), f32)]
         pieces += [state[9 : 8 + step]] if step > 1 else []
         pieces += [alpha, jnp.zeros((7 - step, LANES), f32)]
@@ -372,36 +438,18 @@
     z_ref[...] = z
     g_ref[...] = g
     u_ref[...] = u
-    base = comps * high
+    gs_ref[...] = gs
+    s_ref[...] = both
     inst_rows = z[base : base + 8]
     att_rows = z[base + 8 : base + 13]
-    extra = 8 * comps + 8
-    here = 16 * chips + 16 + chip * extra
-    pieces = [inst_rows[place : place + 1] for place in range(8)]
-    rows, insts, atts = [], [], []
+    rows = [both[0:8], both[8:16]]
+    insts, atts = [], []
     for half in range(2):
-        starts = ints[half][slots * 8 :]
-        own = jnp.where(core == half, att_rows[0:3], att_rows[2:5])
-        part = att_forward(own, att2s[half][...], starts, width)
-        packed = keep[half][pl.ds(pl.multiple_of(here, 8), extra)]
-        star = packed[comps * 8 :].astype(jnp.int32)
-        star_high, star_low = star >> 7, star & (LANES - 1)
-        for comp in range(comps):
-            picked = jnp.zeros((blocks, LANES), f32)
-            for place in range(high):
-                at = comp * high + place
-                picked = jnp.where(star_high == place, lane_pick(z[at : at + 1], star_low), picked)
-            part = part + packed[comp * 8 : comp * 8 + 8] * picked
-        coefs = [packs[half].at[slot * 8 : slot * 8 + 8] for slot in range(slots)]
-        indices = [ints[half].at[slot * 8 : slot * 8 + 8] for slot in range(slots)]
-        for slot in range(slots):
-            part = part + coefs[slot][...] * table_pick(pieces, indices[slot][...])
-        rows.append(part)
         if step < ITERS - 1:
-            insts.append(inst_back(part, coefs, indices, tables[half], spread_ref.at[half]))
-            atts.append(att_back(part, att2s[half][...], starts, width))
-    both = jnp.concatenate(rows, axis=0)
-    s_ref[...] = both
+            insts.append(
+                inst_back(rows[half], coefs[half], indices[half], tables[half], spread_ref.at[half])
+            )
+            atts.append(att_back(rows[half], att2s[half][...], starts[half], width))
 
     def squared(value):
         return jnp.sum(value * value, axis=0, keepdims=True)
@@ -411,7 +459,7 @@
     mixed = [jnp.sum(rows[half] * u[half * 8 : half * 8 + 8], axis=0, keepdims=True) for half in range(2)]
     scalars = [squared(rows[0]) + squared(rows[1]), mixed[0] + mixed[1], size]
     if step == ITERS - 1:
-        send_ref[...] = (jnp.concatenate([jnp.zeros((5, LANES), f32)] + scalars, axis=0))
+        send_ref[...] = jnp.concatenate([jnp.zeros((5, LANES), f32)] + scalars, axis=0)
         return
     send_ref[0:16] = jnp.where(core == 0, both, jnp.concatenate(rows[::-1], axis=0))
     send_ref[16:24] = insts[0] + insts[1]
@@ -535,12 +583,13 @@
         + [spread, pltpu.SemaphoreType.DMA((len(args),))],
         pl.ANY,
     )
-    keep = star_table = state = z = g = u = rows = None
-    kept = []
+    state = z = g = u = rows = gs = None
+    solutions = []
     group_type = rows_type(16)
     for step in range(ITERS):
-        wide = [pltpu.VMEM((2, 2 * comps * high, blocks * height), bf16)]
-        sums_type = ((comps * high, LANES), f32)
+        wide = (2 * comps * high, blocks * height)
+        sums_type = rows_type(comps * high)
+        pair = rows_type(2 * blocks)
         got = exchange(send, "tm") if step else direct(send, "tm", far)
         if step == 0:
             (gathered,) = call(
@@ -550,6 +599,15 @@
                 got,
             )
             keep = direct(gathered, "tm", [1])
+            table_type = ((LANES, chips * blocks * height), bf16)
+            own_sums, own_table = call(
+                functools.partial(astro_own_kernel, chips),
+                "astro_own",
+                [sums_type, table_type],
+                [gathered],
+                [pltpu.VMEM(wide, bf16)],
+            )
+            keep[1], own_sums = lax.optimization_barrier((keep[1], own_sums))
             (group,) = call(
                 functools.partial(first_group_kernel, chips), "group", [group_type], keep
             )
@@ -571,39 +629,39 @@
             )
         across = exchange(group, "star")
         if step == 0:
-            sums, star_table = call(
-                functools.partial(astro_kernel, True, chips),
+            sums, ya, other_table = call(
+                functools.partial(astro_other_kernel, chips),
                 "astro",
-                [sums_type, ((LANES, tm_count * blocks * height), bf16)],
-                keep,
-                wide,
+                [sums_type, pair, table_type],
+                keep + [own_sums],
+                [pltpu.VMEM(wide, bf16)],
             )
         else:
-            (sums,) = call(
-                functools.partial(astro_kernel, False, chips),
+            sums, ya = call(
+                functools.partial(astro_kernel, chips),
                 "astro",
-                [sums_type],
-                keep + [star_table, all_rows],
-                wide,
+                [sums_type, pair],
+                keep + [own_table, other_table, all_rows],
+                [pltpu.VMEM((2,) + wide, bf16)],
             )
         tall = ((comps * high + 16, LANES), f32)
-        pair = ((2 * blocks, height), f32)
-        older = [] if step == 0 else [state, z, g, u, rows]
-        send, state, z, g, u, rows = call(
+        older = keep if step == 0 else [state, z, g, u, rows, gs]
+        send, state, z, g, u, rows, gs = call(
             functools.partial(step_kernel, step, width, slots, chips, star_count),
             "step",
-            [rows_type(32 if step < ITERS - 1 else 8), group_type, tall, tall, pair, pair],
-            keep + basics + [sums] + older + across,
+            [rows_type(32 if step < ITERS - 1 else 8), group_type, tall, tall, pair, pair,
+             pair],
+            basics + [sums, ya] + older + across,
             [pltpu.VMEM((2, 16, long), bf16)],
         )
-        kept.append(z)
+        solutions.append(z)
     (send,) = call(sum_kernel, "sum", [rows_type(8)], exchange(send, "tm"))
     across = exchange(send, "star")
     out_astro, out_att, out_inst = call(
         functools.partial(last_kernel, comps, share, star_count),
         "last",
         [((comps, share), f32), ((ATT_DEV // LANES, LANES), f32), ((NINST // LANES, LANES), f32)],
-        [state] + across + kept,
+        [state] + across + solutions,
     )
     return out_astro, out_att.reshape(-1), out_inst.reshape(-1)
 

time: 59.5 us -> 58.9 us (0.990)
  waiting for transfers between devices: 15.4 us -> 14 us
  Pallas kernels: 12.8 us -> 13.4 us
    ppermute x5, waiting for transfers between devices: 5.57 us -> 4.22 us  [direct(): lax.ppermute(value, axis, [(i, i ^ gap) for i in range(count)])]
    pallas_call x14 -> x15, Pallas kernels: 12.8 us -> 13.4 us  [call(): pl.pallas_call(kernel, name=name, out_shape=[jax.ShapeDtypeStruct(shape,...]
  transfers between devices with their start and end apart: 26 -> 26, of which waited for: 16 -> 18; matrix products, arithmetic and copies ran while one was open for 0% -> 0% of each run, Pallas kernels for 10% -> 12%
where the time goes in v5:
time: 58.9 us; the launch traced here: 58.8 us
  starting transfers between devices  30.5 us (52%)
  waiting for transfers between devices  14 us (24%)
  Pallas kernels  13.4 us (23%)
  between operations  0.78 us (1%)
    ppermute x21, starting transfers between devices, exchange(): got.append(lax.ppermute(value, ('star', 'tm'), steps))  24.1 us
    pallas_call x15, Pallas kernels, call(): pl.pallas_call(kernel, name=name, out_shape=[jax.ShapeDtypeStruct(shape,...  13.4 us
    ppermute x21, waiting for transfers between devices, exchange(): got.append(lax.ppermute(value, ('star', 'tm'), steps))  9.8 us
    ppermute x5, starting transfers between devices, direct(): lax.ppermute(value, axis, [(i, i ^ gap) for i in range(count)])  6.39 us
    ppermute x5, waiting for transfers between devices, direct(): lax.ppermute(value, axis, [(i, i ^ gap) for i in range(count)])  4.22 us
  transfers between devices with their start and end apart: 26, of which 18 were waited for; matrix products, arithmetic and copies ran while one was open for 0% of the time, Pallas kernels for 12%

profile of v5, /device:TPU:0, one launch (start us, length us, event | category | flops | bytes accessed | tf_op | source)
XLA Modules:
  0.0 58.8 jit_solution(4013182591518385100)
XLA Ops:
  0.6 1.9 %first.1 = (f32[72,128]{1,0:T(8,128)S(1)}, f32[616,128]{1,0:T(8,128)S(1)}, bf16[128,6144]{1,0:T(8,128)(2,1)S(1)}, bf16[1024,128]{1,0:T(8,128)(2,1)S(1)}, s32[56,128]{1,0:T(8,128)S(1)}) custom-call(f32[8,128]{1,0:T(8,128)} %bitcast.12, f32[5,8,128]{2,1,0:T(8,128)} %bitcast.11, s32[8,128]{1,0:T(8,128)} %bitcast.13, f32[512,128]{1,0:T(8,128)} %bitcast.8, ...), custom_call_target="tpu_custom_call" | custom-call | tf_op jit(solution)/shard_map/first/pallas_call | solution.py:518
  2.6 5.1 %collective-permute-start.2 = (f32[72,128]{1,0:T(8,128)S(1)}, f32[72,128]{1,0:T(8,128)S(1)}, u32[]{:S(2)}, u32[]{:S(2)}) collective-permute-start(f32[72,128]{1,0:T(8,128)S(1)} %get-tuple-element.49.refs_0_), channel_id=1, source_target_pairs={{0,6},{1,7},{2,4},{3,5},{4,2},{5,3},{6,0},{7,1},{8,14},{9,15},{10,... | collective-permute-start | bytes 110600 | tf_op jit(solution)/shard_map/ppermute | solution.py:532
  7.7 0.6 %collective-permute-start = (f32[72,128]{1,0:T(8,128)S(1)}, f32[72,128]{1,0:T(8,128)S(1)}, u32[]{:S(2)}, u32[]{:S(2)}) collective-permute-start(f32[72,128]{1,0:T(8,128)S(1)} %get-tuple-element.49.refs_0_), channel_id=1, source_target_pairs={{0,2},{1,3},{2,0},{3,1},{4,6},{5,7},{6,4},{7,5},{8,10},{9,11},{10,... | collective-permute-start | bytes 110600 | tf_op jit(solution)/shard_map/ppermute | solution.py:532
  8.3 1.3 %collective-permute-done.2.refs_3_ = f32[72,128]{1,0:T(8,128)S(1)} collective-permute-done((f32[72,128]{1,0:T(8,128)S(1)}, f32[72,128]{1,0:T(8,128)S(1)}, u32[]{:S(2)}, u32[]{:S(2)}) %collective-permute-start.2) | collective-permute-done | bytes 36896 | tf_op jit(solution)/shard_map/ppermute | solution.py:532
  9.6 2.9 %collective-permute-done.1.refs_2_ = f32[72,128]{1,0:T(8,128)S(1)} collective-permute-done((f32[72,128]{1,0:T(8,128)S(1)}, f32[72,128]{1,0:T(8,128)S(1)}, u32[]{:S(2)}, u32[]{:S(2)}) %collective-permute-start.1) | collective-permute-done | bytes 36896 | tf_op jit(solution)/shard_map/ppermute | solution.py:532
  12.7 1.4 %astro_own.1 = (f32[80,128]{1,0:T(8,128)S(1)}, bf16[128,4096]{1,0:T(8,128)(2,1)S(1)}) custom-call(f32[272,128]{1,0:T(8,128)S(1)} %chip.1.keep_ref.own_ref.refs_10_), custom_call_target="tpu_custom_call" | custom-call | tf_op jit(solution)/shard_map/astro_own/pallas_call | solution.py:518
  14.1 0.6 collective-permute-start.4
  14.7 2.1 %collective-permute-start.7 = (f32[16,128]{1,0:T(8,128)S(1)}, f32[16,128]{1,0:T(8,128)S(1)}, u32[]{:S(2)}, u32[]{:S(2)}) collective-permute-start(f32[16,128]{1,0:T(8,128)S(1)} %group.3.refs_12_), channel_id=1, source_target_pairs={{0,25},{1,24},{2,27},{3,26},{4,29},{5,28},{6,31},{7,30},{8,17},{9,... | collective-permute-start | bytes 24584 | tf_op jit(solution)/shard_map/ppermute | solution.py:545
  16.8 0.6 collective-permute-start.6
  17.6 1.7 %astro.3 = (f32[80,128]{1,0:T(8,128)S(1)}, f32[16,128]{1,0:T(8,128)S(1)}, bf16[128,4096]{1,0:T(8,128)(2,1)S(1)}) custom-call(f32[272,128]{1,0:T(8,128)S(1)} %chip.1.keep_ref.own_ref.refs_10_, f32[272,128]{1,0:T(8,128)S(1)} %collective-permute-done.3.other_ref.keep_ref.refs_11_, f32[80,128]{1,0:T(8,128)S(1)} %get-tuple-element.60.part_ref), custom_call_target="tpu_custom_call" | custom-call | tf_op jit(solution)/shard_map/astro/pallas_call | solution.py:518
  19.3 0.5 prepare.1
  19.9 0.6 collective-permute-done.5.refs_13_
  20.5 1.4 %step.3 = (f32[32,128]{1,0:T(8,128)S(1)}, f32[16,128]{1,0:T(8,128)S(1)}, f32[96,128]{1,0:T(8,128)S(1)}, f32[96,128]{1,0:T(8,128)S(1)}, f32[16,128]{1,0:T(8,128)S...) custom-call(f32[616,128]{1,0:T(8,128)S(1)} %get-tuple-element.52.refs_0_, ...), custom_call_target="tpu_custom_call" | custom-call | tf_op jit(solution)/shard_map/step/pallas_call | solution.py:518
  21.8 1.2 %collective-permute-start.10 = (f32[32,128]{1,0:T(8,128)S(1)}, f32[32,128]{1,0:T(8,128)S(1)}, u32[]{:S(2)}, u32[]{:S(2)}) collective-permute-start(f32[32,128]{1,0:T(8,128)S(1)} %get-tuple-element.65.refs_0_), channel_id=1, source_target_pairs={{0,7},{1,6},{2,5},{3,4},{4,3},{5,2},{6,1},{7,0},{8,15},{9,14},{10,... | collective-permute-start | bytes 49160 | tf_op jit(solution)/shard_map/ppermute | solution.py:545
  23.1 0.6 %collective-permute-start.9 = (f32[32,128]{1,0:T(8,128)S(1)}, f32[32,128]{1,0:T(8,128)S(1)}, u32[]{:S(2)}, u32[]{:S(2)}) collective-permute-start(f32[32,128]{1,0:T(8,128)S(1)} %get-tuple-element.65.refs_0_), channel_id=1, source_target_pairs={{0,5},{1,4},{2,7},{3,6},{4,1},{5,0},{6,3},{7,2},{8,13},{9,12},{10,... | collective-permute-start | bytes 49160 | tf_op jit(solution)/shard_map/ppermute | solution.py:545
  23.7 2.0 %collective-permute-start.8 = (f32[32,128]{1,0:T(8,128)S(1)}, f32[32,128]{1,0:T(8,128)S(1)}, u32[]{:S(2)}, u32[]{:S(2)}) collective-permute-start(f32[32,128]{1,0:T(8,128)S(1)} %get-tuple-element.65.refs_0_), channel_id=1, source_target_pairs={{0,3},{1,2},{2,1},{3,0},{4,7},{5,6},{6,5},{7,4},{8,11},{9,10},{10,... | collective-permute-start | bytes 49160 | tf_op jit(solution)/shard_map/ppermute | solution.py:545
  25.8 1.1 %collective-permute-done.10.refs_3_ = f32[32,128]{1,0:T(8,128)S(1)} collective-permute-done((f32[32,128]{1,0:T(8,128)S(1)}, f32[32,128]{1,0:T(8,128)S(1)}, u32[]{:S(2)}, u32[]{:S(2)}) %collective-permute-start.10) | collective-permute-done | bytes 16416 | tf_op jit(solution)/shard_map/ppermute | solution.py:545
  26.9 0.5 collective-permute-done.9.refs_2_
  27.5 2.3 %collective-permute-start.13 = (f32[16,128]{1,0:T(8,128)S(1)}, f32[16,128]{1,0:T(8,128)S(1)}, u32[]{:S(2)}, u32[]{:S(2)}) collective-permute-start(f32[16,128]{1,0:T(8,128)S(1)} %get-tuple-element.75.refs_16_), channel_id=1, source_target_pairs={{0,25},{1,24},{2,27},{3,26},{4,29},{5,28},{6,31},{7,30},{8,17},{9,... | collective-permute-start | bytes 24584 | tf_op jit(solution)/shard_map/ppermute | solution.py:545
  29.8 0.5 collective-permute-start.12
  30.4 0.3 collective-permute-start.11
  30.6 1.7 %astro.4 = (f32[80,128]{1,0:T(8,128)S(1)}, f32[16,128]{1,0:T(8,128)S(1)}) custom-call(f32[272,128]{1,0:T(8,128)S(1)} %chip.1.keep_ref.own_ref.refs_10_, f32[272,128]{1,0:T(8,128)S(1)} %collective-permute-done.3.other_ref.keep_ref.refs_11_, bf16[128,4096]{1,0:T(8,128)(2,1)S(1)} %get-tuple-element.59.own_table, ...), custom_call_target="tpu_custom_call" | custom-call | tf_op jit(solution)/shard_map/astro/pallas_call | solution.py:518
  32.3 0.6 collective-permute-done.12.refs_18_
  32.9 0.5 collective-permute-done.11.refs_17_
  33.4 1.4 %step.4 = (f32[32,128]{1,0:T(8,128)S(1)}, f32[16,128]{1,0:T(8,128)S(1)}, f32[96,128]{1,0:T(8,128)S(1)}, f32[96,128]{1,0:T(8,128)S(1)}, f32[16,128]{1,0:T(8,128)S...) custom-call(f32[616,128]{1,0:T(8,128)S(1)} %get-tuple-element.52.refs_0_, ...), custom_call_target="tpu_custom_call" | custom-call | tf_op jit(solution)/shard_map/step/pallas_call | solution.py:518
  34.8 1.7 %collective-permute-start.16 = (f32[32,128]{1,0:T(8,128)S(1)}, f32[32,128]{1,0:T(8,128)S(1)}, u32[]{:S(2)}, u32[]{:S(2)}) collective-permute-start(f32[32,128]{1,0:T(8,128)S(1)} %get-tuple-element.76.refs_0_), channel_id=1, source_target_pairs={{0,7},{1,6},{2,5},{3,4},{4,3},{5,2},{6,1},{7,0},{8,15},{9,14},{10,... | collective-permute-start | bytes 49160 | tf_op jit(solution)/shard_map/ppermute | solution.py:545
  36.5 0.6 collective-permute-start.15
  37.1 1.7 %collective-permute-start.14 = (f32[32,128]{1,0:T(8,128)S(1)}, f32[32,128]{1,0:T(8,128)S(1)}, u32[]{:S(2)}, u32[]{:S(2)}) collective-permute-start(f32[32,128]{1,0:T(8,128)S(1)} %get-tuple-element.76.refs_0_), channel_id=1, source_target_pairs={{0,3},{1,2},{2,1},{3,0},{4,7},{5,6},{6,5},{7,4},{8,11},{9,10},{10,... | collective-permute-start | bytes 49160 | tf_op jit(solution)/shard_map/ppermute | solution.py:545
  38.8 1.1 %collective-permute-done.16.refs_3_ = f32[32,128]{1,0:T(8,128)S(1)} collective-permute-done((f32[32,128]{1,0:T(8,128)S(1)}, f32[32,128]{1,0:T(8,128)S(1)}, u32[]{:S(2)}, u32[]{:S(2)}) %collective-permute-start.16) | collective-permute-done | bytes 16416 | tf_op jit(solution)/shard_map/ppermute | solution.py:545
  39.9 0.7 %collective-permute-done.15.refs_2_ = f32[32,128]{1,0:T(8,128)S(1)} collective-permute-done((f32[32,128]{1,0:T(8,128)S(1)}, f32[32,128]{1,0:T(8,128)S(1)}, u32[]{:S(2)}, u32[]{:S(2)}) %collective-permute-start.15) | collective-permute-done | bytes 16416 | tf_op jit(solution)/shard_map/ppermute | solution.py:545
  40.6 1.9 %collective-permute-start.19 = (f32[16,128]{1,0:T(8,128)S(1)}, f32[16,128]{1,0:T(8,128)S(1)}, u32[]{:S(2)}, u32[]{:S(2)}) collective-permute-start(f32[16,128]{1,0:T(8,128)S(1)} %get-tuple-element.86.refs_16_), channel_id=1, source_target_pairs={{0,25},{1,24},{2,27},{3,26},{4,29},{5,28},{6,31},{7,30},{8,17},{9,... | collective-permute-start | bytes 24584 | tf_op jit(solution)/shard_map/ppermute | solution.py:545
  42.5 0.4 collective-permute-start.18
  42.9 0.9 %collective-permute-start.17 = (f32[16,128]{1,0:T(8,128)S(1)}, f32[16,128]{1,0:T(8,128)S(1)}, u32[]{:S(2)}, u32[]{:S(2)}) collective-permute-start(f32[16,128]{1,0:T(8,128)S(1)} %get-tuple-element.86.refs_16_), channel_id=1, source_target_pairs={{0,9},{1,8},{2,11},{3,10},{4,13},{5,12},{6,15},{7,14},{8,1},{9,0},... | collective-permute-start | bytes 24584 | tf_op jit(solution)/shard_map/ppermute | solution.py:545
  43.8 1.7 %astro.5 = (f32[80,128]{1,0:T(8,128)S(1)}, f32[16,128]{1,0:T(8,128)S(1)}) custom-call(f32[272,128]{1,0:T(8,128)S(1)} %chip.1.keep_ref.own_ref.refs_10_, f32[272,128]{1,0:T(8,128)S(1)} %collective-permute-done.3.other_ref.keep_ref.refs_11_, bf16[128,4096]{1,0:T(8,128)(2,1)S(1)} %get-tuple-element.59.own_table, ...), custom_call_target="tpu_custom_call" | custom-call | tf_op jit(solution)/shard_map/astro/pallas_call | solution.py:518
  45.6 0.4 collective-permute-done.17.refs_17_
  46.0 0.9 %step.5 = (f32[8,128]{1,0:T(8,128)S(1)}, f32[16,128]{1,0:T(8,128)S(1)}, f32[96,128]{1,0:T(8,128)S(1)}, f32[96,128]{1,0:T(8,128)}, f32[16,128]{1,0:T(8,128)}, /*index=5*/f32[16,128]{1,0:T(8,128)}, f32[16,128]{1,0:T(8,128)}) custom-call(f32[616,128]{1,0:T(8,128)S(1)} %get-tuple-element.52.refs_0_, f32[616,128]{1,0:T(8,128)S(1)} %collective-permute-done.4.pack_ref.refs_1_, ...), custom_call_target="tpu_custom_call" | custom-call | tf_op jit(solution)/shard_map/step/pallas_call | solution.py:518
  46.9 1.6 %collective-permute-start.22 = (f32[8,128]{1,0:T(8,128)S(1)}, f32[8,128]{1,0:T(8,128)S(1)}, u32[]{:S(2)}, u32[]{:S(2)}) collective-permute-start(f32[8,128]{1,0:T(8,128)S(1)} %get-tuple-element.88.refs_0_), channel_id=1, source_target_pairs={{0,7},{1,6},{2,5},{3,4},{4,3},{5,2},{6,1},{7,0},{8,15},{9,14},{10,... | collective-permute-start | bytes 12296 | tf_op jit(solution)/shard_map/ppermute | solution.py:545
  48.5 0.6 %collective-permute-start.21 = (f32[8,128]{1,0:T(8,128)S(1)}, f32[8,128]{1,0:T(8,128)S(1)}, u32[]{:S(2)}, u32[]{:S(2)}) collective-permute-start(f32[8,128]{1,0:T(8,128)S(1)} %get-tuple-element.88.refs_0_), channel_id=1, source_target_pairs={{0,5},{1,4},{2,7},{3,6},{4,1},{5,0},{6,3},{7,2},{8,13},{9,12},{10,... | collective-permute-start | bytes 12296 | tf_op jit(solution)/shard_map/ppermute | solution.py:545
  49.1 1.7 %collective-permute-start.20 = (f32[8,128]{1,0:T(8,128)S(1)}, f32[8,128]{1,0:T(8,128)S(1)}, u32[]{:S(2)}, u32[]{:S(2)}) collective-permute-start(f32[8,128]{1,0:T(8,128)S(1)} %get-tuple-element.88.refs_0_), channel_id=1, source_target_pairs={{0,3},{1,2},{2,1},{3,0},{4,7},{5,6},{6,5},{7,4},{8,11},{9,10},{10,... | collective-permute-start | bytes 12296 | tf_op jit(solution)/shard_map/ppermute | solution.py:545
  50.7 0.9 %collective-permute-done.22.refs_3_ = f32[8,128]{1,0:T(8,128)S(1)} collective-permute-done((f32[8,128]{1,0:T(8,128)S(1)}, f32[8,128]{1,0:T(8,128)S(1)}, u32[]{:S(2)}, u32[]{:S(2)}) %collective-permute-start.22) | collective-permute-done | bytes 4128 | tf_op jit(solution)/shard_map/ppermute | solution.py:545
  51.7 0.7 %collective-permute-done.21.refs_2_ = f32[8,128]{1,0:T(8,128)S(1)} collective-permute-done((f32[8,128]{1,0:T(8,128)S(1)}, f32[8,128]{1,0:T(8,128)S(1)}, u32[]{:S(2)}, u32[]{:S(2)}) %collective-permute-start.21) | collective-permute-done | bytes 4128 | tf_op jit(solution)/shard_map/ppermute | solution.py:545
  52.4 2.3 %collective-permute-start.25 = (f32[8,128]{1,0:T(8,128)S(1)}, f32[8,128]{1,0:T(8,128)S(1)}, u32[]{:S(2)}, u32[]{:S(2)}) collective-permute-start(f32[8,128]{1,0:T(8,128)S(1)} %sum.1.refs_0_), channel_id=1, source_target_pairs={{0,25},{1,24},{2,27},{3,26},{4,29},{5,28},{6,31},{7,30},{8,17},{9,... | collective-permute-start | bytes 12296 | tf_op jit(solution)/shard_map/ppermute | solution.py:545
  54.7 0.3 collective-permute-start.24
  55.0 0.7 %collective-permute-start.23 = (f32[8,128]{1,0:T(8,128)S(1)}, f32[8,128]{1,0:T(8,128)S(1)}, u32[]{:S(2)}, u32[]{:S(2)}) collective-permute-start(f32[8,128]{1,0:T(8,128)S(1)} %sum.1.refs_0_), channel_id=1, source_target_pairs={{0,9},{1,8},{2,11},{3,10},{4,13},{5,12},{6,15},{7,14},{8,1},{9,0},... | collective-permute-start | bytes 12296 | tf_op jit(solution)/shard_map/ppermute | solution.py:545
  55.7 0.8 %collective-permute-done.25.refs_3_ = f32[8,128]{1,0:T(8,128)S(1)} collective-permute-done((f32[8,128]{1,0:T(8,128)S(1)}, f32[8,128]{1,0:T(8,128)S(1)}, u32[]{:S(2)}, u32[]{:S(2)}) %collective-permute-start.25) | collective-permute-done | bytes 4128 | tf_op jit(solution)/shard_map/ppermute | solution.py:545
  56.5 1.3 %collective-permute-done.24.refs_2_ = f32[8,128]{1,0:T(8,128)S(1)} collective-permute-done((f32[8,128]{1,0:T(8,128)S(1)}, f32[8,128]{1,0:T(8,128)S(1)}, u32[]{:S(2)}, u32[]{:S(2)}) %collective-permute-start.24) | collective-permute-done | bytes 4128 | tf_op jit(solution)/shard_map/ppermute | solution.py:545
  57.7 0.3 collective-permute-done.23.refs_1_
  58.0 0.7 %last.1 = (f32[5,256]{1,0:T(8,128)}, f32[2,128]{1,0:T(2,128)}, f32[8,128]{1,0:T(8,128)}) custom-call(f32[16,128]{1,0:T(8,128)S(1)} %get-tuple-element.87.state_ref, f32[8,128]{1,0:T(8,128)S(1)} %sum.1.refs_0_, f32[8,128]{1,0:T(8,128)S(1)} %collective-permute-done.23.refs_1_, f32[8,128]{1,0:T(8,128)S(1)} %collective-permute-done.24.refs_2_, ...), custom_call_target="tpu_custom_call" | custom-call | tf_op jit(solution)/shard_map/last/pallas_call | solution.py:518
  (19 shorter events, 0.8 us)
Async XLA Ops:
  2.6 7.1 %collective-permute-start.2 = (f32[72,128]{1,0:T(8,128)S(1)}, f32[72,128]{1,0:T(8,128)S(1)}, u32[]{:S(2)}, u32[]{:S(2)}) collective-permute-start(f32[72,128]{1,0:T(8,128)S(1)} %get-tuple-element.49.refs_0_), channel_id=1, source_target_pairs={{0,6},{1,7},{2,4},{3,5},{4,2},{5,3},{6,0},{7,1},{8,14},{9,15},{10,... | collective-permute-start | bytes 110600 | tf_op jit(solution)/shard_map/ppermute | solution.py:532
  7.7 4.9 %collective-permute-start.1 = (f32[72,128]{1,0:T(8,128)S(1)}, f32[72,128]{1,0:T(8,128)S(1)}, u32[]{:S(2)}, u32[]{:S(2)}) collective-permute-start(f32[72,128]{1,0:T(8,128)S(1)} %get-tuple-element.49.refs_0_), channel_id=1, source_target_pairs={{0,4},{1,5},{2,6},{3,7},{4,0},{5,1},{6,2},{7,3},{8,12},{9,13},{10,... | collective-permute-start | bytes 110600 | tf_op jit(solution)/shard_map/ppermute | solution.py:532
  7.7 4.9 %collective-permute-start = (f32[72,128]{1,0:T(8,128)S(1)}, f32[72,128]{1,0:T(8,128)S(1)}, u32[]{:S(2)}, u32[]{:S(2)}) collective-permute-start(f32[72,128]{1,0:T(8,128)S(1)} %get-tuple-element.49.refs_0_), channel_id=1, source_target_pairs={{0,2},{1,3},{2,0},{3,1},{4,6},{5,7},{6,4},{7,5},{8,10},{9,11},{10,... | collective-permute-start | bytes 110600 | tf_op jit(solution)/shard_map/ppermute | solution.py:532
  12.6 1.5 %collective-permute-start.3 = (f32[272,128]{1,0:T(8,128)S(1)}, f32[272,128]{1,0:T(8,128)S(1)}, u32[]{:S(2)}, u32[]{:S(2)}) collective-permute-start(f32[272,128]{1,0:T(8,128)S(1)} %chip.1.keep_ref.own_ref.refs_10_), channel_id=1, source_target_pairs={{0,1},{1,0},{2,3},{3,2},{4,5},{5,4},{6,7},{7,6},{8,9},{9,8},{10,11... | collective-permute-start | bytes 417800 | tf_op jit(solution)/shard_map/ppermute | solution.py:532
  14.1 5.2 %collective-permute-start.4 = (f32[616,128]{1,0:T(8,128)S(1)}, f32[616,128]{1,0:T(8,128)S(1)}, u32[]{:S(2)}, u32[]{:S(2)}) collective-permute-start(f32[616,128]{1,0:T(8,128)S(1)} %get-tuple-element.52.refs_0_), channel_id=1, source_target_pairs={{0,1},{1,0},{2,3},{3,2},{4,5},{5,4},{6,7},{7,6},{8,9},{9,8},{10,11... | collective-permute-start | bytes 946184 | tf_op jit(solution)/shard_map/ppermute | solution.py:532
  14.7 5.1 %collective-permute-start.7 = (f32[16,128]{1,0:T(8,128)S(1)}, f32[16,128]{1,0:T(8,128)S(1)}, u32[]{:S(2)}, u32[]{:S(2)}) collective-permute-start(f32[16,128]{1,0:T(8,128)S(1)} %group.3.refs_12_), channel_id=1, source_target_pairs={{0,25},{1,24},{2,27},{3,26},{4,29},{5,28},{6,31},{7,30},{8,17},{9,... | collective-permute-start | bytes 24584 | tf_op jit(solution)/shard_map/ppermute | solution.py:545
  16.8 3.1 %collective-permute-start.6 = (f32[16,128]{1,0:T(8,128)S(1)}, f32[16,128]{1,0:T(8,128)S(1)}, u32[]{:S(2)}, u32[]{:S(2)}) collective-permute-start(f32[16,128]{1,0:T(8,128)S(1)} %group.3.refs_12_), channel_id=1, source_target_pairs={{0,17},{1,16},{2,19},{3,18},{4,21},{5,20},{6,23},{7,22},{8,25},{9,... | collective-permute-start | bytes 24584 | tf_op jit(solution)/shard_map/ppermute | solution.py:545
  17.4 3.1 %collective-permute-start.5 = (f32[16,128]{1,0:T(8,128)S(1)}, f32[16,128]{1,0:T(8,128)S(1)}, u32[]{:S(2)}, u32[]{:S(2)}) collective-permute-start(f32[16,128]{1,0:T(8,128)S(1)} %group.3.refs_12_), channel_id=1, source_target_pairs={{0,9},{1,8},{2,11},{3,10},{4,13},{5,12},{6,15},{7,14},{8,1},{9,0},... | collective-permute-start | bytes 24584 | tf_op jit(solution)/shard_map/ppermute | solution.py:545
  21.8 5.0 %collective-permute-start.10 = (f32[32,128]{1,0:T(8,128)S(1)}, f32[32,128]{1,0:T(8,128)S(1)}, u32[]{:S(2)}, u32[]{:S(2)}) collective-permute-start(f32[32,128]{1,0:T(8,128)S(1)} %get-tuple-element.65.refs_0_), channel_id=1, source_target_pairs={{0,7},{1,6},{2,5},{3,4},{4,3},{5,2},{6,1},{7,0},{8,15},{9,14},{10,... | collective-permute-start | bytes 49160 | tf_op jit(solution)/shard_map/ppermute | solution.py:545
  23.1 4.3 %collective-permute-start.9 = (f32[32,128]{1,0:T(8,128)S(1)}, f32[32,128]{1,0:T(8,128)S(1)}, u32[]{:S(2)}, u32[]{:S(2)}) collective-permute-start(f32[32,128]{1,0:T(8,128)S(1)} %get-tuple-element.65.refs_0_), channel_id=1, source_target_pairs={{0,5},{1,4},{2,7},{3,6},{4,1},{5,0},{6,3},{7,2},{8,13},{9,12},{10,... | collective-permute-start | bytes 49160 | tf_op jit(solution)/shard_map/ppermute | solution.py:545
  23.7 3.8 %collective-permute-start.8 = (f32[32,128]{1,0:T(8,128)S(1)}, f32[32,128]{1,0:T(8,128)S(1)}, u32[]{:S(2)}, u32[]{:S(2)}) collective-permute-start(f32[32,128]{1,0:T(8,128)S(1)} %get-tuple-element.65.refs_0_), channel_id=1, source_target_pairs={{0,3},{1,2},{2,1},{3,0},{4,7},{5,6},{6,5},{7,4},{8,11},{9,10},{10,... | collective-permute-start | bytes 49160 | tf_op jit(solution)/shard_map/ppermute | solution.py:545
  27.5 4.8 %collective-permute-start.13 = (f32[16,128]{1,0:T(8,128)S(1)}, f32[16,128]{1,0:T(8,128)S(1)}, u32[]{:S(2)}, u32[]{:S(2)}) collective-permute-start(f32[16,128]{1,0:T(8,128)S(1)} %get-tuple-element.75.refs_16_), channel_id=1, source_target_pairs={{0,25},{1,24},{2,27},{3,26},{4,29},{5,28},{6,31},{7,30},{8,17},{9,... | collective-permute-start | bytes 24584 | tf_op jit(solution)/shard_map/ppermute | solution.py:545
  29.8 3.1 %collective-permute-start.12 = (f32[16,128]{1,0:T(8,128)S(1)}, f32[16,128]{1,0:T(8,128)S(1)}, u32[]{:S(2)}, u32[]{:S(2)}) collective-permute-start(f32[16,128]{1,0:T(8,128)S(1)} %get-tuple-element.75.refs_16_), channel_id=1, source_target_pairs={{0,17},{1,16},{2,19},{3,18},{4,21},{5,20},{6,23},{7,22},{8,25},{9,... | collective-permute-start | bytes 24584 | tf_op jit(solution)/shard_map/ppermute | solution.py:545
  30.4 3.1 %collective-permute-start.11 = (f32[16,128]{1,0:T(8,128)S(1)}, f32[16,128]{1,0:T(8,128)S(1)}, u32[]{:S(2)}, u32[]{:S(2)}) collective-permute-start(f32[16,128]{1,0:T(8,128)S(1)} %get-tuple-element.75.refs_16_), channel_id=1, source_target_pairs={{0,9},{1,8},{2,11},{3,10},{4,13},{5,12},{6,15},{7,14},{8,1},{9,0},... | collective-permute-start | bytes 24584 | tf_op jit(solution)/shard_map/ppermute | solution.py:545
  34.8 5.0 %collective-permute-start.16 = (f32[32,128]{1,0:T(8,128)S(1)}, f32[32,128]{1,0:T(8,128)S(1)}, u32[]{:S(2)}, u32[]{:S(2)}) collective-permute-start(f32[32,128]{1,0:T(8,128)S(1)} %get-tuple-element.76.refs_0_), channel_id=1, source_target_pairs={{0,7},{1,6},{2,5},{3,4},{4,3},{5,2},{6,1},{7,0},{8,15},{9,14},{10,... | collective-permute-start | bytes 49160 | tf_op jit(solution)/shard_map/ppermute | solution.py:545
  36.5 4.1 %collective-permute-start.15 = (f32[32,128]{1,0:T(8,128)S(1)}, f32[32,128]{1,0:T(8,128)S(1)}, u32[]{:S(2)}, u32[]{:S(2)}) collective-permute-start(f32[32,128]{1,0:T(8,128)S(1)} %get-tuple-element.76.refs_0_), channel_id=1, source_target_pairs={{0,5},{1,4},{2,7},{3,6},{4,1},{5,0},{6,3},{7,2},{8,13},{9,12},{10,... | collective-permute-start | bytes 49160 | tf_op jit(solution)/shard_map/ppermute | solution.py:545
  37.1 3.5 %collective-permute-start.14 = (f32[32,128]{1,0:T(8,128)S(1)}, f32[32,128]{1,0:T(8,128)S(1)}, u32[]{:S(2)}, u32[]{:S(2)}) collective-permute-start(f32[32,128]{1,0:T(8,128)S(1)} %get-tuple-element.76.refs_0_), channel_id=1, source_target_pairs={{0,3},{1,2},{2,1},{3,0},{4,7},{5,6},{6,5},{7,4},{8,11},{9,10},{10,... | collective-permute-start | bytes 49160 | tf_op jit(solution)/shard_map/ppermute | solution.py:545
  40.6 4.8 %collective-permute-start.19 = (f32[16,128]{1,0:T(8,128)S(1)}, f32[16,128]{1,0:T(8,128)S(1)}, u32[]{:S(2)}, u32[]{:S(2)}) collective-permute-start(f32[16,128]{1,0:T(8,128)S(1)} %get-tuple-element.86.refs_16_), channel_id=1, source_target_pairs={{0,25},{1,24},{2,27},{3,26},{4,29},{5,28},{6,31},{7,30},{8,17},{9,... | collective-permute-start | bytes 24584 | tf_op jit(solution)/shard_map/ppermute | solution.py:545
  42.5 3.1 %collective-permute-start.18 = (f32[16,128]{1,0:T(8,128)S(1)}, f32[16,128]{1,0:T(8,128)S(1)}, u32[]{:S(2)}, u32[]{:S(2)}) collective-permute-start(f32[16,128]{1,0:T(8,128)S(1)} %get-tuple-element.86.refs_16_), channel_id=1, source_target_pairs={{0,17},{1,16},{2,19},{3,18},{4,21},{5,20},{6,23},{7,22},{8,25},{9,... | collective-permute-start | bytes 24584 | tf_op jit(solution)/shard_map/ppermute | solution.py:545
  42.9 3.1 %collective-permute-start.17 = (f32[16,128]{1,0:T(8,128)S(1)}, f32[16,128]{1,0:T(8,128)S(1)}, u32[]{:S(2)}, u32[]{:S(2)}) collective-permute-start(f32[16,128]{1,0:T(8,128)S(1)} %get-tuple-element.86.refs_16_), channel_id=1, source_target_pairs={{0,9},{1,8},{2,11},{3,10},{4,13},{5,12},{6,15},{7,14},{8,1},{9,0},... | collective-permute-start | bytes 24584 | tf_op jit(solution)/shard_map/ppermute | solution.py:545
  46.9 4.8 %collective-permute-start.22 = (f32[8,128]{1,0:T(8,128)S(1)}, f32[8,128]{1,0:T(8,128)S(1)}, u32[]{:S(2)}, u32[]{:S(2)}) collective-permute-start(f32[8,128]{1,0:T(8,128)S(1)} %get-tuple-element.88.refs_0_), channel_id=1, source_target_pairs={{0,7},{1,6},{2,5},{3,4},{4,3},{5,2},{6,1},{7,0},{8,15},{9,14},{10,... | collective-permute-start | bytes 12296 | tf_op jit(solution)/shard_map/ppermute | solution.py:545
  48.5 4.0 %collective-permute-start.21 = (f32[8,128]{1,0:T(8,128)S(1)}, f32[8,128]{1,0:T(8,128)S(1)}, u32[]{:S(2)}, u32[]{:S(2)}) collective-permute-start(f32[8,128]{1,0:T(8,128)S(1)} %get-tuple-element.88.refs_0_), channel_id=1, source_target_pairs={{0,5},{1,4},{2,7},{3,6},{4,1},{5,0},{6,3},{7,2},{8,13},{9,12},{10,... | collective-permute-start | bytes 12296 | tf_op jit(solution)/shard_map/ppermute | solution.py:545
  49.1 3.3 %collective-permute-start.20 = (f32[8,128]{1,0:T(8,128)S(1)}, f32[8,128]{1,0:T(8,128)S(1)}, u32[]{:S(2)}, u32[]{:S(2)}) collective-permute-start(f32[8,128]{1,0:T(8,128)S(1)} %get-tuple-element.88.refs_0_), channel_id=1, source_target_pairs={{0,3},{1,2},{2,1},{3,0},{4,7},{5,6},{6,5},{7,4},{8,11},{9,10},{10,... | collective-permute-start | bytes 12296 | tf_op jit(solution)/shard_map/ppermute | solution.py:545
  52.4 4.0 %collective-permute-start.25 = (f32[8,128]{1,0:T(8,128)S(1)}, f32[8,128]{1,0:T(8,128)S(1)}, u32[]{:S(2)}, u32[]{:S(2)}) collective-permute-start(f32[8,128]{1,0:T(8,128)S(1)} %sum.1.refs_0_), channel_id=1, source_target_pairs={{0,25},{1,24},{2,27},{3,26},{4,29},{5,28},{6,31},{7,30},{8,17},{9,... | collective-permute-start | bytes 12296 | tf_op jit(solution)/shard_map/ppermute | solution.py:545
  54.7 3.0 %collective-permute-start.24 = (f32[8,128]{1,0:T(8,128)S(1)}, f32[8,128]{1,0:T(8,128)S(1)}, u32[]{:S(2)}, u32[]{:S(2)}) collective-permute-start(f32[8,128]{1,0:T(8,128)S(1)} %sum.1.refs_0_), channel_id=1, source_target_pairs={{0,17},{1,16},{2,19},{3,18},{4,21},{5,20},{6,23},{7,22},{8,25},{9,... | collective-permute-start | bytes 12296 | tf_op jit(solution)/shard_map/ppermute | solution.py:545
  55.0 3.0 %collective-permute-start.23 = (f32[8,128]{1,0:T(8,128)S(1)}, f32[8,128]{1,0:T(8,128)S(1)}, u32[]{:S(2)}, u32[]{:S(2)}) collective-permute-start(f32[8,128]{1,0:T(8,128)S(1)} %sum.1.refs_0_), channel_id=1, source_target_pairs={{0,9},{1,8},{2,11},{3,10},{4,13},{5,12},{6,15},{7,14},{8,1},{9,0},... | collective-permute-start | bytes 12296 | tf_op jit(solution)/shard_map/ppermute | solution.py:545

commit v6 on v5

--- a/solution.py
+++ b/solution.py
@@ -203,16 +203,10 @@
 def first_chip_kernel(count, *refs):
     ins, out_ref = refs[:count], refs[count]
     chip = lax.axis_index("tm") // 2
-    extra = ins[0].shape[0] - 24
-    base = 8 * count + 16
+    size = ins[0].shape[0]
     for gap in range(count):
-        where = chip ^ gap
-        out_ref[pl.ds(pl.multiple_of(where * 8, 8), 8)] = ins[gap][0:8]
-        out_ref[pl.ds(pl.multiple_of(base + where * 8, 8), 8)] = ins[gap][16:24]
-        at = pl.multiple_of(base + 8 * count + where * extra, 8)
-        out_ref[pl.ds(at, extra)] = ins[gap][24:]
-    out_ref[8 * count : 8 * count + 8] = tree_sum([ref[8:16] for ref in ins])
-    out_ref[8 * count + 8 : base] = tree_sum([ref[16:24] for ref in ins])
+        at = pl.multiple_of((chip ^ gap) * size, 8)
+        out_ref[pl.ds(at, size)] = ins[gap][...]
 
 
 def group_rows(chip, count, mine, prev_row, after_row):
@@ -231,22 +225,26 @@
 def first_group_kernel(count, own_ref, other_ref, out_ref):
     me = lax.axis_index("tm")
     chip, core = me // 2, me % 2
-    low = 8 * count
-    base = low + 16
-
-    def part(ref, where):
+    size = own_ref.shape[0] // count
+
+    def part(ref, where, start):
         where = jnp.clip(where, 0, count - 1)
-        return ref[pl.ds(pl.multiple_of(base + where * 8, 8), 8)]
+        return ref[pl.ds(pl.multiple_of(where * size + start, 8), 8)]
 
     def of_core(which, where):
-        return jnp.where(core == which, part(own_ref, where), part(other_ref, where))
-
-    mine = chip_parts(core, part(own_ref, chip)[0:3], part(other_ref, chip)[0:3])
+        mine = (core == which) == (where == chip)
+        return jnp.where(mine, part(own_ref, where, 16), part(other_ref, where, 16))
+
+    def total(start):
+        return tree_sum(
+            [part(own_ref, chip ^ gap, start) + part(other_ref, chip ^ gap, start) for gap in range(count)]
+        )
+
+    mine = chip_parts(core, part(own_ref, chip, 16)[0:3], part(other_ref, chip, 16)[0:3])
     prev, after = of_core(1, chip - 1), of_core(0, chip + 1)
-    scalars = own_ref[low + 8 : low + 16] + other_ref[low + 8 : low + 16]
-    out_ref[0:8] = own_ref[low : low + 8] + other_ref[low : low + 8]
+    out_ref[0:8] = total(8)
     att = group_rows(chip, count, mine, prev[2:3], after[0:1])
-    out_ref[8:16] = jnp.concatenate(att + [scalars[3:6]], axis=0)
+    out_ref[8:16] = jnp.concatenate(att + [total(16)[3:6]], axis=0)
 
 
 def group_kernel(count, *refs):
@@ -271,16 +269,15 @@
 
 
 def kept(count, keep_ref):
-    base = 16 * count + 16
-    extra = (keep_ref.shape[0] - base) // count
-    return base, extra, extra // 8 - 1
+    size = keep_ref.shape[0] // count
+    return size, size - 24, (size - 24) // 8 - 1
 
 
 def star_sums(count, place, keep_ref, rows, table_ref, spread_ref, build):
     high = STARS_DEV // LANES
-    base, extra, comps = kept(count, keep_ref)
+    size, extra, comps = kept(count, keep_ref)
     long = 8 * LANES
-    packed = keep_ref[pl.ds(pl.multiple_of(base + place * extra, 8), extra)]
+    packed = keep_ref[pl.ds(pl.multiple_of(place * size + 24, 8), extra)]
     index = packed[comps * 8 :].astype(jnp.int32)
     at0 = pl.multiple_of(place * long, long)
     split = [halves(packed[comp * 8 : comp * 8 + 8] * rows) for comp in range(comps)]
@@ -300,9 +297,9 @@
 
 def star_rows(count, keep_ref, sums):
     high = STARS_DEV // LANES
-    base, extra, comps = kept(count, keep_ref)
+    size, extra, comps = kept(count, keep_ref)
     chip = lax.axis_index("tm") // 2
-    packed = keep_ref[pl.ds(pl.multiple_of(base + chip * extra, 8), extra)]
+    packed = keep_ref[pl.ds(pl.multiple_of(chip * size + 24, 8), extra)]
     star = packed[comps * 8 :].astype(jnp.int32)
     star_high, star_low = star >> 7, star & (LANES - 1)
     total = jnp.zeros((8, LANES), f32)
@@ -319,7 +316,7 @@
     size = spread_ref.shape[0]
 
     def one(place, total):
-        rows = keep_ref[pl.ds(pl.multiple_of(place * 8, 8), 8)]
+        rows = keep_ref[pl.ds(pl.multiple_of(place * kept(count, keep_ref)[0], 8), 8)]
         return total + star_sums(count, place, keep_ref, rows, table_ref, spread_ref, True)
 
     total = lax.fori_loop(0, count, one, jnp.zeros((size, LANES), f32))
@@ -339,14 +336,15 @@
 
 def astro_kernel(count, own_ref, other_ref, own_table, other_table, rows_ref, out_ref, ya_ref,
                  spread_ref):
-    core = lax.axis_index("tm") % 2
+    me = lax.axis_index("tm")
     size = spread_ref.shape[1]
     sources = ((own_ref, own_table), (other_ref, other_table))
 
     def one(place, totals):
         new = []
         for half, (keep_ref, table_ref) in enumerate(sources):
-            at = ((half ^ core) * count + place) * 8
+            core = half ^ (me % 2) ^ jnp.where(place == me // 2, 0, 1)
+            at = (core * count + place) * 8
             rows = rows_ref[pl.ds(pl.multiple_of(at, 8), 8)]
             part = star_sums(count, place, keep_ref, rows, table_ref, spread_ref.at[half], False)
             new.append(totals[half] + part)
@@ -414,7 +412,7 @@
         squares = lane_sum(total[13:14])
         beta2 = squares + epsilon
         beta = jnp.sqrt(beta2)
-        at = pl.ds(pl.multiple_of(chip * 8, 8), 8)
+        at = pl.ds(pl.multiple_of(chip * kept(chips, keep[0])[0], 8), 8)
         u = jnp.concatenate([ref[at] for ref in keep], axis=0) / beta
         g = back / beta
         z = g
@@ -558,7 +556,6 @@
     share = STARS_DEV // tm_count
     high = STARS_DEV // LANES
     chips = tm_count // 2
-    far = [2 * gap for gap in range(1, chips)]
     args = [
         observed.reshape(blocks, height),
         astro_coef.reshape(comps, blocks, height),
@@ -590,12 +587,12 @@
         wide = (2 * comps * high, blocks * height)
         sums_type = rows_type(comps * high)
         pair = rows_type(2 * blocks)
-        got = exchange(send, "tm") if step else direct(send, "tm", far)
+        got = exchange(send, "tm")
         if step == 0:
             (gathered,) = call(
                 functools.partial(first_chip_kernel, chips),
                 "chip",
-                [((16 * chips + 16 + chips * extra, LANES), f32)],
+                [rows_type(chips * (24 + extra))],
                 got,
             )
             keep = direct(gathered, "tm", [1])

time: 58.9 us -> 58.3 us (0.990)
  waiting for transfers between devices: 14 us -> 12.6 us
  starting transfers between devices: 30.5 us -> 31.2 us
    ppermute x21 -> x24, starting transfers between devices: 24.1 us -> 30.5 us  [exchange(): got.append(lax.ppermute(value, ('star', 'tm'), steps))]
    ppermute x5 -> x2, starting transfers between devices: 6.39 us -> 0.64 us  [direct(): lax.ppermute(value, axis, [(i, i ^ gap) for i in range(count)])]
    ppermute x5 -> x2, waiting for transfers between devices: 4.22 us -> 0.01 us  [direct(): lax.ppermute(value, axis, [(i, i ^ gap) for i in range(count)])]
    ppermute x21 -> x24, waiting for transfers between devices: 9.8 us -> 12.6 us  [exchange(): got.append(lax.ppermute(value, ('star', 'tm'), steps))]
  transfers between devices with their start and end apart: 26 -> 26, of which waited for: 18 -> 16; matrix products, arithmetic and copies ran while one was open for 0% -> 0% of each run, Pallas kernels for 12% -> 12%
where the time goes in v6:
time: 58.3 us; the launch traced here: 58.2 us
  starting transfers between devices  31.2 us (54%)
  Pallas kernels  13.6 us (23%)
  waiting for transfers between devices  12.6 us (22%)
  between operations  0.77 us (1%)
    ppermute x24, starting transfers between devices, exchange(): got.append(lax.ppermute(value, ('star', 'tm'), steps))  30.5 us
    pallas_call x15, Pallas kernels, call(): pl.pallas_call(kernel, name=name, out_shape=[jax.ShapeDtypeStruct(shape,...  13.6 us
    ppermute x24, waiting for transfers between devices, exchange(): got.append(lax.ppermute(value, ('star', 'tm'), steps))  12.6 us
  transfers between devices with their start and end apart: 26, of which 16 were waited for; matrix products, arithmetic and copies ran while one was open for 0% of the time, Pallas kernels for 12%

profile of v6, /device:TPU:0, one launch (start us, length us, event | category | flops | bytes accessed | tf_op | source)
XLA Modules:
  0.0 58.2 jit_solution(3999752522188545987)
XLA Ops:
  0.6 1.9 %first.1 = (f32[72,128]{1,0:T(8,128)S(1)}, f32[616,128]{1,0:T(8,128)S(1)}, bf16[128,6144]{1,0:T(8,128)(2,1)S(1)}, bf16[1024,128]{1,0:T(8,128)(2,1)S(1)}, s32[56,128]{1,0:T(8,128)S(1)}) custom-call(f32[8,128]{1,0:T(8,128)} %bitcast.12, f32[5,8,128]{2,1,0:T(8,128)} %bitcast.11, s32[8,128]{1,0:T(8,128)} %bitcast.13, f32[512,128]{1,0:T(8,128)} %bitcast.8, ...), custom_call_target="tpu_custom_call" | custom-call | tf_op jit(solution)/shard_map/first/pallas_call | solution.py:516
  2.6 4.6 %collective-permute-start.2 = (f32[72,128]{1,0:T(8,128)S(1)}, f32[72,128]{1,0:T(8,128)S(1)}, u32[]{:S(2)}, u32[]{:S(2)}) collective-permute-start(f32[72,128]{1,0:T(8,128)S(1)} %get-tuple-element.49.refs_0_), channel_id=1, source_target_pairs={{0,7},{1,6},{2,5},{3,4},{4,3},{5,2},{6,1},{7,0},{8,15},{9,14},{10,... | collective-permute-start | bytes 110600 | tf_op jit(solution)/shard_map/ppermute | solution.py:543
  7.1 0.9 %collective-permute-start = (f32[72,128]{1,0:T(8,128)S(1)}, f32[72,128]{1,0:T(8,128)S(1)}, u32[]{:S(2)}, u32[]{:S(2)}) collective-permute-start(f32[72,128]{1,0:T(8,128)S(1)} %get-tuple-element.49.refs_0_), channel_id=1, source_target_pairs={{0,3},{1,2},{2,1},{3,0},{4,7},{5,6},{6,5},{7,4},{8,11},{9,10},{10,... | collective-permute-start | bytes 110600 | tf_op jit(solution)/shard_map/ppermute | solution.py:543
  8.0 0.9 %collective-permute-done.2.refs_3_ = f32[72,128]{1,0:T(8,128)S(1)} collective-permute-done((f32[72,128]{1,0:T(8,128)S(1)}, f32[72,128]{1,0:T(8,128)S(1)}, u32[]{:S(2)}, u32[]{:S(2)}) %collective-permute-start.2) | collective-permute-done | bytes 36896 | tf_op jit(solution)/shard_map/ppermute | solution.py:543
  9.0 2.8 %collective-permute-done.1.refs_2_ = f32[72,128]{1,0:T(8,128)S(1)} collective-permute-done((f32[72,128]{1,0:T(8,128)S(1)}, f32[72,128]{1,0:T(8,128)S(1)}, u32[]{:S(2)}, u32[]{:S(2)}) %collective-permute-start.1) | collective-permute-done | bytes 36896 | tf_op jit(solution)/shard_map/ppermute | solution.py:543
  11.8 0.4 collective-permute-start.3
  12.2 1.4 %astro_own.1 = (f32[80,128]{1,0:T(8,128)S(1)}, bf16[128,4096]{1,0:T(8,128)(2,1)S(1)}) custom-call(f32[288,128]{1,0:T(8,128)S(1)} %chip.1.keep_ref.own_ref.refs_10_), custom_call_target="tpu_custom_call" | custom-call | tf_op jit(solution)/shard_map/astro_own/pallas_call | solution.py:516
  13.7 0.2 collective-permute-start.4
  13.9 2.4 %collective-permute-start.7 = (f32[16,128]{1,0:T(8,128)S(1)}, f32[16,128]{1,0:T(8,128)S(1)}, u32[]{:S(2)}, u32[]{:S(2)}) collective-permute-start(f32[16,128]{1,0:T(8,128)S(1)} %group.3.refs_12_), channel_id=1, source_target_pairs={{0,25},{1,24},{2,27},{3,26},{4,29},{5,28},{6,31},{7,30},{8,17},{9,... | collective-permute-start | bytes 24584 | tf_op jit(solution)/shard_map/ppermute | solution.py:543
  16.3 0.3 collective-permute-start.6
  16.6 0.5 collective-permute-start.5
  17.1 1.7 %astro.3 = (f32[80,128]{1,0:T(8,128)S(1)}, f32[16,128]{1,0:T(8,128)S(1)}, bf16[128,4096]{1,0:T(8,128)(2,1)S(1)}) custom-call(f32[288,128]{1,0:T(8,128)S(1)} %chip.1.keep_ref.own_ref.refs_10_, f32[288,128]{1,0:T(8,128)S(1)} %collective-permute-done.3.other_ref.keep_ref.refs_11_, f32[80,128]{1,0:T(8,128)S(1)} %get-tuple-element.60.part_ref), custom_call_target="tpu_custom_call" | custom-call | tf_op jit(solution)/shard_map/astro/pallas_call | solution.py:516
  18.8 0.5 prepare.1
  19.4 0.3 collective-permute-done.5.refs_13_
  19.7 1.4 %step.3 = (f32[32,128]{1,0:T(8,128)S(1)}, f32[16,128]{1,0:T(8,128)S(1)}, f32[96,128]{1,0:T(8,128)S(1)}, f32[96,128]{1,0:T(8,128)S(1)}, f32[16,128]{1,0:T(8,128)S...) custom-call(f32[616,128]{1,0:T(8,128)S(1)} %get-tuple-element.52.refs_0_, ...), custom_call_target="tpu_custom_call" | custom-call | tf_op jit(solution)/shard_map/step/pallas_call | solution.py:516
  21.1 2.0 %collective-permute-start.10 = (f32[32,128]{1,0:T(8,128)S(1)}, f32[32,128]{1,0:T(8,128)S(1)}, u32[]{:S(2)}, u32[]{:S(2)}) collective-permute-start(f32[32,128]{1,0:T(8,128)S(1)} %get-tuple-element.65.refs_0_), channel_id=1, source_target_pairs={{0,7},{1,6},{2,5},{3,4},{4,3},{5,2},{6,1},{7,0},{8,15},{9,14},{10,... | collective-permute-start | bytes 49160 | tf_op jit(solution)/shard_map/ppermute | solution.py:543
  23.1 0.5 collective-permute-start.9
  23.6 1.6 %collective-permute-start.8 = (f32[32,128]{1,0:T(8,128)S(1)}, f32[32,128]{1,0:T(8,128)S(1)}, u32[]{:S(2)}, u32[]{:S(2)}) collective-permute-start(f32[32,128]{1,0:T(8,128)S(1)} %get-tuple-element.65.refs_0_), channel_id=1, source_target_pairs={{0,3},{1,2},{2,1},{3,0},{4,7},{5,6},{6,5},{7,4},{8,11},{9,10},{10,... | collective-permute-start | bytes 49160 | tf_op jit(solution)/shard_map/ppermute | solution.py:543
  25.2 0.9 %collective-permute-done.10.refs_3_ = f32[32,128]{1,0:T(8,128)S(1)} collective-permute-done((f32[32,128]{1,0:T(8,128)S(1)}, f32[32,128]{1,0:T(8,128)S(1)}, u32[]{:S(2)}, u32[]{:S(2)}) %collective-permute-start.10) | collective-permute-done | bytes 16416 | tf_op jit(solution)/shard_map/ppermute | solution.py:543
  26.1 1.1 %collective-permute-done.9.refs_2_ = f32[32,128]{1,0:T(8,128)S(1)} collective-permute-done((f32[32,128]{1,0:T(8,128)S(1)}, f32[32,128]{1,0:T(8,128)S(1)}, u32[]{:S(2)}, u32[]{:S(2)}) %collective-permute-start.9) | collective-permute-done | bytes 16416 | tf_op jit(solution)/shard_map/ppermute | solution.py:543
  27.2 2.1 %collective-permute-start.13 = (f32[16,128]{1,0:T(8,128)S(1)}, f32[16,128]{1,0:T(8,128)S(1)}, u32[]{:S(2)}, u32[]{:S(2)}) collective-permute-start(f32[16,128]{1,0:T(8,128)S(1)} %get-tuple-element.75.refs_16_), channel_id=1, source_target_pairs={{0,25},{1,24},{2,27},{3,26},{4,29},{5,28},{6,31},{7,30},{8,17},{9,... | collective-permute-start | bytes 24584 | tf_op jit(solution)/shard_map/ppermute | solution.py:543
  29.4 0.4 collective-permute-start.12
  29.7 0.9 %collective-permute-start.11 = (f32[16,128]{1,0:T(8,128)S(1)}, f32[16,128]{1,0:T(8,128)S(1)}, u32[]{:S(2)}, u32[]{:S(2)}) collective-permute-start(f32[16,128]{1,0:T(8,128)S(1)} %get-tuple-element.75.refs_16_), channel_id=1, source_target_pairs={{0,9},{1,8},{2,11},{3,10},{4,13},{5,12},{6,15},{7,14},{8,1},{9,0},... | collective-permute-start | bytes 24584 | tf_op jit(solution)/shard_map/ppermute | solution.py:543
  30.6 1.8 %astro.4 = (f32[80,128]{1,0:T(8,128)S(1)}, f32[16,128]{1,0:T(8,128)S(1)}) custom-call(f32[288,128]{1,0:T(8,128)S(1)} %chip.1.keep_ref.own_ref.refs_10_, f32[288,128]{1,0:T(8,128)S(1)} %collective-permute-done.3.other_ref.keep_ref.refs_11_, bf16[128,4096]{1,0:T(8,128)(2,1)S(1)} %get-tuple-element.59.own_table, ...), custom_call_target="tpu_custom_call" | custom-call | tf_op jit(solution)/shard_map/astro/pallas_call | solution.py:516
  32.4 0.4 collective-permute-done.11.refs_17_
  32.8 1.4 %step.4 = (f32[32,128]{1,0:T(8,128)S(1)}, f32[16,128]{1,0:T(8,128)S(1)}, f32[96,128]{1,0:T(8,128)S(1)}, f32[96,128]{1,0:T(8,128)S(1)}, f32[16,128]{1,0:T(8,128)S...) custom-call(f32[616,128]{1,0:T(8,128)S(1)} %get-tuple-element.52.refs_0_, ...), custom_call_target="tpu_custom_call" | custom-call | tf_op jit(solution)/shard_map/step/pallas_call | solution.py:516
  34.2 1.9 %collective-permute-start.16 = (f32[32,128]{1,0:T(8,128)S(1)}, f32[32,128]{1,0:T(8,128)S(1)}, u32[]{:S(2)}, u32[]{:S(2)}) collective-permute-start(f32[32,128]{1,0:T(8,128)S(1)} %get-tuple-element.76.refs_0_), channel_id=1, source_target_pairs={{0,7},{1,6},{2,5},{3,4},{4,3},{5,2},{6,1},{7,0},{8,15},{9,14},{10,... | collective-permute-start | bytes 49160 | tf_op jit(solution)/shard_map/ppermute | solution.py:543
  36.1 0.5 collective-permute-start.15
  36.6 1.7 %collective-permute-start.14 = (f32[32,128]{1,0:T(8,128)S(1)}, f32[32,128]{1,0:T(8,128)S(1)}, u32[]{:S(2)}, u32[]{:S(2)}) collective-permute-start(f32[32,128]{1,0:T(8,128)S(1)} %get-tuple-element.76.refs_0_), channel_id=1, source_target_pairs={{0,3},{1,2},{2,1},{3,0},{4,7},{5,6},{6,5},{7,4},{8,11},{9,10},{10,... | collective-permute-start | bytes 49160 | tf_op jit(solution)/shard_map/ppermute | solution.py:543
  38.2 1.0 %collective-permute-done.16.refs_3_ = f32[32,128]{1,0:T(8,128)S(1)} collective-permute-done((f32[32,128]{1,0:T(8,128)S(1)}, f32[32,128]{1,0:T(8,128)S(1)}, u32[]{:S(2)}, u32[]{:S(2)}) %collective-permute-start.16) | collective-permute-done | bytes 16416 | tf_op jit(solution)/shard_map/ppermute | solution.py:543
  39.2 1.1 %collective-permute-done.15.refs_2_ = f32[32,128]{1,0:T(8,128)S(1)} collective-permute-done((f32[32,128]{1,0:T(8,128)S(1)}, f32[32,128]{1,0:T(8,128)S(1)}, u32[]{:S(2)}, u32[]{:S(2)}) %collective-permute-start.15) | collective-permute-done | bytes 16416 | tf_op jit(solution)/shard_map/ppermute | solution.py:543
  40.4 2.0 %collective-permute-start.19 = (f32[16,128]{1,0:T(8,128)S(1)}, f32[16,128]{1,0:T(8,128)S(1)}, u32[]{:S(2)}, u32[]{:S(2)}) collective-permute-start(f32[16,128]{1,0:T(8,128)S(1)} %get-tuple-element.86.refs_16_), channel_id=1, source_target_pairs={{0,25},{1,24},{2,27},{3,26},{4,29},{5,28},{6,31},{7,30},{8,17},{9,... | collective-permute-start | bytes 24584 | tf_op jit(solution)/shard_map/ppermute | solution.py:543
  42.5 0.9 %collective-permute-start.17 = (f32[16,128]{1,0:T(8,128)S(1)}, f32[16,128]{1,0:T(8,128)S(1)}, u32[]{:S(2)}, u32[]{:S(2)}) collective-permute-start(f32[16,128]{1,0:T(8,128)S(1)} %get-tuple-element.86.refs_16_), channel_id=1, source_target_pairs={{0,9},{1,8},{2,11},{3,10},{4,13},{5,12},{6,15},{7,14},{8,1},{9,0},... | collective-permute-start | bytes 24584 | tf_op jit(solution)/shard_map/ppermute | solution.py:543
  43.4 1.8 %astro.5 = (f32[80,128]{1,0:T(8,128)S(1)}, f32[16,128]{1,0:T(8,128)S(1)}) custom-call(f32[288,128]{1,0:T(8,128)S(1)} %chip.1.keep_ref.own_ref.refs_10_, f32[288,128]{1,0:T(8,128)S(1)} %collective-permute-done.3.other_ref.keep_ref.refs_11_, bf16[128,4096]{1,0:T(8,128)(2,1)S(1)} %get-tuple-element.59.own_table, ...), custom_call_target="tpu_custom_call" | custom-call | tf_op jit(solution)/shard_map/astro/pallas_call | solution.py:516
  45.2 0.3 collective-permute-done.18.refs_18_
  45.6 0.9 %step.5 = (f32[8,128]{1,0:T(8,128)S(1)}, f32[16,128]{1,0:T(8,128)S(1)}, f32[96,128]{1,0:T(8,128)S(1)}, f32[96,128]{1,0:T(8,128)}, f32[16,128]{1,0:T(8,128)}, /*index=5*/f32[16,128]{1,0:T(8,128)}, f32[16,128]{1,0:T(8,128)}) custom-call(f32[616,128]{1,0:T(8,128)S(1)} %get-tuple-element.52.refs_0_, f32[616,128]{1,0:T(8,128)S(1)} %collective-permute-done.4.pack_ref.refs_1_, ...), custom_call_target="tpu_custom_call" | custom-call | tf_op jit(solution)/shard_map/step/pallas_call | solution.py:516
  46.5 1.8 %collective-permute-start.22 = (f32[8,128]{1,0:T(8,128)S(1)}, f32[8,128]{1,0:T(8,128)S(1)}, u32[]{:S(2)}, u32[]{:S(2)}) collective-permute-start(f32[8,128]{1,0:T(8,128)S(1)} %get-tuple-element.88.refs_0_), channel_id=1, source_target_pairs={{0,7},{1,6},{2,5},{3,4},{4,3},{5,2},{6,1},{7,0},{8,15},{9,14},{10,... | collective-permute-start | bytes 12296 | tf_op jit(solution)/shard_map/ppermute | solution.py:543
  48.2 0.5 collective-permute-start.21
  48.8 1.8 %collective-permute-start.20 = (f32[8,128]{1,0:T(8,128)S(1)}, f32[8,128]{1,0:T(8,128)S(1)}, u32[]{:S(2)}, u32[]{:S(2)}) collective-permute-start(f32[8,128]{1,0:T(8,128)S(1)} %get-tuple-element.88.refs_0_), channel_id=1, source_target_pairs={{0,3},{1,2},{2,1},{3,0},{4,7},{5,6},{6,5},{7,4},{8,11},{9,10},{10,... | collective-permute-start | bytes 12296 | tf_op jit(solution)/shard_map/ppermute | solution.py:543
  50.5 0.8 %collective-permute-done.22.refs_3_ = f32[8,128]{1,0:T(8,128)S(1)} collective-permute-done((f32[8,128]{1,0:T(8,128)S(1)}, f32[8,128]{1,0:T(8,128)S(1)}, u32[]{:S(2)}, u32[]{:S(2)}) %collective-permute-start.22) | collective-permute-done | bytes 4128 | tf_op jit(solution)/shard_map/ppermute | solution.py:543
  51.3 0.9 %collective-permute-done.21.refs_2_ = f32[8,128]{1,0:T(8,128)S(1)} collective-permute-done((f32[8,128]{1,0:T(8,128)S(1)}, f32[8,128]{1,0:T(8,128)S(1)}, u32[]{:S(2)}, u32[]{:S(2)}) %collective-permute-start.21) | collective-permute-done | bytes 4128 | tf_op jit(solution)/shard_map/ppermute | solution.py:543
  52.2 1.8 %collective-permute-start.25 = (f32[8,128]{1,0:T(8,128)S(1)}, f32[8,128]{1,0:T(8,128)S(1)}, u32[]{:S(2)}, u32[]{:S(2)}) collective-permute-start(f32[8,128]{1,0:T(8,128)S(1)} %sum.1.refs_0_), channel_id=1, source_target_pairs={{0,25},{1,24},{2,27},{3,26},{4,29},{5,28},{6,31},{7,30},{8,17},{9,... | collective-permute-start | bytes 12296 | tf_op jit(solution)/shard_map/ppermute | solution.py:543
  54.1 0.3 collective-permute-start.24
  54.4 1.1 %collective-permute-start.23 = (f32[8,128]{1,0:T(8,128)S(1)}, f32[8,128]{1,0:T(8,128)S(1)}, u32[]{:S(2)}, u32[]{:S(2)}) collective-permute-start(f32[8,128]{1,0:T(8,128)S(1)} %sum.1.refs_0_), channel_id=1, source_target_pairs={{0,9},{1,8},{2,11},{3,10},{4,13},{5,12},{6,15},{7,14},{8,1},{9,0},... | collective-permute-start | bytes 12296 | tf_op jit(solution)/shard_map/ppermute | solution.py:543
  55.5 0.7 %collective-permute-done.25.refs_3_ = f32[8,128]{1,0:T(8,128)S(1)} collective-permute-done((f32[8,128]{1,0:T(8,128)S(1)}, f32[8,128]{1,0:T(8,128)S(1)}, u32[]{:S(2)}, u32[]{:S(2)}) %collective-permute-start.25) | collective-permute-done | bytes 4128 | tf_op jit(solution)/shard_map/ppermute | solution.py:543
  56.2 0.9 %collective-permute-done.24.refs_2_ = f32[8,128]{1,0:T(8,128)S(1)} collective-permute-done((f32[8,128]{1,0:T(8,128)S(1)}, f32[8,128]{1,0:T(8,128)S(1)}, u32[]{:S(2)}, u32[]{:S(2)}) %collective-permute-start.24) | collective-permute-done | bytes 4128 | tf_op jit(solution)/shard_map/ppermute | solution.py:543
  57.1 0.3 collective-permute-done.23.refs_1_
  57.4 0.7 %last.1 = (f32[5,256]{1,0:T(8,128)}, f32[2,128]{1,0:T(2,128)}, f32[8,128]{1,0:T(8,128)}) custom-call(f32[16,128]{1,0:T(8,128)S(1)} %get-tuple-element.87.state_ref, f32[8,128]{1,0:T(8,128)S(1)} %sum.1.refs_0_, f32[8,128]{1,0:T(8,128)S(1)} %collective-permute-done.23.refs_1_, f32[8,128]{1,0:T(8,128)S(1)} %collective-permute-done.24.refs_2_, ...), custom_call_target="tpu_custom_call" | custom-call | tf_op jit(solution)/shard_map/last/pallas_call | solution.py:516
  (19 shorter events, 0.6 us)
Async XLA Ops:
  2.6 6.4 %collective-permute-start.2 = (f32[72,128]{1,0:T(8,128)S(1)}, f32[72,128]{1,0:T(8,128)S(1)}, u32[]{:S(2)}, u32[]{:S(2)}) collective-permute-start(f32[72,128]{1,0:T(8,128)S(1)} %get-tuple-element.49.refs_0_), channel_id=1, source_target_pairs={{0,7},{1,6},{2,5},{3,4},{4,3},{5,2},{6,1},{7,0},{8,15},{9,14},{10,... | collective-permute-start | bytes 110600 | tf_op jit(solution)/shard_map/ppermute | solution.py:543
  7.1 4.6 %collective-permute-start.1 = (f32[72,128]{1,0:T(8,128)S(1)}, f32[72,128]{1,0:T(8,128)S(1)}, u32[]{:S(2)}, u32[]{:S(2)}) collective-permute-start(f32[72,128]{1,0:T(8,128)S(1)} %get-tuple-element.49.refs_0_), channel_id=1, source_target_pairs={{0,5},{1,4},{2,7},{3,6},{4,1},{5,0},{6,3},{7,2},{8,13},{9,12},{10,... | collective-permute-start | bytes 110600 | tf_op jit(solution)/shard_map/ppermute | solution.py:543
  7.1 4.6 %collective-permute-start = (f32[72,128]{1,0:T(8,128)S(1)}, f32[72,128]{1,0:T(8,128)S(1)}, u32[]{:S(2)}, u32[]{:S(2)}) collective-permute-start(f32[72,128]{1,0:T(8,128)S(1)} %get-tuple-element.49.refs_0_), channel_id=1, source_target_pairs={{0,3},{1,2},{2,1},{3,0},{4,7},{5,6},{6,5},{7,4},{8,11},{9,10},{10,... | collective-permute-start | bytes 110600 | tf_op jit(solution)/shard_map/ppermute | solution.py:543
  11.8 1.8 %collective-permute-start.3 = (f32[288,128]{1,0:T(8,128)S(1)}, f32[288,128]{1,0:T(8,128)S(1)}, u32[]{:S(2)}, u32[]{:S(2)}) collective-permute-start(f32[288,128]{1,0:T(8,128)S(1)} %chip.1.keep_ref.own_ref.refs_10_), channel_id=1, source_target_pairs={{0,1},{1,0},{2,3},{3,2},{4,5},{5,4},{6,7},{7,6},{8,9},{9,8},{10,11... | collective-permute-start | bytes 442376 | tf_op jit(solution)/shard_map/ppermute | solution.py:530
  13.7 5.1 %collective-permute-start.4 = (f32[616,128]{1,0:T(8,128)S(1)}, f32[616,128]{1,0:T(8,128)S(1)}, u32[]{:S(2)}, u32[]{:S(2)}) collective-permute-start(f32[616,128]{1,0:T(8,128)S(1)} %get-tuple-element.52.refs_0_), channel_id=1, source_target_pairs={{0,1},{1,0},{2,3},{3,2},{4,5},{5,4},{6,7},{7,6},{8,9},{9,8},{10,11... | collective-permute-start | bytes 946184 | tf_op jit(solution)/shard_map/ppermute | solution.py:530
  13.9 5.4 %collective-permute-start.7 = (f32[16,128]{1,0:T(8,128)S(1)}, f32[16,128]{1,0:T(8,128)S(1)}, u32[]{:S(2)}, u32[]{:S(2)}) collective-permute-start(f32[16,128]{1,0:T(8,128)S(1)} %group.3.refs_12_), channel_id=1, source_target_pairs={{0,25},{1,24},{2,27},{3,26},{4,29},{5,28},{6,31},{7,30},{8,17},{9,... | collective-permute-start | bytes 24584 | tf_op jit(solution)/shard_map/ppermute | solution.py:543
  16.3 3.1 %collective-permute-start.6 = (f32[16,128]{1,0:T(8,128)S(1)}, f32[16,128]{1,0:T(8,128)S(1)}, u32[]{:S(2)}, u32[]{:S(2)}) collective-permute-start(f32[16,128]{1,0:T(8,128)S(1)} %group.3.refs_12_), channel_id=1, source_target_pairs={{0,17},{1,16},{2,19},{3,18},{4,21},{5,20},{6,23},{7,22},{8,25},{9,... | collective-permute-start | bytes 24584 | tf_op jit(solution)/shard_map/ppermute | solution.py:543
  16.6 3.1 %collective-permute-start.5 = (f32[16,128]{1,0:T(8,128)S(1)}, f32[16,128]{1,0:T(8,128)S(1)}, u32[]{:S(2)}, u32[]{:S(2)}) collective-permute-start(f32[16,128]{1,0:T(8,128)S(1)} %group.3.refs_12_), channel_id=1, source_target_pairs={{0,9},{1,8},{2,11},{3,10},{4,13},{5,12},{6,15},{7,14},{8,1},{9,0},... | collective-permute-start | bytes 24584 | tf_op jit(solution)/shard_map/ppermute | solution.py:543
  21.1 5.0 %collective-permute-start.10 = (f32[32,128]{1,0:T(8,128)S(1)}, f32[32,128]{1,0:T(8,128)S(1)}, u32[]{:S(2)}, u32[]{:S(2)}) collective-permute-start(f32[32,128]{1,0:T(8,128)S(1)} %get-tuple-element.65.refs_0_), channel_id=1, source_target_pairs={{0,7},{1,6},{2,5},{3,4},{4,3},{5,2},{6,1},{7,0},{8,15},{9,14},{10,... | collective-permute-start | bytes 49160 | tf_op jit(solution)/shard_map/ppermute | solution.py:543
  23.1 4.1 %collective-permute-start.9 = (f32[32,128]{1,0:T(8,128)S(1)}, f32[32,128]{1,0:T(8,128)S(1)}, u32[]{:S(2)}, u32[]{:S(2)}) collective-permute-start(f32[32,128]{1,0:T(8,128)S(1)} %get-tuple-element.65.refs_0_), channel_id=1, source_target_pairs={{0,5},{1,4},{2,7},{3,6},{4,1},{5,0},{6,3},{7,2},{8,13},{9,12},{10,... | collective-permute-start | bytes 49160 | tf_op jit(solution)/shard_map/ppermute | solution.py:543
  23.6 3.6 %collective-permute-start.8 = (f32[32,128]{1,0:T(8,128)S(1)}, f32[32,128]{1,0:T(8,128)S(1)}, u32[]{:S(2)}, u32[]{:S(2)}) collective-permute-start(f32[32,128]{1,0:T(8,128)S(1)} %get-tuple-element.65.refs_0_), channel_id=1, source_target_pairs={{0,3},{1,2},{2,1},{3,0},{4,7},{5,6},{6,5},{7,4},{8,11},{9,10},{10,... | collective-permute-start | bytes 49160 | tf_op jit(solution)/shard_map/ppermute | solution.py:543
  27.2 5.2 %collective-permute-start.13 = (f32[16,128]{1,0:T(8,128)S(1)}, f32[16,128]{1,0:T(8,128)S(1)}, u32[]{:S(2)}, u32[]{:S(2)}) collective-permute-start(f32[16,128]{1,0:T(8,128)S(1)} %get-tuple-element.75.refs_16_), channel_id=1, source_target_pairs={{0,25},{1,24},{2,27},{3,26},{4,29},{5,28},{6,31},{7,30},{8,17},{9,... | collective-permute-start | bytes 24584 | tf_op jit(solution)/shard_map/ppermute | solution.py:543
  29.4 3.1 %collective-permute-start.12 = (f32[16,128]{1,0:T(8,128)S(1)}, f32[16,128]{1,0:T(8,128)S(1)}, u32[]{:S(2)}, u32[]{:S(2)}) collective-permute-start(f32[16,128]{1,0:T(8,128)S(1)} %get-tuple-element.75.refs_16_), channel_id=1, source_target_pairs={{0,17},{1,16},{2,19},{3,18},{4,21},{5,20},{6,23},{7,22},{8,25},{9,... | collective-permute-start | bytes 24584 | tf_op jit(solution)/shard_map/ppermute | solution.py:543
  29.7 3.1 %collective-permute-start.11 = (f32[16,128]{1,0:T(8,128)S(1)}, f32[16,128]{1,0:T(8,128)S(1)}, u32[]{:S(2)}, u32[]{:S(2)}) collective-permute-start(f32[16,128]{1,0:T(8,128)S(1)} %get-tuple-element.75.refs_16_), channel_id=1, source_target_pairs={{0,9},{1,8},{2,11},{3,10},{4,13},{5,12},{6,15},{7,14},{8,1},{9,0},... | collective-permute-start | bytes 24584 | tf_op jit(solution)/shard_map/ppermute | solution.py:543
  34.2 5.0 %collective-permute-start.16 = (f32[32,128]{1,0:T(8,128)S(1)}, f32[32,128]{1,0:T(8,128)S(1)}, u32[]{:S(2)}, u32[]{:S(2)}) collective-permute-start(f32[32,128]{1,0:T(8,128)S(1)} %get-tuple-element.76.refs_0_), channel_id=1, source_target_pairs={{0,7},{1,6},{2,5},{3,4},{4,3},{5,2},{6,1},{7,0},{8,15},{9,14},{10,... | collective-permute-start | bytes 49160 | tf_op jit(solution)/shard_map/ppermute | solution.py:543
  36.1 4.3 %collective-permute-start.15 = (f32[32,128]{1,0:T(8,128)S(1)}, f32[32,128]{1,0:T(8,128)S(1)}, u32[]{:S(2)}, u32[]{:S(2)}) collective-permute-start(f32[32,128]{1,0:T(8,128)S(1)} %get-tuple-element.76.refs_0_), channel_id=1, source_target_pairs={{0,5},{1,4},{2,7},{3,6},{4,1},{5,0},{6,3},{7,2},{8,13},{9,12},{10,... | collective-permute-start | bytes 49160 | tf_op jit(solution)/shard_map/ppermute | solution.py:543
  36.6 3.8 %collective-permute-start.14 = (f32[32,128]{1,0:T(8,128)S(1)}, f32[32,128]{1,0:T(8,128)S(1)}, u32[]{:S(2)}, u32[]{:S(2)}) collective-permute-start(f32[32,128]{1,0:T(8,128)S(1)} %get-tuple-element.76.refs_0_), channel_id=1, source_target_pairs={{0,3},{1,2},{2,1},{3,0},{4,7},{5,6},{6,5},{7,4},{8,11},{9,10},{10,... | collective-permute-start | bytes 49160 | tf_op jit(solution)/shard_map/ppermute | solution.py:543
  40.4 4.8 %collective-permute-start.19 = (f32[16,128]{1,0:T(8,128)S(1)}, f32[16,128]{1,0:T(8,128)S(1)}, u32[]{:S(2)}, u32[]{:S(2)}) collective-permute-start(f32[16,128]{1,0:T(8,128)S(1)} %get-tuple-element.86.refs_16_), channel_id=1, source_target_pairs={{0,25},{1,24},{2,27},{3,26},{4,29},{5,28},{6,31},{7,30},{8,17},{9,... | collective-permute-start | bytes 24584 | tf_op jit(solution)/shard_map/ppermute | solution.py:543
  42.3 3.1 %collective-permute-start.18 = (f32[16,128]{1,0:T(8,128)S(1)}, f32[16,128]{1,0:T(8,128)S(1)}, u32[]{:S(2)}, u32[]{:S(2)}) collective-permute-start(f32[16,128]{1,0:T(8,128)S(1)} %get-tuple-element.86.refs_16_), channel_id=1, source_target_pairs={{0,17},{1,16},{2,19},{3,18},{4,21},{5,20},{6,23},{7,22},{8,25},{9,... | collective-permute-start | bytes 24584 | tf_op jit(solution)/shard_map/ppermute | solution.py:543
  42.5 3.1 %collective-permute-start.17 = (f32[16,128]{1,0:T(8,128)S(1)}, f32[16,128]{1,0:T(8,128)S(1)}, u32[]{:S(2)}, u32[]{:S(2)}) collective-permute-start(f32[16,128]{1,0:T(8,128)S(1)} %get-tuple-element.86.refs_16_), channel_id=1, source_target_pairs={{0,9},{1,8},{2,11},{3,10},{4,13},{5,12},{6,15},{7,14},{8,1},{9,0},... | collective-permute-start | bytes 24584 | tf_op jit(solution)/shard_map/ppermute | solution.py:543
  46.5 4.8 %collective-permute-start.22 = (f32[8,128]{1,0:T(8,128)S(1)}, f32[8,128]{1,0:T(8,128)S(1)}, u32[]{:S(2)}, u32[]{:S(2)}) collective-permute-start(f32[8,128]{1,0:T(8,128)S(1)} %get-tuple-element.88.refs_0_), channel_id=1, source_target_pairs={{0,7},{1,6},{2,5},{3,4},{4,3},{5,2},{6,1},{7,0},{8,15},{9,14},{10,... | collective-permute-start | bytes 12296 | tf_op jit(solution)/shard_map/ppermute | solution.py:543
  48.2 3.9 %collective-permute-start.21 = (f32[8,128]{1,0:T(8,128)S(1)}, f32[8,128]{1,0:T(8,128)S(1)}, u32[]{:S(2)}, u32[]{:S(2)}) collective-permute-start(f32[8,128]{1,0:T(8,128)S(1)} %get-tuple-element.88.refs_0_), channel_id=1, source_target_pairs={{0,5},{1,4},{2,7},{3,6},{4,1},{5,0},{6,3},{7,2},{8,13},{9,12},{10,... | collective-permute-start | bytes 12296 | tf_op jit(solution)/shard_map/ppermute | solution.py:543
  48.8 3.4 %collective-permute-start.20 = (f32[8,128]{1,0:T(8,128)S(1)}, f32[8,128]{1,0:T(8,128)S(1)}, u32[]{:S(2)}, u32[]{:S(2)}) collective-permute-start(f32[8,128]{1,0:T(8,128)S(1)} %get-tuple-element.88.refs_0_), channel_id=1, source_target_pairs={{0,3},{1,2},{2,1},{3,0},{4,7},{5,6},{6,5},{7,4},{8,11},{9,10},{10,... | collective-permute-start | bytes 12296 | tf_op jit(solution)/shard_map/ppermute | solution.py:543
  52.2 4.0 %collective-permute-start.25 = (f32[8,128]{1,0:T(8,128)S(1)}, f32[8,128]{1,0:T(8,128)S(1)}, u32[]{:S(2)}, u32[]{:S(2)}) collective-permute-start(f32[8,128]{1,0:T(8,128)S(1)} %sum.1.refs_0_), channel_id=1, source_target_pairs={{0,25},{1,24},{2,27},{3,26},{4,29},{5,28},{6,31},{7,30},{8,17},{9,... | collective-permute-start | bytes 12296 | tf_op jit(solution)/shard_map/ppermute | solution.py:543
  54.1 3.0 %collective-permute-start.24 = (f32[8,128]{1,0:T(8,128)S(1)}, f32[8,128]{1,0:T(8,128)S(1)}, u32[]{:S(2)}, u32[]{:S(2)}) collective-permute-start(f32[8,128]{1,0:T(8,128)S(1)} %sum.1.refs_0_), channel_id=1, source_target_pairs={{0,17},{1,16},{2,19},{3,18},{4,21},{5,20},{6,23},{7,22},{8,25},{9,... | collective-permute-start | bytes 12296 | tf_op jit(solution)/shard_map/ppermute | solution.py:543
  54.4 3.0 %collective-permute-start.23 = (f32[8,128]{1,0:T(8,128)S(1)}, f32[8,128]{1,0:T(8,128)S(1)}, u32[]{:S(2)}, u32[]{:S(2)}) collective-permute-start(f32[8,128]{1,0:T(8,128)S(1)} %sum.1.refs_0_), channel_id=1, source_target_pairs={{0,9},{1,8},{2,11},{3,10},{4,13},{5,12},{6,15},{7,14},{8,1},{9,0},... | collective-permute-start | bytes 12296 | tf_op jit(solution)/shard_map/ppermute | solution.py:543

commit v7 on v6

--- a/solution.py
+++ b/solution.py
@@ -533,15 +533,16 @@
 
 def exchange(value, axis):
     tm_count, star_count = lax.axis_size("tm"), lax.axis_size("star")
-    got = [value]
-    for gap in range(1, star_count if axis == "star" else tm_count // 2):
+    count = star_count if axis == "star" else tm_count // 2
+    got = {0: value}
+    for gap in range(count - 1, 0, -1) if axis == "tm" else range(1, count):
         steps = []
         for star in range(star_count):
             for tm in range(tm_count):
                 far = (star ^ gap, tm ^ 1) if axis == "star" else (star, tm ^ (2 * gap + 1))
                 steps.append((star * tm_count + tm, far[0] * tm_count + far[1]))
-        got.append(lax.ppermute(value, ("star", "tm"), steps))
-    return got
+        got[gap] = lax.ppermute(value, ("star", "tm"), steps)
+    return [got[gap] for gap in range(count)]
 
 
 def rows_type(rows):

time: 58.3 us -> 58.3 us (level)
  no operation moved by 1% of the time
where the time goes in v7:
time: 58.3 us; the launch traced here: 58.2 us
  starting transfers between devices  31.2 us (54%)
  Pallas kernels  13.6 us (23%)
  waiting for transfers between devices  12.6 us (22%)
  between operations  0.77 us (1%)
    ppermute x24, starting transfers between devices, exchange(): got[gap] = lax.ppermute(value, ('star', 'tm'), steps)  30.5 us
    pallas_call x15, Pallas kernels, call(): pl.pallas_call(kernel, name=name, out_shape=[jax.ShapeDtypeStruct(shape,...  13.6 us
    ppermute x24, waiting for transfers between devices, exchange(): got[gap] = lax.ppermute(value, ('star', 'tm'), steps)  12.6 us
  transfers between devices with their start and end apart: 26, of which 16 were waited for; matrix products, arithmetic and copies ran while one was open for 0% of the time, Pallas kernels for 12%

profile of v7, /device:TPU:0, one launch (start us, length us, event | category | flops | bytes accessed | tf_op | source)
XLA Modules:
  0.0 58.2 jit_solution(3999752522188545987)
XLA Ops:
  0.6 1.9 %first.1 = (f32[72,128]{1,0:T(8,128)S(1)}, f32[616,128]{1,0:T(8,128)S(1)}, bf16[128,6144]{1,0:T(8,128)(2,1)S(1)}, bf16[1024,128]{1,0:T(8,128)(2,1)S(1)}, s32[56,128]{1,0:T(8,128)S(1)}) custom-call(f32[8,128]{1,0:T(8,128)} %bitcast.12, f32[5,8,128]{2,1,0:T(8,128)} %bitcast.11, s32[8,128]{1,0:T(8,128)} %bitcast.13, f32[512,128]{1,0:T(8,128)} %bitcast.8, ...), custom_call_target="tpu_custom_call" | custom-call | tf_op jit(solution)/shard_map/first/pallas_call | solution.py:516
  2.6 4.6 %collective-permute-start.2 = (f32[72,128]{1,0:T(8,128)S(1)}, f32[72,128]{1,0:T(8,128)S(1)}, u32[]{:S(2)}, u32[]{:S(2)}) collective-permute-start(f32[72,128]{1,0:T(8,128)S(1)} %get-tuple-element.49.refs_0_), channel_id=1, source_target_pairs={{0,7},{1,6},{2,5},{3,4},{4,3},{5,2},{6,1},{7,0},{8,15},{9,14},{10,... | collective-permute-start | bytes 110600 | tf_op jit(solution)/shard_map/ppermute | solution.py:544
  7.1 0.9 %collective-permute-start = (f32[72,128]{1,0:T(8,128)S(1)}, f32[72,128]{1,0:T(8,128)S(1)}, u32[]{:S(2)}, u32[]{:S(2)}) collective-permute-start(f32[72,128]{1,0:T(8,128)S(1)} %get-tuple-element.49.refs_0_), channel_id=1, source_target_pairs={{0,3},{1,2},{2,1},{3,0},{4,7},{5,6},{6,5},{7,4},{8,11},{9,10},{10,... | collective-permute-start | bytes 110600 | tf_op jit(solution)/shard_map/ppermute | solution.py:544
  8.0 0.9 %collective-permute-done.2.refs_3_ = f32[72,128]{1,0:T(8,128)S(1)} collective-permute-done((f32[72,128]{1,0:T(8,128)S(1)}, f32[72,128]{1,0:T(8,128)S(1)}, u32[]{:S(2)}, u32[]{:S(2)}) %collective-permute-start.2) | collective-permute-done | bytes 36896 | tf_op jit(solution)/shard_map/ppermute | solution.py:544
  9.0 2.8 %collective-permute-done.1.refs_2_ = f32[72,128]{1,0:T(8,128)S(1)} collective-permute-done((f32[72,128]{1,0:T(8,128)S(1)}, f32[72,128]{1,0:T(8,128)S(1)}, u32[]{:S(2)}, u32[]{:S(2)}) %collective-permute-start.1) | collective-permute-done | bytes 36896 | tf_op jit(solution)/shard_map/ppermute | solution.py:544
  11.8 0.4 collective-permute-start.3
  12.2 1.4 %astro_own.1 = (f32[80,128]{1,0:T(8,128)S(1)}, bf16[128,4096]{1,0:T(8,128)(2,1)S(1)}) custom-call(f32[288,128]{1,0:T(8,128)S(1)} %chip.1.keep_ref.own_ref.refs_10_), custom_call_target="tpu_custom_call" | custom-call | tf_op jit(solution)/shard_map/astro_own/pallas_call | solution.py:516
  13.7 0.2 collective-permute-start.4
  13.9 2.4 %collective-permute-start.7 = (f32[16,128]{1,0:T(8,128)S(1)}, f32[16,128]{1,0:T(8,128)S(1)}, u32[]{:S(2)}, u32[]{:S(2)}) collective-permute-start(f32[16,128]{1,0:T(8,128)S(1)} %group.3.refs_12_), channel_id=1, source_target_pairs={{0,25},{1,24},{2,27},{3,26},{4,29},{5,28},{6,31},{7,30},{8,17},{9,... | collective-permute-start | bytes 24584 | tf_op jit(solution)/shard_map/ppermute | solution.py:544
  16.3 0.3 collective-permute-start.6
  16.6 0.5 collective-permute-start.5
  17.1 1.7 %astro.3 = (f32[80,128]{1,0:T(8,128)S(1)}, f32[16,128]{1,0:T(8,128)S(1)}, bf16[128,4096]{1,0:T(8,128)(2,1)S(1)}) custom-call(f32[288,128]{1,0:T(8,128)S(1)} %chip.1.keep_ref.own_ref.refs_10_, f32[288,128]{1,0:T(8,128)S(1)} %collective-permute-done.3.other_ref.keep_ref.refs_11_, f32[80,128]{1,0:T(8,128)S(1)} %get-tuple-element.60.part_ref), custom_call_target="tpu_custom_call" | custom-call | tf_op jit(solution)/shard_map/astro/pallas_call | solution.py:516
  18.8 0.5 prepare.1
  19.4 0.3 collective-permute-done.5.refs_13_
  19.7 1.4 %step.3 = (f32[32,128]{1,0:T(8,128)S(1)}, f32[16,128]{1,0:T(8,128)S(1)}, f32[96,128]{1,0:T(8,128)S(1)}, f32[96,128]{1,0:T(8,128)S(1)}, f32[16,128]{1,0:T(8,128)S...) custom-call(f32[616,128]{1,0:T(8,128)S(1)} %get-tuple-element.52.refs_0_, ...), custom_call_target="tpu_custom_call" | custom-call | tf_op jit(solution)/shard_map/step/pallas_call | solution.py:516
  21.1 2.0 %collective-permute-start.10 = (f32[32,128]{1,0:T(8,128)S(1)}, f32[32,128]{1,0:T(8,128)S(1)}, u32[]{:S(2)}, u32[]{:S(2)}) collective-permute-start(f32[32,128]{1,0:T(8,128)S(1)} %get-tuple-element.65.refs_0_), channel_id=1, source_target_pairs={{0,7},{1,6},{2,5},{3,4},{4,3},{5,2},{6,1},{7,0},{8,15},{9,14},{10,... | collective-permute-start | bytes 49160 | tf_op jit(solution)/shard_map/ppermute | solution.py:544
  23.1 0.5 collective-permute-start.9
  23.6 1.6 %collective-permute-start.8 = (f32[32,128]{1,0:T(8,128)S(1)}, f32[32,128]{1,0:T(8,128)S(1)}, u32[]{:S(2)}, u32[]{:S(2)}) collective-permute-start(f32[32,128]{1,0:T(8,128)S(1)} %get-tuple-element.65.refs_0_), channel_id=1, source_target_pairs={{0,3},{1,2},{2,1},{3,0},{4,7},{5,6},{6,5},{7,4},{8,11},{9,10},{10,... | collective-permute-start | bytes 49160 | tf_op jit(solution)/shard_map/ppermute | solution.py:544
  25.2 0.9 %collective-permute-done.10.refs_3_ = f32[32,128]{1,0:T(8,128)S(1)} collective-permute-done((f32[32,128]{1,0:T(8,128)S(1)}, f32[32,128]{1,0:T(8,128)S(1)}, u32[]{:S(2)}, u32[]{:S(2)}) %collective-permute-start.10) | collective-permute-done | bytes 16416 | tf_op jit(solution)/shard_map/ppermute | solution.py:544
  26.1 1.1 %collective-permute-done.9.refs_2_ = f32[32,128]{1,0:T(8,128)S(1)} collective-permute-done((f32[32,128]{1,0:T(8,128)S(1)}, f32[32,128]{1,0:T(8,128)S(1)}, u32[]{:S(2)}, u32[]{:S(2)}) %collective-permute-start.9) | collective-permute-done | bytes 16416 | tf_op jit(solution)/shard_map/ppermute | solution.py:544
  27.2 2.1 %collective-permute-start.13 = (f32[16,128]{1,0:T(8,128)S(1)}, f32[16,128]{1,0:T(8,128)S(1)}, u32[]{:S(2)}, u32[]{:S(2)}) collective-permute-start(f32[16,128]{1,0:T(8,128)S(1)} %get-tuple-element.75.refs_16_), channel_id=1, source_target_pairs={{0,25},{1,24},{2,27},{3,26},{4,29},{5,28},{6,31},{7,30},{8,17},{9,... | collective-permute-start | bytes 24584 | tf_op jit(solution)/shard_map/ppermute | solution.py:544
  29.4 0.4 collective-permute-start.12
  29.7 0.9 %collective-permute-start.11 = (f32[16,128]{1,0:T(8,128)S(1)}, f32[16,128]{1,0:T(8,128)S(1)}, u32[]{:S(2)}, u32[]{:S(2)}) collective-permute-start(f32[16,128]{1,0:T(8,128)S(1)} %get-tuple-element.75.refs_16_), channel_id=1, source_target_pairs={{0,9},{1,8},{2,11},{3,10},{4,13},{5,12},{6,15},{7,14},{8,1},{9,0},... | collective-permute-start | bytes 24584 | tf_op jit(solution)/shard_map/ppermute | solution.py:544
  30.6 1.8 %astro.4 = (f32[80,128]{1,0:T(8,128)S(1)}, f32[16,128]{1,0:T(8,128)S(1)}) custom-call(f32[288,128]{1,0:T(8,128)S(1)} %chip.1.keep_ref.own_ref.refs_10_, f32[288,128]{1,0:T(8,128)S(1)} %collective-permute-done.3.other_ref.keep_ref.refs_11_, bf16[128,4096]{1,0:T(8,128)(2,1)S(1)} %get-tuple-element.59.own_table, ...), custom_call_target="tpu_custom_call" | custom-call | tf_op jit(solution)/shard_map/astro/pallas_call | solution.py:516
  32.4 0.4 collective-permute-done.11.refs_17_
  32.8 1.4 %step.4 = (f32[32,128]{1,0:T(8,128)S(1)}, f32[16,128]{1,0:T(8,128)S(1)}, f32[96,128]{1,0:T(8,128)S(1)}, f32[96,128]{1,0:T(8,128)S(1)}, f32[16,128]{1,0:T(8,128)S...) custom-call(f32[616,128]{1,0:T(8,128)S(1)} %get-tuple-element.52.refs_0_, ...), custom_call_target="tpu_custom_call" | custom-call | tf_op jit(solution)/shard_map/step/pallas_call | solution.py:516
  34.2 1.9 %collective-permute-start.16 = (f32[32,128]{1,0:T(8,128)S(1)}, f32[32,128]{1,0:T(8,128)S(1)}, u32[]{:S(2)}, u32[]{:S(2)}) collective-permute-start(f32[32,128]{1,0:T(8,128)S(1)} %get-tuple-element.76.refs_0_), channel_id=1, source_target_pairs={{0,7},{1,6},{2,5},{3,4},{4,3},{5,2},{6,1},{7,0},{8,15},{9,14},{10,... | collective-permute-start | bytes 49160 | tf_op jit(solution)/shard_map/ppermute | solution.py:544
  36.1 0.5 collective-permute-start.15
  36.6 1.7 %collective-permute-start.14 = (f32[32,128]{1,0:T(8,128)S(1)}, f32[32,128]{1,0:T(8,128)S(1)}, u32[]{:S(2)}, u32[]{:S(2)}) collective-permute-start(f32[32,128]{1,0:T(8,128)S(1)} %get-tuple-element.76.refs_0_), channel_id=1, source_target_pairs={{0,3},{1,2},{2,1},{3,0},{4,7},{5,6},{6,5},{7,4},{8,11},{9,10},{10,... | collective-permute-start | bytes 49160 | tf_op jit(solution)/shard_map/ppermute | solution.py:544
  38.2 1.0 %collective-permute-done.16.refs_3_ = f32[32,128]{1,0:T(8,128)S(1)} collective-permute-done((f32[32,128]{1,0:T(8,128)S(1)}, f32[32,128]{1,0:T(8,128)S(1)}, u32[]{:S(2)}, u32[]{:S(2)}) %collective-permute-start.16) | collective-permute-done | bytes 16416 | tf_op jit(solution)/shard_map/ppermute | solution.py:544
  39.2 1.1 %collective-permute-done.15.refs_2_ = f32[32,128]{1,0:T(8,128)S(1)} collective-permute-done((f32[32,128]{1,0:T(8,128)S(1)}, f32[32,128]{1,0:T(8,128)S(1)}, u32[]{:S(2)}, u32[]{:S(2)}) %collective-permute-start.15) | collective-permute-done | bytes 16416 | tf_op jit(solution)/shard_map/ppermute | solution.py:544
  40.4 2.0 %collective-permute-start.19 = (f32[16,128]{1,0:T(8,128)S(1)}, f32[16,128]{1,0:T(8,128)S(1)}, u32[]{:S(2)}, u32[]{:S(2)}) collective-permute-start(f32[16,128]{1,0:T(8,128)S(1)} %get-tuple-element.86.refs_16_), channel_id=1, source_target_pairs={{0,25},{1,24},{2,27},{3,26},{4,29},{5,28},{6,31},{7,30},{8,17},{9,... | collective-permute-start | bytes 24584 | tf_op jit(solution)/shard_map/ppermute | solution.py:544
  42.5 0.9 %collective-permute-start.17 = (f32[16,128]{1,0:T(8,128)S(1)}, f32[16,128]{1,0:T(8,128)S(1)}, u32[]{:S(2)}, u32[]{:S(2)}) collective-permute-start(f32[16,128]{1,0:T(8,128)S(1)} %get-tuple-element.86.refs_16_), channel_id=1, source_target_pairs={{0,9},{1,8},{2,11},{3,10},{4,13},{5,12},{6,15},{7,14},{8,1},{9,0},... | collective-permute-start | bytes 24584 | tf_op jit(solution)/shard_map/ppermute | solution.py:544
  43.4 1.8 %astro.5 = (f32[80,128]{1,0:T(8,128)S(1)}, f32[16,128]{1,0:T(8,128)S(1)}) custom-call(f32[288,128]{1,0:T(8,128)S(1)} %chip.1.keep_ref.own_ref.refs_10_, f32[288,128]{1,0:T(8,128)S(1)} %collective-permute-done.3.other_ref.keep_ref.refs_11_, bf16[128,4096]{1,0:T(8,128)(2,1)S(1)} %get-tuple-element.59.own_table, ...), custom_call_target="tpu_custom_call" | custom-call | tf_op jit(solution)/shard_map/astro/pallas_call | solution.py:516
  45.2 0.3 collective-permute-done.18.refs_18_
  45.6 0.9 %step.5 = (f32[8,128]{1,0:T(8,128)S(1)}, f32[16,128]{1,0:T(8,128)S(1)}, f32[96,128]{1,0:T(8,128)S(1)}, f32[96,128]{1,0:T(8,128)}, f32[16,128]{1,0:T(8,128)}, /*index=5*/f32[16,128]{1,0:T(8,128)}, f32[16,128]{1,0:T(8,128)}) custom-call(f32[616,128]{1,0:T(8,128)S(1)} %get-tuple-element.52.refs_0_, f32[616,128]{1,0:T(8,128)S(1)} %collective-permute-done.4.pack_ref.refs_1_, ...), custom_call_target="tpu_custom_call" | custom-call | tf_op jit(solution)/shard_map/step/pallas_call | solution.py:516
  46.5 1.8 %collective-permute-start.22 = (f32[8,128]{1,0:T(8,128)S(1)}, f32[8,128]{1,0:T(8,128)S(1)}, u32[]{:S(2)}, u32[]{:S(2)}) collective-permute-start(f32[8,128]{1,0:T(8,128)S(1)} %get-tuple-element.88.refs_0_), channel_id=1, source_target_pairs={{0,7},{1,6},{2,5},{3,4},{4,3},{5,2},{6,1},{7,0},{8,15},{9,14},{10,... | collective-permute-start | bytes 12296 | tf_op jit(solution)/shard_map/ppermute | solution.py:544
  48.2 0.5 collective-permute-start.21
  48.8 1.8 %collective-permute-start.20 = (f32[8,128]{1,0:T(8,128)S(1)}, f32[8,128]{1,0:T(8,128)S(1)}, u32[]{:S(2)}, u32[]{:S(2)}) collective-permute-start(f32[8,128]{1,0:T(8,128)S(1)} %get-tuple-element.88.refs_0_), channel_id=1, source_target_pairs={{0,3},{1,2},{2,1},{3,0},{4,7},{5,6},{6,5},{7,4},{8,11},{9,10},{10,... | collective-permute-start | bytes 12296 | tf_op jit(solution)/shard_map/ppermute | solution.py:544
  50.5 0.8 %collective-permute-done.22.refs_3_ = f32[8,128]{1,0:T(8,128)S(1)} collective-permute-done((f32[8,128]{1,0:T(8,128)S(1)}, f32[8,128]{1,0:T(8,128)S(1)}, u32[]{:S(2)}, u32[]{:S(2)}) %collective-permute-start.22) | collective-permute-done | bytes 4128 | tf_op jit(solution)/shard_map/ppermute | solution.py:544
  51.3 0.9 %collective-permute-done.21.refs_2_ = f32[8,128]{1,0:T(8,128)S(1)} collective-permute-done((f32[8,128]{1,0:T(8,128)S(1)}, f32[8,128]{1,0:T(8,128)S(1)}, u32[]{:S(2)}, u32[]{:S(2)}) %collective-permute-start.21) | collective-permute-done | bytes 4128 | tf_op jit(solution)/shard_map/ppermute | solution.py:544
  52.2 1.8 %collective-permute-start.25 = (f32[8,128]{1,0:T(8,128)S(1)}, f32[8,128]{1,0:T(8,128)S(1)}, u32[]{:S(2)}, u32[]{:S(2)}) collective-permute-start(f32[8,128]{1,0:T(8,128)S(1)} %sum.1.refs_0_), channel_id=1, source_target_pairs={{0,25},{1,24},{2,27},{3,26},{4,29},{5,28},{6,31},{7,30},{8,17},{9,... | collective-permute-start | bytes 12296 | tf_op jit(solution)/shard_map/ppermute | solution.py:544
  54.1 0.3 collective-permute-start.24
  54.4 1.1 %collective-permute-start.23 = (f32[8,128]{1,0:T(8,128)S(1)}, f32[8,128]{1,0:T(8,128)S(1)}, u32[]{:S(2)}, u32[]{:S(2)}) collective-permute-start(f32[8,128]{1,0:T(8,128)S(1)} %sum.1.refs_0_), channel_id=1, source_target_pairs={{0,9},{1,8},{2,11},{3,10},{4,13},{5,12},{6,15},{7,14},{8,1},{9,0},... | collective-permute-start | bytes 12296 | tf_op jit(solution)/shard_map/ppermute | solution.py:544
  55.5 0.7 %collective-permute-done.25.refs_3_ = f32[8,128]{1,0:T(8,128)S(1)} collective-permute-done((f32[8,128]{1,0:T(8,128)S(1)}, f32[8,128]{1,0:T(8,128)S(1)}, u32[]{:S(2)}, u32[]{:S(2)}) %collective-permute-start.25) | collective-permute-done | bytes 4128 | tf_op jit(solution)/shard_map/ppermute | solution.py:544
  56.2 0.9 %collective-permute-done.24.refs_2_ = f32[8,128]{1,0:T(8,128)S(1)} collective-permute-done((f32[8,128]{1,0:T(8,128)S(1)}, f32[8,128]{1,0:T(8,128)S(1)}, u32[]{:S(2)}, u32[]{:S(2)}) %collective-permute-start.24) | collective-permute-done | bytes 4128 | tf_op jit(solution)/shard_map/ppermute | solution.py:544
  57.1 0.3 collective-permute-done.23.refs_1_
  57.4 0.7 %last.1 = (f32[5,256]{1,0:T(8,128)}, f32[2,128]{1,0:T(2,128)}, f32[8,128]{1,0:T(8,128)}) custom-call(f32[16,128]{1,0:T(8,128)S(1)} %get-tuple-element.87.state_ref, f32[8,128]{1,0:T(8,128)S(1)} %sum.1.refs_0_, f32[8,128]{1,0:T(8,128)S(1)} %collective-permute-done.23.refs_1_, f32[8,128]{1,0:T(8,128)S(1)} %collective-permute-done.24.refs_2_, ...), custom_call_target="tpu_custom_call" | custom-call | tf_op jit(solution)/shard_map/last/pallas_call | solution.py:516
  (19 shorter events, 0.6 us)
Async XLA Ops:
  2.6 6.4 %collective-permute-start.2 = (f32[72,128]{1,0:T(8,128)S(1)}, f32[72,128]{1,0:T(8,128)S(1)}, u32[]{:S(2)}, u32[]{:S(2)}) collective-permute-start(f32[72,128]{1,0:T(8,128)S(1)} %get-tuple-element.49.refs_0_), channel_id=1, source_target_pairs={{0,7},{1,6},{2,5},{3,4},{4,3},{5,2},{6,1},{7,0},{8,15},{9,14},{10,... | collective-permute-start | bytes 110600 | tf_op jit(solution)/shard_map/ppermute | solution.py:544
  7.1 4.6 %collective-permute-start.1 = (f32[72,128]{1,0:T(8,128)S(1)}, f32[72,128]{1,0:T(8,128)S(1)}, u32[]{:S(2)}, u32[]{:S(2)}) collective-permute-start(f32[72,128]{1,0:T(8,128)S(1)} %get-tuple-element.49.refs_0_), channel_id=1, source_target_pairs={{0,5},{1,4},{2,7},{3,6},{4,1},{5,0},{6,3},{7,2},{8,13},{9,12},{10,... | collective-permute-start | bytes 110600 | tf_op jit(solution)/shard_map/ppermute | solution.py:544
  7.1 4.6 %collective-permute-start = (f32[72,128]{1,0:T(8,128)S(1)}, f32[72,128]{1,0:T(8,128)S(1)}, u32[]{:S(2)}, u32[]{:S(2)}) collective-permute-start(f32[72,128]{1,0:T(8,128)S(1)} %get-tuple-element.49.refs_0_), channel_id=1, source_target_pairs={{0,3},{1,2},{2,1},{3,0},{4,7},{5,6},{6,5},{7,4},{8,11},{9,10},{10,... | collective-permute-start | bytes 110600 | tf_op jit(solution)/shard_map/ppermute | solution.py:544
  11.8 1.8 %collective-permute-start.3 = (f32[288,128]{1,0:T(8,128)S(1)}, f32[288,128]{1,0:T(8,128)S(1)}, u32[]{:S(2)}, u32[]{:S(2)}) collective-permute-start(f32[288,128]{1,0:T(8,128)S(1)} %chip.1.keep_ref.own_ref.refs_10_), channel_id=1, source_target_pairs={{0,1},{1,0},{2,3},{3,2},{4,5},{5,4},{6,7},{7,6},{8,9},{9,8},{10,11... | collective-permute-start | bytes 442376 | tf_op jit(solution)/shard_map/ppermute | solution.py:530
  13.7 5.1 %collective-permute-start.4 = (f32[616,128]{1,0:T(8,128)S(1)}, f32[616,128]{1,0:T(8,128)S(1)}, u32[]{:S(2)}, u32[]{:S(2)}) collective-permute-start(f32[616,128]{1,0:T(8,128)S(1)} %get-tuple-element.52.refs_0_), channel_id=1, source_target_pairs={{0,1},{1,0},{2,3},{3,2},{4,5},{5,4},{6,7},{7,6},{8,9},{9,8},{10,11... | collective-permute-start | bytes 946184 | tf_op jit(solution)/shard_map/ppermute | solution.py:530
  13.9 5.4 %collective-permute-start.7 = (f32[16,128]{1,0:T(8,128)S(1)}, f32[16,128]{1,0:T(8,128)S(1)}, u32[]{:S(2)}, u32[]{:S(2)}) collective-permute-start(f32[16,128]{1,0:T(8,128)S(1)} %group.3.refs_12_), channel_id=1, source_target_pairs={{0,25},{1,24},{2,27},{3,26},{4,29},{5,28},{6,31},{7,30},{8,17},{9,... | collective-permute-start | bytes 24584 | tf_op jit(solution)/shard_map/ppermute | solution.py:544
  16.3 3.1 %collective-permute-start.6 = (f32[16,128]{1,0:T(8,128)S(1)}, f32[16,128]{1,0:T(8,128)S(1)}, u32[]{:S(2)}, u32[]{:S(2)}) collective-permute-start(f32[16,128]{1,0:T(8,128)S(1)} %group.3.refs_12_), channel_id=1, source_target_pairs={{0,17},{1,16},{2,19},{3,18},{4,21},{5,20},{6,23},{7,22},{8,25},{9,... | collective-permute-start | bytes 24584 | tf_op jit(solution)/shard_map/ppermute | solution.py:544
  16.6 3.1 %collective-permute-start.5 = (f32[16,128]{1,0:T(8,128)S(1)}, f32[16,128]{1,0:T(8,128)S(1)}, u32[]{:S(2)}, u32[]{:S(2)}) collective-permute-start(f32[16,128]{1,0:T(8,128)S(1)} %group.3.refs_12_), channel_id=1, source_target_pairs={{0,9},{1,8},{2,11},{3,10},{4,13},{5,12},{6,15},{7,14},{8,1},{9,0},... | collective-permute-start | bytes 24584 | tf_op jit(solution)/shard_map/ppermute | solution.py:544
  21.1 5.0 %collective-permute-start.10 = (f32[32,128]{1,0:T(8,128)S(1)}, f32[32,128]{1,0:T(8,128)S(1)}, u32[]{:S(2)}, u32[]{:S(2)}) collective-permute-start(f32[32,128]{1,0:T(8,128)S(1)} %get-tuple-element.65.refs_0_), channel_id=1, source_target_pairs={{0,7},{1,6},{2,5},{3,4},{4,3},{5,2},{6,1},{7,0},{8,15},{9,14},{10,... | collective-permute-start | bytes 49160 | tf_op jit(solution)/shard_map/ppermute | solution.py:544
  23.1 4.1 %collective-permute-start.9 = (f32[32,128]{1,0:T(8,128)S(1)}, f32[32,128]{1,0:T(8,128)S(1)}, u32[]{:S(2)}, u32[]{:S(2)}) collective-permute-start(f32[32,128]{1,0:T(8,128)S(1)} %get-tuple-element.65.refs_0_), channel_id=1, source_target_pairs={{0,5},{1,4},{2,7},{3,6},{4,1},{5,0},{6,3},{7,2},{8,13},{9,12},{10,... | collective-permute-start | bytes 49160 | tf_op jit(solution)/shard_map/ppermute | solution.py:544
  23.6 3.6 %collective-permute-start.8 = (f32[32,128]{1,0:T(8,128)S(1)}, f32[32,128]{1,0:T(8,128)S(1)}, u32[]{:S(2)}, u32[]{:S(2)}) collective-permute-start(f32[32,128]{1,0:T(8,128)S(1)} %get-tuple-element.65.refs_0_), channel_id=1, source_target_pairs={{0,3},{1,2},{2,1},{3,0},{4,7},{5,6},{6,5},{7,4},{8,11},{9,10},{10,... | collective-permute-start | bytes 49160 | tf_op jit(solution)/shard_map/ppermute | solution.py:544
  27.2 5.2 %collective-permute-start.13 = (f32[16,128]{1,0:T(8,128)S(1)}, f32[16,128]{1,0:T(8,128)S(1)}, u32[]{:S(2)}, u32[]{:S(2)}) collective-permute-start(f32[16,128]{1,0:T(8,128)S(1)} %get-tuple-element.75.refs_16_), channel_id=1, source_target_pairs={{0,25},{1,24},{2,27},{3,26},{4,29},{5,28},{6,31},{7,30},{8,17},{9,... | collective-permute-start | bytes 24584 | tf_op jit(solution)/shard_map/ppermute | solution.py:544
  29.4 3.1 %collective-permute-start.12 = (f32[16,128]{1,0:T(8,128)S(1)}, f32[16,128]{1,0:T(8,128)S(1)}, u32[]{:S(2)}, u32[]{:S(2)}) collective-permute-start(f32[16,128]{1,0:T(8,128)S(1)} %get-tuple-element.75.refs_16_), channel_id=1, source_target_pairs={{0,17},{1,16},{2,19},{3,18},{4,21},{5,20},{6,23},{7,22},{8,25},{9,... | collective-permute-start | bytes 24584 | tf_op jit(solution)/shard_map/ppermute | solution.py:544
  29.7 3.1 %collective-permute-start.11 = (f32[16,128]{1,0:T(8,128)S(1)}, f32[16,128]{1,0:T(8,128)S(1)}, u32[]{:S(2)}, u32[]{:S(2)}) collective-permute-start(f32[16,128]{1,0:T(8,128)S(1)} %get-tuple-element.75.refs_16_), channel_id=1, source_target_pairs={{0,9},{1,8},{2,11},{3,10},{4,13},{5,12},{6,15},{7,14},{8,1},{9,0},... | collective-permute-start | bytes 24584 | tf_op jit(solution)/shard_map/ppermute | solution.py:544
  34.2 5.0 %collective-permute-start.16 = (f32[32,128]{1,0:T(8,128)S(1)}, f32[32,128]{1,0:T(8,128)S(1)}, u32[]{:S(2)}, u32[]{:S(2)}) collective-permute-start(f32[32,128]{1,0:T(8,128)S(1)} %get-tuple-element.76.refs_0_), channel_id=1, source_target_pairs={{0,7},{1,6},{2,5},{3,4},{4,3},{5,2},{6,1},{7,0},{8,15},{9,14},{10,... | collective-permute-start | bytes 49160 | tf_op jit(solution)/shard_map/ppermute | solution.py:544
  36.1 4.3 %collective-permute-start.15 = (f32[32,128]{1,0:T(8,128)S(1)}, f32[32,128]{1,0:T(8,128)S(1)}, u32[]{:S(2)}, u32[]{:S(2)}) collective-permute-start(f32[32,128]{1,0:T(8,128)S(1)} %get-tuple-element.76.refs_0_), channel_id=1, source_target_pairs={{0,5},{1,4},{2,7},{3,6},{4,1},{5,0},{6,3},{7,2},{8,13},{9,12},{10,... | collective-permute-start | bytes 49160 | tf_op jit(solution)/shard_map/ppermute | solution.py:544
  36.6 3.8 %collective-permute-start.14 = (f32[32,128]{1,0:T(8,128)S(1)}, f32[32,128]{1,0:T(8,128)S(1)}, u32[]{:S(2)}, u32[]{:S(2)}) collective-permute-start(f32[32,128]{1,0:T(8,128)S(1)} %get-tuple-element.76.refs_0_), channel_id=1, source_target_pairs={{0,3},{1,2},{2,1},{3,0},{4,7},{5,6},{6,5},{7,4},{8,11},{9,10},{10,... | collective-permute-start | bytes 49160 | tf_op jit(solution)/shard_map/ppermute | solution.py:544
  40.4 4.8 %collective-permute-start.19 = (f32[16,128]{1,0:T(8,128)S(1)}, f32[16,128]{1,0:T(8,128)S(1)}, u32[]{:S(2)}, u32[]{:S(2)}) collective-permute-start(f32[16,128]{1,0:T(8,128)S(1)} %get-tuple-element.86.refs_16_), channel_id=1, source_target_pairs={{0,25},{1,24},{2,27},{3,26},{4,29},{5,28},{6,31},{7,30},{8,17},{9,... | collective-permute-start | bytes 24584 | tf_op jit(solution)/shard_map/ppermute | solution.py:544
  42.3 3.1 %collective-permute-start.18 = (f32[16,128]{1,0:T(8,128)S(1)}, f32[16,128]{1,0:T(8,128)S(1)}, u32[]{:S(2)}, u32[]{:S(2)}) collective-permute-start(f32[16,128]{1,0:T(8,128)S(1)} %get-tuple-element.86.refs_16_), channel_id=1, source_target_pairs={{0,17},{1,16},{2,19},{3,18},{4,21},{5,20},{6,23},{7,22},{8,25},{9,... | collective-permute-start | bytes 24584 | tf_op jit(solution)/shard_map/ppermute | solution.py:544
  42.5 3.1 %collective-permute-start.17 = (f32[16,128]{1,0:T(8,128)S(1)}, f32[16,128]{1,0:T(8,128)S(1)}, u32[]{:S(2)}, u32[]{:S(2)}) collective-permute-start(f32[16,128]{1,0:T(8,128)S(1)} %get-tuple-element.86.refs_16_), channel_id=1, source_target_pairs={{0,9},{1,8},{2,11},{3,10},{4,13},{5,12},{6,15},{7,14},{8,1},{9,0},... | collective-permute-start | bytes 24584 | tf_op jit(solution)/shard_map/ppermute | solution.py:544
  46.5 4.8 %collective-permute-start.22 = (f32[8,128]{1,0:T(8,128)S(1)}, f32[8,128]{1,0:T(8,128)S(1)}, u32[]{:S(2)}, u32[]{:S(2)}) collective-permute-start(f32[8,128]{1,0:T(8,128)S(1)} %get-tuple-element.88.refs_0_), channel_id=1, source_target_pairs={{0,7},{1,6},{2,5},{3,4},{4,3},{5,2},{6,1},{7,0},{8,15},{9,14},{10,... | collective-permute-start | bytes 12296 | tf_op jit(solution)/shard_map/ppermute | solution.py:544
  48.2 3.9 %collective-permute-start.21 = (f32[8,128]{1,0:T(8,128)S(1)}, f32[8,128]{1,0:T(8,128)S(1)}, u32[]{:S(2)}, u32[]{:S(2)}) collective-permute-start(f32[8,128]{1,0:T(8,128)S(1)} %get-tuple-element.88.refs_0_), channel_id=1, source_target_pairs={{0,5},{1,4},{2,7},{3,6},{4,1},{5,0},{6,3},{7,2},{8,13},{9,12},{10,... | collective-permute-start | bytes 12296 | tf_op jit(solution)/shard_map/ppermute | solution.py:544
  48.8 3.4 %collective-permute-start.20 = (f32[8,128]{1,0:T(8,128)S(1)}, f32[8,128]{1,0:T(8,128)S(1)}, u32[]{:S(2)}, u32[]{:S(2)}) collective-permute-start(f32[8,128]{1,0:T(8,128)S(1)} %get-tuple-element.88.refs_0_), channel_id=1, source_target_pairs={{0,3},{1,2},{2,1},{3,0},{4,7},{5,6},{6,5},{7,4},{8,11},{9,10},{10,... | collective-permute-start | bytes 12296 | tf_op jit(solution)/shard_map/ppermute | solution.py:544
  52.2 4.0 %collective-permute-start.25 = (f32[8,128]{1,0:T(8,128)S(1)}, f32[8,128]{1,0:T(8,128)S(1)}, u32[]{:S(2)}, u32[]{:S(2)}) collective-permute-start(f32[8,128]{1,0:T(8,128)S(1)} %sum.1.refs_0_), channel_id=1, source_target_pairs={{0,25},{1,24},{2,27},{3,26},{4,29},{5,28},{6,31},{7,30},{8,17},{9,... | collective-permute-start | bytes 12296 | tf_op jit(solution)/shard_map/ppermute | solution.py:544
  54.1 3.0 %collective-permute-start.24 = (f32[8,128]{1,0:T(8,128)S(1)}, f32[8,128]{1,0:T(8,128)S(1)}, u32[]{:S(2)}, u32[]{:S(2)}) collective-permute-start(f32[8,128]{1,0:T(8,128)S(1)} %sum.1.refs_0_), channel_id=1, source_target_pairs={{0,17},{1,16},{2,19},{3,18},{4,21},{5,20},{6,23},{7,22},{8,25},{9,... | collective-permute-start | bytes 12296 | tf_op jit(solution)/shard_map/ppermute | solution.py:544
  54.4 3.0 %collective-permute-start.23 = (f32[8,128]{1,0:T(8,128)S(1)}, f32[8,128]{1,0:T(8,128)S(1)}, u32[]{:S(2)}, u32[]{:S(2)}) collective-permute-start(f32[8,128]{1,0:T(8,128)S(1)} %sum.1.refs_0_), channel_id=1, source_target_pairs={{0,9},{1,8},{2,11},{3,10},{4,13},{5,12},{6,15},{7,14},{8,1},{9,0},... | collective-permute-start | bytes 12296 | tf_op jit(solution)/shard_map/ppermute | solution.py:544

commit v8 on v6

--- a/solution.py
+++ b/solution.py
@@ -68,18 +68,21 @@
     return [row == tile * per_tile + lane // width for tile in range(tiles)], row, lane
 
 
-def inst_back(rows, coef_ref, index_ref, table_ref, spread_ref):
+def inst_back(rows, coef_ref, index_ref, table_ref):
     slots, blocks = len(coef_ref), rows.shape[0]
     count = NINST // LANES
+    long = blocks * LANES
+    both = jnp.zeros((2 * count, LANES), f32)
     for slot in range(slots):
         top, rest = halves(coef_ref[slot][...] * rows)
         index = index_ref[slot][...]
+        wide = []
         for block in range(blocks):
             here = slice(block, block + 1)
             pieces = [spread_high(index[here], part[here], count) for part in (top, rest)]
-            at = (slot * blocks + block) * LANES
-            spread_ref[:, at : at + LANES] = jnp.concatenate(pieces, axis=0).astype(bf16)
-    both = dot_lanes(spread_ref[...], table_ref[...])
+            wide.append(jnp.concatenate(pieces, axis=0).astype(bf16))
+        table = table_ref[:, slot * long : (slot + 1) * long]
+        both = both + dot_lanes(jnp.concatenate(wide, axis=1), table)
     return both[:count] + both[count:]
 
 
@@ -143,7 +146,7 @@
 def first_kernel(width, b_hbm, astro_hbm, star_hbm, att_hbm, starts_hbm, coef_hbm, index_hbm,
                  send_ref, pack_ref, table_ref, att2_ref, ints_ref,
                  b_ref, astro_ref, star_ref, starts_ref, coef_ref, index_ref,
-                 spread_ref, sems):
+                 sems):
     slots, blocks, _ = index_ref.shape
     comps = astro_ref.shape[0]
     places = pack_places(slots, blocks, width)
@@ -177,7 +180,7 @@
     for slot in range(slots):
         pack_ref[slot * 8 : slot * 8 + 8] = coef_ref[slot]
     send_ref[0:8] = rows
-    send_ref[8:16] = inst_back(rows, coefs, indices, table_ref, spread_ref)
+    send_ref[8:16] = inst_back(rows, coefs, indices, table_ref)
     send_ref[16:19] = att_back(rows, att2_ref[...], starts, width)
     send_ref[19:20] = jnp.sum(rows * rows, axis=0, keepdims=True)
     send_ref[20:24] = jnp.zeros((4, LANES), f32)
@@ -384,8 +387,8 @@
         refs = refs[6:]
     else:
         keep, refs = refs[:2], refs[2:]
-    gathered, refs = refs[:-8], refs[-8:]
-    send_ref, state_out, z_ref, g_ref, u_ref, s_ref, gs_ref, spread_ref = refs
+    gathered, refs = refs[:-7], refs[-7:]
+    send_ref, state_out, z_ref, g_ref, u_ref, s_ref, gs_ref = refs
     me = lax.axis_index("tm")
     chip, core = me // 2, me % 2
     high = STARS_DEV // LANES
@@ -444,9 +447,7 @@
     insts, atts = [], []
     for half in range(2):
         if step < ITERS - 1:
-            insts.append(
-                inst_back(rows[half], coefs[half], indices[half], tables[half], spread_ref.at[half])
-            )
+            insts.append(inst_back(rows[half], coefs[half], indices[half], tables[half]))
             atts.append(att_back(rows[half], att2s[half][...], starts[half], width))
 
     def squared(value):
@@ -567,7 +568,6 @@
     ]
     long = slots * blocks * height
     extra = 8 * comps + 8
-    spread = pltpu.VMEM((16, long), bf16)
     prepared = [((LANES, long), bf16), ((2 * blocks * width, height), bf16),
                 ((8 * slots + 8, LANES), jnp.int32)]
     here = [pltpu.with_memory_space_constraint(arg, pltpu.HBM) for arg in args]
@@ -577,7 +577,7 @@
         [((24 + extra, LANES), f32), ((16 * slots + 8 + blocks * width, LANES), f32)] + prepared,
         here,
         [pltpu.VMEM(arg.shape, arg.dtype) for arg in args if arg is not args[3]]
-        + [spread, pltpu.SemaphoreType.DMA((len(args),))],
+        + [pltpu.SemaphoreType.DMA((len(args),))],
         pl.ANY,
     )
     state = z = g = u = rows = gs = None
@@ -649,7 +649,6 @@
             [rows_type(32 if step < ITERS - 1 else 8), group_type, tall, tall, pair, pair,
              pair],
             basics + [sums, ya] + older + across,
-            [pltpu.VMEM((2, 16, long), bf16)],
         )
         solutions.append(z)
     (send,) = call(sum_kernel, "sum", [rows_type(8)], exchange(send, "tm"))

time: 58.3 us -> 58.4 us (level)
  transfers between devices with their start and end apart: 26 -> 26, of which waited for: 16 -> 15; matrix products, arithmetic and copies ran while one was open for 0% -> 0% of each run, Pallas kernels for 12% -> 12%
where the time goes in v8:
time: 58.4 us; the launch traced here: 58.3 us
  starting transfers between devices  31.1 us (53%)
  Pallas kernels  13.6 us (23%)
  waiting for transfers between devices  12.8 us (22%)
  between operations  0.79 us (1%)
    ppermute x24, starting transfers between devices, exchange(): got.append(lax.ppermute(value, ('star', 'tm'), steps))  30.4 us
    pallas_call x15, Pallas kernels, call(): pl.pallas_call(kernel, name=name, out_shape=[jax.ShapeDtypeStruct(shape,...  13.6 us
    ppermute x24, waiting for transfers between devices, exchange(): got.append(lax.ppermute(value, ('star', 'tm'), steps))  12.8 us
  transfers between devices with their start and end apart: 26, of which 15 were waited for; matrix products, arithmetic and copies ran while one was open for 0% of the time, Pallas kernels for 12%

profile of v8, /device:TPU:0, one launch (start us, length us, event | category | flops | bytes accessed | tf_op | source)
XLA Modules:
  0.0 58.3 jit_solution(17812381211007233274)
XLA Ops:
  0.6 1.9 %first.1 = (f32[72,128]{1,0:T(8,128)S(1)}, f32[616,128]{1,0:T(8,128)S(1)}, bf16[128,6144]{1,0:T(8,128)(2,1)S(1)}, bf16[1024,128]{1,0:T(8,128)(2,1)S(1)}, s32[56,128]{1,0:T(8,128)S(1)}) custom-call(f32[8,128]{1,0:T(8,128)} %bitcast.12, f32[5,8,128]{2,1,0:T(8,128)} %bitcast.11, s32[8,128]{1,0:T(8,128)} %bitcast.13, f32[512,128]{1,0:T(8,128)} %bitcast.8, ...), custom_call_target="tpu_custom_call" | custom-call | tf_op jit(solution)/shard_map/first/pallas_call | solution.py:517
  2.6 4.6 %collective-permute-start.2 = (f32[72,128]{1,0:T(8,128)S(1)}, f32[72,128]{1,0:T(8,128)S(1)}, u32[]{:S(2)}, u32[]{:S(2)}) collective-permute-start(f32[72,128]{1,0:T(8,128)S(1)} %get-tuple-element.49.refs_0_), channel_id=1, source_target_pairs={{0,7},{1,6},{2,5},{3,4},{4,3},{5,2},{6,1},{7,0},{8,15},{9,14},{10,... | collective-permute-start | bytes 110600 | tf_op jit(solution)/shard_map/ppermute | solution.py:544
  7.1 0.9 %collective-permute-start = (f32[72,128]{1,0:T(8,128)S(1)}, f32[72,128]{1,0:T(8,128)S(1)}, u32[]{:S(2)}, u32[]{:S(2)}) collective-permute-start(f32[72,128]{1,0:T(8,128)S(1)} %get-tuple-element.49.refs_0_), channel_id=1, source_target_pairs={{0,3},{1,2},{2,1},{3,0},{4,7},{5,6},{6,5},{7,4},{8,11},{9,10},{10,... | collective-permute-start | bytes 110600 | tf_op jit(solution)/shard_map/ppermute | solution.py:544
  8.0 0.9 %collective-permute-done.2.refs_3_ = f32[72,128]{1,0:T(8,128)S(1)} collective-permute-done((f32[72,128]{1,0:T(8,128)S(1)}, f32[72,128]{1,0:T(8,128)S(1)}, u32[]{:S(2)}, u32[]{:S(2)}) %collective-permute-start.2) | collective-permute-done | bytes 36896 | tf_op jit(solution)/shard_map/ppermute | solution.py:544
  9.0 2.8 %collective-permute-done.1.refs_2_ = f32[72,128]{1,0:T(8,128)S(1)} collective-permute-done((f32[72,128]{1,0:T(8,128)S(1)}, f32[72,128]{1,0:T(8,128)S(1)}, u32[]{:S(2)}, u32[]{:S(2)}) %collective-permute-start.1) | collective-permute-done | bytes 36896 | tf_op jit(solution)/shard_map/ppermute | solution.py:544
  11.8 0.4 collective-permute-start.3
  12.2 1.4 %astro_own.1 = (f32[80,128]{1,0:T(8,128)S(1)}, bf16[128,4096]{1,0:T(8,128)(2,1)S(1)}) custom-call(f32[288,128]{1,0:T(8,128)S(1)} %chip.1.keep_ref.own_ref.refs_10_), custom_call_target="tpu_custom_call" | custom-call | tf_op jit(solution)/shard_map/astro_own/pallas_call | solution.py:517
  13.7 0.2 collective-permute-start.4
  13.9 2.4 %collective-permute-start.7 = (f32[16,128]{1,0:T(8,128)S(1)}, f32[16,128]{1,0:T(8,128)S(1)}, u32[]{:S(2)}, u32[]{:S(2)}) collective-permute-start(f32[16,128]{1,0:T(8,128)S(1)} %group.3.refs_12_), channel_id=1, source_target_pairs={{0,25},{1,24},{2,27},{3,26},{4,29},{5,28},{6,31},{7,30},{8,17},{9,... | collective-permute-start | bytes 24584 | tf_op jit(solution)/shard_map/ppermute | solution.py:544
  16.3 0.3 collective-permute-start.6
  16.6 0.5 collective-permute-start.5
  17.1 1.7 %astro.3 = (f32[80,128]{1,0:T(8,128)S(1)}, f32[16,128]{1,0:T(8,128)S(1)}, bf16[128,4096]{1,0:T(8,128)(2,1)S(1)}) custom-call(f32[288,128]{1,0:T(8,128)S(1)} %chip.1.keep_ref.own_ref.refs_10_, f32[288,128]{1,0:T(8,128)S(1)} %collective-permute-done.3.other_ref.keep_ref.refs_11_, f32[80,128]{1,0:T(8,128)S(1)} %get-tuple-element.60.part_ref), custom_call_target="tpu_custom_call" | custom-call | tf_op jit(solution)/shard_map/astro/pallas_call | solution.py:517
  18.8 0.5 prepare.1
  19.4 0.3 collective-permute-done.5.refs_13_
  19.7 1.4 %step.3 = (f32[32,128]{1,0:T(8,128)S(1)}, f32[16,128]{1,0:T(8,128)S(1)}, f32[96,128]{1,0:T(8,128)S(1)}, f32[96,128]{1,0:T(8,128)S(1)}, f32[16,128]{1,0:T(8,128)S...) custom-call(f32[616,128]{1,0:T(8,128)S(1)} %get-tuple-element.52.refs_0_, ...), custom_call_target="tpu_custom_call" | custom-call | tf_op jit(solution)/shard_map/step/pallas_call | solution.py:517
  21.0 2.0 %collective-permute-start.10 = (f32[32,128]{1,0:T(8,128)S(1)}, f32[32,128]{1,0:T(8,128)S(1)}, u32[]{:S(2)}, u32[]{:S(2)}) collective-permute-start(f32[32,128]{1,0:T(8,128)S(1)} %get-tuple-element.65.refs_0_), channel_id=1, source_target_pairs={{0,7},{1,6},{2,5},{3,4},{4,3},{5,2},{6,1},{7,0},{8,15},{9,14},{10,... | collective-permute-start | bytes 49160 | tf_op jit(solution)/shard_map/ppermute | solution.py:544
  23.1 0.5 collective-permute-start.9
  23.5 1.6 %collective-permute-start.8 = (f32[32,128]{1,0:T(8,128)S(1)}, f32[32,128]{1,0:T(8,128)S(1)}, u32[]{:S(2)}, u32[]{:S(2)}) collective-permute-start(f32[32,128]{1,0:T(8,128)S(1)} %get-tuple-element.65.refs_0_), channel_id=1, source_target_pairs={{0,3},{1,2},{2,1},{3,0},{4,7},{5,6},{6,5},{7,4},{8,11},{9,10},{10,... | collective-permute-start | bytes 49160 | tf_op jit(solution)/shard_map/ppermute | solution.py:544
  25.1 0.9 %collective-permute-done.10.refs_3_ = f32[32,128]{1,0:T(8,128)S(1)} collective-permute-done((f32[32,128]{1,0:T(8,128)S(1)}, f32[32,128]{1,0:T(8,128)S(1)}, u32[]{:S(2)}, u32[]{:S(2)}) %collective-permute-start.10) | collective-permute-done | bytes 16416 | tf_op jit(solution)/shard_map/ppermute | solution.py:544
  26.1 1.1 %collective-permute-done.9.refs_2_ = f32[32,128]{1,0:T(8,128)S(1)} collective-permute-done((f32[32,128]{1,0:T(8,128)S(1)}, f32[32,128]{1,0:T(8,128)S(1)}, u32[]{:S(2)}, u32[]{:S(2)}) %collective-permute-start.9) | collective-permute-done | bytes 16416 | tf_op jit(solution)/shard_map/ppermute | solution.py:544
  27.2 2.1 %collective-permute-start.13 = (f32[16,128]{1,0:T(8,128)S(1)}, f32[16,128]{1,0:T(8,128)S(1)}, u32[]{:S(2)}, u32[]{:S(2)}) collective-permute-start(f32[16,128]{1,0:T(8,128)S(1)} %get-tuple-element.75.refs_16_), channel_id=1, source_target_pairs={{0,25},{1,24},{2,27},{3,26},{4,29},{5,28},{6,31},{7,30},{8,17},{9,... | collective-permute-start | bytes 24584 | tf_op jit(solution)/shard_map/ppermute | solution.py:544
  29.3 0.5 collective-permute-start.12
  29.8 0.8 %collective-permute-start.11 = (f32[16,128]{1,0:T(8,128)S(1)}, f32[16,128]{1,0:T(8,128)S(1)}, u32[]{:S(2)}, u32[]{:S(2)}) collective-permute-start(f32[16,128]{1,0:T(8,128)S(1)} %get-tuple-element.75.refs_16_), channel_id=1, source_target_pairs={{0,9},{1,8},{2,11},{3,10},{4,13},{5,12},{6,15},{7,14},{8,1},{9,0},... | collective-permute-start | bytes 24584 | tf_op jit(solution)/shard_map/ppermute | solution.py:544
  30.6 1.8 %astro.4 = (f32[80,128]{1,0:T(8,128)S(1)}, f32[16,128]{1,0:T(8,128)S(1)}) custom-call(f32[288,128]{1,0:T(8,128)S(1)} %chip.1.keep_ref.own_ref.refs_10_, f32[288,128]{1,0:T(8,128)S(1)} %collective-permute-done.3.other_ref.keep_ref.refs_11_, bf16[128,4096]{1,0:T(8,128)(2,1)S(1)} %get-tuple-element.59.own_table, ...), custom_call_target="tpu_custom_call" | custom-call | tf_op jit(solution)/shard_map/astro/pallas_call | solution.py:517
  32.4 0.5 collective-permute-done.11.refs_17_
  32.9 1.4 %step.4 = (f32[32,128]{1,0:T(8,128)S(1)}, f32[16,128]{1,0:T(8,128)S(1)}, f32[96,128]{1,0:T(8,128)S(1)}, f32[96,128]{1,0:T(8,128)S(1)}, f32[16,128]{1,0:T(8,128)S...) custom-call(f32[616,128]{1,0:T(8,128)S(1)} %get-tuple-element.52.refs_0_, ...), custom_call_target="tpu_custom_call" | custom-call | tf_op jit(solution)/shard_map/step/pallas_call | solution.py:517
  34.3 1.8 %collective-permute-start.16 = (f32[32,128]{1,0:T(8,128)S(1)}, f32[32,128]{1,0:T(8,128)S(1)}, u32[]{:S(2)}, u32[]{:S(2)}) collective-permute-start(f32[32,128]{1,0:T(8,128)S(1)} %get-tuple-element.76.refs_0_), channel_id=1, source_target_pairs={{0,7},{1,6},{2,5},{3,4},{4,3},{5,2},{6,1},{7,0},{8,15},{9,14},{10,... | collective-permute-start | bytes 49160 | tf_op jit(solution)/shard_map/ppermute | solution.py:544
  36.1 0.4 collective-permute-start.15
  36.5 1.7 %collective-permute-start.14 = (f32[32,128]{1,0:T(8,128)S(1)}, f32[32,128]{1,0:T(8,128)S(1)}, u32[]{:S(2)}, u32[]{:S(2)}) collective-permute-start(f32[32,128]{1,0:T(8,128)S(1)} %get-tuple-element.76.refs_0_), channel_id=1, source_target_pairs={{0,3},{1,2},{2,1},{3,0},{4,7},{5,6},{6,5},{7,4},{8,11},{9,10},{10,... | collective-permute-start | bytes 49160 | tf_op jit(solution)/shard_map/ppermute | solution.py:544
  38.3 1.1 %collective-permute-done.16.refs_3_ = f32[32,128]{1,0:T(8,128)S(1)} collective-permute-done((f32[32,128]{1,0:T(8,128)S(1)}, f32[32,128]{1,0:T(8,128)S(1)}, u32[]{:S(2)}, u32[]{:S(2)}) %collective-permute-start.16) | collective-permute-done | bytes 16416 | tf_op jit(solution)/shard_map/ppermute | solution.py:544
  39.3 1.0 %collective-permute-done.15.refs_2_ = f32[32,128]{1,0:T(8,128)S(1)} collective-permute-done((f32[32,128]{1,0:T(8,128)S(1)}, f32[32,128]{1,0:T(8,128)S(1)}, u32[]{:S(2)}, u32[]{:S(2)}) %collective-permute-start.15) | collective-permute-done | bytes 16416 | tf_op jit(solution)/shard_map/ppermute | solution.py:544
  40.4 1.8 %collective-permute-start.19 = (f32[16,128]{1,0:T(8,128)S(1)}, f32[16,128]{1,0:T(8,128)S(1)}, u32[]{:S(2)}, u32[]{:S(2)}) collective-permute-start(f32[16,128]{1,0:T(8,128)S(1)} %get-tuple-element.86.refs_16_), channel_id=1, source_target_pairs={{0,25},{1,24},{2,27},{3,26},{4,29},{5,28},{6,31},{7,30},{8,17},{9,... | collective-permute-start | bytes 24584 | tf_op jit(solution)/shard_map/ppermute | solution.py:544
  42.2 0.2 collective-permute-start.18
  42.4 1.1 %collective-permute-start.17 = (f32[16,128]{1,0:T(8,128)S(1)}, f32[16,128]{1,0:T(8,128)S(1)}, u32[]{:S(2)}, u32[]{:S(2)}) collective-permute-start(f32[16,128]{1,0:T(8,128)S(1)} %get-tuple-element.86.refs_16_), channel_id=1, source_target_pairs={{0,9},{1,8},{2,11},{3,10},{4,13},{5,12},{6,15},{7,14},{8,1},{9,0},... | collective-permute-start | bytes 24584 | tf_op jit(solution)/shard_map/ppermute | solution.py:544
  43.5 1.8 %astro.5 = (f32[80,128]{1,0:T(8,128)S(1)}, f32[16,128]{1,0:T(8,128)S(1)}) custom-call(f32[288,128]{1,0:T(8,128)S(1)} %chip.1.keep_ref.own_ref.refs_10_, f32[288,128]{1,0:T(8,128)S(1)} %collective-permute-done.3.other_ref.keep_ref.refs_11_, bf16[128,4096]{1,0:T(8,128)(2,1)S(1)} %get-tuple-element.59.own_table, ...), custom_call_target="tpu_custom_call" | custom-call | tf_op jit(solution)/shard_map/astro/pallas_call | solution.py:517
  45.5 0.9 %step.5 = (f32[8,128]{1,0:T(8,128)S(1)}, f32[16,128]{1,0:T(8,128)S(1)}, f32[96,128]{1,0:T(8,128)S(1)}, f32[96,128]{1,0:T(8,128)}, f32[16,128]{1,0:T(8,128)}, /*index=5*/f32[16,128]{1,0:T(8,128)}, f32[16,128]{1,0:T(8,128)}) custom-call(f32[616,128]{1,0:T(8,128)S(1)} %get-tuple-element.52.refs_0_, f32[616,128]{1,0:T(8,128)S(1)} %collective-permute-done.4.pack_ref.refs_1_, ...), custom_call_target="tpu_custom_call" | custom-call | tf_op jit(solution)/shard_map/step/pallas_call | solution.py:517
  46.4 1.8 %collective-permute-start.22 = (f32[8,128]{1,0:T(8,128)S(1)}, f32[8,128]{1,0:T(8,128)S(1)}, u32[]{:S(2)}, u32[]{:S(2)}) collective-permute-start(f32[8,128]{1,0:T(8,128)S(1)} %get-tuple-element.88.refs_0_), channel_id=1, source_target_pairs={{0,7},{1,6},{2,5},{3,4},{4,3},{5,2},{6,1},{7,0},{8,15},{9,14},{10,... | collective-permute-start | bytes 12296 | tf_op jit(solution)/shard_map/ppermute | solution.py:544
  48.2 0.6 collective-permute-start.21
  48.8 1.7 %collective-permute-start.20 = (f32[8,128]{1,0:T(8,128)S(1)}, f32[8,128]{1,0:T(8,128)S(1)}, u32[]{:S(2)}, u32[]{:S(2)}) collective-permute-start(f32[8,128]{1,0:T(8,128)S(1)} %get-tuple-element.88.refs_0_), channel_id=1, source_target_pairs={{0,3},{1,2},{2,1},{3,0},{4,7},{5,6},{6,5},{7,4},{8,11},{9,10},{10,... | collective-permute-start | bytes 12296 | tf_op jit(solution)/shard_map/ppermute | solution.py:544
  50.5 0.8 %collective-permute-done.22.refs_3_ = f32[8,128]{1,0:T(8,128)S(1)} collective-permute-done((f32[8,128]{1,0:T(8,128)S(1)}, f32[8,128]{1,0:T(8,128)S(1)}, u32[]{:S(2)}, u32[]{:S(2)}) %collective-permute-start.22) | collective-permute-done | bytes 4128 | tf_op jit(solution)/shard_map/ppermute | solution.py:544
  51.2 0.9 %collective-permute-done.21.refs_2_ = f32[8,128]{1,0:T(8,128)S(1)} collective-permute-done((f32[8,128]{1,0:T(8,128)S(1)}, f32[8,128]{1,0:T(8,128)S(1)}, u32[]{:S(2)}, u32[]{:S(2)}) %collective-permute-start.21) | collective-permute-done | bytes 4128 | tf_op jit(solution)/shard_map/ppermute | solution.py:544
  52.2 1.8 %collective-permute-start.25 = (f32[8,128]{1,0:T(8,128)S(1)}, f32[8,128]{1,0:T(8,128)S(1)}, u32[]{:S(2)}, u32[]{:S(2)}) collective-permute-start(f32[8,128]{1,0:T(8,128)S(1)} %sum.1.refs_0_), channel_id=1, source_target_pairs={{0,25},{1,24},{2,27},{3,26},{4,29},{5,28},{6,31},{7,30},{8,17},{9,... | collective-permute-start | bytes 12296 | tf_op jit(solution)/shard_map/ppermute | solution.py:544
  54.0 0.5 collective-permute-start.24
  54.5 0.9 %collective-permute-start.23 = (f32[8,128]{1,0:T(8,128)S(1)}, f32[8,128]{1,0:T(8,128)S(1)}, u32[]{:S(2)}, u32[]{:S(2)}) collective-permute-start(f32[8,128]{1,0:T(8,128)S(1)} %sum.1.refs_0_), channel_id=1, source_target_pairs={{0,9},{1,8},{2,11},{3,10},{4,13},{5,12},{6,15},{7,14},{8,1},{9,0},... | collective-permute-start | bytes 12296 | tf_op jit(solution)/shard_map/ppermute | solution.py:544
  55.4 0.8 %collective-permute-done.25.refs_3_ = f32[8,128]{1,0:T(8,128)S(1)} collective-permute-done((f32[8,128]{1,0:T(8,128)S(1)}, f32[8,128]{1,0:T(8,128)S(1)}, u32[]{:S(2)}, u32[]{:S(2)}) %collective-permute-start.25) | collective-permute-done | bytes 4128 | tf_op jit(solution)/shard_map/ppermute | solution.py:544
  56.2 0.9 %collective-permute-done.24.refs_2_ = f32[8,128]{1,0:T(8,128)S(1)} collective-permute-done((f32[8,128]{1,0:T(8,128)S(1)}, f32[8,128]{1,0:T(8,128)S(1)}, u32[]{:S(2)}, u32[]{:S(2)}) %collective-permute-start.24) | collective-permute-done | bytes 4128 | tf_op jit(solution)/shard_map/ppermute | solution.py:544
  57.0 0.5 collective-permute-done.23.refs_1_
  57.5 0.7 %last.1 = (f32[5,256]{1,0:T(8,128)}, f32[2,128]{1,0:T(2,128)}, f32[8,128]{1,0:T(8,128)}) custom-call(f32[16,128]{1,0:T(8,128)S(1)} %get-tuple-element.87.state_ref, f32[8,128]{1,0:T(8,128)S(1)} %sum.1.refs_0_, f32[8,128]{1,0:T(8,128)S(1)} %collective-permute-done.23.refs_1_, f32[8,128]{1,0:T(8,128)S(1)} %collective-permute-done.24.refs_2_, ...), custom_call_target="tpu_custom_call" | custom-call | tf_op jit(solution)/shard_map/last/pallas_call | solution.py:517
  (19 shorter events, 0.4 us)
Async XLA Ops:
  2.6 6.4 %collective-permute-start.2 = (f32[72,128]{1,0:T(8,128)S(1)}, f32[72,128]{1,0:T(8,128)S(1)}, u32[]{:S(2)}, u32[]{:S(2)}) collective-permute-start(f32[72,128]{1,0:T(8,128)S(1)} %get-tuple-element.49.refs_0_), channel_id=1, source_target_pairs={{0,7},{1,6},{2,5},{3,4},{4,3},{5,2},{6,1},{7,0},{8,15},{9,14},{10,... | collective-permute-start | bytes 110600 | tf_op jit(solution)/shard_map/ppermute | solution.py:544
  7.1 4.6 %collective-permute-start.1 = (f32[72,128]{1,0:T(8,128)S(1)}, f32[72,128]{1,0:T(8,128)S(1)}, u32[]{:S(2)}, u32[]{:S(2)}) collective-permute-start(f32[72,128]{1,0:T(8,128)S(1)} %get-tuple-element.49.refs_0_), channel_id=1, source_target_pairs={{0,5},{1,4},{2,7},{3,6},{4,1},{5,0},{6,3},{7,2},{8,13},{9,12},{10,... | collective-permute-start | bytes 110600 | tf_op jit(solution)/shard_map/ppermute | solution.py:544
  7.1 4.6 %collective-permute-start = (f32[72,128]{1,0:T(8,128)S(1)}, f32[72,128]{1,0:T(8,128)S(1)}, u32[]{:S(2)}, u32[]{:S(2)}) collective-permute-start(f32[72,128]{1,0:T(8,128)S(1)} %get-tuple-element.49.refs_0_), channel_id=1, source_target_pairs={{0,3},{1,2},{2,1},{3,0},{4,7},{5,6},{6,5},{7,4},{8,11},{9,10},{10,... | collective-permute-start | bytes 110600 | tf_op jit(solution)/shard_map/ppermute | solution.py:544
  11.8 1.8 %collective-permute-start.3 = (f32[288,128]{1,0:T(8,128)S(1)}, f32[288,128]{1,0:T(8,128)S(1)}, u32[]{:S(2)}, u32[]{:S(2)}) collective-permute-start(f32[288,128]{1,0:T(8,128)S(1)} %chip.1.keep_ref.own_ref.refs_10_), channel_id=1, source_target_pairs={{0,1},{1,0},{2,3},{3,2},{4,5},{5,4},{6,7},{7,6},{8,9},{9,8},{10,11... | collective-permute-start | bytes 442376 | tf_op jit(solution)/shard_map/ppermute | solution.py:531
  13.7 5.1 %collective-permute-start.4 = (f32[616,128]{1,0:T(8,128)S(1)}, f32[616,128]{1,0:T(8,128)S(1)}, u32[]{:S(2)}, u32[]{:S(2)}) collective-permute-start(f32[616,128]{1,0:T(8,128)S(1)} %get-tuple-element.52.refs_0_), channel_id=1, source_target_pairs={{0,1},{1,0},{2,3},{3,2},{4,5},{5,4},{6,7},{7,6},{8,9},{9,8},{10,11... | collective-permute-start | bytes 946184 | tf_op jit(solution)/shard_map/ppermute | solution.py:531
  13.9 5.4 %collective-permute-start.7 = (f32[16,128]{1,0:T(8,128)S(1)}, f32[16,128]{1,0:T(8,128)S(1)}, u32[]{:S(2)}, u32[]{:S(2)}) collective-permute-start(f32[16,128]{1,0:T(8,128)S(1)} %group.3.refs_12_), channel_id=1, source_target_pairs={{0,25},{1,24},{2,27},{3,26},{4,29},{5,28},{6,31},{7,30},{8,17},{9,... | collective-permute-start | bytes 24584 | tf_op jit(solution)/shard_map/ppermute | solution.py:544
  16.3 3.1 %collective-permute-start.6 = (f32[16,128]{1,0:T(8,128)S(1)}, f32[16,128]{1,0:T(8,128)S(1)}, u32[]{:S(2)}, u32[]{:S(2)}) collective-permute-start(f32[16,128]{1,0:T(8,128)S(1)} %group.3.refs_12_), channel_id=1, source_target_pairs={{0,17},{1,16},{2,19},{3,18},{4,21},{5,20},{6,23},{7,22},{8,25},{9,... | collective-permute-start | bytes 24584 | tf_op jit(solution)/shard_map/ppermute | solution.py:544
  16.6 3.1 %collective-permute-start.5 = (f32[16,128]{1,0:T(8,128)S(1)}, f32[16,128]{1,0:T(8,128)S(1)}, u32[]{:S(2)}, u32[]{:S(2)}) collective-permute-start(f32[16,128]{1,0:T(8,128)S(1)} %group.3.refs_12_), channel_id=1, source_target_pairs={{0,9},{1,8},{2,11},{3,10},{4,13},{5,12},{6,15},{7,14},{8,1},{9,0},... | collective-permute-start | bytes 24584 | tf_op jit(solution)/shard_map/ppermute | solution.py:544
  21.0 5.0 %collective-permute-start.10 = (f32[32,128]{1,0:T(8,128)S(1)}, f32[32,128]{1,0:T(8,128)S(1)}, u32[]{:S(2)}, u32[]{:S(2)}) collective-permute-start(f32[32,128]{1,0:T(8,128)S(1)} %get-tuple-element.65.refs_0_), channel_id=1, source_target_pairs={{0,7},{1,6},{2,5},{3,4},{4,3},{5,2},{6,1},{7,0},{8,15},{9,14},{10,... | collective-permute-start | bytes 49160 | tf_op jit(solution)/shard_map/ppermute | solution.py:544
  23.1 4.1 %collective-permute-start.9 = (f32[32,128]{1,0:T(8,128)S(1)}, f32[32,128]{1,0:T(8,128)S(1)}, u32[]{:S(2)}, u32[]{:S(2)}) collective-permute-start(f32[32,128]{1,0:T(8,128)S(1)} %get-tuple-element.65.refs_0_), channel_id=1, source_target_pairs={{0,5},{1,4},{2,7},{3,6},{4,1},{5,0},{6,3},{7,2},{8,13},{9,12},{10,... | collective-permute-start | bytes 49160 | tf_op jit(solution)/shard_map/ppermute | solution.py:544
  23.5 3.6 %collective-permute-start.8 = (f32[32,128]{1,0:T(8,128)S(1)}, f32[32,128]{1,0:T(8,128)S(1)}, u32[]{:S(2)}, u32[]{:S(2)}) collective-permute-start(f32[32,128]{1,0:T(8,128)S(1)} %get-tuple-element.65.refs_0_), channel_id=1, source_target_pairs={{0,3},{1,2},{2,1},{3,0},{4,7},{5,6},{6,5},{7,4},{8,11},{9,10},{10,... | collective-permute-start | bytes 49160 | tf_op jit(solution)/shard_map/ppermute | solution.py:544
  27.2 5.2 %collective-permute-start.13 = (f32[16,128]{1,0:T(8,128)S(1)}, f32[16,128]{1,0:T(8,128)S(1)}, u32[]{:S(2)}, u32[]{:S(2)}) collective-permute-start(f32[16,128]{1,0:T(8,128)S(1)} %get-tuple-element.75.refs_16_), channel_id=1, source_target_pairs={{0,25},{1,24},{2,27},{3,26},{4,29},{5,28},{6,31},{7,30},{8,17},{9,... | collective-permute-start | bytes 24584 | tf_op jit(solution)/shard_map/ppermute | solution.py:544
  29.3 3.1 %collective-permute-start.12 = (f32[16,128]{1,0:T(8,128)S(1)}, f32[16,128]{1,0:T(8,128)S(1)}, u32[]{:S(2)}, u32[]{:S(2)}) collective-permute-start(f32[16,128]{1,0:T(8,128)S(1)} %get-tuple-element.75.refs_16_), channel_id=1, source_target_pairs={{0,17},{1,16},{2,19},{3,18},{4,21},{5,20},{6,23},{7,22},{8,25},{9,... | collective-permute-start | bytes 24584 | tf_op jit(solution)/shard_map/ppermute | solution.py:544
  29.8 3.1 %collective-permute-start.11 = (f32[16,128]{1,0:T(8,128)S(1)}, f32[16,128]{1,0:T(8,128)S(1)}, u32[]{:S(2)}, u32[]{:S(2)}) collective-permute-start(f32[16,128]{1,0:T(8,128)S(1)} %get-tuple-element.75.refs_16_), channel_id=1, source_target_pairs={{0,9},{1,8},{2,11},{3,10},{4,13},{5,12},{6,15},{7,14},{8,1},{9,0},... | collective-permute-start | bytes 24584 | tf_op jit(solution)/shard_map/ppermute | solution.py:544
  34.3 5.0 %collective-permute-start.16 = (f32[32,128]{1,0:T(8,128)S(1)}, f32[32,128]{1,0:T(8,128)S(1)}, u32[]{:S(2)}, u32[]{:S(2)}) collective-permute-start(f32[32,128]{1,0:T(8,128)S(1)} %get-tuple-element.76.refs_0_), channel_id=1, source_target_pairs={{0,7},{1,6},{2,5},{3,4},{4,3},{5,2},{6,1},{7,0},{8,15},{9,14},{10,... | collective-permute-start | bytes 49160 | tf_op jit(solution)/shard_map/ppermute | solution.py:544
  36.1 4.3 %collective-permute-start.15 = (f32[32,128]{1,0:T(8,128)S(1)}, f32[32,128]{1,0:T(8,128)S(1)}, u32[]{:S(2)}, u32[]{:S(2)}) collective-permute-start(f32[32,128]{1,0:T(8,128)S(1)} %get-tuple-element.76.refs_0_), channel_id=1, source_target_pairs={{0,5},{1,4},{2,7},{3,6},{4,1},{5,0},{6,3},{7,2},{8,13},{9,12},{10,... | collective-permute-start | bytes 49160 | tf_op jit(solution)/shard_map/ppermute | solution.py:544
  36.5 3.9 %collective-permute-start.14 = (f32[32,128]{1,0:T(8,128)S(1)}, f32[32,128]{1,0:T(8,128)S(1)}, u32[]{:S(2)}, u32[]{:S(2)}) collective-permute-start(f32[32,128]{1,0:T(8,128)S(1)} %get-tuple-element.76.refs_0_), channel_id=1, source_target_pairs={{0,3},{1,2},{2,1},{3,0},{4,7},{5,6},{6,5},{7,4},{8,11},{9,10},{10,... | collective-permute-start | bytes 49160 | tf_op jit(solution)/shard_map/ppermute | solution.py:544
  40.4 4.8 %collective-permute-start.19 = (f32[16,128]{1,0:T(8,128)S(1)}, f32[16,128]{1,0:T(8,128)S(1)}, u32[]{:S(2)}, u32[]{:S(2)}) collective-permute-start(f32[16,128]{1,0:T(8,128)S(1)} %get-tuple-element.86.refs_16_), channel_id=1, source_target_pairs={{0,25},{1,24},{2,27},{3,26},{4,29},{5,28},{6,31},{7,30},{8,17},{9,... | collective-permute-start | bytes 24584 | tf_op jit(solution)/shard_map/ppermute | solution.py:544
  42.2 3.1 %collective-permute-start.18 = (f32[16,128]{1,0:T(8,128)S(1)}, f32[16,128]{1,0:T(8,128)S(1)}, u32[]{:S(2)}, u32[]{:S(2)}) collective-permute-start(f32[16,128]{1,0:T(8,128)S(1)} %get-tuple-element.86.refs_16_), channel_id=1, source_target_pairs={{0,17},{1,16},{2,19},{3,18},{4,21},{5,20},{6,23},{7,22},{8,25},{9,... | collective-permute-start | bytes 24584 | tf_op jit(solution)/shard_map/ppermute | solution.py:544
  42.4 3.1 %collective-permute-start.17 = (f32[16,128]{1,0:T(8,128)S(1)}, f32[16,128]{1,0:T(8,128)S(1)}, u32[]{:S(2)}, u32[]{:S(2)}) collective-permute-start(f32[16,128]{1,0:T(8,128)S(1)} %get-tuple-element.86.refs_16_), channel_id=1, source_target_pairs={{0,9},{1,8},{2,11},{3,10},{4,13},{5,12},{6,15},{7,14},{8,1},{9,0},... | collective-permute-start | bytes 24584 | tf_op jit(solution)/shard_map/ppermute | solution.py:544
  46.4 4.8 %collective-permute-start.22 = (f32[8,128]{1,0:T(8,128)S(1)}, f32[8,128]{1,0:T(8,128)S(1)}, u32[]{:S(2)}, u32[]{:S(2)}) collective-permute-start(f32[8,128]{1,0:T(8,128)S(1)} %get-tuple-element.88.refs_0_), channel_id=1, source_target_pairs={{0,7},{1,6},{2,5},{3,4},{4,3},{5,2},{6,1},{7,0},{8,15},{9,14},{10,... | collective-permute-start | bytes 12296 | tf_op jit(solution)/shard_map/ppermute | solution.py:544
  48.2 4.0 %collective-permute-start.21 = (f32[8,128]{1,0:T(8,128)S(1)}, f32[8,128]{1,0:T(8,128)S(1)}, u32[]{:S(2)}, u32[]{:S(2)}) collective-permute-start(f32[8,128]{1,0:T(8,128)S(1)} %get-tuple-element.88.refs_0_), channel_id=1, source_target_pairs={{0,5},{1,4},{2,7},{3,6},{4,1},{5,0},{6,3},{7,2},{8,13},{9,12},{10,... | collective-permute-start | bytes 12296 | tf_op jit(solution)/shard_map/ppermute | solution.py:544
  48.8 3.4 %collective-permute-start.20 = (f32[8,128]{1,0:T(8,128)S(1)}, f32[8,128]{1,0:T(8,128)S(1)}, u32[]{:S(2)}, u32[]{:S(2)}) collective-permute-start(f32[8,128]{1,0:T(8,128)S(1)} %get-tuple-element.88.refs_0_), channel_id=1, source_target_pairs={{0,3},{1,2},{2,1},{3,0},{4,7},{5,6},{6,5},{7,4},{8,11},{9,10},{10,... | collective-permute-start | bytes 12296 | tf_op jit(solution)/shard_map/ppermute | solution.py:544
  52.2 4.0 %collective-permute-start.25 = (f32[8,128]{1,0:T(8,128)S(1)}, f32[8,128]{1,0:T(8,128)S(1)}, u32[]{:S(2)}, u32[]{:S(2)}) collective-permute-start(f32[8,128]{1,0:T(8,128)S(1)} %sum.1.refs_0_), channel_id=1, source_target_pairs={{0,25},{1,24},{2,27},{3,26},{4,29},{5,28},{6,31},{7,30},{8,17},{9,... | collective-permute-start | bytes 12296 | tf_op jit(solution)/shard_map/ppermute | solution.py:544
  54.0 3.0 %collective-permute-start.24 = (f32[8,128]{1,0:T(8,128)S(1)}, f32[8,128]{1,0:T(8,128)S(1)}, u32[]{:S(2)}, u32[]{:S(2)}) collective-permute-start(f32[8,128]{1,0:T(8,128)S(1)} %sum.1.refs_0_), channel_id=1, source_target_pairs={{0,17},{1,16},{2,19},{3,18},{4,21},{5,20},{6,23},{7,22},{8,25},{9,... | collective-permute-start | bytes 12296 | tf_op jit(solution)/shard_map/ppermute | solution.py:544
  54.5 3.0 %collective-permute-start.23 = (f32[8,128]{1,0:T(8,128)S(1)}, f32[8,128]{1,0:T(8,128)S(1)}, u32[]{:S(2)}, u32[]{:S(2)}) collective-permute-start(f32[8,128]{1,0:T(8,128)S(1)} %sum.1.refs_0_), channel_id=1, source_target_pairs={{0,9},{1,8},{2,11},{3,10},{4,13},{5,12},{6,15},{7,14},{8,1},{9,0},... | collective-permute-start | bytes 12296 | tf_op jit(solution)/shard_map/ppermute | solution.py:544

commit v9 on v6

--- a/solution.py
+++ b/solution.py
@@ -604,11 +604,11 @@
                 [gathered],
                 [pltpu.VMEM(wide, bf16)],
             )
+            own_sums, late_pack = lax.optimization_barrier((own_sums, pack))
             keep[1], own_sums = lax.optimization_barrier((keep[1], own_sums))
             (group,) = call(
                 functools.partial(first_group_kernel, chips), "group", [group_type], keep
             )
-            group, late_pack = lax.optimization_barrier((group, pack))
             _, other_pack = direct(late_pack, "tm", [1])
             theirs = call(
                 functools.partial(prepare_kernel, slots, blocks, width),

time: 58.3 us -> 59.6 us (1.022)
  waiting for transfers between devices: 12.6 us -> 13.7 us
    ppermute x2, waiting for transfers between devices: 0.01 us -> 1.31 us  [direct(): lax.ppermute(value, axis, [(i, i ^ gap) for i in range(count)])]
  transfers between devices with their start and end apart: 26 -> 26, of which waited for: 16 -> 16; matrix products, arithmetic and copies ran while one was open for 0% -> 0% of each run, Pallas kernels for 12% -> 10%
where the time goes in v9:
time: 59.6 us; the launch traced here: 59.4 us
  starting transfers between devices  31.3 us (53%)
  Pallas kernels  13.7 us (23%)
  waiting for transfers between devices  13.7 us (23%)
  between operations  0.77 us (1%)
    ppermute x24, starting transfers between devices, exchange(): got.append(lax.ppermute(value, ('star', 'tm'), steps))  30.7 us
    pallas_call x15, Pallas kernels, call(): pl.pallas_call(kernel, name=name, out_shape=[jax.ShapeDtypeStruct(shape,...  13.7 us
    ppermute x24, waiting for transfers between devices, exchange(): got.append(lax.ppermute(value, ('star', 'tm'), steps))  12.4 us
    ppermute x2, waiting for transfers between devices, direct(): lax.ppermute(value, axis, [(i, i ^ gap) for i in range(count)])  1.31 us
  transfers between devices with their start and end apart: 26, of which 16 were waited for; matrix products, arithmetic and copies ran while one was open for 0% of the time, Pallas kernels for 10%

profile of v9, /device:TPU:0, one launch (start us, length us, event | category | flops | bytes accessed | tf_op | source)
XLA Modules:
  0.0 59.4 jit_solution(5238001724476600105)
XLA Ops:
  0.6 1.9 %first.1 = (f32[72,128]{1,0:T(8,128)S(1)}, f32[616,128]{1,0:T(8,128)S(1)}, bf16[128,6144]{1,0:T(8,128)(2,1)S(1)}, bf16[1024,128]{1,0:T(8,128)(2,1)S(1)}, s32[56,128]{1,0:T(8,128)S(1)}) custom-call(f32[8,128]{1,0:T(8,128)} %bitcast.12, f32[5,8,128]{2,1,0:T(8,128)} %bitcast.11, s32[8,128]{1,0:T(8,128)} %bitcast.13, f32[512,128]{1,0:T(8,128)} %bitcast.8, ...), custom_call_target="tpu_custom_call" | custom-call | tf_op jit(solution)/shard_map/first/pallas_call | solution.py:516
  2.6 4.6 %collective-permute-start.2 = (f32[72,128]{1,0:T(8,128)S(1)}, f32[72,128]{1,0:T(8,128)S(1)}, u32[]{:S(2)}, u32[]{:S(2)}) collective-permute-start(f32[72,128]{1,0:T(8,128)S(1)} %get-tuple-element.49.refs_0_), channel_id=1, source_target_pairs={{0,7},{1,6},{2,5},{3,4},{4,3},{5,2},{6,1},{7,0},{8,15},{9,14},{10,... | collective-permute-start | bytes 110600 | tf_op jit(solution)/shard_map/ppermute | solution.py:543
  7.1 0.9 %collective-permute-start = (f32[72,128]{1,0:T(8,128)S(1)}, f32[72,128]{1,0:T(8,128)S(1)}, u32[]{:S(2)}, u32[]{:S(2)}) collective-permute-start(f32[72,128]{1,0:T(8,128)S(1)} %get-tuple-element.49.refs_0_), channel_id=1, source_target_pairs={{0,3},{1,2},{2,1},{3,0},{4,7},{5,6},{6,5},{7,4},{8,11},{9,10},{10,... | collective-permute-start | bytes 110600 | tf_op jit(solution)/shard_map/ppermute | solution.py:543
  8.0 0.9 %collective-permute-done.2.refs_3_ = f32[72,128]{1,0:T(8,128)S(1)} collective-permute-done((f32[72,128]{1,0:T(8,128)S(1)}, f32[72,128]{1,0:T(8,128)S(1)}, u32[]{:S(2)}, u32[]{:S(2)}) %collective-permute-start.2) | collective-permute-done | bytes 36896 | tf_op jit(solution)/shard_map/ppermute | solution.py:543
  9.0 2.8 %collective-permute-done.1.refs_2_ = f32[72,128]{1,0:T(8,128)S(1)} collective-permute-done((f32[72,128]{1,0:T(8,128)S(1)}, f32[72,128]{1,0:T(8,128)S(1)}, u32[]{:S(2)}, u32[]{:S(2)}) %collective-permute-start.1) | collective-permute-done | bytes 36896 | tf_op jit(solution)/shard_map/ppermute | solution.py:543
  11.8 1.4 %astro_own.1 = (f32[80,128]{1,0:T(8,128)S(1)}, bf16[128,4096]{1,0:T(8,128)(2,1)S(1)}) custom-call(f32[288,128]{1,0:T(8,128)S(1)} %chip.1.keep_ref.own_ref.refs_10_), custom_call_target="tpu_custom_call" | custom-call | tf_op jit(solution)/shard_map/astro_own/pallas_call | solution.py:516
  13.2 0.4 collective-permute-start.3
  13.8 1.3 %collective-permute-done.4.keep_ref.other_ref.refs_11_ = f32[288,128]{1,0:T(8,128)S(1)} collective-permute-done((f32[288,128]{1,0:T(8,128)S(1)}, f32[288,128]{1,0:T(8,128)S(1)}, u32[]{:S(2)}, u32[]{:S(2)}) %collective-permute-start.4) | collective-permute-done | bytes 147488 | tf_op jit(solution)/shard_map/ppermute | solution.py:530
  15.1 2.4 %collective-permute-start.7 = (f32[16,128]{1,0:T(8,128)S(1)}, f32[16,128]{1,0:T(8,128)S(1)}, u32[]{:S(2)}, u32[]{:S(2)}) collective-permute-start(f32[16,128]{1,0:T(8,128)S(1)} %group.3.refs_12_), channel_id=1, source_target_pairs={{0,25},{1,24},{2,27},{3,26},{4,29},{5,28},{6,31},{7,30},{8,17},{9,... | collective-permute-start | bytes 24584 | tf_op jit(solution)/shard_map/ppermute | solution.py:543
  17.6 0.3 collective-permute-start.6
  17.9 0.5 collective-permute-start.5
  18.4 1.7 %astro.3 = (f32[80,128]{1,0:T(8,128)S(1)}, f32[16,128]{1,0:T(8,128)S(1)}, bf16[128,4096]{1,0:T(8,128)(2,1)S(1)}) custom-call(f32[288,128]{1,0:T(8,128)S(1)} %chip.1.keep_ref.own_ref.refs_10_, f32[288,128]{1,0:T(8,128)S(1)} %collective-permute-done.4.keep_ref.other_ref.refs_11_, f32[80,128]{1,0:T(8,128)S(1)} %get-tuple-element.61.part_ref), custom_call_target="tpu_custom_call" | custom-call | tf_op jit(solution)/shard_map/astro/pallas_call | solution.py:516
  20.1 0.5 prepare.1
  20.7 0.3 collective-permute-done.5.refs_13_
  21.0 1.4 %step.3 = (f32[32,128]{1,0:T(8,128)S(1)}, f32[16,128]{1,0:T(8,128)S(1)}, f32[96,128]{1,0:T(8,128)S(1)}, f32[96,128]{1,0:T(8,128)S(1)}, f32[16,128]{1,0:T(8,128)S...) custom-call(f32[616,128]{1,0:T(8,128)S(1)} %get-tuple-element.51.refs_0_, ...), custom_call_target="tpu_custom_call" | custom-call | tf_op jit(solution)/shard_map/step/pallas_call | solution.py:516
  22.3 2.0 %collective-permute-start.10 = (f32[32,128]{1,0:T(8,128)S(1)}, f32[32,128]{1,0:T(8,128)S(1)}, u32[]{:S(2)}, u32[]{:S(2)}) collective-permute-start(f32[32,128]{1,0:T(8,128)S(1)} %get-tuple-element.65.refs_0_), channel_id=1, source_target_pairs={{0,7},{1,6},{2,5},{3,4},{4,3},{5,2},{6,1},{7,0},{8,15},{9,14},{10,... | collective-permute-start | bytes 49160 | tf_op jit(solution)/shard_map/ppermute | solution.py:543
  24.4 0.5 collective-permute-start.9
  24.9 1.6 %collective-permute-start.8 = (f32[32,128]{1,0:T(8,128)S(1)}, f32[32,128]{1,0:T(8,128)S(1)}, u32[]{:S(2)}, u32[]{:S(2)}) collective-permute-start(f32[32,128]{1,0:T(8,128)S(1)} %get-tuple-element.65.refs_0_), channel_id=1, source_target_pairs={{0,3},{1,2},{2,1},{3,0},{4,7},{5,6},{6,5},{7,4},{8,11},{9,10},{10,... | collective-permute-start | bytes 49160 | tf_op jit(solution)/shard_map/ppermute | solution.py:543
  26.5 0.9 %collective-permute-done.10.refs_3_ = f32[32,128]{1,0:T(8,128)S(1)} collective-permute-done((f32[32,128]{1,0:T(8,128)S(1)}, f32[32,128]{1,0:T(8,128)S(1)}, u32[]{:S(2)}, u32[]{:S(2)}) %collective-permute-start.10) | collective-permute-done | bytes 16416 | tf_op jit(solution)/shard_map/ppermute | solution.py:543
  27.4 1.1 %collective-permute-done.9.refs_2_ = f32[32,128]{1,0:T(8,128)S(1)} collective-permute-done((f32[32,128]{1,0:T(8,128)S(1)}, f32[32,128]{1,0:T(8,128)S(1)}, u32[]{:S(2)}, u32[]{:S(2)}) %collective-permute-start.9) | collective-permute-done | bytes 16416 | tf_op jit(solution)/shard_map/ppermute | solution.py:543
  28.5 2.1 %collective-permute-start.13 = (f32[16,128]{1,0:T(8,128)S(1)}, f32[16,128]{1,0:T(8,128)S(1)}, u32[]{:S(2)}, u32[]{:S(2)}) collective-permute-start(f32[16,128]{1,0:T(8,128)S(1)} %get-tuple-element.75.refs_16_), channel_id=1, source_target_pairs={{0,25},{1,24},{2,27},{3,26},{4,29},{5,28},{6,31},{7,30},{8,17},{9,... | collective-permute-start | bytes 24584 | tf_op jit(solution)/shard_map/ppermute | solution.py:543
  30.6 0.4 collective-permute-start.12
  31.0 0.9 %collective-permute-start.11 = (f32[16,128]{1,0:T(8,128)S(1)}, f32[16,128]{1,0:T(8,128)S(1)}, u32[]{:S(2)}, u32[]{:S(2)}) collective-permute-start(f32[16,128]{1,0:T(8,128)S(1)} %get-tuple-element.75.refs_16_), channel_id=1, source_target_pairs={{0,9},{1,8},{2,11},{3,10},{4,13},{5,12},{6,15},{7,14},{8,1},{9,0},... | collective-permute-start | bytes 24584 | tf_op jit(solution)/shard_map/ppermute | solution.py:543
  31.9 1.8 %astro.4 = (f32[80,128]{1,0:T(8,128)S(1)}, f32[16,128]{1,0:T(8,128)S(1)}) custom-call(f32[288,128]{1,0:T(8,128)S(1)} %chip.1.keep_ref.own_ref.refs_10_, f32[288,128]{1,0:T(8,128)S(1)} %collective-permute-done.4.keep_ref.other_ref.refs_11_, bf16[128,4096]{1,0:T(8,128)(2,1)S(1)} %get-tuple-element.60.own_table, ...), custom_call_target="tpu_custom_call" | custom-call | tf_op jit(solution)/shard_map/astro/pallas_call | solution.py:516
  33.7 0.4 collective-permute-done.11.refs_17_
  34.1 1.4 %step.4 = (f32[32,128]{1,0:T(8,128)S(1)}, f32[16,128]{1,0:T(8,128)S(1)}, f32[96,128]{1,0:T(8,128)S(1)}, f32[96,128]{1,0:T(8,128)S(1)}, f32[16,128]{1,0:T(8,128)S...) custom-call(f32[616,128]{1,0:T(8,128)S(1)} %get-tuple-element.51.refs_0_, ...), custom_call_target="tpu_custom_call" | custom-call | tf_op jit(solution)/shard_map/step/pallas_call | solution.py:516
  35.5 2.0 %collective-permute-start.16 = (f32[32,128]{1,0:T(8,128)S(1)}, f32[32,128]{1,0:T(8,128)S(1)}, u32[]{:S(2)}, u32[]{:S(2)}) collective-permute-start(f32[32,128]{1,0:T(8,128)S(1)} %get-tuple-element.76.refs_0_), channel_id=1, source_target_pairs={{0,7},{1,6},{2,5},{3,4},{4,3},{5,2},{6,1},{7,0},{8,15},{9,14},{10,... | collective-permute-start | bytes 49160 | tf_op jit(solution)/shard_map/ppermute | solution.py:543
  37.4 0.4 collective-permute-start.15
  37.9 1.7 %collective-permute-start.14 = (f32[32,128]{1,0:T(8,128)S(1)}, f32[32,128]{1,0:T(8,128)S(1)}, u32[]{:S(2)}, u32[]{:S(2)}) collective-permute-start(f32[32,128]{1,0:T(8,128)S(1)} %get-tuple-element.76.refs_0_), channel_id=1, source_target_pairs={{0,3},{1,2},{2,1},{3,0},{4,7},{5,6},{6,5},{7,4},{8,11},{9,10},{10,... | collective-permute-start | bytes 49160 | tf_op jit(solution)/shard_map/ppermute | solution.py:543
  39.5 1.0 %collective-permute-done.16.refs_3_ = f32[32,128]{1,0:T(8,128)S(1)} collective-permute-done((f32[32,128]{1,0:T(8,128)S(1)}, f32[32,128]{1,0:T(8,128)S(1)}, u32[]{:S(2)}, u32[]{:S(2)}) %collective-permute-start.16) | collective-permute-done | bytes 16416 | tf_op jit(solution)/shard_map/ppermute | solution.py:543
  40.5 1.0 %collective-permute-done.15.refs_2_ = f32[32,128]{1,0:T(8,128)S(1)} collective-permute-done((f32[32,128]{1,0:T(8,128)S(1)}, f32[32,128]{1,0:T(8,128)S(1)}, u32[]{:S(2)}, u32[]{:S(2)}) %collective-permute-start.15) | collective-permute-done | bytes 16416 | tf_op jit(solution)/shard_map/ppermute | solution.py:543
  41.6 1.9 %collective-permute-start.19 = (f32[16,128]{1,0:T(8,128)S(1)}, f32[16,128]{1,0:T(8,128)S(1)}, u32[]{:S(2)}, u32[]{:S(2)}) collective-permute-start(f32[16,128]{1,0:T(8,128)S(1)} %get-tuple-element.86.refs_16_), channel_id=1, source_target_pairs={{0,25},{1,24},{2,27},{3,26},{4,29},{5,28},{6,31},{7,30},{8,17},{9,... | collective-permute-start | bytes 24584 | tf_op jit(solution)/shard_map/ppermute | solution.py:543
  43.5 0.2 collective-permute-start.18
  43.7 1.1 %collective-permute-start.17 = (f32[16,128]{1,0:T(8,128)S(1)}, f32[16,128]{1,0:T(8,128)S(1)}, u32[]{:S(2)}, u32[]{:S(2)}) collective-permute-start(f32[16,128]{1,0:T(8,128)S(1)} %get-tuple-element.86.refs_16_), channel_id=1, source_target_pairs={{0,9},{1,8},{2,11},{3,10},{4,13},{5,12},{6,15},{7,14},{8,1},{9,0},... | collective-permute-start | bytes 24584 | tf_op jit(solution)/shard_map/ppermute | solution.py:543
  44.8 1.8 %astro.5 = (f32[80,128]{1,0:T(8,128)S(1)}, f32[16,128]{1,0:T(8,128)S(1)}) custom-call(f32[288,128]{1,0:T(8,128)S(1)} %chip.1.keep_ref.own_ref.refs_10_, f32[288,128]{1,0:T(8,128)S(1)} %collective-permute-done.4.keep_ref.other_ref.refs_11_, bf16[128,4096]{1,0:T(8,128)(2,1)S(1)} %get-tuple-element.60.own_table, ...), custom_call_target="tpu_custom_call" | custom-call | tf_op jit(solution)/shard_map/astro/pallas_call | solution.py:516
  46.8 0.9 %step.5 = (f32[8,128]{1,0:T(8,128)S(1)}, f32[16,128]{1,0:T(8,128)S(1)}, f32[96,128]{1,0:T(8,128)S(1)}, f32[96,128]{1,0:T(8,128)}, f32[16,128]{1,0:T(8,128)}, /*index=5*/f32[16,128]{1,0:T(8,128)}, f32[16,128]{1,0:T(8,128)}) custom-call(f32[616,128]{1,0:T(8,128)S(1)} %get-tuple-element.51.refs_0_, f32[616,128]{1,0:T(8,128)S(1)} %collective-permute-done.3.pack_ref.refs_1_, ...), custom_call_target="tpu_custom_call" | custom-call | tf_op jit(solution)/shard_map/step/pallas_call | solution.py:516
  47.7 1.8 %collective-permute-start.22 = (f32[8,128]{1,0:T(8,128)S(1)}, f32[8,128]{1,0:T(8,128)S(1)}, u32[]{:S(2)}, u32[]{:S(2)}) collective-permute-start(f32[8,128]{1,0:T(8,128)S(1)} %get-tuple-element.88.refs_0_), channel_id=1, source_target_pairs={{0,7},{1,6},{2,5},{3,4},{4,3},{5,2},{6,1},{7,0},{8,15},{9,14},{10,... | collective-permute-start | bytes 12296 | tf_op jit(solution)/shard_map/ppermute | solution.py:543
  49.5 0.5 collective-permute-start.21
  50.1 1.7 %collective-permute-start.20 = (f32[8,128]{1,0:T(8,128)S(1)}, f32[8,128]{1,0:T(8,128)S(1)}, u32[]{:S(2)}, u32[]{:S(2)}) collective-permute-start(f32[8,128]{1,0:T(8,128)S(1)} %get-tuple-element.88.refs_0_), channel_id=1, source_target_pairs={{0,3},{1,2},{2,1},{3,0},{4,7},{5,6},{6,5},{7,4},{8,11},{9,10},{10,... | collective-permute-start | bytes 12296 | tf_op jit(solution)/shard_map/ppermute | solution.py:543
  51.8 0.8 %collective-permute-done.22.refs_3_ = f32[8,128]{1,0:T(8,128)S(1)} collective-permute-done((f32[8,128]{1,0:T(8,128)S(1)}, f32[8,128]{1,0:T(8,128)S(1)}, u32[]{:S(2)}, u32[]{:S(2)}) %collective-permute-start.22) | collective-permute-done | bytes 4128 | tf_op jit(solution)/shard_map/ppermute | solution.py:543
  52.6 0.9 %collective-permute-done.21.refs_2_ = f32[8,128]{1,0:T(8,128)S(1)} collective-permute-done((f32[8,128]{1,0:T(8,128)S(1)}, f32[8,128]{1,0:T(8,128)S(1)}, u32[]{:S(2)}, u32[]{:S(2)}) %collective-permute-start.21) | collective-permute-done | bytes 4128 | tf_op jit(solution)/shard_map/ppermute | solution.py:543
  53.5 1.8 %collective-permute-start.25 = (f32[8,128]{1,0:T(8,128)S(1)}, f32[8,128]{1,0:T(8,128)S(1)}, u32[]{:S(2)}, u32[]{:S(2)}) collective-permute-start(f32[8,128]{1,0:T(8,128)S(1)} %sum.1.refs_0_), channel_id=1, source_target_pairs={{0,25},{1,24},{2,27},{3,26},{4,29},{5,28},{6,31},{7,30},{8,17},{9,... | collective-permute-start | bytes 12296 | tf_op jit(solution)/shard_map/ppermute | solution.py:543
  55.3 0.3 collective-permute-start.24
  55.7 1.1 %collective-permute-start.23 = (f32[8,128]{1,0:T(8,128)S(1)}, f32[8,128]{1,0:T(8,128)S(1)}, u32[]{:S(2)}, u32[]{:S(2)}) collective-permute-start(f32[8,128]{1,0:T(8,128)S(1)} %sum.1.refs_0_), channel_id=1, source_target_pairs={{0,9},{1,8},{2,11},{3,10},{4,13},{5,12},{6,15},{7,14},{8,1},{9,0},... | collective-permute-start | bytes 12296 | tf_op jit(solution)/shard_map/ppermute | solution.py:543
  56.8 0.8 %collective-permute-done.25.refs_3_ = f32[8,128]{1,0:T(8,128)S(1)} collective-permute-done((f32[8,128]{1,0:T(8,128)S(1)}, f32[8,128]{1,0:T(8,128)S(1)}, u32[]{:S(2)}, u32[]{:S(2)}) %collective-permute-start.25) | collective-permute-done | bytes 4128 | tf_op jit(solution)/shard_map/ppermute | solution.py:543
  57.5 0.8 %collective-permute-done.24.refs_2_ = f32[8,128]{1,0:T(8,128)S(1)} collective-permute-done((f32[8,128]{1,0:T(8,128)S(1)}, f32[8,128]{1,0:T(8,128)S(1)}, u32[]{:S(2)}, u32[]{:S(2)}) %collective-permute-start.24) | collective-permute-done | bytes 4128 | tf_op jit(solution)/shard_map/ppermute | solution.py:543
  58.4 0.3 collective-permute-done.23.refs_1_
  58.7 0.7 %last.1 = (f32[5,256]{1,0:T(8,128)}, f32[2,128]{1,0:T(2,128)}, f32[8,128]{1,0:T(8,128)}) custom-call(f32[16,128]{1,0:T(8,128)S(1)} %get-tuple-element.87.state_ref, f32[8,128]{1,0:T(8,128)S(1)} %sum.1.refs_0_, f32[8,128]{1,0:T(8,128)S(1)} %collective-permute-done.23.refs_1_, f32[8,128]{1,0:T(8,128)S(1)} %collective-permute-done.24.refs_2_, ...), custom_call_target="tpu_custom_call" | custom-call | tf_op jit(solution)/shard_map/last/pallas_call | solution.py:516
  (19 shorter events, 0.6 us)
Async XLA Ops:
  2.6 6.4 %collective-permute-start.2 = (f32[72,128]{1,0:T(8,128)S(1)}, f32[72,128]{1,0:T(8,128)S(1)}, u32[]{:S(2)}, u32[]{:S(2)}) collective-permute-start(f32[72,128]{1,0:T(8,128)S(1)} %get-tuple-element.49.refs_0_), channel_id=1, source_target_pairs={{0,7},{1,6},{2,5},{3,4},{4,3},{5,2},{6,1},{7,0},{8,15},{9,14},{10,... | collective-permute-start | bytes 110600 | tf_op jit(solution)/shard_map/ppermute | solution.py:543
  7.1 4.6 %collective-permute-start.1 = (f32[72,128]{1,0:T(8,128)S(1)}, f32[72,128]{1,0:T(8,128)S(1)}, u32[]{:S(2)}, u32[]{:S(2)}) collective-permute-start(f32[72,128]{1,0:T(8,128)S(1)} %get-tuple-element.49.refs_0_), channel_id=1, source_target_pairs={{0,5},{1,4},{2,7},{3,6},{4,1},{5,0},{6,3},{7,2},{8,13},{9,12},{10,... | collective-permute-start | bytes 110600 | tf_op jit(solution)/shard_map/ppermute | solution.py:543
  7.1 4.6 %collective-permute-start = (f32[72,128]{1,0:T(8,128)S(1)}, f32[72,128]{1,0:T(8,128)S(1)}, u32[]{:S(2)}, u32[]{:S(2)}) collective-permute-start(f32[72,128]{1,0:T(8,128)S(1)} %get-tuple-element.49.refs_0_), channel_id=1, source_target_pairs={{0,3},{1,2},{2,1},{3,0},{4,7},{5,6},{6,5},{7,4},{8,11},{9,10},{10,... | collective-permute-start | bytes 110600 | tf_op jit(solution)/shard_map/ppermute | solution.py:543
  13.2 6.8 %collective-permute-start.3 = (f32[616,128]{1,0:T(8,128)S(1)}, f32[616,128]{1,0:T(8,128)S(1)}, u32[]{:S(2)}, u32[]{:S(2)}) collective-permute-start(f32[616,128]{1,0:T(8,128)S(1)} %get-tuple-element.51.refs_0_), channel_id=1, source_target_pairs={{0,1},{1,0},{2,3},{3,2},{4,5},{5,4},{6,7},{7,6},{8,9},{9,8},{10,11... | collective-permute-start | bytes 946184 | tf_op jit(solution)/shard_map/ppermute | solution.py:530
  13.6 1.5 %collective-permute-start.4 = (f32[288,128]{1,0:T(8,128)S(1)}, f32[288,128]{1,0:T(8,128)S(1)}, u32[]{:S(2)}, u32[]{:S(2)}) collective-permute-start(f32[288,128]{1,0:T(8,128)S(1)} %chip.1.keep_ref.own_ref.refs_10_), channel_id=1, source_target_pairs={{0,1},{1,0},{2,3},{3,2},{4,5},{5,4},{6,7},{7,6},{8,9},{9,8},{10,11... | collective-permute-start | bytes 442376 | tf_op jit(solution)/shard_map/ppermute | solution.py:530
  15.1 5.4 %collective-permute-start.7 = (f32[16,128]{1,0:T(8,128)S(1)}, f32[16,128]{1,0:T(8,128)S(1)}, u32[]{:S(2)}, u32[]{:S(2)}) collective-permute-start(f32[16,128]{1,0:T(8,128)S(1)} %group.3.refs_12_), channel_id=1, source_target_pairs={{0,25},{1,24},{2,27},{3,26},{4,29},{5,28},{6,31},{7,30},{8,17},{9,... | collective-permute-start | bytes 24584 | tf_op jit(solution)/shard_map/ppermute | solution.py:543
  17.6 3.1 %collective-permute-start.6 = (f32[16,128]{1,0:T(8,128)S(1)}, f32[16,128]{1,0:T(8,128)S(1)}, u32[]{:S(2)}, u32[]{:S(2)}) collective-permute-start(f32[16,128]{1,0:T(8,128)S(1)} %group.3.refs_12_), channel_id=1, source_target_pairs={{0,17},{1,16},{2,19},{3,18},{4,21},{5,20},{6,23},{7,22},{8,25},{9,... | collective-permute-start | bytes 24584 | tf_op jit(solution)/shard_map/ppermute | solution.py:543
  17.9 3.1 %collective-permute-start.5 = (f32[16,128]{1,0:T(8,128)S(1)}, f32[16,128]{1,0:T(8,128)S(1)}, u32[]{:S(2)}, u32[]{:S(2)}) collective-permute-start(f32[16,128]{1,0:T(8,128)S(1)} %group.3.refs_12_), channel_id=1, source_target_pairs={{0,9},{1,8},{2,11},{3,10},{4,13},{5,12},{6,15},{7,14},{8,1},{9,0},... | collective-permute-start | bytes 24584 | tf_op jit(solution)/shard_map/ppermute | solution.py:543
  22.3 5.0 %collective-permute-start.10 = (f32[32,128]{1,0:T(8,128)S(1)}, f32[32,128]{1,0:T(8,128)S(1)}, u32[]{:S(2)}, u32[]{:S(2)}) collective-permute-start(f32[32,128]{1,0:T(8,128)S(1)} %get-tuple-element.65.refs_0_), channel_id=1, source_target_pairs={{0,7},{1,6},{2,5},{3,4},{4,3},{5,2},{6,1},{7,0},{8,15},{9,14},{10,... | collective-permute-start | bytes 49160 | tf_op jit(solution)/shard_map/ppermute | solution.py:543
  24.4 4.1 %collective-permute-start.9 = (f32[32,128]{1,0:T(8,128)S(1)}, f32[32,128]{1,0:T(8,128)S(1)}, u32[]{:S(2)}, u32[]{:S(2)}) collective-permute-start(f32[32,128]{1,0:T(8,128)S(1)} %get-tuple-element.65.refs_0_), channel_id=1, source_target_pairs={{0,5},{1,4},{2,7},{3,6},{4,1},{5,0},{6,3},{7,2},{8,13},{9,12},{10,... | collective-permute-start | bytes 49160 | tf_op jit(solution)/shard_map/ppermute | solution.py:543
  24.9 3.6 %collective-permute-start.8 = (f32[32,128]{1,0:T(8,128)S(1)}, f32[32,128]{1,0:T(8,128)S(1)}, u32[]{:S(2)}, u32[]{:S(2)}) collective-permute-start(f32[32,128]{1,0:T(8,128)S(1)} %get-tuple-element.65.refs_0_), channel_id=1, source_target_pairs={{0,3},{1,2},{2,1},{3,0},{4,7},{5,6},{6,5},{7,4},{8,11},{9,10},{10,... | collective-permute-start | bytes 49160 | tf_op jit(solution)/shard_map/ppermute | solution.py:543
  28.5 5.2 %collective-permute-start.13 = (f32[16,128]{1,0:T(8,128)S(1)}, f32[16,128]{1,0:T(8,128)S(1)}, u32[]{:S(2)}, u32[]{:S(2)}) collective-permute-start(f32[16,128]{1,0:T(8,128)S(1)} %get-tuple-element.75.refs_16_), channel_id=1, source_target_pairs={{0,25},{1,24},{2,27},{3,26},{4,29},{5,28},{6,31},{7,30},{8,17},{9,... | collective-permute-start | bytes 24584 | tf_op jit(solution)/shard_map/ppermute | solution.py:543
  30.6 3.1 %collective-permute-start.12 = (f32[16,128]{1,0:T(8,128)S(1)}, f32[16,128]{1,0:T(8,128)S(1)}, u32[]{:S(2)}, u32[]{:S(2)}) collective-permute-start(f32[16,128]{1,0:T(8,128)S(1)} %get-tuple-element.75.refs_16_), channel_id=1, source_target_pairs={{0,17},{1,16},{2,19},{3,18},{4,21},{5,20},{6,23},{7,22},{8,25},{9,... | collective-permute-start | bytes 24584 | tf_op jit(solution)/shard_map/ppermute | solution.py:543
  31.0 3.1 %collective-permute-start.11 = (f32[16,128]{1,0:T(8,128)S(1)}, f32[16,128]{1,0:T(8,128)S(1)}, u32[]{:S(2)}, u32[]{:S(2)}) collective-permute-start(f32[16,128]{1,0:T(8,128)S(1)} %get-tuple-element.75.refs_16_), channel_id=1, source_target_pairs={{0,9},{1,8},{2,11},{3,10},{4,13},{5,12},{6,15},{7,14},{8,1},{9,0},... | collective-permute-start | bytes 24584 | tf_op jit(solution)/shard_map/ppermute | solution.py:543
  35.5 5.0 %collective-permute-start.16 = (f32[32,128]{1,0:T(8,128)S(1)}, f32[32,128]{1,0:T(8,128)S(1)}, u32[]{:S(2)}, u32[]{:S(2)}) collective-permute-start(f32[32,128]{1,0:T(8,128)S(1)} %get-tuple-element.76.refs_0_), channel_id=1, source_target_pairs={{0,7},{1,6},{2,5},{3,4},{4,3},{5,2},{6,1},{7,0},{8,15},{9,14},{10,... | collective-permute-start | bytes 49160 | tf_op jit(solution)/shard_map/ppermute | solution.py:543
  37.4 4.1 %collective-permute-start.15 = (f32[32,128]{1,0:T(8,128)S(1)}, f32[32,128]{1,0:T(8,128)S(1)}, u32[]{:S(2)}, u32[]{:S(2)}) collective-permute-start(f32[32,128]{1,0:T(8,128)S(1)} %get-tuple-element.76.refs_0_), channel_id=1, source_target_pairs={{0,5},{1,4},{2,7},{3,6},{4,1},{5,0},{6,3},{7,2},{8,13},{9,12},{10,... | collective-permute-start | bytes 49160 | tf_op jit(solution)/shard_map/ppermute | solution.py:543
  37.9 3.7 %collective-permute-start.14 = (f32[32,128]{1,0:T(8,128)S(1)}, f32[32,128]{1,0:T(8,128)S(1)}, u32[]{:S(2)}, u32[]{:S(2)}) collective-permute-start(f32[32,128]{1,0:T(8,128)S(1)} %get-tuple-element.76.refs_0_), channel_id=1, source_target_pairs={{0,3},{1,2},{2,1},{3,0},{4,7},{5,6},{6,5},{7,4},{8,11},{9,10},{10,... | collective-permute-start | bytes 49160 | tf_op jit(solution)/shard_map/ppermute | solution.py:543
  41.6 5.0 %collective-permute-start.19 = (f32[16,128]{1,0:T(8,128)S(1)}, f32[16,128]{1,0:T(8,128)S(1)}, u32[]{:S(2)}, u32[]{:S(2)}) collective-permute-start(f32[16,128]{1,0:T(8,128)S(1)} %get-tuple-element.86.refs_16_), channel_id=1, source_target_pairs={{0,25},{1,24},{2,27},{3,26},{4,29},{5,28},{6,31},{7,30},{8,17},{9,... | collective-permute-start | bytes 24584 | tf_op jit(solution)/shard_map/ppermute | solution.py:543
  43.5 3.1 %collective-permute-start.18 = (f32[16,128]{1,0:T(8,128)S(1)}, f32[16,128]{1,0:T(8,128)S(1)}, u32[]{:S(2)}, u32[]{:S(2)}) collective-permute-start(f32[16,128]{1,0:T(8,128)S(1)} %get-tuple-element.86.refs_16_), channel_id=1, source_target_pairs={{0,17},{1,16},{2,19},{3,18},{4,21},{5,20},{6,23},{7,22},{8,25},{9,... | collective-permute-start | bytes 24584 | tf_op jit(solution)/shard_map/ppermute | solution.py:543
  43.7 3.1 %collective-permute-start.17 = (f32[16,128]{1,0:T(8,128)S(1)}, f32[16,128]{1,0:T(8,128)S(1)}, u32[]{:S(2)}, u32[]{:S(2)}) collective-permute-start(f32[16,128]{1,0:T(8,128)S(1)} %get-tuple-element.86.refs_16_), channel_id=1, source_target_pairs={{0,9},{1,8},{2,11},{3,10},{4,13},{5,12},{6,15},{7,14},{8,1},{9,0},... | collective-permute-start | bytes 24584 | tf_op jit(solution)/shard_map/ppermute | solution.py:543
  47.7 4.8 %collective-permute-start.22 = (f32[8,128]{1,0:T(8,128)S(1)}, f32[8,128]{1,0:T(8,128)S(1)}, u32[]{:S(2)}, u32[]{:S(2)}) collective-permute-start(f32[8,128]{1,0:T(8,128)S(1)} %get-tuple-element.88.refs_0_), channel_id=1, source_target_pairs={{0,7},{1,6},{2,5},{3,4},{4,3},{5,2},{6,1},{7,0},{8,15},{9,14},{10,... | collective-permute-start | bytes 12296 | tf_op jit(solution)/shard_map/ppermute | solution.py:543
  49.5 4.0 %collective-permute-start.21 = (f32[8,128]{1,0:T(8,128)S(1)}, f32[8,128]{1,0:T(8,128)S(1)}, u32[]{:S(2)}, u32[]{:S(2)}) collective-permute-start(f32[8,128]{1,0:T(8,128)S(1)} %get-tuple-element.88.refs_0_), channel_id=1, source_target_pairs={{0,5},{1,4},{2,7},{3,6},{4,1},{5,0},{6,3},{7,2},{8,13},{9,12},{10,... | collective-permute-start | bytes 12296 | tf_op jit(solution)/shard_map/ppermute | solution.py:543
  50.1 3.4 %collective-permute-start.20 = (f32[8,128]{1,0:T(8,128)S(1)}, f32[8,128]{1,0:T(8,128)S(1)}, u32[]{:S(2)}, u32[]{:S(2)}) collective-permute-start(f32[8,128]{1,0:T(8,128)S(1)} %get-tuple-element.88.refs_0_), channel_id=1, source_target_pairs={{0,3},{1,2},{2,1},{3,0},{4,7},{5,6},{6,5},{7,4},{8,11},{9,10},{10,... | collective-permute-start | bytes 12296 | tf_op jit(solution)/shard_map/ppermute | solution.py:543
  53.5 4.0 %collective-permute-start.25 = (f32[8,128]{1,0:T(8,128)S(1)}, f32[8,128]{1,0:T(8,128)S(1)}, u32[]{:S(2)}, u32[]{:S(2)}) collective-permute-start(f32[8,128]{1,0:T(8,128)S(1)} %sum.1.refs_0_), channel_id=1, source_target_pairs={{0,25},{1,24},{2,27},{3,26},{4,29},{5,28},{6,31},{7,30},{8,17},{9,... | collective-permute-start | bytes 12296 | tf_op jit(solution)/shard_map/ppermute | solution.py:543
  55.3 3.0 %collective-permute-start.24 = (f32[8,128]{1,0:T(8,128)S(1)}, f32[8,128]{1,0:T(8,128)S(1)}, u32[]{:S(2)}, u32[]{:S(2)}) collective-permute-start(f32[8,128]{1,0:T(8,128)S(1)} %sum.1.refs_0_), channel_id=1, source_target_pairs={{0,17},{1,16},{2,19},{3,18},{4,21},{5,20},{6,23},{7,22},{8,25},{9,... | collective-permute-start | bytes 12296 | tf_op jit(solution)/shard_map/ppermute | solution.py:543
  55.7 3.0 %collective-permute-start.23 = (f32[8,128]{1,0:T(8,128)S(1)}, f32[8,128]{1,0:T(8,128)S(1)}, u32[]{:S(2)}, u32[]{:S(2)}) collective-permute-start(f32[8,128]{1,0:T(8,128)S(1)} %sum.1.refs_0_), channel_id=1, source_target_pairs={{0,9},{1,8},{2,11},{3,10},{4,13},{5,12},{6,15},{7,14},{8,1},{9,0},... | collective-permute-start | bytes 12296 | tf_op jit(solution)/shard_map/ppermute | solution.py:543

commit v10 on v9

--- a/solution.py
+++ b/solution.py
@@ -604,8 +604,7 @@
                 [gathered],
                 [pltpu.VMEM(wide, bf16)],
             )
-            own_sums, late_pack = lax.optimization_barrier((own_sums, pack))
-            keep[1], own_sums = lax.optimization_barrier((keep[1], own_sums))
+            keep[1], own_sums, late_pack = lax.optimization_barrier((keep[1], own_sums, pack))
             (group,) = call(
                 functools.partial(first_group_kernel, chips), "group", [group_type], keep
             )

time: 59.6 us -> 58.4 us (0.980)
  waiting for transfers between devices: 13.7 us -> 12.6 us
    ppermute x2, waiting for transfers between devices: 1.31 us -> 0.01 us  [direct(): lax.ppermute(value, axis, [(i, i ^ gap) for i in range(count)])]
  transfers between devices with their start and end apart: 26 -> 26, of which waited for: 16 -> 16; matrix products, arithmetic and copies ran while one was open for 0% -> 0% of each run, Pallas kernels for 10% -> 12%
where the time goes in v10:
time: 58.4 us; the launch traced here: 58.2 us
  starting transfers between devices  31.2 us (53%)
  Pallas kernels  13.6 us (23%)
  waiting for transfers between devices  12.6 us (22%)
  between operations  0.77 us (1%)
    ppermute x24, starting transfers between devices, exchange(): got.append(lax.ppermute(value, ('star', 'tm'), steps))  30.6 us
    pallas_call x15, Pallas kernels, call(): pl.pallas_call(kernel, name=name, out_shape=[jax.ShapeDtypeStruct(shape,...  13.6 us
    ppermute x24, waiting for transfers between devices, exchange(): got.append(lax.ppermute(value, ('star', 'tm'), steps))  12.6 us
  transfers between devices with their start and end apart: 26, of which 16 were waited for; matrix products, arithmetic and copies ran while one was open for 0% of the time, Pallas kernels for 12%

profile of v10, /device:TPU:0, one launch (start us, length us, event | category | flops | bytes accessed | tf_op | source)
XLA Modules:
  0.0 58.2 jit_solution(6846780578679750631)
XLA Ops:
  0.6 1.9 %first.1 = (f32[72,128]{1,0:T(8,128)S(1)}, f32[616,128]{1,0:T(8,128)S(1)}, bf16[128,6144]{1,0:T(8,128)(2,1)S(1)}, bf16[1024,128]{1,0:T(8,128)(2,1)S(1)}, s32[56,128]{1,0:T(8,128)S(1)}) custom-call(f32[8,128]{1,0:T(8,128)} %bitcast.12, f32[5,8,128]{2,1,0:T(8,128)} %bitcast.11, s32[8,128]{1,0:T(8,128)} %bitcast.13, f32[512,128]{1,0:T(8,128)} %bitcast.8, ...), custom_call_target="tpu_custom_call" | custom-call | tf_op jit(solution)/shard_map/first/pallas_call | solution.py:516
  2.6 4.6 %collective-permute-start.2 = (f32[72,128]{1,0:T(8,128)S(1)}, f32[72,128]{1,0:T(8,128)S(1)}, u32[]{:S(2)}, u32[]{:S(2)}) collective-permute-start(f32[72,128]{1,0:T(8,128)S(1)} %get-tuple-element.48.refs_0_), channel_id=1, source_target_pairs={{0,7},{1,6},{2,5},{3,4},{4,3},{5,2},{6,1},{7,0},{8,15},{9,14},{10,... | collective-permute-start | bytes 110600 | tf_op jit(solution)/shard_map/ppermute | solution.py:543
  7.1 0.9 %collective-permute-start = (f32[72,128]{1,0:T(8,128)S(1)}, f32[72,128]{1,0:T(8,128)S(1)}, u32[]{:S(2)}, u32[]{:S(2)}) collective-permute-start(f32[72,128]{1,0:T(8,128)S(1)} %get-tuple-element.48.refs_0_), channel_id=1, source_target_pairs={{0,3},{1,2},{2,1},{3,0},{4,7},{5,6},{6,5},{7,4},{8,11},{9,10},{10,... | collective-permute-start | bytes 110600 | tf_op jit(solution)/shard_map/ppermute | solution.py:543
  8.0 0.9 %collective-permute-done.2.refs_3_ = f32[72,128]{1,0:T(8,128)S(1)} collective-permute-done((f32[72,128]{1,0:T(8,128)S(1)}, f32[72,128]{1,0:T(8,128)S(1)}, u32[]{:S(2)}, u32[]{:S(2)}) %collective-permute-start.2) | collective-permute-done | bytes 36896 | tf_op jit(solution)/shard_map/ppermute | solution.py:543
  9.0 2.8 %collective-permute-done.1.refs_2_ = f32[72,128]{1,0:T(8,128)S(1)} collective-permute-done((f32[72,128]{1,0:T(8,128)S(1)}, f32[72,128]{1,0:T(8,128)S(1)}, u32[]{:S(2)}, u32[]{:S(2)}) %collective-permute-start.1) | collective-permute-done | bytes 36896 | tf_op jit(solution)/shard_map/ppermute | solution.py:543
  11.8 0.4 collective-permute-start.3
  12.2 1.4 %astro_own.1 = (f32[80,128]{1,0:T(8,128)S(1)}, bf16[128,4096]{1,0:T(8,128)(2,1)S(1)}) custom-call(f32[288,128]{1,0:T(8,128)S(1)} %chip.1.keep_ref.own_ref.refs_10_), custom_call_target="tpu_custom_call" | custom-call | tf_op jit(solution)/shard_map/astro_own/pallas_call | solution.py:516
  13.6 0.2 collective-permute-start.4
  13.9 2.4 %collective-permute-start.7 = (f32[16,128]{1,0:T(8,128)S(1)}, f32[16,128]{1,0:T(8,128)S(1)}, u32[]{:S(2)}, u32[]{:S(2)}) collective-permute-start(f32[16,128]{1,0:T(8,128)S(1)} %group.3.refs_12_), channel_id=1, source_target_pairs={{0,25},{1,24},{2,27},{3,26},{4,29},{5,28},{6,31},{7,30},{8,17},{9,... | collective-permute-start | bytes 24584 | tf_op jit(solution)/shard_map/ppermute | solution.py:543
  16.4 0.3 collective-permute-start.6
  16.6 0.5 collective-permute-start.5
  17.1 1.7 %astro.3 = (f32[80,128]{1,0:T(8,128)S(1)}, f32[16,128]{1,0:T(8,128)S(1)}, bf16[128,4096]{1,0:T(8,128)(2,1)S(1)}) custom-call(f32[288,128]{1,0:T(8,128)S(1)} %chip.1.keep_ref.own_ref.refs_10_, f32[288,128]{1,0:T(8,128)S(1)} %collective-permute-done.3.keep_ref.other_ref.refs_11_, f32[80,128]{1,0:T(8,128)S(1)} %get-tuple-element.59.part_ref), custom_call_target="tpu_custom_call" | custom-call | tf_op jit(solution)/shard_map/astro/pallas_call | solution.py:516
  18.8 0.5 prepare.1
  19.4 0.3 collective-permute-done.5.refs_13_
  19.7 1.4 %step.3 = (f32[32,128]{1,0:T(8,128)S(1)}, f32[16,128]{1,0:T(8,128)S(1)}, f32[96,128]{1,0:T(8,128)S(1)}, f32[96,128]{1,0:T(8,128)S(1)}, f32[16,128]{1,0:T(8,128)S...) custom-call(f32[616,128]{1,0:T(8,128)S(1)} %get-tuple-element.50.refs_0_, ...), custom_call_target="tpu_custom_call" | custom-call | tf_op jit(solution)/shard_map/step/pallas_call | solution.py:516
  21.1 2.0 %collective-permute-start.10 = (f32[32,128]{1,0:T(8,128)S(1)}, f32[32,128]{1,0:T(8,128)S(1)}, u32[]{:S(2)}, u32[]{:S(2)}) collective-permute-start(f32[32,128]{1,0:T(8,128)S(1)} %get-tuple-element.63.refs_0_), channel_id=1, source_target_pairs={{0,7},{1,6},{2,5},{3,4},{4,3},{5,2},{6,1},{7,0},{8,15},{9,14},{10,... | collective-permute-start | bytes 49160 | tf_op jit(solution)/shard_map/ppermute | solution.py:543
  23.1 0.5 collective-permute-start.9
  23.6 1.6 %collective-permute-start.8 = (f32[32,128]{1,0:T(8,128)S(1)}, f32[32,128]{1,0:T(8,128)S(1)}, u32[]{:S(2)}, u32[]{:S(2)}) collective-permute-start(f32[32,128]{1,0:T(8,128)S(1)} %get-tuple-element.63.refs_0_), channel_id=1, source_target_pairs={{0,3},{1,2},{2,1},{3,0},{4,7},{5,6},{6,5},{7,4},{8,11},{9,10},{10,... | collective-permute-start | bytes 49160 | tf_op jit(solution)/shard_map/ppermute | solution.py:543
  25.2 0.9 %collective-permute-done.10.refs_3_ = f32[32,128]{1,0:T(8,128)S(1)} collective-permute-done((f32[32,128]{1,0:T(8,128)S(1)}, f32[32,128]{1,0:T(8,128)S(1)}, u32[]{:S(2)}, u32[]{:S(2)}) %collective-permute-start.10) | collective-permute-done | bytes 16416 | tf_op jit(solution)/shard_map/ppermute | solution.py:543
  26.1 1.1 %collective-permute-done.9.refs_2_ = f32[32,128]{1,0:T(8,128)S(1)} collective-permute-done((f32[32,128]{1,0:T(8,128)S(1)}, f32[32,128]{1,0:T(8,128)S(1)}, u32[]{:S(2)}, u32[]{:S(2)}) %collective-permute-start.9) | collective-permute-done | bytes 16416 | tf_op jit(solution)/shard_map/ppermute | solution.py:543
  27.3 2.1 %collective-permute-start.13 = (f32[16,128]{1,0:T(8,128)S(1)}, f32[16,128]{1,0:T(8,128)S(1)}, u32[]{:S(2)}, u32[]{:S(2)}) collective-permute-start(f32[16,128]{1,0:T(8,128)S(1)} %get-tuple-element.73.refs_16_), channel_id=1, source_target_pairs={{0,25},{1,24},{2,27},{3,26},{4,29},{5,28},{6,31},{7,30},{8,17},{9,... | collective-permute-start | bytes 24584 | tf_op jit(solution)/shard_map/ppermute | solution.py:543
  29.4 0.4 collective-permute-start.12
  29.8 0.9 %collective-permute-start.11 = (f32[16,128]{1,0:T(8,128)S(1)}, f32[16,128]{1,0:T(8,128)S(1)}, u32[]{:S(2)}, u32[]{:S(2)}) collective-permute-start(f32[16,128]{1,0:T(8,128)S(1)} %get-tuple-element.73.refs_16_), channel_id=1, source_target_pairs={{0,9},{1,8},{2,11},{3,10},{4,13},{5,12},{6,15},{7,14},{8,1},{9,0},... | collective-permute-start | bytes 24584 | tf_op jit(solution)/shard_map/ppermute | solution.py:543
  30.7 1.8 %astro.4 = (f32[80,128]{1,0:T(8,128)S(1)}, f32[16,128]{1,0:T(8,128)S(1)}) custom-call(f32[288,128]{1,0:T(8,128)S(1)} %chip.1.keep_ref.own_ref.refs_10_, f32[288,128]{1,0:T(8,128)S(1)} %collective-permute-done.3.keep_ref.other_ref.refs_11_, bf16[128,4096]{1,0:T(8,128)(2,1)S(1)} %get-tuple-element.58.own_table, ...), custom_call_target="tpu_custom_call" | custom-call | tf_op jit(solution)/shard_map/astro/pallas_call | solution.py:516
  32.5 0.4 collective-permute-done.11.refs_17_
  32.8 1.4 %step.4 = (f32[32,128]{1,0:T(8,128)S(1)}, f32[16,128]{1,0:T(8,128)S(1)}, f32[96,128]{1,0:T(8,128)S(1)}, f32[96,128]{1,0:T(8,128)S(1)}, f32[16,128]{1,0:T(8,128)S...) custom-call(f32[616,128]{1,0:T(8,128)S(1)} %get-tuple-element.50.refs_0_, ...), custom_call_target="tpu_custom_call" | custom-call | tf_op jit(solution)/shard_map/step/pallas_call | solution.py:516
  34.2 1.9 %collective-permute-start.16 = (f32[32,128]{1,0:T(8,128)S(1)}, f32[32,128]{1,0:T(8,128)S(1)}, u32[]{:S(2)}, u32[]{:S(2)}) collective-permute-start(f32[32,128]{1,0:T(8,128)S(1)} %get-tuple-element.74.refs_0_), channel_id=1, source_target_pairs={{0,7},{1,6},{2,5},{3,4},{4,3},{5,2},{6,1},{7,0},{8,15},{9,14},{10,... | collective-permute-start | bytes 49160 | tf_op jit(solution)/shard_map/ppermute | solution.py:543
  36.1 0.5 collective-permute-start.15
  36.6 1.7 %collective-permute-start.14 = (f32[32,128]{1,0:T(8,128)S(1)}, f32[32,128]{1,0:T(8,128)S(1)}, u32[]{:S(2)}, u32[]{:S(2)}) collective-permute-start(f32[32,128]{1,0:T(8,128)S(1)} %get-tuple-element.74.refs_0_), channel_id=1, source_target_pairs={{0,3},{1,2},{2,1},{3,0},{4,7},{5,6},{6,5},{7,4},{8,11},{9,10},{10,... | collective-permute-start | bytes 49160 | tf_op jit(solution)/shard_map/ppermute | solution.py:543
  38.3 1.0 %collective-permute-done.16.refs_3_ = f32[32,128]{1,0:T(8,128)S(1)} collective-permute-done((f32[32,128]{1,0:T(8,128)S(1)}, f32[32,128]{1,0:T(8,128)S(1)}, u32[]{:S(2)}, u32[]{:S(2)}) %collective-permute-start.16) | collective-permute-done | bytes 16416 | tf_op jit(solution)/shard_map/ppermute | solution.py:543
  39.3 1.1 %collective-permute-done.15.refs_2_ = f32[32,128]{1,0:T(8,128)S(1)} collective-permute-done((f32[32,128]{1,0:T(8,128)S(1)}, f32[32,128]{1,0:T(8,128)S(1)}, u32[]{:S(2)}, u32[]{:S(2)}) %collective-permute-start.15) | collective-permute-done | bytes 16416 | tf_op jit(solution)/shard_map/ppermute | solution.py:543
  40.4 2.0 %collective-permute-start.19 = (f32[16,128]{1,0:T(8,128)S(1)}, f32[16,128]{1,0:T(8,128)S(1)}, u32[]{:S(2)}, u32[]{:S(2)}) collective-permute-start(f32[16,128]{1,0:T(8,128)S(1)} %get-tuple-element.84.refs_16_), channel_id=1, source_target_pairs={{0,25},{1,24},{2,27},{3,26},{4,29},{5,28},{6,31},{7,30},{8,17},{9,... | collective-permute-start | bytes 24584 | tf_op jit(solution)/shard_map/ppermute | solution.py:543
  42.6 0.9 %collective-permute-start.17 = (f32[16,128]{1,0:T(8,128)S(1)}, f32[16,128]{1,0:T(8,128)S(1)}, u32[]{:S(2)}, u32[]{:S(2)}) collective-permute-start(f32[16,128]{1,0:T(8,128)S(1)} %get-tuple-element.84.refs_16_), channel_id=1, source_target_pairs={{0,9},{1,8},{2,11},{3,10},{4,13},{5,12},{6,15},{7,14},{8,1},{9,0},... | collective-permute-start | bytes 24584 | tf_op jit(solution)/shard_map/ppermute | solution.py:543
  43.4 1.8 %astro.5 = (f32[80,128]{1,0:T(8,128)S(1)}, f32[16,128]{1,0:T(8,128)S(1)}) custom-call(f32[288,128]{1,0:T(8,128)S(1)} %chip.1.keep_ref.own_ref.refs_10_, f32[288,128]{1,0:T(8,128)S(1)} %collective-permute-done.3.keep_ref.other_ref.refs_11_, bf16[128,4096]{1,0:T(8,128)(2,1)S(1)} %get-tuple-element.58.own_table, ...), custom_call_target="tpu_custom_call" | custom-call | tf_op jit(solution)/shard_map/astro/pallas_call | solution.py:516
  45.2 0.3 collective-permute-done.18.refs_18_
  45.6 0.9 %step.5 = (f32[8,128]{1,0:T(8,128)S(1)}, f32[16,128]{1,0:T(8,128)S(1)}, f32[96,128]{1,0:T(8,128)S(1)}, f32[96,128]{1,0:T(8,128)}, f32[16,128]{1,0:T(8,128)}, /*index=5*/f32[16,128]{1,0:T(8,128)}, f32[16,128]{1,0:T(8,128)}) custom-call(f32[616,128]{1,0:T(8,128)S(1)} %get-tuple-element.50.refs_0_, f32[616,128]{1,0:T(8,128)S(1)} %collective-permute-done.4.pack_ref.refs_1_, ...), custom_call_target="tpu_custom_call" | custom-call | tf_op jit(solution)/shard_map/step/pallas_call | solution.py:516
  46.5 1.8 %collective-permute-start.22 = (f32[8,128]{1,0:T(8,128)S(1)}, f32[8,128]{1,0:T(8,128)S(1)}, u32[]{:S(2)}, u32[]{:S(2)}) collective-permute-start(f32[8,128]{1,0:T(8,128)S(1)} %get-tuple-element.86.refs_0_), channel_id=1, source_target_pairs={{0,7},{1,6},{2,5},{3,4},{4,3},{5,2},{6,1},{7,0},{8,15},{9,14},{10,... | collective-permute-start | bytes 12296 | tf_op jit(solution)/shard_map/ppermute | solution.py:543
  48.3 0.5 collective-permute-start.21
  48.8 1.8 %collective-permute-start.20 = (f32[8,128]{1,0:T(8,128)S(1)}, f32[8,128]{1,0:T(8,128)S(1)}, u32[]{:S(2)}, u32[]{:S(2)}) collective-permute-start(f32[8,128]{1,0:T(8,128)S(1)} %get-tuple-element.86.refs_0_), channel_id=1, source_target_pairs={{0,3},{1,2},{2,1},{3,0},{4,7},{5,6},{6,5},{7,4},{8,11},{9,10},{10,... | collective-permute-start | bytes 12296 | tf_op jit(solution)/shard_map/ppermute | solution.py:543
  50.6 0.8 %collective-permute-done.22.refs_3_ = f32[8,128]{1,0:T(8,128)S(1)} collective-permute-done((f32[8,128]{1,0:T(8,128)S(1)}, f32[8,128]{1,0:T(8,128)S(1)}, u32[]{:S(2)}, u32[]{:S(2)}) %collective-permute-start.22) | collective-permute-done | bytes 4128 | tf_op jit(solution)/shard_map/ppermute | solution.py:543
  51.4 0.9 %collective-permute-done.21.refs_2_ = f32[8,128]{1,0:T(8,128)S(1)} collective-permute-done((f32[8,128]{1,0:T(8,128)S(1)}, f32[8,128]{1,0:T(8,128)S(1)}, u32[]{:S(2)}, u32[]{:S(2)}) %collective-permute-start.21) | collective-permute-done | bytes 4128 | tf_op jit(solution)/shard_map/ppermute | solution.py:543
  52.2 1.8 %collective-permute-start.25 = (f32[8,128]{1,0:T(8,128)S(1)}, f32[8,128]{1,0:T(8,128)S(1)}, u32[]{:S(2)}, u32[]{:S(2)}) collective-permute-start(f32[8,128]{1,0:T(8,128)S(1)} %sum.1.refs_0_), channel_id=1, source_target_pairs={{0,25},{1,24},{2,27},{3,26},{4,29},{5,28},{6,31},{7,30},{8,17},{9,... | collective-permute-start | bytes 12296 | tf_op jit(solution)/shard_map/ppermute | solution.py:543
  54.1 0.3 collective-permute-start.24
  54.4 1.1 %collective-permute-start.23 = (f32[8,128]{1,0:T(8,128)S(1)}, f32[8,128]{1,0:T(8,128)S(1)}, u32[]{:S(2)}, u32[]{:S(2)}) collective-permute-start(f32[8,128]{1,0:T(8,128)S(1)} %sum.1.refs_0_), channel_id=1, source_target_pairs={{0,9},{1,8},{2,11},{3,10},{4,13},{5,12},{6,15},{7,14},{8,1},{9,0},... | collective-permute-start | bytes 12296 | tf_op jit(solution)/shard_map/ppermute | solution.py:543
  55.6 0.7 %collective-permute-done.25.refs_3_ = f32[8,128]{1,0:T(8,128)S(1)} collective-permute-done((f32[8,128]{1,0:T(8,128)S(1)}, f32[8,128]{1,0:T(8,128)S(1)}, u32[]{:S(2)}, u32[]{:S(2)}) %collective-permute-start.25) | collective-permute-done | bytes 4128 | tf_op jit(solution)/shard_map/ppermute | solution.py:543
  56.2 0.9 %collective-permute-done.24.refs_2_ = f32[8,128]{1,0:T(8,128)S(1)} collective-permute-done((f32[8,128]{1,0:T(8,128)S(1)}, f32[8,128]{1,0:T(8,128)S(1)}, u32[]{:S(2)}, u32[]{:S(2)}) %collective-permute-start.24) | collective-permute-done | bytes 4128 | tf_op jit(solution)/shard_map/ppermute | solution.py:543
  57.1 0.3 collective-permute-done.23.refs_1_
  57.5 0.7 %last.1 = (f32[5,256]{1,0:T(8,128)}, f32[2,128]{1,0:T(2,128)}, f32[8,128]{1,0:T(8,128)}) custom-call(f32[16,128]{1,0:T(8,128)S(1)} %get-tuple-element.85.state_ref, f32[8,128]{1,0:T(8,128)S(1)} %sum.1.refs_0_, f32[8,128]{1,0:T(8,128)S(1)} %collective-permute-done.23.refs_1_, f32[8,128]{1,0:T(8,128)S(1)} %collective-permute-done.24.refs_2_, ...), custom_call_target="tpu_custom_call" | custom-call | tf_op jit(solution)/shard_map/last/pallas_call | solution.py:516
  (19 shorter events, 0.6 us)
Async XLA Ops:
  2.6 6.4 %collective-permute-start.2 = (f32[72,128]{1,0:T(8,128)S(1)}, f32[72,128]{1,0:T(8,128)S(1)}, u32[]{:S(2)}, u32[]{:S(2)}) collective-permute-start(f32[72,128]{1,0:T(8,128)S(1)} %get-tuple-element.48.refs_0_), channel_id=1, source_target_pairs={{0,7},{1,6},{2,5},{3,4},{4,3},{5,2},{6,1},{7,0},{8,15},{9,14},{10,... | collective-permute-start | bytes 110600 | tf_op jit(solution)/shard_map/ppermute | solution.py:543
  7.1 4.6 %collective-permute-start.1 = (f32[72,128]{1,0:T(8,128)S(1)}, f32[72,128]{1,0:T(8,128)S(1)}, u32[]{:S(2)}, u32[]{:S(2)}) collective-permute-start(f32[72,128]{1,0:T(8,128)S(1)} %get-tuple-element.48.refs_0_), channel_id=1, source_target_pairs={{0,5},{1,4},{2,7},{3,6},{4,1},{5,0},{6,3},{7,2},{8,13},{9,12},{10,... | collective-permute-start | bytes 110600 | tf_op jit(solution)/shard_map/ppermute | solution.py:543
  7.1 4.6 %collective-permute-start = (f32[72,128]{1,0:T(8,128)S(1)}, f32[72,128]{1,0:T(8,128)S(1)}, u32[]{:S(2)}, u32[]{:S(2)}) collective-permute-start(f32[72,128]{1,0:T(8,128)S(1)} %get-tuple-element.48.refs_0_), channel_id=1, source_target_pairs={{0,3},{1,2},{2,1},{3,0},{4,7},{5,6},{6,5},{7,4},{8,11},{9,10},{10,... | collective-permute-start | bytes 110600 | tf_op jit(solution)/shard_map/ppermute | solution.py:543
  11.8 1.8 %collective-permute-start.3 = (f32[288,128]{1,0:T(8,128)S(1)}, f32[288,128]{1,0:T(8,128)S(1)}, u32[]{:S(2)}, u32[]{:S(2)}) collective-permute-start(f32[288,128]{1,0:T(8,128)S(1)} %chip.1.keep_ref.own_ref.refs_10_), channel_id=1, source_target_pairs={{0,1},{1,0},{2,3},{3,2},{4,5},{5,4},{6,7},{7,6},{8,9},{9,8},{10,11... | collective-permute-start | bytes 442376 | tf_op jit(solution)/shard_map/ppermute | solution.py:530
  13.6 5.2 %collective-permute-start.4 = (f32[616,128]{1,0:T(8,128)S(1)}, f32[616,128]{1,0:T(8,128)S(1)}, u32[]{:S(2)}, u32[]{:S(2)}) collective-permute-start(f32[616,128]{1,0:T(8,128)S(1)} %get-tuple-element.50.refs_0_), channel_id=1, source_target_pairs={{0,1},{1,0},{2,3},{3,2},{4,5},{5,4},{6,7},{7,6},{8,9},{9,8},{10,11... | collective-permute-start | bytes 946184 | tf_op jit(solution)/shard_map/ppermute | solution.py:530
  13.9 5.4 %collective-permute-start.7 = (f32[16,128]{1,0:T(8,128)S(1)}, f32[16,128]{1,0:T(8,128)S(1)}, u32[]{:S(2)}, u32[]{:S(2)}) collective-permute-start(f32[16,128]{1,0:T(8,128)S(1)} %group.3.refs_12_), channel_id=1, source_target_pairs={{0,25},{1,24},{2,27},{3,26},{4,29},{5,28},{6,31},{7,30},{8,17},{9,... | collective-permute-start | bytes 24584 | tf_op jit(solution)/shard_map/ppermute | solution.py:543
  16.4 3.1 %collective-permute-start.6 = (f32[16,128]{1,0:T(8,128)S(1)}, f32[16,128]{1,0:T(8,128)S(1)}, u32[]{:S(2)}, u32[]{:S(2)}) collective-permute-start(f32[16,128]{1,0:T(8,128)S(1)} %group.3.refs_12_), channel_id=1, source_target_pairs={{0,17},{1,16},{2,19},{3,18},{4,21},{5,20},{6,23},{7,22},{8,25},{9,... | collective-permute-start | bytes 24584 | tf_op jit(solution)/shard_map/ppermute | solution.py:543
  16.6 3.1 %collective-permute-start.5 = (f32[16,128]{1,0:T(8,128)S(1)}, f32[16,128]{1,0:T(8,128)S(1)}, u32[]{:S(2)}, u32[]{:S(2)}) collective-permute-start(f32[16,128]{1,0:T(8,128)S(1)} %group.3.refs_12_), channel_id=1, source_target_pairs={{0,9},{1,8},{2,11},{3,10},{4,13},{5,12},{6,15},{7,14},{8,1},{9,0},... | collective-permute-start | bytes 24584 | tf_op jit(solution)/shard_map/ppermute | solution.py:543
  21.1 5.0 %collective-permute-start.10 = (f32[32,128]{1,0:T(8,128)S(1)}, f32[32,128]{1,0:T(8,128)S(1)}, u32[]{:S(2)}, u32[]{:S(2)}) collective-permute-start(f32[32,128]{1,0:T(8,128)S(1)} %get-tuple-element.63.refs_0_), channel_id=1, source_target_pairs={{0,7},{1,6},{2,5},{3,4},{4,3},{5,2},{6,1},{7,0},{8,15},{9,14},{10,... | collective-permute-start | bytes 49160 | tf_op jit(solution)/shard_map/ppermute | solution.py:543
  23.1 4.1 %collective-permute-start.9 = (f32[32,128]{1,0:T(8,128)S(1)}, f32[32,128]{1,0:T(8,128)S(1)}, u32[]{:S(2)}, u32[]{:S(2)}) collective-permute-start(f32[32,128]{1,0:T(8,128)S(1)} %get-tuple-element.63.refs_0_), channel_id=1, source_target_pairs={{0,5},{1,4},{2,7},{3,6},{4,1},{5,0},{6,3},{7,2},{8,13},{9,12},{10,... | collective-permute-start | bytes 49160 | tf_op jit(solution)/shard_map/ppermute | solution.py:543
  23.6 3.6 %collective-permute-start.8 = (f32[32,128]{1,0:T(8,128)S(1)}, f32[32,128]{1,0:T(8,128)S(1)}, u32[]{:S(2)}, u32[]{:S(2)}) collective-permute-start(f32[32,128]{1,0:T(8,128)S(1)} %get-tuple-element.63.refs_0_), channel_id=1, source_target_pairs={{0,3},{1,2},{2,1},{3,0},{4,7},{5,6},{6,5},{7,4},{8,11},{9,10},{10,... | collective-permute-start | bytes 49160 | tf_op jit(solution)/shard_map/ppermute | solution.py:543
  27.3 5.2 %collective-permute-start.13 = (f32[16,128]{1,0:T(8,128)S(1)}, f32[16,128]{1,0:T(8,128)S(1)}, u32[]{:S(2)}, u32[]{:S(2)}) collective-permute-start(f32[16,128]{1,0:T(8,128)S(1)} %get-tuple-element.73.refs_16_), channel_id=1, source_target_pairs={{0,25},{1,24},{2,27},{3,26},{4,29},{5,28},{6,31},{7,30},{8,17},{9,... | collective-permute-start | bytes 24584 | tf_op jit(solution)/shard_map/ppermute | solution.py:543
  29.4 3.1 %collective-permute-start.12 = (f32[16,128]{1,0:T(8,128)S(1)}, f32[16,128]{1,0:T(8,128)S(1)}, u32[]{:S(2)}, u32[]{:S(2)}) collective-permute-start(f32[16,128]{1,0:T(8,128)S(1)} %get-tuple-element.73.refs_16_), channel_id=1, source_target_pairs={{0,17},{1,16},{2,19},{3,18},{4,21},{5,20},{6,23},{7,22},{8,25},{9,... | collective-permute-start | bytes 24584 | tf_op jit(solution)/shard_map/ppermute | solution.py:543
  29.8 3.1 %collective-permute-start.11 = (f32[16,128]{1,0:T(8,128)S(1)}, f32[16,128]{1,0:T(8,128)S(1)}, u32[]{:S(2)}, u32[]{:S(2)}) collective-permute-start(f32[16,128]{1,0:T(8,128)S(1)} %get-tuple-element.73.refs_16_), channel_id=1, source_target_pairs={{0,9},{1,8},{2,11},{3,10},{4,13},{5,12},{6,15},{7,14},{8,1},{9,0},... | collective-permute-start | bytes 24584 | tf_op jit(solution)/shard_map/ppermute | solution.py:543
  34.2 5.0 %collective-permute-start.16 = (f32[32,128]{1,0:T(8,128)S(1)}, f32[32,128]{1,0:T(8,128)S(1)}, u32[]{:S(2)}, u32[]{:S(2)}) collective-permute-start(f32[32,128]{1,0:T(8,128)S(1)} %get-tuple-element.74.refs_0_), channel_id=1, source_target_pairs={{0,7},{1,6},{2,5},{3,4},{4,3},{5,2},{6,1},{7,0},{8,15},{9,14},{10,... | collective-permute-start | bytes 49160 | tf_op jit(solution)/shard_map/ppermute | solution.py:543
  36.1 4.3 %collective-permute-start.15 = (f32[32,128]{1,0:T(8,128)S(1)}, f32[32,128]{1,0:T(8,128)S(1)}, u32[]{:S(2)}, u32[]{:S(2)}) collective-permute-start(f32[32,128]{1,0:T(8,128)S(1)} %get-tuple-element.74.refs_0_), channel_id=1, source_target_pairs={{0,5},{1,4},{2,7},{3,6},{4,1},{5,0},{6,3},{7,2},{8,13},{9,12},{10,... | collective-permute-start | bytes 49160 | tf_op jit(solution)/shard_map/ppermute | solution.py:543
  36.6 3.8 %collective-permute-start.14 = (f32[32,128]{1,0:T(8,128)S(1)}, f32[32,128]{1,0:T(8,128)S(1)}, u32[]{:S(2)}, u32[]{:S(2)}) collective-permute-start(f32[32,128]{1,0:T(8,128)S(1)} %get-tuple-element.74.refs_0_), channel_id=1, source_target_pairs={{0,3},{1,2},{2,1},{3,0},{4,7},{5,6},{6,5},{7,4},{8,11},{9,10},{10,... | collective-permute-start | bytes 49160 | tf_op jit(solution)/shard_map/ppermute | solution.py:543
  40.4 4.8 %collective-permute-start.19 = (f32[16,128]{1,0:T(8,128)S(1)}, f32[16,128]{1,0:T(8,128)S(1)}, u32[]{:S(2)}, u32[]{:S(2)}) collective-permute-start(f32[16,128]{1,0:T(8,128)S(1)} %get-tuple-element.84.refs_16_), channel_id=1, source_target_pairs={{0,25},{1,24},{2,27},{3,26},{4,29},{5,28},{6,31},{7,30},{8,17},{9,... | collective-permute-start | bytes 24584 | tf_op jit(solution)/shard_map/ppermute | solution.py:543
  42.4 3.1 %collective-permute-start.18 = (f32[16,128]{1,0:T(8,128)S(1)}, f32[16,128]{1,0:T(8,128)S(1)}, u32[]{:S(2)}, u32[]{:S(2)}) collective-permute-start(f32[16,128]{1,0:T(8,128)S(1)} %get-tuple-element.84.refs_16_), channel_id=1, source_target_pairs={{0,17},{1,16},{2,19},{3,18},{4,21},{5,20},{6,23},{7,22},{8,25},{9,... | collective-permute-start | bytes 24584 | tf_op jit(solution)/shard_map/ppermute | solution.py:543
  42.6 3.1 %collective-permute-start.17 = (f32[16,128]{1,0:T(8,128)S(1)}, f32[16,128]{1,0:T(8,128)S(1)}, u32[]{:S(2)}, u32[]{:S(2)}) collective-permute-start(f32[16,128]{1,0:T(8,128)S(1)} %get-tuple-element.84.refs_16_), channel_id=1, source_target_pairs={{0,9},{1,8},{2,11},{3,10},{4,13},{5,12},{6,15},{7,14},{8,1},{9,0},... | collective-permute-start | bytes 24584 | tf_op jit(solution)/shard_map/ppermute | solution.py:543
  46.5 4.8 %collective-permute-start.22 = (f32[8,128]{1,0:T(8,128)S(1)}, f32[8,128]{1,0:T(8,128)S(1)}, u32[]{:S(2)}, u32[]{:S(2)}) collective-permute-start(f32[8,128]{1,0:T(8,128)S(1)} %get-tuple-element.86.refs_0_), channel_id=1, source_target_pairs={{0,7},{1,6},{2,5},{3,4},{4,3},{5,2},{6,1},{7,0},{8,15},{9,14},{10,... | collective-permute-start | bytes 12296 | tf_op jit(solution)/shard_map/ppermute | solution.py:543
  48.3 3.9 %collective-permute-start.21 = (f32[8,128]{1,0:T(8,128)S(1)}, f32[8,128]{1,0:T(8,128)S(1)}, u32[]{:S(2)}, u32[]{:S(2)}) collective-permute-start(f32[8,128]{1,0:T(8,128)S(1)} %get-tuple-element.86.refs_0_), channel_id=1, source_target_pairs={{0,5},{1,4},{2,7},{3,6},{4,1},{5,0},{6,3},{7,2},{8,13},{9,12},{10,... | collective-permute-start | bytes 12296 | tf_op jit(solution)/shard_map/ppermute | solution.py:543
  48.8 3.4 %collective-permute-start.20 = (f32[8,128]{1,0:T(8,128)S(1)}, f32[8,128]{1,0:T(8,128)S(1)}, u32[]{:S(2)}, u32[]{:S(2)}) collective-permute-start(f32[8,128]{1,0:T(8,128)S(1)} %get-tuple-element.86.refs_0_), channel_id=1, source_target_pairs={{0,3},{1,2},{2,1},{3,0},{4,7},{5,6},{6,5},{7,4},{8,11},{9,10},{10,... | collective-permute-start | bytes 12296 | tf_op jit(solution)/shard_map/ppermute | solution.py:543
  52.2 4.0 %collective-permute-start.25 = (f32[8,128]{1,0:T(8,128)S(1)}, f32[8,128]{1,0:T(8,128)S(1)}, u32[]{:S(2)}, u32[]{:S(2)}) collective-permute-start(f32[8,128]{1,0:T(8,128)S(1)} %sum.1.refs_0_), channel_id=1, source_target_pairs={{0,25},{1,24},{2,27},{3,26},{4,29},{5,28},{6,31},{7,30},{8,17},{9,... | collective-permute-start | bytes 12296 | tf_op jit(solution)/shard_map/ppermute | solution.py:543
  54.1 3.0 %collective-permute-start.24 = (f32[8,128]{1,0:T(8,128)S(1)}, f32[8,128]{1,0:T(8,128)S(1)}, u32[]{:S(2)}, u32[]{:S(2)}) collective-permute-start(f32[8,128]{1,0:T(8,128)S(1)} %sum.1.refs_0_), channel_id=1, source_target_pairs={{0,17},{1,16},{2,19},{3,18},{4,21},{5,20},{6,23},{7,22},{8,25},{9,... | collective-permute-start | bytes 12296 | tf_op jit(solution)/shard_map/ppermute | solution.py:543
  54.4 3.0 %collective-permute-start.23 = (f32[8,128]{1,0:T(8,128)S(1)}, f32[8,128]{1,0:T(8,128)S(1)}, u32[]{:S(2)}, u32[]{:S(2)}) collective-permute-start(f32[8,128]{1,0:T(8,128)S(1)} %sum.1.refs_0_), channel_id=1, source_target_pairs={{0,9},{1,8},{2,11},{3,10},{4,13},{5,12},{6,15},{7,14},{8,1},{9,0},... | collective-permute-start | bytes 12296 | tf_op jit(solution)/shard_map/ppermute | solution.py:543
